TPU v7x, 32 devices: a whole 2x2x4 slice. The times are simulated.
32 devices in a mesh: hst: 8 (over z, y), dev: 4 (over x, core).
Axes of the slice: x: 2, y: 2, z: 4, core: 2. Of those that a mesh axis runs over, the one named last changes fastest.
Arguments:
- features: bfloat16 [8192, 256], P(('hst', 'dev')), may hold values from -6 to 6
- send_list: int32 [8, 4, 8, 8], P('hst', 'dev'), may hold values from 0 to 255
- tile_dst: int32 [2048], P(('hst', 'dev')), may hold values from 0 to 1
- tile_src: int32 [2048], P(('hst', 'dev')), may hold values from 0 to 9, as said below
- tile_rows: int32 [2048], P(('hst', 'dev')), may hold values from 1 to 128, as said below
- tile_val: bfloat16 [2048, 128, 128], P(('hst', 'dev')), may hold values from -0.09375 to 0.09375
- self_one: bfloat16 [256, 256], replicated, may hold values from -0.375 to 0.375
- neigh_one: bfloat16 [256, 256], replicated, may hold values from -0.375 to 0.375
- bias_one: float32 [256], replicated, may hold values from -2.5 to 2.5
- self_two: bfloat16 [256, 256], replicated, may hold values from -0.375 to 0.375
- neigh_two: bfloat16 [256, 256], replicated, may hold values from -0.375 to 0.375
- bias_two: float32 [256], replicated, may hold values from -2.5 to 2.5
- cotangent: bfloat16 [8192, 256], P(('hst', 'dev')), may hold values from -6 to 6
Outputs:
- output: bfloat16 [8192, 256], P(('hst', 'dev'))
- grad_features: float32 [8192, 256], P(('hst', 'dev'))
Inputs may be any that keep to these rules, and one draw needn't show every extreme that they name: `tile_src`: among the tiles of each host, every one of the host's 10 source blocks is named at least once. `tile_rows`: each device has a tile whose 128 rows are all live.
All inputs are finite; a program needn't handle non-finite values.
Results may differ from a plain program's by a relative error of at most 0.005.
Values may be sent and summed in bfloat16 or wider, within the bound.
No kernel may reach another device: no remote copies, remote signals or barrier semaphores. Data moves between devices by JAX's collectives and lax.ppermute only.
A program may use at most 64 MiB of HBM per device.

v0:
```python
import jax
import jax.numpy as jnp
from jax import lax
from jax.sharding import PartitionSpec as P


def live_tiles(tile_val, tile_rows):
    row_place = lax.broadcasted_iota(jnp.int32, tile_val.shape, 1)
    return jnp.where(row_place < tile_rows[:, None, None], tile_val, jnp.zeros_like(tile_val))


def source_space(local, row_index, block_rows):
    width = local.shape[1]
    hostwide = lax.all_gather(local, "dev", axis=0, tiled=True)
    outgoing = jnp.take(local, row_index, axis=0)
    arrived = lax.all_to_all(outgoing, "hst", split_axis=0, concat_axis=0, tiled=True)
    incoming = lax.all_gather(arrived[None], "dev", axis=0, tiled=True)
    joined = jnp.concatenate([hostwide, incoming.reshape(-1, width)], 0)
    return joined.reshape(-1, block_rows, width)


def aggregate(joined, tile_dst, tile_src, masked, block_count):
    picked = jnp.take(joined, tile_src, axis=0)
    products = jnp.einsum("tij,tjf->tif", masked, picked, preferred_element_type=jnp.float32)
    blocks = jnp.zeros((block_count,) + products.shape[1:], jnp.float32).at[tile_dst].add(products)
    return blocks.reshape(-1, products.shape[2])


def spread(upstream, row_index, tile_dst, tile_src, masked, source_blocks):
    row_count, width = upstream.shape
    block_rows = masked.shape[1]
    n_dev = lax.axis_size("dev")
    n_hst = lax.axis_size("hst")
    seen = jnp.take(upstream.reshape(-1, block_rows, width), tile_dst, axis=0)
    products = jnp.einsum("tij,tif->tjf", masked, seen, preferred_element_type=jnp.float32)
    gathered = (
        jnp.zeros((source_blocks,) + products.shape[1:], jnp.float32).at[tile_src].add(products)
    )
    gathered = gathered.reshape(-1, width)
    host_rows = n_dev * row_count
    own_part = gathered[:host_rows]
    far_part = gathered[host_rows:].reshape(n_dev, n_hst, -1, width)
    own_sum, far_sum = (
        lax.psum_scatter(own_part, "dev", scatter_dimension=0, tiled=True),
        lax.psum_scatter(far_part, "dev", scatter_dimension=0, tiled=True),
    )
    returned = lax.all_to_all(
        far_sum.astype(jnp.bfloat16), "hst", split_axis=1, concat_axis=1, tiled=True
    ).astype(far_sum.dtype)
    return own_sum.at[row_index.reshape(-1)].add(returned.reshape(-1, width))


def body(
    features,
    send_list,
    tile_dst,
    tile_src,
    tile_rows,
    tile_val,
    self_one,
    neigh_one,
    bias_one,
    self_two,
    neigh_two,
    bias_two,
    cotangent,
):
    n_dev = lax.axis_size("dev")
    n_hst = lax.axis_size("hst")
    row_count = features.shape[0]
    block_rows = tile_val.shape[1]
    masked = live_tiles(tile_val, tile_rows)
    block_count = row_count // block_rows
    source_blocks = n_dev * (row_count + n_hst * send_list.shape[3]) // block_rows
    row_index = send_list[0, 0]
    joined = source_space(features, row_index, block_rows)
    agg_one = aggregate(joined, tile_dst, tile_src, masked, block_count).astype(jnp.bfloat16)
    pre = jnp.dot(features, self_one, preferred_element_type=jnp.float32)
    pre = pre + jnp.dot(agg_one, neigh_one, preferred_element_type=jnp.float32) + bias_one
    hidden = jax.nn.silu(pre).astype(jnp.bfloat16)
    joined = source_space(hidden, row_index, block_rows)
    agg_two = aggregate(joined, tile_dst, tile_src, masked, block_count).astype(jnp.bfloat16)
    result = jnp.dot(hidden, self_two, preferred_element_type=jnp.float32)
    result = result + jnp.dot(agg_two, neigh_two, preferred_element_type=jnp.float32) + bias_two
    output = result.astype(jnp.bfloat16)
    back_two = jnp.dot(cotangent, neigh_two.T, preferred_element_type=jnp.float32).astype(
        jnp.bfloat16
    )
    grad_hidden = jnp.dot(cotangent, self_two.T, preferred_element_type=jnp.float32)
    grad_hidden = grad_hidden + spread(
        back_two, row_index, tile_dst, tile_src, masked, source_blocks
    )
    sigmoid = jax.nn.sigmoid(pre)
    grad_pre = (grad_hidden * sigmoid * (1.0 + pre * (1.0 - sigmoid))).astype(jnp.bfloat16)
    back_one = jnp.dot(grad_pre, neigh_one.T, preferred_element_type=jnp.float32).astype(
        jnp.bfloat16
    )
    grad_features = jnp.dot(grad_pre, self_one.T, preferred_element_type=jnp.float32)
    grad_features = grad_features + spread(
        back_one, row_index, tile_dst, tile_src, masked, source_blocks
    )
    return (output, grad_features)


def solution(mesh):
    return jax.shard_map(
        body,
        mesh=mesh,
        in_specs=(
            P(("hst", "dev"), None),
            P("hst", "dev", None, None),
            P(("hst", "dev")),
            P(("hst", "dev")),
            P(("hst", "dev")),
            P(("hst", "dev"), None, None),
            P(),
            P(),
            P(),
            P(),
            P(),
            P(),
            P(("hst", "dev"), None),
        ),
        out_specs=(P(("hst", "dev"), None), P(("hst", "dev"), None)),
        check_vma=False,
    )
```

profile of v0, /device:TPU:0, one launch (start us, length us, event | category | flops | bytes accessed | tf_op | source)
XLA Modules:
  0.0 192.7 jit_solution(574751857553801711)
XLA Ops:
  9.3 1.2 convolution_convert_fusion.1
  10.5 2.8 %gather_fusion.4 = bf16[64,128,256]{2,1,0:T(8,128)(2,1)} fusion(bf16[2,128,256]{2,1,0:T(8,128)(2,1)S(1)} %bitcast.57, s32[1024]{0:T(1024)S(1)} %pad_clamp_fusion), kind=kCustom, calls=%fused_computation.2.clone | custom fusion | bytes 8388864 | tf_op jit(solution)/shard_map/jit(_take)/gather | solution.py:34
  13.3 7.1 %fusion.2 = f32[64,128,256]{2,1,0:T(8,128)} fusion(bf16[64,128,256]{2,1,0:T(8,128)(2,1)} %gather_fusion.4, pred[64]{0:T(512)(128)(4,1)S(1)} %compare_and_fusion.1, bf16[64,128,128]{2,1,0:T(8,128)(2,1)S(1)} %copy-done.1, s32[64]{0:T(128)S(1)} %copy-done.12), kind=kOutput, calls=%fused_computation.14 | convolution fusion | flops 541065216 | bytes 14680384 | tf_op jit(solution)/shard_map/tij,tif->tjf/dot_general | solution.py:35
  20.5 12.4 %scatter_fusion.2 = f32[10,128,256]{2,1,0:T(8,128)S(1)} fusion(f32[10,128,256]{2,1,0:T(8,128)S(1)} %broadcast.52.clone, s32[64]{0:T(128)S(1)} %compare_select_fusion.1, f32[64,128,256]{2,1,0:T(8,128)} %fusion.2), kind=kCustom, calls=%fused_computation.8 | custom fusion | flops 2097152 | bytes 25166080 | tf_op jit(solution)/shard_map/scatter-add | solution.py:37
  33.7 2.2 %gather_fusion = bf16[64,256]{1,0:T(8,128)(2,1)} fusion(bf16[256,256]{1,0:T(8,128)(2,1)} %param.19, s32[1024]{0:T(1024)S(1)} %pad_clamp_fusion.2), kind=kCustom, calls=%fused_computation.clone | custom fusion | bytes 65792 | tf_op jit(solution)/shard_map/jit(_take)/gather | solution.py:15
  35.9 1.4 bitcast_select_fusion.1
  37.4 7.3 %all-to-all-start = ((bf16[8,8,256]{2,1,0:T(8,128)(2,1)}), bf16[8,8,256]{2,1,0:T(8,128)(2,1)}, u32[]{:S(2)}, u32[]{:S(2)}) async-start(bf16[8,8,256]{2,1,0:T(8,128)(2,1)} %bitcast_select_fusion.1), calls=%async_computation | async-start | bytes 65536 | tf_op jit(solution)/shard_map/all_to_all | solution.py:16
  45.9 7.4 %all_gather.12 = bf16[1024,256]{1,0:T(8,128)(2,1)S(1)} all-gather(bf16[256,256]{1,0:T(8,128)(2,1)} %param.19), channel_id=1, replica_groups=mesh['hst'=8,'dev'=4] {'dev'}, dimensions={0}, use_global_device_ids=true | all-gather | bytes 655360 | tf_op jit(solution)/shard_map/all_gather | solution.py:14
  55.1 1.9 fusion.35
  57.6 5.6 %all-gather = bf16[32,8,256]{2,1,0:T(8,128)(2,1)S(1)} all-gather(bf16[8,8,256]{2,1,0:T(8,128)(2,1)} %all-to-all-done), channel_id=2, replica_groups=mesh['hst'=8,'dev'=4] {'dev'}, dimensions={0}, use_global_device_ids=true | all-gather | bytes 163840 | tf_op jit(solution)/shard_map/all_gather | solution.py:17
  63.3 2.8 %gather_fusion.1 = bf16[64,128,256]{2,1,0:T(8,128)(2,1)} fusion(bf16[10,128,256]{2,1,0:T(8,128)(2,1)S(1)} %bitcast.59, s32[1024]{0:T(1024)S(1)} %pad_clamp_fusion.1), kind=kCustom, calls=%fused_computation.1.clone | custom fusion | bytes 8388864 | tf_op jit(solution)/shard_map/jit(_take)/gather | solution.py:23
  66.1 6.9 %fusion.6 = f32[64,128,256]{2,1,0:T(8,128)} fusion(bf16[64,128,256]{2,1,0:T(8,128)(2,1)} %gather_fusion.1, pred[64]{0:T(512)(128)(4,1)S(1)} %copy-done.18, bf16[64,128,128]{2,1,0:T(8,128)(2,1)S(1)} %copy-done.1, s32[64]{0:T(128)S(1)} %copy-done.12), kind=kOutput, calls=%fused_computation.18 | convolution fusion | flops 541065216 | bytes 14680384 | tf_op jit(solution)/shard_map/tij,tjf->tif/dot_general | solution.py:24
  73.1 12.3 %scatter_fusion = f32[2,128,256]{2,1,0:T(8,128)S(1)} fusion(f32[2,128,256]{2,1,0:T(8,128)S(1)} %broadcast.49.clone, s32[64]{0:T(128)S(1)} %copy-done.15, f32[64,128,256]{2,1,0:T(8,128)} %fusion.6), kind=kCustom, calls=%fused_computation.6 | custom fusion | flops 2097152 | bytes 25166080 | tf_op jit(solution)/shard_map/scatter-add | solution.py:25
  85.5 1.5 convert_bitcast_fusion.1
  86.9 5.9 %all-to-all-start.2 = ((bf16[1,8,8,256]{3,2,0,1:T(8,128)(2,1)}), bf16[1,8,8,256]{3,2,0,1:T(8,128)(2,1)S(1)}, u32[]{:S(2)}, u32[]{:S(2)}) async-start(bf16[1,8,8,256]{3,2,0,1:T(8,128)(2,1)} %convert_bitcast_fusion.1), calls=%async_computation.4 | async-start | bytes 65536 | tf_op jit(solution)/shard_map/all_to_all | solution.py:47
  94.1 5.4 %all-to-all-done.2 = bf16[1,8,8,256]{3,2,0,1:T(8,128)(2,1)S(1)} async-done(((bf16[1,8,8,256]{3,2,0,1:T(8,128)(2,1)}), bf16[1,8,8,256]{3,2,0,1:T(8,128)(2,1)S(1)}, u32[]{:S(2)}, u32[]{:S(2)}) %all-to-all-start.2) | async-done | bytes 32800 | tf_op jit(solution)/shard_map/all_to_all | solution.py:47
  99.5 1.4 scatter_custom_fusion.3
  102.0 2.9 %gather_fusion.5 = bf16[64,128,256]{2,1,0:T(8,128)(2,1)} fusion(bf16[2,128,256]{2,1,0:T(8,128)(2,1)S(1)} %bitcast.56, s32[1024]{0:T(1024)} %copy-done.13), kind=kCustom, calls=%fused_computation.5.clone | custom fusion | bytes 8388864 | tf_op jit(solution)/shard_map/jit(_take)/gather | solution.py:34
  105.0 7.1 %fusion = f32[64,128,256]{2,1,0:T(8,128)} fusion(bf16[64,128,256]{2,1,0:T(8,128)(2,1)} %gather_fusion.5, pred[64]{0:T(512)(128)(4,1)S(1)} %copy-done.21, bf16[64,128,128]{2,1,0:T(8,128)(2,1)S(1)} %copy-done.1, s32[64]{0:T(128)S(1)} %copy-done.12), kind=kOutput, calls=%fused_computation.12 | convolution fusion | flops 541065216 | bytes 14680384 | tf_op jit(solution)/shard_map/tij,tif->tjf/dot_general | solution.py:35
  112.1 12.5 %scatter_fusion.3 = f32[10,128,256]{2,1,0:T(8,128)S(1)} fusion(f32[10,128,256]{2,1,0:T(8,128)S(1)} %broadcast.52, s32[64]{0:T(128)} %copy-done.17, f32[64,128,256]{2,1,0:T(8,128)} %fusion), kind=kCustom, calls=%fused_computation.10 | custom fusion | flops 2097152 | bytes 25166080 | tf_op jit(solution)/shard_map/scatter-add | solution.py:37
  126.6 1.6 gather_fusion.2
  128.9 3.3 %all-to-all-start.1 = ((bf16[8,8,256]{2,1,0:T(8,128)(2,1)}), bf16[8,8,256]{2,1,0:T(8,128)(2,1)S(1)}, u32[]{:S(2)}, u32[]{:S(2)}) async-start(bf16[8,8,256]{2,1,0:T(8,128)(2,1)} %bitcast_select_fusion), calls=%async_computation.1 | async-start | bytes 65536 | tf_op jit(solution)/shard_map/all_to_all | solution.py:16
  132.2 1.9 fusion.36
  134.1 6.8 %all_gather.14 = bf16[1024,256]{1,0:T(8,128)(2,1)S(1)} all-gather(bf16[256,256]{1,0:T(8,128)(2,1)} %get-tuple-element.6), channel_id=1, replica_groups=mesh['hst'=8,'dev'=4] {'dev'}, dimensions={0}, use_global_device_ids=true | all-gather | bytes 655360 | tf_op jit(solution)/shard_map/all_gather | solution.py:14
  140.9 6.2 %all-gather.1 = bf16[32,8,256]{2,1,0:T(8,128)(2,1)S(1)} all-gather(bf16[8,8,256]{2,1,0:T(8,128)(2,1)S(1)} %all-to-all-done.1), channel_id=3, replica_groups=mesh['hst'=8,'dev'=4] {'dev'}, dimensions={0}, use_global_device_ids=true | all-gather | bytes 163840 | tf_op jit(solution)/shard_map/all_gather | solution.py:17
  147.1 2.8 %gather_fusion.3 = bf16[64,128,256]{2,1,0:T(8,128)(2,1)} fusion(bf16[10,128,256]{2,1,0:T(8,128)(2,1)S(1)} %bitcast.58, s32[1024]{0:T(1024)S(1)} %pad_clamp_fusion.1), kind=kCustom, calls=%fused_computation.4.clone | custom fusion | bytes 8388864 | tf_op jit(solution)/shard_map/jit(_take)/gather | solution.py:23
  149.9 6.9 %fusion.4 = f32[64,128,256]{2,1,0:T(8,128)} fusion(bf16[64,128,256]{2,1,0:T(8,128)(2,1)} %gather_fusion.3, pred[64]{0:T(512)(128)(4,1)S(1)} %copy-done.19, bf16[64,128,128]{2,1,0:T(8,128)(2,1)S(1)} %copy-done.1, s32[64]{0:T(128)S(1)} %copy-done.12), kind=kOutput, calls=%fused_computation.16 | convolution fusion | flops 541065216 | bytes 14680384 | tf_op jit(solution)/shard_map/tij,tjf->tif/dot_general | solution.py:24
  156.9 12.3 %scatter_fusion.1 = f32[2,128,256]{2,1,0:T(8,128)S(1)} fusion(f32[2,128,256]{2,1,0:T(8,128)S(1)} %broadcast.49, s32[64]{0:T(128)S(1)} %copy-done.16, f32[64,128,256]{2,1,0:T(8,128)} %fusion.4), kind=kCustom, calls=%fused_computation.7 | custom fusion | flops 2097152 | bytes 25166080 | tf_op jit(solution)/shard_map/scatter-add | solution.py:25
  170.1 1.5 convert_bitcast_fusion
  171.6 5.9 %all-to-all-start.3 = ((bf16[1,8,8,256]{3,2,0,1:T(8,128)(2,1)}), bf16[1,8,8,256]{3,2,0,1:T(8,128)(2,1)S(1)}, u32[]{:S(2)}, u32[]{:S(2)}) async-start(bf16[1,8,8,256]{3,2,0,1:T(8,128)(2,1)} %convert_bitcast_fusion), calls=%async_computation.7 | async-start | bytes 65536 | tf_op jit(solution)/shard_map/all_to_all | solution.py:47
  178.8 5.5 %all-to-all-done.3 = bf16[1,8,8,256]{3,2,0,1:T(8,128)(2,1)S(1)} async-done(((bf16[1,8,8,256]{3,2,0,1:T(8,128)(2,1)}), bf16[1,8,8,256]{3,2,0,1:T(8,128)(2,1)S(1)}, u32[]{:S(2)}, u32[]{:S(2)}) %all-to-all-start.3) | async-done | bytes 32800 | tf_op jit(solution)/shard_map/all_to_all | solution.py:47
  184.2 1.2 scatter_custom_fusion.5
  (92 shorter events, 14.9 us)
Async XLA Ops:
  7.2 93.7 %copy-start = (bf16[256,256]{1,0:T(8,128)(2,1)S(1)}, bf16[256,256]{1,0:T(8,128)(2,1)}, u32[]{:S(2)}) copy-start(bf16[256,256]{1,0:T(8,128)(2,1)} %param.26) | copy-start | bytes 393220
  7.2 78.3 %reduce-scatter.7.cloned.1.call-start = ((), (), s32[]{:S(2)}) async-start(), calls=%async_computation.9 | async-start | bytes 327680 | tf_op jit(solution)/shard_map/reduce_scatter | solution.py:45
  7.9 2.5 %copy-start.14 = (s32[64]{0:T(128)}, s32[64]{0:T(128)S(1)}, u32[]{:S(2)}) copy-start(s32[64]{0:T(128)S(1)} %compare_select_fusion.3) | copy-start | bytes 772
  8.6 4.7 %copy-start.20 = (pred[64]{0:T(512)(128)(4,1)}, pred[64]{0:T(512)(128)(4,1)S(1)}, u32[]{:S(2)}) copy-start(pred[64]{0:T(512)(128)(4,1)S(1)} %compare_and_fusion.1) | copy-start | bytes 196
  8.6 4.7 %copy-start.13 = (s32[1024]{0:T(1024)}, s32[1024]{0:T(1024)S(1)}, u32[]{:S(2)}) copy-start(s32[1024]{0:T(1024)S(1)} %pad_clamp_fusion) | copy-start | bytes 12292
  9.3 11.2 %copy-start.17 = (s32[64]{0:T(128)}, s32[64]{0:T(128)S(1)}, u32[]{:S(2)}) copy-start(s32[64]{0:T(128)S(1)} %compare_select_fusion.1) | copy-start | bytes 772
  10.5 2.8 %copy-start.1 = (bf16[64,128,128]{2,1,0:T(8,128)(2,1)S(1)}, bf16[64,128,128]{2,1,0:T(8,128)(2,1)}, u32[]{:S(2)}) copy-start(bf16[64,128,128]{2,1,0:T(8,128)(2,1)} %param.24) | copy-start | bytes 6291460
  10.5 2.8 %copy-start.12 = (s32[64]{0:T(128)S(1)}, s32[64]{0:T(128)}, u32[]{:S(2)}) copy-start(s32[64]{0:T(128)} %param.23) | copy-start | bytes 772
  20.5 13.2 %copy-start.11 = (s32[1,1,8,8]{3,2,1,0:T(8,128)S(1)}, s32[1,1,8,8]{3,2,1,0:T(8,128)}, u32[]{:S(2)}) copy-start(s32[1,1,8,8]{3,2,1,0:T(8,128)} %param.20) | copy-start | bytes 772
  37.4 20.3 %all-to-all-start = ((bf16[8,8,256]{2,1,0:T(8,128)(2,1)}), bf16[8,8,256]{2,1,0:T(8,128)(2,1)}, u32[]{:S(2)}, u32[]{:S(2)}) async-start(bf16[8,8,256]{2,1,0:T(8,128)(2,1)} %bitcast_select_fusion.1), calls=%async_computation | async-start | bytes 65536 | tf_op jit(solution)/shard_map/all_to_all | solution.py:16
  44.6 48.2 %reduce-scatter.5.cloned.1.call-start = ((), (), s32[]{:S(2)}) async-start(), calls=%async_computation.8 | async-start | bytes 1310720 | tf_op jit(solution)/shard_map/reduce_scatter | solution.py:44
  63.3 2.8 %copy-start.18 = (pred[64]{0:T(512)(128)(4,1)S(1)}, pred[64]{0:T(512)(128)(4,1)}, u32[]{:S(2)}) copy-start(pred[64]{0:T(512)(128)(4,1)} %compare_and_fusion.2) | copy-start | bytes 196
  66.1 6.9 %copy-start.15 = (s32[64]{0:T(128)S(1)}, s32[64]{0:T(128)}, u32[]{:S(2)}) copy-start(s32[64]{0:T(128)} %copy-done.14) | copy-start | bytes 772
  73.0 19.8 %copy-start.4 = (bf16[256,256]{1,0:T(8,128)(2,1)S(1)}, bf16[256,256]{1,0:T(8,128)(2,1)}, u32[]{:S(2)}) copy-start(bf16[256,256]{1,0:T(8,128)(2,1)} %param.31) | copy-start | bytes 393220
  73.0 19.8 %copy-start.7 = (bf16[256,256]{1,0:T(8,128)(2,1)S(1)}, bf16[256,256]{1,0:T(8,128)(2,1)}, u32[]{:S(2)}) copy-start(bf16[256,256]{1,0:T(8,128)(2,1)} %param.28) | copy-start | bytes 393220
  73.1 27.8 %copy-start.10 = (f32[256,256]{1,0:T(8,128)S(1)}, f32[256,256]{1,0:T(8,128)}, u32[]{:S(2)}) copy-start(f32[256,256]{1,0:T(8,128)} %fusion.35) | copy-start | bytes 786436
  73.1 27.8 %copy-start.23 = (f32[256]{0:T(256)S(1)}, f32[256]{0:T(256)}, u32[]{:S(2)}) copy-start(f32[256]{0:T(256)} %param.27) | copy-start | bytes 3076
  86.9 12.6 %all-to-all-start.2 = ((bf16[1,8,8,256]{3,2,0,1:T(8,128)(2,1)}), bf16[1,8,8,256]{3,2,0,1:T(8,128)(2,1)S(1)}, u32[]{:S(2)}, u32[]{:S(2)}) async-start(bf16[1,8,8,256]{3,2,0,1:T(8,128)(2,1)} %convert_bitcast_fusion.1), calls=%async_computation.4 | async-start | bytes 65536 | tf_op jit(solution)/shard_map/all_to_all | solution.py:47
  92.8 77.4 %reduce-scatter.11.cloned.1.call-start = ((), (), s32[]{:S(2)}) async-start(), calls=%async_computation.11 | async-start | bytes 327680 | tf_op jit(solution)/shard_map/reduce_scatter | solution.py:45
  101.8 3.1 %copy-start.5 = (bf16[256,256]{1,0:T(8,128)(2,1)}, bf16[256,256]{1,0:T(8,128)(2,1)S(1)}, u32[]{:S(2)}) copy-start(bf16[256,256]{1,0:T(8,128)(2,1)S(1)} %get-tuple-element.4) | copy-start | bytes 393220
  102.0 2.9 %copy-start.21 = (pred[64]{0:T(512)(128)(4,1)S(1)}, pred[64]{0:T(512)(128)(4,1)}, u32[]{:S(2)}) copy-start(pred[64]{0:T(512)(128)(4,1)} %copy-done.20) | copy-start | bytes 196
  125.4 52.2 %reduce-scatter.9.cloned.1.call-start = ((), (), s32[]{:S(2)}) async-start(), calls=%async_computation.10 | async-start | bytes 1310720 | tf_op jit(solution)/shard_map/reduce_scatter | solution.py:44
  128.9 12.0 %all-to-all-start.1 = ((bf16[8,8,256]{2,1,0:T(8,128)(2,1)}), bf16[8,8,256]{2,1,0:T(8,128)(2,1)S(1)}, u32[]{:S(2)}, u32[]{:S(2)}) async-start(bf16[8,8,256]{2,1,0:T(8,128)(2,1)} %bitcast_select_fusion), calls=%async_computation.1 | async-start | bytes 65536 | tf_op jit(solution)/shard_map/all_to_all | solution.py:16
  147.1 2.8 %copy-start.19 = (pred[64]{0:T(512)(128)(4,1)S(1)}, pred[64]{0:T(512)(128)(4,1)}, u32[]{:S(2)}) copy-start(pred[64]{0:T(512)(128)(4,1)} %compare_and_fusion.2) | copy-start | bytes 196
  149.9 6.9 %copy-start.16 = (s32[64]{0:T(128)S(1)}, s32[64]{0:T(128)}, u32[]{:S(2)}) copy-start(s32[64]{0:T(128)} %copy-done.14) | copy-start | bytes 772
  156.9 12.4 %copy-start.2 = (f32[256,256]{1,0:T(8,128)S(1)}, f32[256,256]{1,0:T(8,128)}, u32[]{:S(2)}) copy-start(f32[256,256]{1,0:T(8,128)} %fusion.36) | copy-start | bytes 786436
  156.9 12.4 %copy-start.3 = (bf16[256,256]{1,0:T(8,128)(2,1)S(1)}, bf16[256,256]{1,0:T(8,128)(2,1)}, u32[]{:S(2)}) copy-start(bf16[256,256]{1,0:T(8,128)(2,1)} %param.29) | copy-start | bytes 393220
  156.9 12.4 %copy-start.22 = (f32[256]{0:T(256)S(1)}, f32[256]{0:T(256)}, u32[]{:S(2)}) copy-start(f32[256]{0:T(256)} %param.30) | copy-start | bytes 3076
  156.9 20.7 %copy-start.6 = (bf16[256,256]{1,0:T(8,128)(2,1)S(1)}, bf16[256,256]{1,0:T(8,128)(2,1)}, u32[]{:S(2)}) copy-start(bf16[256,256]{1,0:T(8,128)(2,1)} %copy-done.5) | copy-start | bytes 393220
  156.9 20.7 %copy-start.8 = (bf16[256,256]{1,0:T(8,128)(2,1)S(1)}, bf16[256,256]{1,0:T(8,128)(2,1)}, u32[]{:S(2)}) copy-start(bf16[256,256]{1,0:T(8,128)(2,1)} %param.25) | copy-start | bytes 393220
  171.6 12.6 %all-to-all-start.3 = ((bf16[1,8,8,256]{3,2,0,1:T(8,128)(2,1)}), bf16[1,8,8,256]{3,2,0,1:T(8,128)(2,1)S(1)}, u32[]{:S(2)}, u32[]{:S(2)}) async-start(bf16[1,8,8,256]{3,2,0,1:T(8,128)(2,1)} %convert_bitcast_fusion), calls=%async_computation.7 | async-start | bytes 65536 | tf_op jit(solution)/shard_map/all_to_all | solution.py:47
  185.4 0.7 copy-start.9
Sparse Core Ops, SparseCore 0:
  33.7 22.7 reduce-scatter.6
  59.2 24.8 reduce-scatter.4
  125.5 16.8 reduce-scatter.10
  145.0 25.5 reduce-scatter.8
where the time goes:
time: 194 us; the launch traced here: 193 us
  other arithmetic  61.7 us (32%)
  matrix products  37.2 us (19%)
  blocking collectives  26 us (13%)
  starting transfers between devices  22.5 us (12%)
  local copies, waits for them, and re-layouts  20 us (10%)
  between operations  14.2 us (7%)
  waiting for transfers between devices  11 us (6%)
    scatter-add x2, other arithmetic, spread(): jnp.zeros((source_blocks,) + products.shape[1:], jnp.float32).at[tile_src]  24.9 us
    scatter-add x2, other arithmetic, aggregate(): jnp.zeros((block_count,) + products.shape[1:], jnp.float32).at[tile_dst]  24.6 us
    all_gather x2, blocking collectives, source_space(): hostwide = lax.all_gather(local, 'dev', axis=0, tiled=True)  14.2 us
    dot_general x2, matrix products, spread(): jnp.einsum('tij,tif->tjf', masked, seen, preferred_element_type=jnp.float32)  14.1 us
    dot_general x2, matrix products, aggregate(): jnp.einsum('tij,tjf->tif', masked, picked, preferred_element_type=jnp.flo...  13.8 us
    all_gather x2, blocking collectives, source_space(): incoming = lax.all_gather(arrived[None], 'dev', axis=0, tiled=True)  11.8 us
    all_to_all x2, starting transfers between devices, spread(): lax.all_to_all(far_sum.astype(jnp.bfloat16), 'hst', split_axis=1, concat_...  11.8 us
    all_to_all x2, waiting for transfers between devices, spread(): lax.all_to_all(far_sum.astype(jnp.bfloat16), 'hst', split_axis=1, concat_...  10.9 us
  transfers between devices with their start and end apart: 8, of which 2 were waited for; matrix products, arithmetic and copies ran while one was open for 34% of the time, Pallas kernels for 0%

commit v1 on v0

v1 whole, which is shorter than its diff:
```python
import functools

import jax
import jax.numpy as jnp
from jax import lax
from jax.experimental import pallas as pl
from jax.experimental.pallas import tpu as pltpu
from jax.sharding import PartitionSpec as P

F32 = jnp.float32
BF16 = jnp.bfloat16
VMEM_LIMIT = 40 * 1024 * 1024
CHUNKS = 8


def dot(a, b):
    return jnp.dot(a, b, preferred_element_type=F32)


def dot_nt(a, b):
    return lax.dot_general(a, b, (((1,), (1,)), ((), ())), preferred_element_type=F32)


def dot_tn(a, b):
    return lax.dot_general(a, b, (((0,), (0,)), ((), ())), preferred_element_type=F32)


def pick_matrix(send_ref, rows):
    hosts, send = send_ref.shape[2], send_ref.shape[3]
    place = lax.broadcasted_iota(jnp.int32, (send, rows), 0)
    column = lax.broadcasted_iota(jnp.int32, (send, rows), 1)
    parts = []
    for g in range(hosts):
        index = jnp.zeros((send, rows), jnp.int32)
        for s in range(send):
            index = jnp.where(place == s, send_ref[0, 0, g, s], index)
        parts.append(jnp.where(index == column, 1.0, 0.0).astype(F32))
    return jnp.concatenate(parts, 0).astype(BF16)


def pack(picked, far, msg_ref, hosts, devs):
    send = picked.shape[0] // hosts
    for g in range(hosts):
        for d in range(devs):
            low = (d * hosts + g) * send
            both = jnp.concatenate(
                [picked[g * send : (g + 1) * send], far[low : low + send]], 0
            )
            msg_ref[g * devs + d] = both.astype(BF16)


def unpack(recv_ref, hosts, devs):
    send = recv_ref.shape[1] // 2
    halo, back = [], []
    for d in range(devs):
        for g in range(hosts):
            both = recv_ref[g * devs + d].astype(F32)
            halo.append(both[:send])
            back.append(both[send:])
    return jnp.concatenate(halo, 0).astype(BF16), jnp.concatenate(back, 0).astype(BF16)


def spread_parts(adj, u, own_ref, own_rows):
    own_ref[...] = dot_tn(adj[:, :own_rows], u).astype(BF16)
    return dot_tn(adj[:, own_rows:], u)


def prep_kernel(
    hosts,
    devs,
    dst_ref,
    src_ref,
    rows_ref,
    send_ref,
    tile_hbm,
    features_ref,
    cot_ref,
    neigh_two_ref,
    adj_ref,
    msg_ref,
    own_ref,
    tile_buf,
    acc,
    sems,
):
    tiles, blk = tile_buf.shape[0], tile_buf.shape[1]
    each = tiles // CHUNKS
    copies = [
        pltpu.make_async_copy(
            tile_hbm.at[pl.ds(c * each, each)], tile_buf.at[pl.ds(c * each, each)], sems.at[c]
        )
        for c in range(CHUNKS)
    ]
    for copy in copies:
        copy.start()
    rows = features_ref.shape[0]
    bpd = rows // blk
    slots = acc.shape[0]
    sources = slots // bpd
    acc[...] = jnp.zeros_like(acc)
    picked = dot(pick_matrix(send_ref, rows), features_ref[...])
    u = dot_nt(cot_ref[...], neigh_two_ref[...]).astype(BF16)
    place = lax.broadcasted_iota(jnp.int32, (blk, blk), 0)
    for c in range(CHUNKS):
        copies[c].wait()

        def add(t, carry):
            slot = dst_ref[t] * sources + src_ref[t]
            live = jnp.where(place < rows_ref[t], tile_buf[t].astype(F32), 0.0)
            acc[slot] = acc[slot] + live
            return carry

        lax.fori_loop(c * each, (c + 1) * each, add, 0, unroll=True)
    for b in range(bpd):
        for j in range(sources):
            adj_ref[b * blk : (b + 1) * blk, j * blk : (j + 1) * blk] = acc[
                b * sources + j
            ].astype(BF16)
    far = spread_parts(adj_ref[...], u, own_ref, devs * rows)
    pack(picked, far, msg_ref, hosts, devs)


def middle_kernel(
    hosts,
    devs,
    send_ref,
    adj_ref,
    wide_ref,
    recv_ref,
    terms_ref,
    features_ref,
    cot_ref,
    self_one_ref,
    neigh_one_ref,
    bias_ref,
    self_two_ref,
    hidden_ref,
    grad_pre_ref,
    msg_ref,
    own_ref,
):
    rows = features_ref.shape[0]
    own_rows = devs * rows
    pick = pick_matrix(send_ref, rows)
    halo, back = unpack(recv_ref, hosts, devs)
    adj = adj_ref[...]
    agg = dot(adj[:, :own_rows], wide_ref[...]) + dot(adj[:, own_rows:], halo)
    pre = dot(features_ref[...], self_one_ref[...])
    pre = pre + dot(agg.astype(BF16), neigh_one_ref[...]) + bias_ref[...].reshape(1, -1)
    sigmoid = jax.nn.sigmoid(pre)
    hidden = (pre * sigmoid).astype(BF16)
    hidden_ref[...] = hidden
    grad = dot_nt(cot_ref[...], self_two_ref[...])
    grad = grad + dot_tn(jnp.concatenate([pick] * devs, 0), back)
    for d in range(devs):
        grad = grad + terms_ref[d * rows : (d + 1) * rows, :].astype(F32)
    grad_pre = (grad * sigmoid * (1.0 + pre * (1.0 - sigmoid))).astype(BF16)
    grad_pre_ref[...] = grad_pre
    u = dot_nt(grad_pre, neigh_one_ref[...]).astype(BF16)
    far = spread_parts(adj, u, own_ref, own_rows)
    pack(dot(pick, hidden), far, msg_ref, hosts, devs)


def last_kernel(
    hosts,
    devs,
    send_ref,
    adj_ref,
    wide_ref,
    recv_ref,
    terms_ref,
    hidden_ref,
    grad_pre_ref,
    self_one_ref,
    self_two_ref,
    neigh_two_ref,
    bias_ref,
    output_ref,
    grad_ref,
):
    rows = hidden_ref.shape[0]
    own_rows = devs * rows
    pick = pick_matrix(send_ref, rows)
    halo, back = unpack(recv_ref, hosts, devs)
    adj = adj_ref[...]
    agg = dot(adj[:, :own_rows], wide_ref[...]) + dot(adj[:, own_rows:], halo)
    result = dot(hidden_ref[...], self_two_ref[...])
    result = result + dot(agg.astype(BF16), neigh_two_ref[...]) + bias_ref[...].reshape(1, -1)
    output_ref[...] = result.astype(BF16)
    grad = dot_nt(grad_pre_ref[...], self_one_ref[...])
    grad = grad + dot_tn(jnp.concatenate([pick] * devs, 0), back)
    for d in range(devs):
        grad = grad + terms_ref[d * rows : (d + 1) * rows, :].astype(F32)
    grad_ref[...] = grad


VMEM = pl.BlockSpec(memory_space=pltpu.VMEM)
SMEM = pl.BlockSpec(memory_space=pltpu.SMEM)
PARAMS = pltpu.CompilerParams(vmem_limit_bytes=VMEM_LIMIT)


def exchange(value, msg, own):
    wide = lax.all_gather(value, "dev", axis=0, tiled=True)
    recv = lax.all_to_all(msg, ("hst", "dev"), split_axis=0, concat_axis=0, tiled=True)
    terms = lax.all_to_all(own, "dev", split_axis=0, concat_axis=0, tiled=True)
    return wide, recv, terms


def body(
    features,
    send_list,
    tile_dst,
    tile_src,
    tile_rows,
    tile_val,
    self_one,
    neigh_one,
    bias_one,
    self_two,
    neigh_two,
    bias_two,
    cotangent,
):
    devs = lax.axis_size("dev")
    hosts = lax.axis_size("hst")
    rows, width = features.shape
    tiles, blk = tile_val.shape[:2]
    send = send_list.shape[3]
    own_rows = devs * rows
    all_rows = own_rows + devs * hosts * send
    bpd = rows // blk
    adj_shape = jax.ShapeDtypeStruct((rows, all_rows), BF16)
    msg_shape = jax.ShapeDtypeStruct((hosts * devs, 2 * send, width), BF16)
    own_shape = jax.ShapeDtypeStruct((own_rows, width), BF16)
    rows_shape = jax.ShapeDtypeStruct((rows, width), BF16)

    adj, msg, own = pl.pallas_call(
        functools.partial(prep_kernel, hosts, devs),
        out_shape=(adj_shape, msg_shape, own_shape),
        in_specs=[SMEM] * 4 + [pl.BlockSpec(memory_space=pl.ANY)] + [VMEM] * 3,
        out_specs=(VMEM,) * 3,
        scratch_shapes=[
            pltpu.VMEM((tiles, blk, blk), BF16),
            pltpu.VMEM((bpd * (all_rows // blk), blk, blk), F32),
            pltpu.SemaphoreType.DMA((CHUNKS,)),
        ],
        compiler_params=PARAMS,
        name="prep",
    )(tile_dst, tile_src, tile_rows, send_list, tile_val, features, cotangent, neigh_two)

    wide, recv, terms = exchange(features, msg, own)
    hidden, grad_pre, msg, own = pl.pallas_call(
        functools.partial(middle_kernel, hosts, devs),
        out_shape=(rows_shape, rows_shape, msg_shape, own_shape),
        in_specs=[SMEM] + [VMEM] * 10,
        out_specs=(VMEM,) * 4,
        compiler_params=PARAMS,
        name="middle",
    )(
        send_list,
        adj,
        wide,
        recv,
        terms,
        features,
        cotangent,
        self_one,
        neigh_one,
        bias_one,
        self_two,
    )

    wide, recv, terms = exchange(hidden, msg, own)
    return pl.pallas_call(
        functools.partial(last_kernel, hosts, devs),
        out_shape=(rows_shape, jax.ShapeDtypeStruct((rows, width), F32)),
        in_specs=[SMEM] + [VMEM] * 10,
        out_specs=(VMEM,) * 2,
        compiler_params=PARAMS,
        name="last",
    )(
        send_list,
        adj,
        wide,
        recv,
        terms,
        hidden,
        grad_pre,
        self_one,
        self_two,
        neigh_two,
        bias_two,
    )


def solution(mesh):
    split = P(("hst", "dev"))
    return jax.shard_map(
        body,
        mesh=mesh,
        in_specs=(
            P(("hst", "dev"), None),
            P("hst", "dev", None, None),
            split,
            split,
            split,
            P(("hst", "dev"), None, None),
            P(),
            P(),
            P(),
            P(),
            P(),
            P(),
            P(("hst", "dev"), None),
        ),
        out_specs=(P(("hst", "dev"), None), P(("hst", "dev"), None)),
        check_vma=False,
    )
```

time: 194 us -> 69.4 us (0.36)
  other arithmetic: 61.7 us -> 0 us
  matrix products: 37.2 us -> 0 us
  blocking collectives: 26 us -> 42.7 us
  starting transfers between devices: 22.5 us -> 8.28 us
  between operations: 14.2 us -> 0.76 us
  local copies, waits for them, and re-layouts: 20 us -> 6.99 us
  waiting for transfers between devices: 11 us -> 2.6 us
  Pallas kernels: 0 us -> 7.64 us
    scatter-add x6 -> x0, other arithmetic: 52.1 us -> none  [the longest x2 24.9 us: spread(): jnp.zeros((source_blocks,) + products.shape[1:], jnp.float32).at[tile_src]]
    dot_general x12 -> x0, matrix products: 37.2 us -> none  [the longest x2 14.1 us: spread(): jnp.einsum('tij,tif->tjf', masked, seen, preferred_element_type=jnp.float32)]
    all_to_all x0 -> x2, blocking collectives: none -> 24.1 us  [exchange(): terms = lax.all_to_all(own, 'dev', split_axis=0, concat_axis=0, tiled=True)]
    gather x6 -> x0, local copies, waits for them, and re-layouts: 15 us -> none  [the longest x2 5.67 us: spread(): seen = jnp.take(upstream.reshape(-1, block_rows, width), tile_dst, axis=0)]
    all_to_all x4 -> x2, starting transfers between devices: 22.4 us -> 8.28 us  [exchange(): lax.all_to_all(msg, ('hst', 'dev'), split_axis=0, concat_axis=0, tiled=True)]
    all_to_all x4 -> x2, waiting for transfers between devices: 10.9 us -> 2.6 us  [exchange(): lax.all_to_all(msg, ('hst', 'dev'), split_axis=0, concat_axis=0, tiled=True)]
    pallas_call x0 -> x3, Pallas kernels: none -> 7.64 us  [the longest x1 2.95 us: body(): pl.pallas_call(functools.partial(prep_kernel, hosts, devs), out_shape=(ad...]
    all_gather x4 -> x2, blocking collectives: 26 us -> 18.6 us  [exchange(): wide = lax.all_gather(value, 'dev', axis=0, tiled=True)]
  transfers between devices with their start and end apart: 8 -> 2, of which waited for: 2 -> 2; matrix products, arithmetic and copies ran while one was open for 34% -> 0% of each run, Pallas kernels for 0% -> 0%
where the time goes in v1:
time: 69.4 us; the launch traced here: 68.9 us
  blocking collectives  42.7 us (62%)
  starting transfers between devices  8.28 us (12%)
  Pallas kernels  7.64 us (11%)
  local copies, waits for them, and re-layouts  6.99 us (10%)
  waiting for transfers between devices  2.6 us (4%)
  between operations  0.76 us (1%)
    all_to_all x2, blocking collectives, exchange(): terms = lax.all_to_all(own, 'dev', split_axis=0, concat_axis=0, tiled=True)  24.1 us
    all_gather x2, blocking collectives, exchange(): wide = lax.all_gather(value, 'dev', axis=0, tiled=True)  18.6 us
    all_to_all x2, starting transfers between devices, exchange(): lax.all_to_all(msg, ('hst', 'dev'), split_axis=0, concat_axis=0, tiled=True)  8.28 us
    unnamed x34, local copies, waits for them, and re-layouts  6.99 us
    pallas_call x1, Pallas kernels, body(): pl.pallas_call(functools.partial(prep_kernel, hosts, devs), out_shape=(ad...  2.95 us
    all_to_all x2, waiting for transfers between devices, exchange(): lax.all_to_all(msg, ('hst', 'dev'), split_axis=0, concat_axis=0, tiled=True)  2.6 us
    pallas_call x1, Pallas kernels, body(): pl.pallas_call(functools.partial(middle_kernel, hosts, devs), out_shape=(...  2.6 us
    pallas_call x1, Pallas kernels, body(): pl.pallas_call(functools.partial(last_kernel, hosts, devs), out_shape=(ro...  2.09 us
  transfers between devices with their start and end apart: 2, of which 2 were waited for; matrix products, arithmetic and copies ran while one was open for 0% of the time, Pallas kernels for 0%

profile of v1, /device:TPU:0, one launch (start us, length us, event | category | flops | bytes accessed | tf_op | source)
XLA Modules:
  0.0 68.9 jit_solution(14922420952683034912)
XLA Ops:
  0.6 0.0 copy-start
  0.6 1.6 %copy-done = bf16[64,128,128]{2,1,0:T(8,128)(2,1)S(1)} copy-done((bf16[64,128,128]{2,1,0:T(8,128)(2,1)S(1)}, bf16[64,128,128]{2,1,0:T(8,128)(2,1)}, u32[]{:S(2)}) %copy-start) | copy-done | bytes 2097176
  2.2 0.9 %copy-done.1 = bf16[256,256]{1,0:T(8,128)(2,1)S(1)} copy-done((bf16[256,256]{1,0:T(8,128)(2,1)S(1)}, bf16[256,256]{1,0:T(8,128)(2,1)}, u32[]{:S(2)}) %copy-start.1) | copy-done | bytes 131096
  3.1 0.9 %copy-done.3 = bf16[256,256]{1,0:T(8,128)(2,1)S(1)} copy-done((bf16[256,256]{1,0:T(8,128)(2,1)S(1)}, bf16[256,256]{1,0:T(8,128)(2,1)}, u32[]{:S(2)}) %copy-start.3) | copy-done | bytes 131096
  4.0 0.9 %copy-done.5 = bf16[256,256]{1,0:T(8,128)(2,1)S(1)} copy-done((bf16[256,256]{1,0:T(8,128)(2,1)S(1)}, bf16[256,256]{1,0:T(8,128)(2,1)}, u32[]{:S(2)}) %copy-start.5) | copy-done | bytes 131096
  4.9 0.7 copy-done.10
  5.6 0.7 copy-done.14
  6.3 0.7 copy-done.15
  6.9 0.7 copy-done.16
  7.6 0.0 copy-start.9
  7.6 0.0 copy-start.11
  7.6 0.0 copy-start.12
  7.6 3.0 %prep.1 = (bf16[256,1280]{1,0:T(8,128)(2,1)S(1)}, bf16[32,16,256]{2,1,0:T(8,128)(2,1)}, bf16[1024,256]{1,0:T(8,128)(2,1)S(1)}) custom-call(s32[64]{0:T(128)S(1)} %copy-done.14, s32[64]{0:T(128)S(1)} %copy-done.15, s32[64]{0:T(128)S(1)} %copy-done.16, s32[1,1,8,8]{3,2,1,0:T(8,128)S(1)} %copy-done.10, bf16[64,128,128]{2,1,0:T(8,128)(2,1)S(1)} %copy-done, ...), custom_call_target="tpu_custom_call" | custom-call | tf_op jit(solution)/shard_map/prep/pallas_call | solution.py:237
  10.6 12.9 %all_to_all.32 = bf16[4,256,256]{2,1,0:T(8,128)(2,1)S(1)} all-to-all(bf16[4,256,256]{2,1,0:T(8,128)(2,1)S(1)} %bitcast.7), channel_id=1, replica_groups=mesh['hst'=8,'dev'=4] {'dev'}, dimensions={0} | all-to-all | bytes 1048576 | tf_op jit(solution)/shard_map/all_to_all | solution.py:205
  23.5 4.9 %all-to-all-start = ((bf16[32,16,256]{2,1,0:T(8,128)(2,1)}), bf16[32,16,256]{2,1,0:T(8,128)(2,1)S(1)}, u32[]{:S(2)}, u32[]{:S(2)}) async-start(bf16[32,16,256]{2,1,0:T(8,128)(2,1)} %get-tuple-element.10), calls=%async_computation | async-start | bytes 524288 | tf_op jit(solution)/shard_map/all_to_all | solution.py:204
  28.4 0.0 copy-done.2
  28.4 9.3 %all_gather.6.wide_ref = bf16[1024,256]{1,0:T(8,128)(2,1)S(1)} all-gather(bf16[256,256]{1,0:T(8,128)(2,1)S(1)} %copy-done.2), channel_id=1, replica_groups=mesh['hst'=8,'dev'=4] {'dev'}, dimensions={0}, use_global_device_ids=true | all-gather | bytes 655360 | tf_op jit(solution)/shard_map/all_gather | solution.py:203
  37.7 1.3 %all-to-all-done.recv_ref = bf16[32,16,256]{2,1,0:T(8,128)(2,1)S(1)} async-done(((bf16[32,16,256]{2,1,0:T(8,128)(2,1)}), bf16[32,16,256]{2,1,0:T(8,128)(2,1)S(1)}, u32[]{:S(2)}, u32[]{:S(2)}) %all-to-all-start) | async-done | bytes 262176 | tf_op jit(solution)/shard_map/all_to_all | solution.py:204
  39.0 0.0 copy-done.4
  39.0 0.0 copy-done.7
  39.0 0.0 copy-done.8
  39.0 0.0 copy-done.9
  39.0 0.0 copy-done.11
  39.0 0.0 copy-done.12
  39.0 0.0 copy-start.6
  39.0 0.0 copy-start.13
  39.0 2.6 %middle.1 = (bf16[256,256]{1,0:T(8,128)(2,1)S(1)}, bf16[256,256]{1,0:T(8,128)(2,1)S(1)}, bf16[32,16,256]{2,1,0:T(8,128)(2,1)}, bf16[1024,256]{1,0:T(8,128)(2,1)S(1)}) custom-call(s32[1,1,8,8]{3,2,1,0:T(8,128)S(1)} %copy-done.11, bf16[256,1280]{1,0:T(8,128)(2,1)S(1)} %get-tuple-element.9.adj_ref, bf16[1024,256]{1,0:T(8,128)(2,1)S(1)} %all_gather.6.wide_ref, ...), custom_call_target="tpu_custom_call" | custom-call | tf_op jit(solution)/shard_map/middle/pallas_call | solution.py:252
  41.6 11.2 %all_to_all.33 = bf16[4,256,256]{2,1,0:T(8,128)(2,1)S(1)} all-to-all(bf16[4,256,256]{2,1,0:T(8,128)(2,1)S(1)} %bitcast.6), channel_id=1, replica_groups=mesh['hst'=8,'dev'=4] {'dev'}, dimensions={0} | all-to-all | bytes 1048576 | tf_op jit(solution)/shard_map/all_to_all | solution.py:205
  52.9 3.4 %all-to-all-start.2 = ((bf16[32,16,256]{2,1,0:T(8,128)(2,1)}), bf16[32,16,256]{2,1,0:T(8,128)(2,1)S(1)}, u32[]{:S(2)}, u32[]{:S(2)}) async-start(bf16[32,16,256]{2,1,0:T(8,128)(2,1)} %get-tuple-element.13), calls=%async_computation.2 | async-start | bytes 524288 | tf_op jit(solution)/shard_map/all_to_all | solution.py:204
  56.2 9.3 %all_gather.7.wide_ref = bf16[1024,256]{1,0:T(8,128)(2,1)S(1)} all-gather(bf16[256,256]{1,0:T(8,128)(2,1)S(1)} %get-tuple-element.12.hidden_ref), channel_id=1, replica_groups=mesh['hst'=8,'dev'=4] {'dev'}, dimensions={0}, use_global_device_ids=true | all-gather | bytes 655360 | tf_op jit(solution)/shard_map/all_gather | solution.py:203
  65.5 1.3 %all-to-all-done.2.recv_ref = bf16[32,16,256]{2,1,0:T(8,128)(2,1)S(1)} async-done(((bf16[32,16,256]{2,1,0:T(8,128)(2,1)}), bf16[32,16,256]{2,1,0:T(8,128)(2,1)S(1)}, u32[]{:S(2)}, u32[]{:S(2)}) %all-to-all-start.2) | async-done | bytes 262176 | tf_op jit(solution)/shard_map/all_to_all | solution.py:204
  66.8 2.1 %last.1 = (bf16[256,256]{1,0:T(8,128)(2,1)}, f32[256,256]{1,0:T(8,128)}) custom-call(s32[1,1,8,8]{3,2,1,0:T(8,128)S(1)} %copy-done.11, bf16[256,1280]{1,0:T(8,128)(2,1)S(1)} %get-tuple-element.9.adj_ref, bf16[1024,256]{1,0:T(8,128)(2,1)S(1)} %all_gather.7.wide_ref, bf16[32,16,256]{2,1,0:T(8,128)(2,1)S(1)} %all-to-all-done.2.recv_ref, ...), custom_call_target="tpu_custom_call" | custom-call | tf_op jit(solution)/shard_map/last/pallas_call | solution.py:274
  (13 shorter events, 0.0 us)
Async XLA Ops:
  0.6 1.6 %copy-start = (bf16[64,128,128]{2,1,0:T(8,128)(2,1)S(1)}, bf16[64,128,128]{2,1,0:T(8,128)(2,1)}, u32[]{:S(2)}) copy-start(bf16[64,128,128]{2,1,0:T(8,128)(2,1)} %tile_hbm.1) | copy-start | bytes 6291460
  2.2 0.9 %copy-start.1 = (bf16[256,256]{1,0:T(8,128)(2,1)S(1)}, bf16[256,256]{1,0:T(8,128)(2,1)}, u32[]{:S(2)}) copy-start(bf16[256,256]{1,0:T(8,128)(2,1)} %features_ref.3) | copy-start | bytes 393220
  3.1 0.9 %copy-start.3 = (bf16[256,256]{1,0:T(8,128)(2,1)S(1)}, bf16[256,256]{1,0:T(8,128)(2,1)}, u32[]{:S(2)}) copy-start(bf16[256,256]{1,0:T(8,128)(2,1)} %cot_ref.3) | copy-start | bytes 393220
  4.0 0.9 %copy-start.5 = (bf16[256,256]{1,0:T(8,128)(2,1)S(1)}, bf16[256,256]{1,0:T(8,128)(2,1)}, u32[]{:S(2)}) copy-start(bf16[256,256]{1,0:T(8,128)(2,1)} %neigh_two_ref.3) | copy-start | bytes 393220
  4.9 0.7 copy-start.10
  5.6 0.7 copy-start.14
  6.3 0.7 copy-start.15
  6.9 0.7 copy-start.16
  7.6 20.8 %copy-start.2 = (bf16[256,256]{1,0:T(8,128)(2,1)S(1)}, bf16[256,256]{1,0:T(8,128)(2,1)}, u32[]{:S(2)}) copy-start(bf16[256,256]{1,0:T(8,128)(2,1)} %features_ref.3) | copy-start | bytes 393220
  7.6 31.4 %copy-start.4 = (bf16[256,256]{1,0:T(8,128)(2,1)S(1)}, bf16[256,256]{1,0:T(8,128)(2,1)}, u32[]{:S(2)}) copy-start(bf16[256,256]{1,0:T(8,128)(2,1)} %cot_ref.3) | copy-start | bytes 393220
  7.6 31.4 %copy-start.7 = (bf16[256,256]{1,0:T(8,128)(2,1)S(1)}, bf16[256,256]{1,0:T(8,128)(2,1)}, u32[]{:S(2)}) copy-start(bf16[256,256]{1,0:T(8,128)(2,1)} %self_one_ref.3) | copy-start | bytes 393220
  7.6 31.4 %copy-start.8 = (bf16[256,256]{1,0:T(8,128)(2,1)S(1)}, bf16[256,256]{1,0:T(8,128)(2,1)}, u32[]{:S(2)}) copy-start(bf16[256,256]{1,0:T(8,128)(2,1)} %self_two_ref.3) | copy-start | bytes 393220
  7.6 31.4 %copy-start.9 = (bf16[256,256]{1,0:T(8,128)(2,1)S(1)}, bf16[256,256]{1,0:T(8,128)(2,1)}, u32[]{:S(2)}) copy-start(bf16[256,256]{1,0:T(8,128)(2,1)} %neigh_one_ref.1) | copy-start | bytes 393220
  7.6 31.4 %copy-start.11 = (s32[1,1,8,8]{3,2,1,0:T(8,128)S(1)}, s32[1,1,8,8]{3,2,1,0:T(8,128)}, u32[]{:S(2)}) copy-start(s32[1,1,8,8]{3,2,1,0:T(8,128)} %send_ref.5) | copy-start | bytes 772
  7.6 31.4 %copy-start.12 = (f32[256]{0:T(256)S(1)}, f32[256]{0:T(256)}, u32[]{:S(2)}) copy-start(f32[256]{0:T(256)} %bias_ref.2) | copy-start | bytes 3076
  23.5 15.5 %all-to-all-start = ((bf16[32,16,256]{2,1,0:T(8,128)(2,1)}), bf16[32,16,256]{2,1,0:T(8,128)(2,1)S(1)}, u32[]{:S(2)}, u32[]{:S(2)}) async-start(bf16[32,16,256]{2,1,0:T(8,128)(2,1)} %get-tuple-element.10), calls=%async_computation | async-start | bytes 524288 | tf_op jit(solution)/shard_map/all_to_all | solution.py:204
  39.0 27.8 %copy-start.6 = (bf16[256,256]{1,0:T(8,128)(2,1)S(1)}, bf16[256,256]{1,0:T(8,128)(2,1)}, u32[]{:S(2)}) copy-start(bf16[256,256]{1,0:T(8,128)(2,1)} %neigh_two_ref.3) | copy-start | bytes 393220
  39.0 27.8 %copy-start.13 = (f32[256]{0:T(256)S(1)}, f32[256]{0:T(256)}, u32[]{:S(2)}) copy-start(f32[256]{0:T(256)} %bias_ref.3) | copy-start | bytes 3076
  52.9 14.0 %all-to-all-start.2 = ((bf16[32,16,256]{2,1,0:T(8,128)(2,1)}), bf16[32,16,256]{2,1,0:T(8,128)(2,1)S(1)}, u32[]{:S(2)}, u32[]{:S(2)}) async-start(bf16[32,16,256]{2,1,0:T(8,128)(2,1)} %get-tuple-element.13), calls=%async_computation.2 | async-start | bytes 524288 | tf_op jit(solution)/shard_map/all_to_all | solution.py:204

commit v2 on v0

v2 whole, which is shorter than its diff:
```python
import functools

import jax
import jax.numpy as jnp
from jax import lax
from jax.experimental import pallas as pl
from jax.experimental.pallas import tpu as pltpu
from jax.sharding import PartitionSpec as P

F32 = jnp.float32
BF16 = jnp.bfloat16
MIB = 1024 * 1024
CHUNKS = 8
CORES = 2

VMEM = pl.BlockSpec(memory_space=pltpu.VMEM)
SMEM = pl.BlockSpec(memory_space=pltpu.SMEM)
ANY = pl.BlockSpec(memory_space=pl.ANY)


def dot(a, b):
    return jnp.dot(a, b, preferred_element_type=F32)


def dot_nt(a, b):
    return lax.dot_general(a, b, (((1,), (1,)), ((), ())), preferred_element_type=F32)


def dot_tn(a, b):
    return lax.dot_general(a, b, (((0,), (0,)), ((), ())), preferred_element_type=F32)


def place_of(devs):
    dev = lax.axis_index("dev")
    return lax.div(dev, CORES), lax.rem(dev, CORES)


def pick_rows(send_ref, host, rows):
    send = send_ref.shape[3]
    place = lax.broadcasted_iota(jnp.int32, (send, rows), 0)
    column = lax.broadcasted_iota(jnp.int32, (send, rows), 1)
    index = jnp.zeros((send, rows), jnp.int32)
    for s in range(send):
        index = jnp.where(place == s, send_ref[0, 0, host, s], index)
    return jnp.where(index == column, 1.0, 0.0).astype(F32)


def pick_matrix(send_ref, rows, sign):
    hosts = send_ref.shape[2]
    me = lax.axis_index("hst")
    order = [lax.rem(me + sign * k + hosts, hosts) for k in range(hosts)]
    return jnp.concatenate([pick_rows(send_ref, g, rows) for g in order], 0).astype(BF16)


def put_picked(send_ref, value, out_refs):
    send = send_ref.shape[3]
    picked = dot(pick_matrix(send_ref, value.shape[0], 1), value)
    for k, out in enumerate(out_refs):
        out[...] = picked[k * send : (k + 1) * send].astype(BF16)


def spread_parts(devs, far, adj, u, whole, keep_ref, give_ref):
    rows = u.shape[0]
    own_rows = devs * rows
    whole[...] = dot_tn(adj, u).astype(BF16)
    chip, core = place_of(devs)
    for side, ref in ((core, keep_ref), (1 - core, give_ref)):
        for x in range(devs // CORES):
            d = x * CORES + side
            low = pl.multiple_of(d * rows, rows)
            ref[x, :rows, :] = whole[pl.ds(low, rows), :]
            low = pl.multiple_of(own_rows + d * far, far)
            ref[x, rows:, :] = whole[pl.ds(low, far), :]


def prep_kernel(
    devs,
    dst_ref,
    src_ref,
    rows_ref,
    send_ref,
    tile_hbm,
    features_ref,
    cot_ref,
    neigh_two_ref,
    adj_ref,
    keep_ref,
    give_ref,
    *rest,
):
    picked_refs, (tile_buf, acc, whole, sems) = rest[:-4], rest[-4:]
    tiles, blk = tile_buf.shape[0], tile_buf.shape[1]
    each = tiles // CHUNKS
    copies = [
        pltpu.make_async_copy(
            tile_hbm.at[pl.ds(c * each, each)], tile_buf.at[pl.ds(c * each, each)], sems.at[c]
        )
        for c in range(CHUNKS)
    ]
    for copy in copies:
        copy.start()
    rows = features_ref.shape[0]
    bpd = rows // blk
    sources = acc.shape[0] // bpd
    far = send_ref.shape[2] * send_ref.shape[3]
    acc[...] = jnp.zeros_like(acc)
    put_picked(send_ref, features_ref[...], picked_refs)
    u = dot_nt(cot_ref[...], neigh_two_ref[...]).astype(BF16)
    place = lax.broadcasted_iota(jnp.int32, (blk, blk), 0)
    for c in range(CHUNKS):
        copies[c].wait()

        def add(t, carry):
            slot = dst_ref[t] * sources + src_ref[t]
            live = jnp.where(place < rows_ref[t], tile_buf[t].astype(F32), 0.0)
            acc[slot] = acc[slot] + live
            return carry

        lax.fori_loop(c * each, (c + 1) * each, add, 0, unroll=True)
    for b in range(bpd):
        for j in range(sources):
            adj_ref[b * blk : (b + 1) * blk, j * blk : (j + 1) * blk] = acc[
                b * sources + j
            ].astype(BF16)
    spread_parts(devs, far, adj_ref[...], u, whole, keep_ref, give_ref)


def core_sum_kernel(devs, keep_ref, came_ref, mine_ref, *to_refs):
    chips = devs // CORES
    chip, _ = place_of(devs)
    mine_ref[...] = keep_ref[chip].astype(F32) + came_ref[chip].astype(F32)
    for k, ref in enumerate(to_refs):
        other = lax.rem(chip + k + 1, chips)
        ref[...] = (keep_ref[other].astype(F32) + came_ref[other].astype(F32)).astype(BF16)


def chip_sum_kernel(hosts, send, count, *refs):
    mine_ref, came, own_ref, outs = refs[0], refs[1 : 1 + count], refs[1 + count], refs[2 + count : -1]
    far_buf = refs[-1]
    total = mine_ref[...]
    for ref in came:
        total = total + ref[...].astype(F32)
    rows = own_ref.shape[0]
    own_ref[...] = total[:rows]
    far_buf[...] = total[rows:]
    me = lax.axis_index("hst")
    for k, out in enumerate(outs):
        low = pl.multiple_of(lax.rem(me + k, hosts) * send, send)
        out[...] = far_buf[pl.ds(low, send), :].astype(BF16)


def join_kernel(hosts, send, *refs):
    outs, buf = refs[-2], refs[-1]
    me = lax.axis_index("hst")
    for k in range(hosts):
        low = pl.multiple_of(lax.rem(me - k + hosts, hosts) * send, send)
        buf[pl.ds(low, send), :] = refs[k][...].astype(F32)
    outs[...] = buf[...].astype(BF16)


def gather_sources(devs, wide_refs, halo_refs, space):
    chips = devs // CORES
    chip, core = place_of(devs)
    rows, far = wide_refs[0].shape[0], halo_refs[0].shape[0]
    for k in range(chips):
        for i, side in enumerate((core, 1 - core)):
            d = lax.rem(chip - k + chips, chips) * CORES + side
            space[pl.ds(pl.multiple_of(d * rows, rows), rows), :] = wide_refs[k * CORES + i][...]
            low = pl.multiple_of(devs * rows + d * far, far)
            space[pl.ds(low, far), :] = halo_refs[k * CORES + i][...]


def forward_one_kernel(
    devs, send_ref, adj_ref, self_ref, neigh_ref, bias_ref, *refs
):
    wide, halo, rest = refs[:devs], refs[devs : 2 * devs], refs[2 * devs :]
    pre_ref, hidden_ref, picked_refs, space = rest[0], rest[1], rest[2:-1], rest[-1]
    gather_sources(devs, wide, halo, space)
    agg = dot(adj_ref[...], space[...]).astype(BF16)
    pre = dot(wide[0][...], self_ref[...])
    pre = pre + dot(agg, neigh_ref[...]) + bias_ref[...].reshape(1, -1)
    pre_ref[...] = pre
    hidden = (pre * jax.nn.sigmoid(pre)).astype(BF16)
    hidden_ref[...] = hidden
    put_picked(send_ref, hidden, picked_refs)


def forward_two_kernel(devs, adj_ref, self_ref, neigh_ref, bias_ref, *refs):
    wide, halo, out_ref, space = refs[:devs], refs[devs : 2 * devs], refs[-2], refs[-1]
    gather_sources(devs, wide, halo, space)
    agg = dot(adj_ref[...], space[...]).astype(BF16)
    result = dot(wide[0][...], self_ref[...])
    result = result + dot(agg, neigh_ref[...]) + bias_ref[...].reshape(1, -1)
    out_ref[...] = result.astype(BF16)


def spread_total(send_ref, own_ref, back_refs):
    back = jnp.concatenate([ref[...].astype(F32) for ref in back_refs], 0).astype(BF16)
    return own_ref[...] + dot_tn(pick_matrix(send_ref, own_ref.shape[0], -1), back)


def backward_two_kernel(
    devs,
    hosts,
    send_ref,
    adj_ref,
    pre_ref,
    cot_ref,
    self_two_ref,
    neigh_one_ref,
    own_ref,
    *refs,
):
    back, (grad_pre_ref, keep_ref, give_ref, whole) = refs[:hosts], refs[hosts:]
    pre = pre_ref[...]
    sigmoid = jax.nn.sigmoid(pre)
    grad = dot_nt(cot_ref[...], self_two_ref[...]) + spread_total(send_ref, own_ref, back)
    grad_pre = (grad * sigmoid * (1.0 + pre * (1.0 - sigmoid))).astype(BF16)
    grad_pre_ref[...] = grad_pre
    u = dot_nt(grad_pre, neigh_one_ref[...]).astype(BF16)
    far = send_ref.shape[2] * send_ref.shape[3]
    spread_parts(devs, far, adj_ref[...], u, whole, keep_ref, give_ref)


def backward_one_kernel(hosts, send_ref, grad_pre_ref, self_one_ref, own_ref, *refs):
    back, grad_ref = refs[:hosts], refs[hosts]
    grad_ref[...] = dot_nt(grad_pre_ref[...], self_one_ref[...]) + spread_total(
        send_ref, own_ref, back
    )


def call(kernel, name, out_shape, in_specs, args, scratch=(), limit=40):
    return pl.pallas_call(
        kernel,
        out_shape=out_shape,
        in_specs=in_specs,
        out_specs=jax.tree.map(lambda _: VMEM, out_shape),
        scratch_shapes=scratch,
        compiler_params=pltpu.CompilerParams(vmem_limit_bytes=limit * MIB),
        name=name,
    )(*args)


def core_permute(value):
    devs = lax.axis_size("dev")
    return lax.ppermute(value, "dev", [(d, d ^ 1) for d in range(devs)])


def chip_permute(value, k):
    devs = lax.axis_size("dev")
    return lax.ppermute(value, "dev", [(d, (d + k * CORES) % devs) for d in range(devs)])


def host_permute(value, k):
    hosts = lax.axis_size("hst")
    return lax.ppermute(value, "hst", [(h, (h + k) % hosts) for h in range(hosts)])


def across_hosts(blocks):
    return [blocks[0]] + [host_permute(blocks[k], k) for k in range(1, len(blocks))]


def across_devs(value):
    chips = lax.axis_size("dev") // CORES
    held = [value] + [chip_permute(value, k) for k in range(1, chips)]
    out = []
    for block in held:
        out += [block, core_permute(block)]
    return out


def shape(rows, width, kind=BF16):
    return jax.ShapeDtypeStruct((rows, width), kind)


def body(
    features,
    send_list,
    tile_dst,
    tile_src,
    tile_rows,
    tile_val,
    self_one,
    neigh_one,
    bias_one,
    self_two,
    neigh_two,
    bias_two,
    cotangent,
):
    devs = lax.axis_size("dev")
    hosts = lax.axis_size("hst")
    chips = devs // CORES
    rows, width = features.shape
    tiles, blk = tile_val.shape[:2]
    send = send_list.shape[3]
    far = hosts * send
    all_rows = devs * (rows + far)
    half = jax.ShapeDtypeStruct((chips, rows + far, width), BF16)
    blocks = (shape(send, width),) * hosts
    space = pltpu.VMEM((all_rows, width), BF16)

    def halo_of(picked):
        arrived = across_hosts(picked)
        joined = call(
            functools.partial(join_kernel, hosts, send),
            "join",
            shape(far, width),
            [VMEM] * hosts,
            arrived,
            [pltpu.VMEM((far, width), F32)],
        )
        return across_devs(joined)

    def reduced(keep, give):
        came = core_permute(give)
        sums = call(
            functools.partial(core_sum_kernel, devs),
            "core_sum",
            (shape(rows + far, width, F32),) + (shape(rows + far, width),) * (chips - 1),
            [VMEM] * 2,
            (keep, came),
        )
        terms = [chip_permute(sums[k], k) for k in range(1, chips)]
        sums = call(
            functools.partial(chip_sum_kernel, hosts, send, chips - 1),
            "chip_sum",
            (shape(rows, width, F32),) + blocks,
            [VMEM] * chips,
            (sums[0], *terms),
            [pltpu.VMEM((far, width), F32)],
        )
        return sums[0], across_hosts(sums[1:])

    wide = across_devs(features)
    adj, keep, give, *picked = call(
        functools.partial(prep_kernel, devs),
        "prep",
        (shape(rows, all_rows), half, half) + blocks,
        [SMEM] * 4 + [ANY] + [VMEM] * 3,
        (tile_dst, tile_src, tile_rows, send_list, tile_val, features, cotangent, neigh_two),
        [
            pltpu.VMEM((tiles, blk, blk), BF16),
            pltpu.VMEM(((rows // blk) * (all_rows // blk), blk, blk), F32),
            space,
            pltpu.SemaphoreType.DMA((CHUNKS,)),
        ],
        limit=56,
    )
    halo = halo_of(picked)
    own, back = reduced(keep, give)
    pre, hidden, *picked = call(
        functools.partial(forward_one_kernel, devs),
        "forward_one",
        (shape(rows, width, F32), shape(rows, width)) + blocks,
        [SMEM] + [VMEM] * (4 + 2 * devs),
        (send_list, adj, self_one, neigh_one, bias_one, *wide, *halo),
        [space],
    )
    wide = across_devs(hidden)
    halo = halo_of(picked)
    grad_pre, keep, give = call(
        functools.partial(backward_two_kernel, devs, hosts),
        "backward_two",
        (shape(rows, width), half, half),
        [SMEM] + [VMEM] * (6 + hosts),
        (send_list, adj, pre, cotangent, self_two, neigh_one, own, *back),
        [space],
    )
    own, back = reduced(keep, give)
    output = call(
        functools.partial(forward_two_kernel, devs),
        "forward_two",
        shape(rows, width),
        [VMEM] * (4 + 2 * devs),
        (adj, self_two, neigh_two, bias_two, *wide, *halo),
        [space],
    )
    grad = call(
        functools.partial(backward_one_kernel, hosts),
        "backward_one",
        shape(rows, width, F32),
        [SMEM] + [VMEM] * (3 + hosts),
        (send_list, grad_pre, self_one, own, *back),
    )
    return output, grad


def solution(mesh):
    split = P(("hst", "dev"))
    return jax.shard_map(
        body,
        mesh=mesh,
        in_specs=(
            P(("hst", "dev"), None),
            P("hst", "dev", None, None),
            split,
            split,
            split,
            P(("hst", "dev"), None, None),
            P(),
            P(),
            P(),
            P(),
            P(),
            P(),
            P(("hst", "dev"), None),
        ),
        out_specs=(P(("hst", "dev"), None), P(("hst", "dev"), None)),
        check_vma=False,
    )
```

time: 194 us -> 99.3 us (0.51)
  other arithmetic: 61.7 us -> 0 us
  matrix products: 37.2 us -> 0 us
  waiting for transfers between devices: 11 us -> 37.9 us
  blocking collectives: 26 us -> 0 us
  starting transfers between devices: 22.5 us -> 47.1 us
  local copies, waits for them, and re-layouts: 20 us -> 2.78 us
  between operations: 14.2 us -> 0.84 us
  Pallas kernels: 0 us -> 10.4 us
    scatter-add x6 -> x0, other arithmetic: 52.1 us -> none  [the longest x2 24.9 us: spread(): jnp.zeros((source_blocks,) + products.shape[1:], jnp.float32).at[tile_src]]
    ppermute x0 -> x44, starting transfers between devices: none -> 47.1 us  [the longest x28 35.7 us: host_permute(): lax.ppermute(value, 'hst', [(h, (h + k) % hosts) for h in range(hosts)])]
    ppermute x0 -> x44, waiting for transfers between devices: none -> 37.9 us  [the longest x28 28.7 us: host_permute(): lax.ppermute(value, 'hst', [(h, (h + k) % hosts) for h in range(hosts)])]
    dot_general x12 -> x0, matrix products: 37.2 us -> none  [the longest x2 14.1 us: spread(): jnp.einsum('tij,tif->tjf', masked, seen, preferred_element_type=jnp.float32)]
    all_gather x4 -> x0, blocking collectives: 26 us -> none  [the longest x2 14.2 us: source_space(): hostwide = lax.all_gather(local, 'dev', axis=0, tiled=True)]
    all_to_all x4 -> x0, starting transfers between devices: 22.4 us -> none  [the longest x2 11.8 us: spread(): lax.all_to_all(far_sum.astype(jnp.bfloat16), 'hst', split_axis=1, concat_...]
    gather x6 -> x0, local copies, waits for them, and re-layouts: 15 us -> none  [the longest x2 5.67 us: spread(): seen = jnp.take(upstream.reshape(-1, block_rows, width), tile_dst, axis=0)]
    all_to_all x4 -> x0, waiting for transfers between devices: 10.9 us -> none  [the longest x2 10.9 us: spread(): lax.all_to_all(far_sum.astype(jnp.bfloat16), 'hst', split_axis=1, concat_...]
  transfers between devices with their start and end apart: 8 -> 44, of which waited for: 2 -> 18; matrix products, arithmetic and copies ran while one was open for 34% -> 0% of each run, Pallas kernels for 0% -> 3%
where the time goes in v2:
time: 99.3 us; the launch traced here: 99 us
  starting transfers between devices  47.1 us (47%)
  waiting for transfers between devices  37.9 us (38%)
  Pallas kernels  10.4 us (10%)
  local copies, waits for them, and re-layouts  2.78 us (3%)
    ppermute x28, starting transfers between devices, host_permute(): lax.ppermute(value, 'hst', [(h, (h + k) % hosts) for h in range(hosts)])  35.7 us
    ppermute x28, waiting for transfers between devices, host_permute(): lax.ppermute(value, 'hst', [(h, (h + k) % hosts) for h in range(hosts)])  28.7 us
    ppermute x6, starting transfers between devices, chip_permute(): lax.ppermute(value, 'dev', [(d, (d + k * CORES) % devs) for d in range(de...  10.8 us
    pallas_call x11, Pallas kernels, call(): pl.pallas_call(kernel, out_shape=out_shape, in_specs=in_specs, out_specs=...  10.4 us
    ppermute x6, waiting for transfers between devices, chip_permute(): lax.ppermute(value, 'dev', [(d, (d + k * CORES) % devs) for d in range(de...  9.14 us
    unnamed x26, local copies, waits for them, and re-layouts  2.78 us
  transfers between devices with their start and end apart: 44, of which 18 were waited for; matrix products, arithmetic and copies ran while one was open for 0% of the time, Pallas kernels for 3%

profile of v2, /device:TPU:0, one launch (start us, length us, event | category | flops | bytes accessed | tf_op | source)
XLA Modules:
  0.0 99.0 jit_solution(12354980477511650017)
XLA Ops:
  0.7 4.4 %prep.1 = (bf16[256,1280]{1,0:T(8,128)(2,1)}, bf16[2,320,256]{2,1,0:T(8,128)(2,1)}, bf16[2,320,256]{2,1,0:T(8,128)(2,1)}, bf16[8,256]{1,0:T(8,128)(2,1)}, bf16[8...) custom-call(s32[64]{0:T(128)} %dst_ref.1, ...), custom_call_target="tpu_custom_call" | custom-call | tf_op jit(solution)/shard_map/prep/pallas_call | solution.py:233
  5.6 2.6 %collective-permute-start.1 = (bf16[256,256]{1,0:T(8,128)(2,1)S(1)}, bf16[256,256]{1,0:T(8,128)(2,1)S(1)}, u32[]{:S(2)}, u32[]{:S(2)}) collective-permute-start(bf16[256,256]{1,0:T(8,128)(2,1)S(1)} %copy-done.5), channel_id=1, source_target_pairs={{0,2},{1,3},{2,0},{3,1},{4,6},{5,7},{6,4},{7,5},{8,10},{9,11},{10,... | collective-permute-start | bytes 393224 | tf_op jit(solution)/shard_map/ppermute | solution.py:251
  9.3 1.8 %collective-permute-start.27 = (bf16[320,256]{1,0:T(8,128)(2,1)S(1)}, bf16[320,256]{1,0:T(8,128)(2,1)S(1)}, u32[]{:S(2)}, u32[]{:S(2)}) collective-permute-start(bf16[320,256]{1,0:T(8,128)(2,1)S(1)} %get-tuple-element.70), channel_id=1, source_target_pairs={{0,2},{1,3},{2,0},{3,1},{4,6},{5,7},{6,4},{7,5},{8,10},{9,11},{10,... | collective-permute-start | bytes 491528 | tf_op jit(solution)/shard_map/ppermute | solution.py:251
  12.4 1.8 %collective-permute-start.3 = (bf16[8,256]{1,0:T(8,128)(2,1)}, bf16[8,256]{1,0:T(8,128)(2,1)S(1)}, u32[]{:S(2)}, u32[]{:S(2)}) collective-permute-start(bf16[8,256]{1,0:T(8,128)(2,1)} %get-tuple-element.50), channel_id=1, source_target_pairs={{0,4},{4,8},{8,12},{12,16},{16,20},{20,24},{24,28},{28,0},{1,5},{5... | collective-permute-start | bytes 12296 | tf_op jit(solution)/shard_map/ppermute | solution.py:256
  14.2 1.6 %collective-permute-start.4 = (bf16[8,256]{1,0:T(8,128)(2,1)}, bf16[8,256]{1,0:T(8,128)(2,1)S(1)}, u32[]{:S(2)}, u32[]{:S(2)}) collective-permute-start(bf16[8,256]{1,0:T(8,128)(2,1)} %get-tuple-element.51), channel_id=1, source_target_pairs={{0,8},{4,12},{8,16},{12,20},{16,24},{20,28},{24,0},{28,4},{1,9},{5... | collective-permute-start | bytes 12296 | tf_op jit(solution)/shard_map/ppermute | solution.py:256
  15.8 3.3 %collective-permute-done.3.refs_1_ = bf16[8,256]{1,0:T(8,128)(2,1)S(1)} collective-permute-done((bf16[8,256]{1,0:T(8,128)(2,1)}, bf16[8,256]{1,0:T(8,128)(2,1)S(1)}, u32[]{:S(2)}, u32[]{:S(2)}) %collective-permute-start.3) | collective-permute-done | bytes 4128 | tf_op jit(solution)/shard_map/ppermute | solution.py:256
  19.9 1.8 %collective-permute-start.6 = (bf16[8,256]{1,0:T(8,128)(2,1)}, bf16[8,256]{1,0:T(8,128)(2,1)S(1)}, u32[]{:S(2)}, u32[]{:S(2)}) collective-permute-start(bf16[8,256]{1,0:T(8,128)(2,1)} %get-tuple-element.53), channel_id=1, source_target_pairs={{0,16},{4,20},{8,24},{12,28},{16,0},{20,4},{24,8},{28,12},{1,17},{... | collective-permute-start | bytes 12296 | tf_op jit(solution)/shard_map/ppermute | solution.py:256
  21.7 3.0 %collective-permute-done.5.refs_3_ = bf16[8,256]{1,0:T(8,128)(2,1)S(1)} collective-permute-done((bf16[8,256]{1,0:T(8,128)(2,1)}, bf16[8,256]{1,0:T(8,128)(2,1)S(1)}, u32[]{:S(2)}, u32[]{:S(2)}) %collective-permute-start.5) | collective-permute-done | bytes 4128 | tf_op jit(solution)/shard_map/ppermute | solution.py:256
  24.8 1.8 %collective-permute-start.8 = (bf16[8,256]{1,0:T(8,128)(2,1)}, bf16[8,256]{1,0:T(8,128)(2,1)S(1)}, u32[]{:S(2)}, u32[]{:S(2)}) collective-permute-start(bf16[8,256]{1,0:T(8,128)(2,1)} %get-tuple-element.55), channel_id=1, source_target_pairs={{0,24},{4,28},{8,0},{12,4},{16,8},{20,12},{24,16},{28,20},{1,25},{... | collective-permute-start | bytes 12296 | tf_op jit(solution)/shard_map/ppermute | solution.py:256
  26.7 2.7 %collective-permute-done.7.refs_5_ = bf16[8,256]{1,0:T(8,128)(2,1)S(1)} collective-permute-done((bf16[8,256]{1,0:T(8,128)(2,1)}, bf16[8,256]{1,0:T(8,128)(2,1)S(1)}, u32[]{:S(2)}, u32[]{:S(2)}) %collective-permute-start.7) | collective-permute-done | bytes 4128 | tf_op jit(solution)/shard_map/ppermute | solution.py:256
  29.4 2.0 %collective-permute-start.9 = (bf16[8,256]{1,0:T(8,128)(2,1)}, bf16[8,256]{1,0:T(8,128)(2,1)S(1)}, u32[]{:S(2)}, u32[]{:S(2)}) collective-permute-start(bf16[8,256]{1,0:T(8,128)(2,1)} %get-tuple-element.56), channel_id=1, source_target_pairs={{0,28},{4,0},{8,4},{12,8},{16,12},{20,16},{24,20},{28,24},{1,29},{... | collective-permute-start | bytes 12296 | tf_op jit(solution)/shard_map/ppermute | solution.py:256
  31.4 1.8 %collective-permute-done.9.refs_7_ = bf16[8,256]{1,0:T(8,128)(2,1)S(1)} collective-permute-done((bf16[8,256]{1,0:T(8,128)(2,1)}, bf16[8,256]{1,0:T(8,128)(2,1)S(1)}, u32[]{:S(2)}, u32[]{:S(2)}) %collective-permute-start.9) | collective-permute-done | bytes 4128 | tf_op jit(solution)/shard_map/ppermute | solution.py:256
  33.9 1.7 %collective-permute-start.11 = (bf16[64,256]{1,0:T(8,128)(2,1)S(1)}, bf16[64,256]{1,0:T(8,128)(2,1)S(1)}, u32[]{:S(2)}, u32[]{:S(2)}) collective-permute-start(bf16[64,256]{1,0:T(8,128)(2,1)S(1)} %join.2.refs_4_), channel_id=1, source_target_pairs={{0,2},{1,3},{2,0},{3,1},{4,6},{5,7},{6,4},{7,5},{8,10},{9,11},{10,... | collective-permute-start | bytes 98312 | tf_op jit(solution)/shard_map/ppermute | solution.py:251
  35.7 2.3 %collective-permute-done.11.refs_6_ = bf16[64,256]{1,0:T(8,128)(2,1)S(1)} collective-permute-done((bf16[64,256]{1,0:T(8,128)(2,1)S(1)}, bf16[64,256]{1,0:T(8,128)(2,1)S(1)}, u32[]{:S(2)}, u32[]{:S(2)}) %collective-permute-start.11) | collective-permute-done | bytes 32800 | tf_op jit(solution)/shard_map/ppermute | solution.py:251
  38.0 1.7 %collective-permute-start.28 = (bf16[8,256]{1,0:T(8,128)(2,1)S(1)}, bf16[8,256]{1,0:T(8,128)(2,1)S(1)}, u32[]{:S(2)}, u32[]{:S(2)}) collective-permute-start(bf16[8,256]{1,0:T(8,128)(2,1)S(1)} %get-tuple-element.73), channel_id=1, source_target_pairs={{0,4},{4,8},{8,12},{12,16},{16,20},{20,24},{24,28},{28,0},{1,5},{5... | collective-permute-start | bytes 12296 | tf_op jit(solution)/shard_map/ppermute | solution.py:256
  40.0 3.8 %collective-permute-start.30 = (bf16[8,256]{1,0:T(8,128)(2,1)S(1)}, bf16[8,256]{1,0:T(8,128)(2,1)S(1)}, u32[]{:S(2)}, u32[]{:S(2)}) collective-permute-start(bf16[8,256]{1,0:T(8,128)(2,1)S(1)} %get-tuple-element.75), channel_id=1, source_target_pairs={{0,12},{4,16},{8,20},{12,24},{16,28},{20,0},{24,4},{28,8},{1,13},{... | collective-permute-start | bytes 12296 | tf_op jit(solution)/shard_map/ppermute | solution.py:256
  44.4 3.3 %collective-permute-start.32 = (bf16[8,256]{1,0:T(8,128)(2,1)S(1)}, bf16[8,256]{1,0:T(8,128)(2,1)S(1)}, u32[]{:S(2)}, u32[]{:S(2)}) collective-permute-start(bf16[8,256]{1,0:T(8,128)(2,1)S(1)} %get-tuple-element.77), channel_id=1, source_target_pairs={{0,20},{4,24},{8,28},{12,0},{16,4},{20,8},{24,12},{28,16},{1,21},{... | collective-permute-start | bytes 12296 | tf_op jit(solution)/shard_map/ppermute | solution.py:256
  53.7 1.6 %collective-permute-start.14 = (bf16[256,256]{1,0:T(8,128)(2,1)S(1)}, bf16[256,256]{1,0:T(8,128)(2,1)S(1)}, u32[]{:S(2)}, u32[]{:S(2)}) collective-permute-start(bf16[256,256]{1,0:T(8,128)(2,1)S(1)} %get-tuple-element.57.refs_0_), channel_id=1, source_target_pairs={{0,2},{1,3},{2,0},{3,1},{4,6},{5,7},{6,4},{7,5},{8,10},{9,11},{10,... | collective-permute-start | bytes 393224 | tf_op jit(solution)/shard_map/ppermute | solution.py:251
  55.4 1.6 %collective-permute-start.36 = (bf16[320,256]{1,0:T(8,128)(2,1)S(1)}, bf16[320,256]{1,0:T(8,128)(2,1)S(1)}, u32[]{:S(2)}, u32[]{:S(2)}) collective-permute-start(bf16[320,256]{1,0:T(8,128)(2,1)S(1)} %get-tuple-element.84), channel_id=1, source_target_pairs={{0,2},{1,3},{2,0},{3,1},{4,6},{5,7},{6,4},{7,5},{8,10},{9,11},{10,... | collective-permute-start | bytes 491528 | tf_op jit(solution)/shard_map/ppermute | solution.py:251
  57.0 3.1 %collective-permute-done.14.refs_2_ = bf16[256,256]{1,0:T(8,128)(2,1)S(1)} collective-permute-done((bf16[256,256]{1,0:T(8,128)(2,1)S(1)}, bf16[256,256]{1,0:T(8,128)(2,1)S(1)}, u32[]{:S(2)}, u32[]{:S(2)}) %collective-permute-start.14) | collective-permute-done | bytes 131104 | tf_op jit(solution)/shard_map/ppermute | solution.py:251
  60.1 2.0 %collective-permute-start.16 = (bf16[8,256]{1,0:T(8,128)(2,1)S(1)}, bf16[8,256]{1,0:T(8,128)(2,1)S(1)}, u32[]{:S(2)}, u32[]{:S(2)}) collective-permute-start(bf16[8,256]{1,0:T(8,128)(2,1)S(1)} %get-tuple-element.59), channel_id=1, source_target_pairs={{0,4},{4,8},{8,12},{12,16},{16,20},{20,24},{24,28},{28,0},{1,5},{5... | collective-permute-start | bytes 12296 | tf_op jit(solution)/shard_map/ppermute | solution.py:256
  62.3 4.1 %collective-permute-done.16.refs_1_ = bf16[8,256]{1,0:T(8,128)(2,1)S(1)} collective-permute-done((bf16[8,256]{1,0:T(8,128)(2,1)S(1)}, bf16[8,256]{1,0:T(8,128)(2,1)S(1)}, u32[]{:S(2)}, u32[]{:S(2)}) %collective-permute-start.16) | collective-permute-done | bytes 4128 | tf_op jit(solution)/shard_map/ppermute | solution.py:256
  67.6 4.2 %collective-permute-done.18.refs_3_ = bf16[8,256]{1,0:T(8,128)(2,1)S(1)} collective-permute-done((bf16[8,256]{1,0:T(8,128)(2,1)S(1)}, bf16[8,256]{1,0:T(8,128)(2,1)S(1)}, u32[]{:S(2)}, u32[]{:S(2)}) %collective-permute-start.18) | collective-permute-done | bytes 4128 | tf_op jit(solution)/shard_map/ppermute | solution.py:256
  73.5 2.8 %collective-permute-done.20.refs_5_ = bf16[8,256]{1,0:T(8,128)(2,1)S(1)} collective-permute-done((bf16[8,256]{1,0:T(8,128)(2,1)S(1)}, bf16[8,256]{1,0:T(8,128)(2,1)S(1)}, u32[]{:S(2)}, u32[]{:S(2)}) %collective-permute-start.20) | collective-permute-done | bytes 4128 | tf_op jit(solution)/shard_map/ppermute | solution.py:256
  77.0 2.9 %collective-permute-done.22.refs_7_ = bf16[8,256]{1,0:T(8,128)(2,1)S(1)} collective-permute-done((bf16[8,256]{1,0:T(8,128)(2,1)S(1)}, bf16[8,256]{1,0:T(8,128)(2,1)S(1)}, u32[]{:S(2)}, u32[]{:S(2)}) %collective-permute-start.22) | collective-permute-done | bytes 4128 | tf_op jit(solution)/shard_map/ppermute | solution.py:256
  79.9 1.6 %collective-permute-start.24 = (bf16[64,256]{1,0:T(8,128)(2,1)S(1)}, bf16[64,256]{1,0:T(8,128)(2,1)S(1)}, u32[]{:S(2)}, u32[]{:S(2)}) collective-permute-start(bf16[64,256]{1,0:T(8,128)(2,1)S(1)} %join.3.refs_4_), channel_id=1, source_target_pairs={{0,2},{1,3},{2,0},{3,1},{4,6},{5,7},{6,4},{7,5},{8,10},{9,11},{10,... | collective-permute-start | bytes 98312 | tf_op jit(solution)/shard_map/ppermute | solution.py:251
  81.5 2.4 %collective-permute-done.24.refs_6_ = bf16[64,256]{1,0:T(8,128)(2,1)S(1)} collective-permute-done((bf16[64,256]{1,0:T(8,128)(2,1)S(1)}, bf16[64,256]{1,0:T(8,128)(2,1)S(1)}, u32[]{:S(2)}, u32[]{:S(2)}) %collective-permute-start.24) | collective-permute-done | bytes 32800 | tf_op jit(solution)/shard_map/ppermute | solution.py:251
  84.0 2.1 %collective-permute-start.37 = (bf16[8,256]{1,0:T(8,128)(2,1)S(1)}, bf16[8,256]{1,0:T(8,128)(2,1)S(1)}, u32[]{:S(2)}, u32[]{:S(2)}) collective-permute-start(bf16[8,256]{1,0:T(8,128)(2,1)S(1)} %get-tuple-element.87), channel_id=1, source_target_pairs={{0,4},{4,8},{8,12},{12,16},{16,20},{20,24},{24,28},{28,0},{1,5},{5... | collective-permute-start | bytes 12296 | tf_op jit(solution)/shard_map/ppermute | solution.py:256
  86.1 1.8 %collective-permute-start.39 = (bf16[8,256]{1,0:T(8,128)(2,1)S(1)}, bf16[8,256]{1,0:T(8,128)(2,1)S(1)}, u32[]{:S(2)}, u32[]{:S(2)}) collective-permute-start(bf16[8,256]{1,0:T(8,128)(2,1)S(1)} %get-tuple-element.89), channel_id=1, source_target_pairs={{0,12},{4,16},{8,20},{12,24},{16,28},{20,0},{24,4},{28,8},{1,13},{... | collective-permute-start | bytes 12296 | tf_op jit(solution)/shard_map/ppermute | solution.py:256
  87.9 2.1 %collective-permute-start.40 = (bf16[8,256]{1,0:T(8,128)(2,1)S(1)}, bf16[8,256]{1,0:T(8,128)(2,1)S(1)}, u32[]{:S(2)}, u32[]{:S(2)}) collective-permute-start(bf16[8,256]{1,0:T(8,128)(2,1)S(1)} %get-tuple-element.90), channel_id=1, source_target_pairs={{0,16},{4,20},{8,24},{12,28},{16,0},{20,4},{24,8},{28,12},{1,17},{... | collective-permute-start | bytes 12296 | tf_op jit(solution)/shard_map/ppermute | solution.py:256
  90.0 2.4 %collective-permute-start.41 = (bf16[8,256]{1,0:T(8,128)(2,1)S(1)}, bf16[8,256]{1,0:T(8,128)(2,1)S(1)}, u32[]{:S(2)}, u32[]{:S(2)}) collective-permute-start(bf16[8,256]{1,0:T(8,128)(2,1)S(1)} %get-tuple-element.91), channel_id=1, source_target_pairs={{0,20},{4,24},{8,28},{12,0},{16,4},{20,8},{24,12},{28,16},{1,21},{... | collective-permute-start | bytes 12296 | tf_op jit(solution)/shard_map/ppermute | solution.py:256
  97.4 1.6 %backward_one.1 = f32[256,256]{1,0:T(8,128)} custom-call(s32[1,1,8,8]{3,2,1,0:T(8,128)S(1)} %copy-done.9, bf16[256,256]{1,0:T(8,128)(2,1)S(1)} %get-tuple-element.80.grad_pre_ref, bf16[256,256]{1,0:T(8,128)(2,1)S(1)} %copy-done.7, f32[256,256]{1,0:T(8,128)S(1)} %get-tuple-element.85.own_ref, bf16[8,256]{1,0:T(8,128)(2,1)S(1)} %get-tuple-element.86.refs_0_, ...), custom_call_target="tpu_custom_call" | custom-call | tf_op jit(solution)/shard_map/backward_one/pallas_call | solution.py:233
  (93 shorter events, 20.4 us)
Async XLA Ops:
  5.6 6.8 %collective-permute-start.1 = (bf16[256,256]{1,0:T(8,128)(2,1)S(1)}, bf16[256,256]{1,0:T(8,128)(2,1)S(1)}, u32[]{:S(2)}, u32[]{:S(2)}) collective-permute-start(bf16[256,256]{1,0:T(8,128)(2,1)S(1)} %copy-done.5), channel_id=1, source_target_pairs={{0,2},{1,3},{2,0},{3,1},{4,6},{5,7},{6,4},{7,5},{8,10},{9,11},{10,... | collective-permute-start | bytes 393224 | tf_op jit(solution)/shard_map/ppermute | solution.py:251
  9.3 28.7 %collective-permute-start.27 = (bf16[320,256]{1,0:T(8,128)(2,1)S(1)}, bf16[320,256]{1,0:T(8,128)(2,1)S(1)}, u32[]{:S(2)}, u32[]{:S(2)}) collective-permute-start(bf16[320,256]{1,0:T(8,128)(2,1)S(1)} %get-tuple-element.70), channel_id=1, source_target_pairs={{0,2},{1,3},{2,0},{3,1},{4,6},{5,7},{6,4},{7,5},{8,10},{9,11},{10,... | collective-permute-start | bytes 491528 | tf_op jit(solution)/shard_map/ppermute | solution.py:251
  11.1 32.8 %collective-permute-start = (bf16[256,256]{1,0:T(8,128)(2,1)S(1)}, bf16[256,256]{1,0:T(8,128)(2,1)S(1)}, u32[]{:S(2)}, u32[]{:S(2)}) collective-permute-start(bf16[256,256]{1,0:T(8,128)(2,1)S(1)} %copy-done.5), channel_id=1, source_target_pairs={{0,1},{1,0},{2,3},{3,2},{4,5},{5,4},{6,7},{7,6},{8,9},{9,8},{10,11... | collective-permute-start | bytes 393224 | tf_op jit(solution)/shard_map/ppermute | solution.py:246
  12.4 32.0 %collective-permute-start.2 = (bf16[256,256]{1,0:T(8,128)(2,1)S(1)}, bf16[256,256]{1,0:T(8,128)(2,1)S(1)}, u32[]{:S(2)}, u32[]{:S(2)}) collective-permute-start(bf16[256,256]{1,0:T(8,128)(2,1)S(1)} %collective-permute-done.1.refs_2_), channel_id=1, source_target_pairs={{0,1},{1,0},{2,3},{3,2},{4,5},{5,4},{6,7},{7,6},{8,9},{9,8},{10,11... | collective-permute-start | bytes 393224 | tf_op jit(solution)/shard_map/ppermute | solution.py:246
  12.4 6.6 %collective-permute-start.3 = (bf16[8,256]{1,0:T(8,128)(2,1)}, bf16[8,256]{1,0:T(8,128)(2,1)S(1)}, u32[]{:S(2)}, u32[]{:S(2)}) collective-permute-start(bf16[8,256]{1,0:T(8,128)(2,1)} %get-tuple-element.50), channel_id=1, source_target_pairs={{0,4},{4,8},{8,12},{12,16},{16,20},{20,24},{24,28},{28,0},{1,5},{5... | collective-permute-start | bytes 12296 | tf_op jit(solution)/shard_map/ppermute | solution.py:256
  14.2 5.6 %collective-permute-start.4 = (bf16[8,256]{1,0:T(8,128)(2,1)}, bf16[8,256]{1,0:T(8,128)(2,1)S(1)}, u32[]{:S(2)}, u32[]{:S(2)}) collective-permute-start(bf16[8,256]{1,0:T(8,128)(2,1)} %get-tuple-element.51), channel_id=1, source_target_pairs={{0,8},{4,12},{8,16},{12,20},{16,24},{20,28},{24,0},{28,4},{1,9},{5... | collective-permute-start | bytes 12296 | tf_op jit(solution)/shard_map/ppermute | solution.py:256
  19.1 5.6 %collective-permute-start.5 = (bf16[8,256]{1,0:T(8,128)(2,1)}, bf16[8,256]{1,0:T(8,128)(2,1)S(1)}, u32[]{:S(2)}, u32[]{:S(2)}) collective-permute-start(bf16[8,256]{1,0:T(8,128)(2,1)} %get-tuple-element.52), channel_id=1, source_target_pairs={{0,12},{4,16},{8,20},{12,24},{16,28},{20,0},{24,4},{28,8},{1,13},{... | collective-permute-start | bytes 12296 | tf_op jit(solution)/shard_map/ppermute | solution.py:256
  19.9 5.0 %collective-permute-start.6 = (bf16[8,256]{1,0:T(8,128)(2,1)}, bf16[8,256]{1,0:T(8,128)(2,1)S(1)}, u32[]{:S(2)}, u32[]{:S(2)}) collective-permute-start(bf16[8,256]{1,0:T(8,128)(2,1)} %get-tuple-element.53), channel_id=1, source_target_pairs={{0,16},{4,20},{8,24},{12,28},{16,0},{20,4},{24,8},{28,12},{1,17},{... | collective-permute-start | bytes 12296 | tf_op jit(solution)/shard_map/ppermute | solution.py:256
  24.7 4.7 %collective-permute-start.7 = (bf16[8,256]{1,0:T(8,128)(2,1)}, bf16[8,256]{1,0:T(8,128)(2,1)S(1)}, u32[]{:S(2)}, u32[]{:S(2)}) collective-permute-start(bf16[8,256]{1,0:T(8,128)(2,1)} %get-tuple-element.54), channel_id=1, source_target_pairs={{0,20},{4,24},{8,28},{12,0},{16,4},{20,8},{24,12},{28,16},{1,21},{... | collective-permute-start | bytes 12296 | tf_op jit(solution)/shard_map/ppermute | solution.py:256
  24.8 6.6 %collective-permute-start.8 = (bf16[8,256]{1,0:T(8,128)(2,1)}, bf16[8,256]{1,0:T(8,128)(2,1)S(1)}, u32[]{:S(2)}, u32[]{:S(2)}) collective-permute-start(bf16[8,256]{1,0:T(8,128)(2,1)} %get-tuple-element.55), channel_id=1, source_target_pairs={{0,24},{4,28},{8,0},{12,4},{16,8},{20,12},{24,16},{28,20},{1,25},{... | collective-permute-start | bytes 12296 | tf_op jit(solution)/shard_map/ppermute | solution.py:256
  38.0 9.7 %collective-permute-start.28 = (bf16[8,256]{1,0:T(8,128)(2,1)S(1)}, bf16[8,256]{1,0:T(8,128)(2,1)S(1)}, u32[]{:S(2)}, u32[]{:S(2)}) collective-permute-start(bf16[8,256]{1,0:T(8,128)(2,1)S(1)} %get-tuple-element.73), channel_id=1, source_target_pairs={{0,4},{4,8},{8,12},{12,16},{16,20},{20,24},{24,28},{28,0},{1,5},{5... | collective-permute-start | bytes 12296 | tf_op jit(solution)/shard_map/ppermute | solution.py:256
  39.7 8.9 %collective-permute-start.29 = (bf16[8,256]{1,0:T(8,128)(2,1)S(1)}, bf16[8,256]{1,0:T(8,128)(2,1)S(1)}, u32[]{:S(2)}, u32[]{:S(2)}) collective-permute-start(bf16[8,256]{1,0:T(8,128)(2,1)S(1)} %get-tuple-element.74), channel_id=1, source_target_pairs={{0,8},{4,12},{8,16},{12,20},{16,24},{20,28},{24,0},{28,4},{1,9},{5... | collective-permute-start | bytes 12296 | tf_op jit(solution)/shard_map/ppermute | solution.py:256
  40.0 11.7 %collective-permute-start.30 = (bf16[8,256]{1,0:T(8,128)(2,1)S(1)}, bf16[8,256]{1,0:T(8,128)(2,1)S(1)}, u32[]{:S(2)}, u32[]{:S(2)}) collective-permute-start(bf16[8,256]{1,0:T(8,128)(2,1)S(1)} %get-tuple-element.75), channel_id=1, source_target_pairs={{0,12},{4,16},{8,20},{12,24},{16,28},{20,0},{24,4},{28,8},{1,13},{... | collective-permute-start | bytes 12296 | tf_op jit(solution)/shard_map/ppermute | solution.py:256
  43.8 7.9 %collective-permute-start.31 = (bf16[8,256]{1,0:T(8,128)(2,1)S(1)}, bf16[8,256]{1,0:T(8,128)(2,1)S(1)}, u32[]{:S(2)}, u32[]{:S(2)}) collective-permute-start(bf16[8,256]{1,0:T(8,128)(2,1)S(1)} %get-tuple-element.76), channel_id=1, source_target_pairs={{0,16},{4,20},{8,24},{12,28},{16,0},{20,4},{24,8},{28,12},{1,17},{... | collective-permute-start | bytes 12296 | tf_op jit(solution)/shard_map/ppermute | solution.py:256
  44.4 7.3 %collective-permute-start.32 = (bf16[8,256]{1,0:T(8,128)(2,1)S(1)}, bf16[8,256]{1,0:T(8,128)(2,1)S(1)}, u32[]{:S(2)}, u32[]{:S(2)}) collective-permute-start(bf16[8,256]{1,0:T(8,128)(2,1)S(1)} %get-tuple-element.77), channel_id=1, source_target_pairs={{0,20},{4,24},{8,28},{12,0},{16,4},{20,8},{24,12},{28,16},{1,21},{... | collective-permute-start | bytes 12296 | tf_op jit(solution)/shard_map/ppermute | solution.py:256
  47.7 4.1 %collective-permute-start.33 = (bf16[8,256]{1,0:T(8,128)(2,1)S(1)}, bf16[8,256]{1,0:T(8,128)(2,1)S(1)}, u32[]{:S(2)}, u32[]{:S(2)}) collective-permute-start(bf16[8,256]{1,0:T(8,128)(2,1)S(1)} %get-tuple-element.78), channel_id=1, source_target_pairs={{0,24},{4,28},{8,0},{12,4},{16,8},{20,12},{24,16},{28,20},{1,25},{... | collective-permute-start | bytes 12296 | tf_op jit(solution)/shard_map/ppermute | solution.py:256
  53.7 6.4 %collective-permute-start.14 = (bf16[256,256]{1,0:T(8,128)(2,1)S(1)}, bf16[256,256]{1,0:T(8,128)(2,1)S(1)}, u32[]{:S(2)}, u32[]{:S(2)}) collective-permute-start(bf16[256,256]{1,0:T(8,128)(2,1)S(1)} %get-tuple-element.57.refs_0_), channel_id=1, source_target_pairs={{0,2},{1,3},{2,0},{3,1},{4,6},{5,7},{6,4},{7,5},{8,10},{9,11},{10,... | collective-permute-start | bytes 393224 | tf_op jit(solution)/shard_map/ppermute | solution.py:251
  55.4 28.5 %collective-permute-start.36 = (bf16[320,256]{1,0:T(8,128)(2,1)S(1)}, bf16[320,256]{1,0:T(8,128)(2,1)S(1)}, u32[]{:S(2)}, u32[]{:S(2)}) collective-permute-start(bf16[320,256]{1,0:T(8,128)(2,1)S(1)} %get-tuple-element.84), channel_id=1, source_target_pairs={{0,2},{1,3},{2,0},{3,1},{4,6},{5,7},{6,4},{7,5},{8,10},{9,11},{10,... | collective-permute-start | bytes 491528 | tf_op jit(solution)/shard_map/ppermute | solution.py:251
  57.0 30.9 %collective-permute-start.13 = (bf16[256,256]{1,0:T(8,128)(2,1)S(1)}, bf16[256,256]{1,0:T(8,128)(2,1)S(1)}, u32[]{:S(2)}, u32[]{:S(2)}) collective-permute-start(bf16[256,256]{1,0:T(8,128)(2,1)S(1)} %get-tuple-element.57.refs_0_), channel_id=1, source_target_pairs={{0,1},{1,0},{2,3},{3,2},{4,5},{5,4},{6,7},{7,6},{8,9},{9,8},{10,11... | collective-permute-start | bytes 393224 | tf_op jit(solution)/shard_map/ppermute | solution.py:246
  60.1 29.9 %collective-permute-start.15 = (bf16[256,256]{1,0:T(8,128)(2,1)S(1)}, bf16[256,256]{1,0:T(8,128)(2,1)S(1)}, u32[]{:S(2)}, u32[]{:S(2)}) collective-permute-start(bf16[256,256]{1,0:T(8,128)(2,1)S(1)} %collective-permute-done.14.refs_2_), channel_id=1, source_target_pairs={{0,1},{1,0},{2,3},{3,2},{4,5},{5,4},{6,7},{7,6},{8,9},{9,8},{10,11... | collective-permute-start | bytes 393224 | tf_op jit(solution)/shard_map/ppermute | solution.py:246
  60.1 6.3 %collective-permute-start.16 = (bf16[8,256]{1,0:T(8,128)(2,1)S(1)}, bf16[8,256]{1,0:T(8,128)(2,1)S(1)}, u32[]{:S(2)}, u32[]{:S(2)}) collective-permute-start(bf16[8,256]{1,0:T(8,128)(2,1)S(1)} %get-tuple-element.59), channel_id=1, source_target_pairs={{0,4},{4,8},{8,12},{12,16},{16,20},{20,24},{24,28},{28,0},{1,5},{5... | collective-permute-start | bytes 12296 | tf_op jit(solution)/shard_map/ppermute | solution.py:256
  62.1 5.4 %collective-permute-start.17 = (bf16[8,256]{1,0:T(8,128)(2,1)S(1)}, bf16[8,256]{1,0:T(8,128)(2,1)S(1)}, u32[]{:S(2)}, u32[]{:S(2)}) collective-permute-start(bf16[8,256]{1,0:T(8,128)(2,1)S(1)} %get-tuple-element.60), channel_id=1, source_target_pairs={{0,8},{4,12},{8,16},{12,20},{16,24},{20,28},{24,0},{28,4},{1,9},{5... | collective-permute-start | bytes 12296 | tf_op jit(solution)/shard_map/ppermute | solution.py:256
  66.4 5.4 %collective-permute-start.18 = (bf16[8,256]{1,0:T(8,128)(2,1)S(1)}, bf16[8,256]{1,0:T(8,128)(2,1)S(1)}, u32[]{:S(2)}, u32[]{:S(2)}) collective-permute-start(bf16[8,256]{1,0:T(8,128)(2,1)S(1)} %get-tuple-element.61), channel_id=1, source_target_pairs={{0,12},{4,16},{8,20},{12,24},{16,28},{20,0},{24,4},{28,8},{1,13},{... | collective-permute-start | bytes 12296 | tf_op jit(solution)/shard_map/ppermute | solution.py:256
  67.5 4.5 %collective-permute-start.19 = (bf16[8,256]{1,0:T(8,128)(2,1)S(1)}, bf16[8,256]{1,0:T(8,128)(2,1)S(1)}, u32[]{:S(2)}, u32[]{:S(2)}) collective-permute-start(bf16[8,256]{1,0:T(8,128)(2,1)S(1)} %get-tuple-element.62), channel_id=1, source_target_pairs={{0,16},{4,20},{8,24},{12,28},{16,0},{20,4},{24,8},{28,12},{1,17},{... | collective-permute-start | bytes 12296 | tf_op jit(solution)/shard_map/ppermute | solution.py:256
  71.8 4.5 %collective-permute-start.20 = (bf16[8,256]{1,0:T(8,128)(2,1)S(1)}, bf16[8,256]{1,0:T(8,128)(2,1)S(1)}, u32[]{:S(2)}, u32[]{:S(2)}) collective-permute-start(bf16[8,256]{1,0:T(8,128)(2,1)S(1)} %get-tuple-element.63), channel_id=1, source_target_pairs={{0,20},{4,24},{8,28},{12,0},{16,4},{20,8},{24,12},{28,16},{1,21},{... | collective-permute-start | bytes 12296 | tf_op jit(solution)/shard_map/ppermute | solution.py:256
  72.0 5.0 %collective-permute-start.21 = (bf16[8,256]{1,0:T(8,128)(2,1)S(1)}, bf16[8,256]{1,0:T(8,128)(2,1)S(1)}, u32[]{:S(2)}, u32[]{:S(2)}) collective-permute-start(bf16[8,256]{1,0:T(8,128)(2,1)S(1)} %get-tuple-element.64), channel_id=1, source_target_pairs={{0,24},{4,28},{8,0},{12,4},{16,8},{20,12},{24,16},{28,20},{1,25},{... | collective-permute-start | bytes 12296 | tf_op jit(solution)/shard_map/ppermute | solution.py:256
  81.5 4.5 %collective-permute-start.23 = (bf16[64,256]{1,0:T(8,128)(2,1)S(1)}, bf16[64,256]{1,0:T(8,128)(2,1)S(1)}, u32[]{:S(2)}, u32[]{:S(2)}) collective-permute-start(bf16[64,256]{1,0:T(8,128)(2,1)S(1)} %join.3.refs_4_), channel_id=1, source_target_pairs={{0,1},{1,0},{2,3},{3,2},{4,5},{5,4},{6,7},{7,6},{8,9},{9,8},{10,11... | collective-permute-start | bytes 98312 | tf_op jit(solution)/shard_map/ppermute | solution.py:246
  84.0 8.4 %collective-permute-start.37 = (bf16[8,256]{1,0:T(8,128)(2,1)S(1)}, bf16[8,256]{1,0:T(8,128)(2,1)S(1)}, u32[]{:S(2)}, u32[]{:S(2)}) collective-permute-start(bf16[8,256]{1,0:T(8,128)(2,1)S(1)} %get-tuple-element.87), channel_id=1, source_target_pairs={{0,4},{4,8},{8,12},{12,16},{16,20},{20,24},{24,28},{28,0},{1,5},{5... | collective-permute-start | bytes 12296 | tf_op jit(solution)/shard_map/ppermute | solution.py:256
  86.1 7.7 %collective-permute-start.38 = (bf16[8,256]{1,0:T(8,128)(2,1)S(1)}, bf16[8,256]{1,0:T(8,128)(2,1)S(1)}, u32[]{:S(2)}, u32[]{:S(2)}) collective-permute-start(bf16[8,256]{1,0:T(8,128)(2,1)S(1)} %get-tuple-element.88), channel_id=1, source_target_pairs={{0,8},{4,12},{8,16},{12,20},{16,24},{20,28},{24,0},{28,4},{1,9},{5... | collective-permute-start | bytes 12296 | tf_op jit(solution)/shard_map/ppermute | solution.py:256
  86.1 10.1 %collective-permute-start.39 = (bf16[8,256]{1,0:T(8,128)(2,1)S(1)}, bf16[8,256]{1,0:T(8,128)(2,1)S(1)}, u32[]{:S(2)}, u32[]{:S(2)}) collective-permute-start(bf16[8,256]{1,0:T(8,128)(2,1)S(1)} %get-tuple-element.89), channel_id=1, source_target_pairs={{0,12},{4,16},{8,20},{12,24},{16,28},{20,0},{24,4},{28,8},{1,13},{... | collective-permute-start | bytes 12296 | tf_op jit(solution)/shard_map/ppermute | solution.py:256
  87.9 8.3 %collective-permute-start.40 = (bf16[8,256]{1,0:T(8,128)(2,1)S(1)}, bf16[8,256]{1,0:T(8,128)(2,1)S(1)}, u32[]{:S(2)}, u32[]{:S(2)}) collective-permute-start(bf16[8,256]{1,0:T(8,128)(2,1)S(1)} %get-tuple-element.90), channel_id=1, source_target_pairs={{0,16},{4,20},{8,24},{12,28},{16,0},{20,4},{24,8},{28,12},{1,17},{... | collective-permute-start | bytes 12296 | tf_op jit(solution)/shard_map/ppermute | solution.py:256
  90.0 6.2 %collective-permute-start.41 = (bf16[8,256]{1,0:T(8,128)(2,1)S(1)}, bf16[8,256]{1,0:T(8,128)(2,1)S(1)}, u32[]{:S(2)}, u32[]{:S(2)}) collective-permute-start(bf16[8,256]{1,0:T(8,128)(2,1)S(1)} %get-tuple-element.91), channel_id=1, source_target_pairs={{0,20},{4,24},{8,28},{12,0},{16,4},{20,8},{24,12},{28,16},{1,21},{... | collective-permute-start | bytes 12296 | tf_op jit(solution)/shard_map/ppermute | solution.py:256
  (25 other events, 478.0 us)

commit v3 on v1

v3 whole, which is shorter than its diff:
```python
import functools

import jax
import jax.numpy as jnp
from jax import lax
from jax.experimental import pallas as pl
from jax.experimental.pallas import tpu as pltpu
from jax.sharding import Mesh, PartitionSpec as P

F32 = jnp.float32
BF16 = jnp.bfloat16
MIB = 1024 * 1024
CHUNKS = 8
CORES = 2

VMEM = pl.BlockSpec(memory_space=pltpu.VMEM)
SMEM = pl.BlockSpec(memory_space=pltpu.SMEM)
HBM = pl.BlockSpec(memory_space=pltpu.HBM)


def dot(a, b):
    return jnp.dot(a, b, preferred_element_type=F32)


def dot_nt(a, b):
    return lax.dot_general(a, b, (((1,), (1,)), ((), ())), preferred_element_type=F32)


def dot_tn(a, b):
    return lax.dot_general(a, b, (((0,), (0,)), ((), ())), preferred_element_type=F32)


def pick_matrix(send_ref, rows):
    hosts, send = send_ref.shape[2], send_ref.shape[3]
    place = lax.broadcasted_iota(jnp.int32, (send, rows), 0)
    column = lax.broadcasted_iota(jnp.int32, (send, rows), 1)
    parts = []
    for g in range(hosts):
        index = jnp.zeros((send, rows), jnp.int32)
        for s in range(send):
            index = jnp.where(place == s, send_ref[0, 0, g, s], index)
        parts.append(jnp.where(index == column, 1.0, 0.0).astype(F32))
    return jnp.concatenate(parts, 0).astype(BF16)


def spread_parts(chips, far, adj_t, u, value, whole, keep_ref, give_ref):
    rows = u.shape[0]
    own_rows = chips * CORES * rows
    whole[...] = dot(adj_t, u).astype(BF16)
    core = lax.axis_index("core")
    each = rows + far
    for side, ref in ((core, keep_ref), (1 - core, give_ref)):
        for x in range(chips):
            d = x * CORES + side
            low = pl.multiple_of(d * rows, rows)
            ref[x * each : x * each + rows, :] = whole[pl.ds(low, rows), :]
            low = pl.multiple_of(own_rows + d * far, far)
            ref[x * each + rows : (x + 1) * each, :] = whole[pl.ds(low, far), :]
    give_ref[chips * each :, :] = value


def prep_kernel(
    chips,
    dst_hbm,
    src_hbm,
    rows_hbm,
    send_hbm,
    tile_hbm,
    features_hbm,
    cot_hbm,
    neigh_two_hbm,
    adj_ref,
    adj_t_ref,
    keep_ref,
    give_ref,
    picked_ref,
    dst_ref,
    src_ref,
    rows_ref,
    send_ref,
    tile_buf,
    features_ref,
    cot_ref,
    neigh_two_ref,
    acc,
    whole,
    sems,
):
    tiles, blk = tile_buf.shape[0], tile_buf.shape[1]
    each = tiles // CHUNKS
    pairs = [
        (cot_hbm, cot_ref),
        (neigh_two_hbm, neigh_two_ref),
        (features_hbm, features_ref),
        (send_hbm, send_ref),
        (dst_hbm, dst_ref),
        (src_hbm, src_ref),
        (rows_hbm, rows_ref),
    ]
    pairs += [
        (tile_hbm.at[pl.ds(c * each, each)], tile_buf.at[pl.ds(c * each, each)])
        for c in range(CHUNKS)
    ]
    copies = [pltpu.make_async_copy(a, b, sems.at[i]) for i, (a, b) in enumerate(pairs)]
    for copy in copies:
        copy.start()
    rows = features_ref.shape[0]
    bpd = rows // blk
    sources = acc.shape[0] // bpd
    far = send_ref.shape[2] * send_ref.shape[3]
    acc[...] = jnp.zeros_like(acc)
    copies[0].wait()
    copies[1].wait()
    u = dot_nt(cot_ref[...], neigh_two_ref[...]).astype(BF16)
    copies[2].wait()
    copies[3].wait()
    picked_ref[...] = dot(pick_matrix(send_ref, rows), features_ref[...]).astype(BF16)
    for copy in copies[4:7]:
        copy.wait()
    place = lax.broadcasted_iota(jnp.int32, (blk, blk), 0)
    for c in range(CHUNKS):
        copies[7 + c].wait()

        def add(t, carry):
            slot = dst_ref[t] * sources + src_ref[t]
            live = jnp.where(place < rows_ref[t], tile_buf[t].astype(F32), 0.0)
            acc[slot] = acc[slot] + live
            return carry

        lax.fori_loop(c * each, (c + 1) * each, add, 0, unroll=True)
    for b in range(bpd):
        for j in range(sources):
            block = acc[b * sources + j].astype(BF16)
            adj_ref[b * blk : (b + 1) * blk, j * blk : (j + 1) * blk] = block
            adj_t_ref[j * blk : (j + 1) * blk, b * blk : (b + 1) * blk] = block.T
    spread_parts(
        chips, far, adj_t_ref[...], u, features_ref[...], whole, keep_ref, give_ref
    )


def core_sum_kernel(
    chips, hosts, keep_ref, came_ref, value_ref, picked_ref, mine_ref, msg_ref, *rest
):
    to_refs, total = rest[:-1], rest[-1]
    rows = value_ref.shape[0]
    far = picked_ref.shape[0]
    send = far // hosts
    each = rows + far
    chip = lax.axis_index("chip")
    total[...] = keep_ref[...].astype(F32) + came_ref[: chips * each, :].astype(F32)
    mine_ref[...] = total[pl.ds(pl.multiple_of(chip * each, 8), rows), :]
    for k, ref in enumerate(to_refs):
        other = lax.rem(chip + k + 1, chips)
        ref[:rows, :] = total[pl.ds(pl.multiple_of(other * each, 8), rows), :].astype(BF16)
        ref[rows:, :] = value_ref[...]
    picked = picked_ref[...].astype(F32)
    for g in range(hosts):
        for x in range(chips):
            low = x * each + rows + g * send
            both = jnp.concatenate(
                [picked[g * send : (g + 1) * send], total[low : low + send, :]], 0
            )
            msg_ref[g * chips + x] = both.astype(BF16)


def halo_part(recv_ref, hosts, chips, part):
    send = recv_ref.shape[1] // 2
    low = part * send
    blocks = [
        recv_ref[g * chips + x].astype(F32)[low : low + send]
        for x in range(chips)
        for g in range(hosts)
    ]
    return jnp.concatenate(blocks, 0).astype(BF16)


def merge_kernel(chips, hosts, recv_ref, *refs):
    came, out_ref = refs[:-1], refs[-1]
    rows = came[0].shape[0] // 2
    for k, ref in enumerate(came):
        out_ref[k * rows : (k + 1) * rows, :] = ref[rows:, :]
    out_ref[len(came) * rows :, :] = halo_part(recv_ref, hosts, chips, 0)


def gather_sources(chips, hosts, value, came_ref, chip_refs, recv_ref, shared_ref, space):
    rows = value.shape[0]
    chip, core = lax.axis_index("chip"), lax.axis_index("core")
    far_rows = recv_ref.shape[0] // chips * recv_ref.shape[1] // 2

    def put(x, side, block):
        low = pl.multiple_of((x * CORES + side) * rows, rows)
        space[pl.ds(low, rows), :] = block

    put(chip, core, value)
    put(chip, 1 - core, came_ref[came_ref.shape[0] - rows :, :])
    for k, ref in enumerate(chip_refs):
        x = lax.rem(chip - k - 1 + chips, chips)
        put(x, core, ref[rows:, :])
        put(x, 1 - core, shared_ref[k * rows : (k + 1) * rows, :])
    base = chips * CORES * rows
    here = halo_part(recv_ref, hosts, chips, 0)
    there = shared_ref[(chips - 1) * rows :, :]
    for x in range(chips):
        for side, block in ((core, here), (1 - core, there)):
            low = pl.multiple_of(base + (x * CORES + side) * far_rows, far_rows)
            space[pl.ds(low, far_rows), :] = block[x * far_rows : (x + 1) * far_rows]


def spread_total(pick, chips, hosts, mine_ref, chip_refs, recv_ref):
    total = mine_ref[...]
    rows = total.shape[0]
    for ref in chip_refs:
        total = total + ref[:rows, :].astype(F32)
    back = halo_part(recv_ref, hosts, chips, 1)
    return total + dot_tn(jnp.concatenate([pick] * chips, 0), back)


def middle_kernel(
    chips,
    hosts,
    send_ref,
    adj_ref,
    adj_t_ref,
    features_ref,
    cot_ref,
    self_one_ref,
    neigh_one_ref,
    bias_ref,
    self_two_ref,
    mine_ref,
    came_ref,
    recv_ref,
    shared_ref,
    *refs,
):
    chip_refs = refs[: chips - 1]
    hidden_ref, grad_pre_ref, keep_ref, give_ref, picked_ref, space = refs[chips - 1 :]
    rows = features_ref.shape[0]
    far = send_ref.shape[2] * send_ref.shape[3]
    pick = pick_matrix(send_ref, rows)
    gather_sources(
        chips, hosts, features_ref[...], came_ref, chip_refs, recv_ref, shared_ref, space
    )
    agg = dot(adj_ref[...], space[...]).astype(BF16)
    pre = dot(features_ref[...], self_one_ref[...])
    pre = pre + dot(agg, neigh_one_ref[...]) + bias_ref[...].reshape(1, -1)
    sigmoid = jax.nn.sigmoid(pre)
    hidden = (pre * sigmoid).astype(BF16)
    hidden_ref[...] = hidden
    picked_ref[...] = dot(pick, hidden).astype(BF16)
    grad = dot_nt(cot_ref[...], self_two_ref[...])
    grad = grad + spread_total(pick, chips, hosts, mine_ref, chip_refs, recv_ref)
    grad_pre = (grad * sigmoid * (1.0 + pre * (1.0 - sigmoid))).astype(BF16)
    grad_pre_ref[...] = grad_pre
    u = dot_nt(grad_pre, neigh_one_ref[...]).astype(BF16)
    spread_parts(chips, far, adj_t_ref[...], u, hidden, space, keep_ref, give_ref)


def last_kernel(
    chips,
    hosts,
    send_ref,
    adj_ref,
    hidden_ref,
    grad_pre_ref,
    self_one_ref,
    self_two_ref,
    neigh_two_ref,
    bias_ref,
    mine_ref,
    came_ref,
    recv_ref,
    shared_ref,
    *refs,
):
    chip_refs = refs[: chips - 1]
    output_ref, grad_ref, space = refs[chips - 1 :]
    rows = hidden_ref.shape[0]
    pick = pick_matrix(send_ref, rows)
    gather_sources(
        chips, hosts, hidden_ref[...], came_ref, chip_refs, recv_ref, shared_ref, space
    )
    agg = dot(adj_ref[...], space[...]).astype(BF16)
    result = dot(hidden_ref[...], self_two_ref[...])
    result = result + dot(agg, neigh_two_ref[...]) + bias_ref[...].reshape(1, -1)
    output_ref[...] = result.astype(BF16)
    grad = dot_nt(grad_pre_ref[...], self_one_ref[...])
    grad_ref[...] = grad + spread_total(pick, chips, hosts, mine_ref, chip_refs, recv_ref)


def call(kernel, name, out_shape, in_specs, args, scratch=(), limit=32):
    return pl.pallas_call(
        kernel,
        out_shape=out_shape,
        in_specs=in_specs,
        out_specs=jax.tree.map(lambda _: VMEM, out_shape),
        scratch_shapes=scratch,
        compiler_params=pltpu.CompilerParams(vmem_limit_bytes=limit * MIB),
        name=name,
    )(*args)


def shift(value, axis, k):
    size = lax.axis_size(axis)
    return lax.ppermute(value, axis, [(i, (i + k) % size) for i in range(size)])


def shape(rows, width, kind=BF16):
    return jax.ShapeDtypeStruct((rows, width), kind)


def body(
    features,
    send_list,
    tile_dst,
    tile_src,
    tile_rows,
    tile_val,
    self_one,
    neigh_one,
    bias_one,
    self_two,
    neigh_two,
    bias_two,
    cotangent,
):
    chips = lax.axis_size("chip")
    hosts = lax.axis_size("hst")
    rows, width = features.shape
    tiles, blk = tile_val.shape[:2]
    send = send_list.shape[3]
    far = hosts * send
    all_rows = chips * CORES * (rows + far)
    keep_shape = shape(chips * (rows + far), width)
    give_shape = shape(chips * (rows + far) + rows, width)
    picked_shape = shape(far, width)
    rows_shape = shape(rows, width)
    space = pltpu.VMEM((all_rows, width), BF16)

    def exchange(keep, give, value, picked):
        came = shift(give, "core", 1)
        mine, msg, *to = call(
            functools.partial(core_sum_kernel, chips, hosts),
            "core_sum",
            (
                shape(rows, width, F32),
                jax.ShapeDtypeStruct((hosts * chips, 2 * send, width), BF16),
            )
            + (shape(2 * rows, width),) * (chips - 1),
            [VMEM] * 4,
            (keep, came, value, picked),
            [pltpu.VMEM(keep_shape.shape, F32)],
        )
        terms = [shift(block, "chip", k + 1) for k, block in enumerate(to)]
        recv = lax.all_to_all(msg, ("hst", "chip"), split_axis=0, concat_axis=0, tiled=True)
        merged = call(
            functools.partial(merge_kernel, chips, hosts),
            "merge",
            shape((chips - 1) * rows + chips * far, width),
            [VMEM] * chips,
            (recv, *terms),
        )
        shared = shift(merged, "core", 1)
        return mine, came, recv, shared, *terms

    adj, adj_t, keep, give, picked = call(
        functools.partial(prep_kernel, chips),
        "prep",
        (shape(rows, all_rows), shape(all_rows, rows), keep_shape, give_shape, picked_shape),
        [HBM] * 8,
        [
            pltpu.with_memory_space_constraint(value, pltpu.HBM)
            for value in (
                tile_dst,
                tile_src,
                tile_rows,
                send_list,
                tile_val,
                features,
                cotangent,
                neigh_two,
            )
        ],
        [
            pltpu.SMEM(tile_dst.shape, jnp.int32),
            pltpu.SMEM(tile_src.shape, jnp.int32),
            pltpu.SMEM(tile_rows.shape, jnp.int32),
            pltpu.SMEM(send_list.shape, jnp.int32),
            pltpu.VMEM(tile_val.shape, BF16),
            pltpu.VMEM(features.shape, BF16),
            pltpu.VMEM(cotangent.shape, BF16),
            pltpu.VMEM(neigh_two.shape, BF16),
            pltpu.VMEM(((rows // blk) * (all_rows // blk), blk, blk), F32),
            space,
            pltpu.SemaphoreType.DMA((7 + CHUNKS,)),
        ],
    )
    came = exchange(keep, give, features, picked)
    hidden, grad_pre, keep, give, picked = call(
        functools.partial(middle_kernel, chips, hosts),
        "middle",
        (rows_shape, rows_shape, keep_shape, give_shape, picked_shape),
        [SMEM] + [VMEM] * (11 + chips),
        (
            send_list,
            adj,
            adj_t,
            features,
            cotangent,
            self_one,
            neigh_one,
            bias_one,
            self_two,
            *came,
        ),
        [space],
    )
    came = exchange(keep, give, hidden, picked)
    return call(
        functools.partial(last_kernel, chips, hosts),
        "last",
        (rows_shape, shape(rows, width, F32)),
        [SMEM] + [VMEM] * (10 + chips),
        (
            send_list,
            adj,
            hidden,
            grad_pre,
            self_one,
            self_two,
            neigh_two,
            bias_two,
            *came,
        ),
        [space],
    )


def solution(mesh):
    hosts, devs = mesh.devices.shape
    mesh = Mesh(mesh.devices.reshape(hosts, devs // CORES, CORES), ("hst", "chip", "core"))
    dev = ("chip", "core")
    every = ("hst", "chip", "core")
    return jax.shard_map(
        body,
        mesh=mesh,
        in_specs=(
            P(every, None),
            P("hst", dev, None, None),
            P(every),
            P(every),
            P(every),
            P(every, None, None),
            P(),
            P(),
            P(),
            P(),
            P(),
            P(),
            P(every, None),
        ),
        out_specs=(P(every, None), P(every, None)),
        check_vma=False,
    )
```

time: 69.4 us -> 43.8 us (0.63)
  blocking collectives: 42.7 us -> 24.3 us
  local copies, waits for them, and re-layouts: 6.99 us -> 0.04 us
  waiting for transfers between devices: 2.6 us -> 5.98 us
  starting transfers between devices: 8.28 us -> 4.94 us
    all_gather x2 -> x0, blocking collectives: 18.6 us -> none  [exchange(): wide = lax.all_gather(value, 'dev', axis=0, tiled=True)]
    all_to_all x2 -> x0, starting transfers between devices: 8.28 us -> none  [exchange(): lax.all_to_all(msg, ('hst', 'dev'), split_axis=0, concat_axis=0, tiled=True)]
    unnamed x34 -> x18, local copies, waits for them, and re-layouts: 6.99 us -> 0.04 us
    ppermute x0 -> x6, waiting for transfers between devices: none -> 5.98 us  [shift(): return lax.ppermute(value, axis, [(i, (i + k) % size) for i in range(size)])]
    ppermute x0 -> x6, starting transfers between devices: none -> 4.94 us  [shift(): return lax.ppermute(value, axis, [(i, (i + k) % size) for i in range(size)])]
    all_to_all x2 -> x0, waiting for transfers between devices: 2.6 us -> none  [exchange(): lax.all_to_all(msg, ('hst', 'dev'), split_axis=0, concat_axis=0, tiled=True)]
    pallas_call x3 -> x7, Pallas kernels: 7.64 us -> 7.53 us  [call(): pl.pallas_call(kernel, out_shape=out_shape, in_specs=in_specs, out_specs=...]
  transfers between devices with their start and end apart: 2 -> 6, of which waited for: 2 -> 4; matrix products, arithmetic and copies ran while one was open for 0% -> 0% of each run, Pallas kernels for 0% -> 0%
where the time goes in v3:
time: 43.8 us; the launch traced here: 43.6 us
  blocking collectives  24.3 us (55%)
  Pallas kernels  7.53 us (17%)
  waiting for transfers between devices  5.98 us (14%)
  starting transfers between devices  4.94 us (11%)
  between operations  0.78 us (2%)
    all_to_all x2, blocking collectives, exchange(): lax.all_to_all(msg, ('hst', 'chip'), split_axis=0, concat_axis=0, tiled=T...  24.3 us
    pallas_call x7, Pallas kernels, call(): pl.pallas_call(kernel, out_shape=out_shape, in_specs=in_specs, out_specs=...  7.53 us
    ppermute x6, waiting for transfers between devices, shift(): return lax.ppermute(value, axis, [(i, (i + k) % size) for i in range(size)])  5.98 us
    ppermute x6, starting transfers between devices, shift(): return lax.ppermute(value, axis, [(i, (i + k) % size) for i in range(size)])  4.94 us
  transfers between devices with their start and end apart: 6, of which 4 were waited for; matrix products, arithmetic and copies ran while one was open for 0% of the time, Pallas kernels for 0%

profile of v3, /device:TPU:0, one launch (start us, length us, event | category | flops | bytes accessed | tf_op | source)
XLA Modules:
  0.0 43.6 jit_solution(4913460915087905947)
XLA Ops:
  0.6 0.0 copy-start.6
  0.6 0.0 copy-start
  0.7 0.0 copy-start.1
  0.7 0.0 copy-start.4
  0.7 0.0 copy-start.3
  0.7 0.0 copy-start.7
  0.7 0.0 copy-start.5
  0.7 2.9 %prep.1 = (bf16[256,1280]{1,0:T(8,128)(2,1)S(1)}, bf16[1280,256]{1,0:T(8,128)(2,1)S(1)}, bf16[640,256]{1,0:T(8,128)(2,1)S(1)}, bf16[896,256]{1,0:T(8,128)(2,1)S(1)}, bf16[64,256]{1,0:T(8,128)(2,1)S(1)}) custom-call(s32[64]{0:T(128)} %dst_hbm.1, s32[64]{0:T(128)} %src_hbm.1, s32[64]{0:T(128)} %rows_hbm.1, s32[1,1,8,8]{3,2,1,0:T(8,128)} %send_ref.3, ...), custom_call_target="tpu_custom_call" | custom-call | tf_op jit(solution)/shard_map/prep/pallas_call | solution.py:292
  3.6 0.5 %collective-permute-start = (bf16[896,256]{1,0:T(8,128)(2,1)S(1)}, bf16[896,256]{1,0:T(8,128)(2,1)S(1)}, u32[]{:S(2)}, u32[]{:S(2)}) collective-permute-start(bf16[896,256]{1,0:T(8,128)(2,1)S(1)} %get-tuple-element.21), channel_id=1, source_target_pairs={{0,1},{1,0},{2,3},{3,2},{4,5},{5,4},{6,7},{7,6},{8,9},{9,8},{10,11... | collective-permute-start | bytes 1376264 | tf_op jit(solution)/shard_map/ppermute | solution.py:305
  4.1 1.4 %collective-permute-done.came_ref = bf16[896,256]{1,0:T(8,128)(2,1)S(1)} collective-permute-done((bf16[896,256]{1,0:T(8,128)(2,1)S(1)}, bf16[896,256]{1,0:T(8,128)(2,1)S(1)}, u32[]{:S(2)}, u32[]{:S(2)}) %collective-permute-start) | collective-permute-done | bytes 458784 | tf_op jit(solution)/shard_map/ppermute | solution.py:305
  5.6 0.0 copy-done
  5.6 0.2 core_sum.2
  5.8 2.9 %collective-permute-start.1 = (bf16[512,256]{1,0:T(8,128)(2,1)S(1)}, bf16[512,256]{1,0:T(8,128)(2,1)S(1)}, u32[]{:S(2)}, u32[]{:S(2)}) collective-permute-start(bf16[512,256]{1,0:T(8,128)(2,1)S(1)} %get-tuple-element.25), channel_id=1, source_target_pairs={{0,2},{2,0},{1,3},{3,1},{4,6},{6,4},{5,7},{7,5},{8,10},{10,8},{9,1... | collective-permute-start | bytes 786440 | tf_op jit(solution)/shard_map/ppermute | solution.py:305
  8.7 13.5 %all_to_all.10.recv_ref = bf16[16,16,256]{2,1,0:T(8,128)(2,1)S(1)} all-to-all(bf16[16,16,256]{2,1,0:T(8,128)(2,1)S(1)} %get-tuple-element.24), channel_id=1, replica_groups=mesh['hst'=8,'chip'=2,'core'=2] {'hst','chip'}, dimensions={0} | all-to-all | bytes 262144 | tf_op jit(solution)/shard_map/all_to_all | solution.py:355
  22.2 0.0 collective-permute-done.1.refs_0_
  22.2 0.1 collective-permute-start.2
  22.3 1.4 %collective-permute-done.2.shared_ref = bf16[384,256]{1,0:T(8,128)(2,1)S(1)} collective-permute-done((bf16[384,256]{1,0:T(8,128)(2,1)S(1)}, bf16[384,256]{1,0:T(8,128)(2,1)S(1)}, u32[]{:S(2)}, u32[]{:S(2)}) %collective-permute-start.2) | collective-permute-done | bytes 196640 | tf_op jit(solution)/shard_map/ppermute | solution.py:305
  23.7 0.0 copy-done.6
  23.7 0.0 copy-done.1
  23.8 0.0 copy-start.2
  23.8 0.0 copy-start.8
  23.8 2.1 %middle.1 = (bf16[256,256]{1,0:T(8,128)(2,1)S(1)}, bf16[256,256]{1,0:T(8,128)(2,1)S(1)}, bf16[640,256]{1,0:T(8,128)(2,1)S(1)}, bf16[896,256]{1,0:T(8,128)(2,1)S(1)}, bf16[64,256]{1,0:T(8,128)(2,1)S(1)}) custom-call(s32[1,1,8,8]{3,2,1,0:T(8,128)S(1)} %copy-done.6, bf16[256,1280]{1,0:T(8,128)(2,1)S(1)} %get-tuple-element.18.adj_ref, ...), custom_call_target="tpu_custom_call" | custom-call | tf_op jit(solution)/shard_map/middle/pallas_call | solution.py:292
  25.9 0.2 collective-permute-start.3
  26.1 1.7 %collective-permute-done.3.came_ref = bf16[896,256]{1,0:T(8,128)(2,1)S(1)} collective-permute-done((bf16[896,256]{1,0:T(8,128)(2,1)S(1)}, bf16[896,256]{1,0:T(8,128)(2,1)S(1)}, u32[]{:S(2)}, u32[]{:S(2)}) %collective-permute-start.3) | collective-permute-done | bytes 458784 | tf_op jit(solution)/shard_map/ppermute | solution.py:305
  27.8 0.2 core_sum.3
  28.0 1.2 %collective-permute-start.4 = (bf16[512,256]{1,0:T(8,128)(2,1)S(1)}, bf16[512,256]{1,0:T(8,128)(2,1)S(1)}, u32[]{:S(2)}, u32[]{:S(2)}) collective-permute-start(bf16[512,256]{1,0:T(8,128)(2,1)S(1)} %get-tuple-element.33), channel_id=1, source_target_pairs={{0,2},{2,0},{1,3},{3,1},{4,6},{6,4},{5,7},{7,5},{8,10},{10,8},{9,1... | collective-permute-start | bytes 786440 | tf_op jit(solution)/shard_map/ppermute | solution.py:305
  29.1 10.8 %all_to_all.11.recv_ref = bf16[16,16,256]{2,1,0:T(8,128)(2,1)S(1)} all-to-all(bf16[16,16,256]{2,1,0:T(8,128)(2,1)S(1)} %get-tuple-element.32), channel_id=1, replica_groups=mesh['hst'=8,'chip'=2,'core'=2] {'hst','chip'}, dimensions={0} | all-to-all | bytes 262144 | tf_op jit(solution)/shard_map/all_to_all | solution.py:355
  39.9 0.0 collective-permute-done.4.refs_0_
  39.9 0.1 collective-permute-start.5
  40.0 1.4 %collective-permute-done.5.shared_ref = bf16[384,256]{1,0:T(8,128)(2,1)S(1)} collective-permute-done((bf16[384,256]{1,0:T(8,128)(2,1)S(1)}, bf16[384,256]{1,0:T(8,128)(2,1)S(1)}, u32[]{:S(2)}, u32[]{:S(2)}) %collective-permute-start.5) | collective-permute-done | bytes 196640 | tf_op jit(solution)/shard_map/ppermute | solution.py:305
  41.5 0.0 copy-done.2
  41.5 2.1 %last.1 = (bf16[256,256]{1,0:T(8,128)(2,1)}, f32[256,256]{1,0:T(8,128)}) custom-call(s32[1,1,8,8]{3,2,1,0:T(8,128)S(1)} %copy-done.6, bf16[256,1280]{1,0:T(8,128)(2,1)S(1)} %get-tuple-element.18.adj_ref, bf16[256,256]{1,0:T(8,128)(2,1)S(1)} %get-tuple-element.26.value_ref.hidden_ref, bf16[256,256]{1,0:T(8,128)(2,1)S(1)} %get-tuple-element.27.grad_pre_ref, ...), custom_call_target="tpu_custom_call" | custom-call | tf_op jit(solution)/shard_map/last/pallas_call | solution.py:292
  (7 shorter events, 0.0 us)
Async XLA Ops:
  0.6 23.1 %copy-start.6 = (s32[1,1,8,8]{3,2,1,0:T(8,128)S(1)}, s32[1,1,8,8]{3,2,1,0:T(8,128)}, u32[]{:S(2)}) copy-start(s32[1,1,8,8]{3,2,1,0:T(8,128)} %send_ref.3) | copy-start | bytes 772
  0.6 4.9 %copy-start = (bf16[256,256]{1,0:T(8,128)(2,1)S(1)}, bf16[256,256]{1,0:T(8,128)(2,1)}, u32[]{:S(2)}) copy-start(bf16[256,256]{1,0:T(8,128)(2,1)} %features_ref.1) | copy-start | bytes 393220
  0.7 23.1 %copy-start.1 = (bf16[256,256]{1,0:T(8,128)(2,1)S(1)}, bf16[256,256]{1,0:T(8,128)(2,1)}, u32[]{:S(2)}) copy-start(bf16[256,256]{1,0:T(8,128)(2,1)} %cot_ref.1) | copy-start | bytes 393220
  0.7 23.1 %copy-start.4 = (bf16[256,256]{1,0:T(8,128)(2,1)S(1)}, bf16[256,256]{1,0:T(8,128)(2,1)}, u32[]{:S(2)}) copy-start(bf16[256,256]{1,0:T(8,128)(2,1)} %self_two_ref.3) | copy-start | bytes 393220
  0.7 23.1 %copy-start.3 = (bf16[256,256]{1,0:T(8,128)(2,1)S(1)}, bf16[256,256]{1,0:T(8,128)(2,1)}, u32[]{:S(2)}) copy-start(bf16[256,256]{1,0:T(8,128)(2,1)} %self_one_ref.3) | copy-start | bytes 393220
  0.7 23.1 %copy-start.7 = (f32[256]{0:T(256)S(1)}, f32[256]{0:T(256)}, u32[]{:S(2)}) copy-start(f32[256]{0:T(256)} %bias_ref.2) | copy-start | bytes 3076
  0.7 23.1 %copy-start.5 = (bf16[256,256]{1,0:T(8,128)(2,1)S(1)}, bf16[256,256]{1,0:T(8,128)(2,1)}, u32[]{:S(2)}) copy-start(bf16[256,256]{1,0:T(8,128)(2,1)} %neigh_one_ref.1) | copy-start | bytes 393220
  3.6 2.0 %collective-permute-start = (bf16[896,256]{1,0:T(8,128)(2,1)S(1)}, bf16[896,256]{1,0:T(8,128)(2,1)S(1)}, u32[]{:S(2)}, u32[]{:S(2)}) collective-permute-start(bf16[896,256]{1,0:T(8,128)(2,1)S(1)} %get-tuple-element.21), channel_id=1, source_target_pairs={{0,1},{1,0},{2,3},{3,2},{4,5},{5,4},{6,7},{7,6},{8,9},{9,8},{10,11... | collective-permute-start | bytes 1376264 | tf_op jit(solution)/shard_map/ppermute | solution.py:305
  5.8 16.5 %collective-permute-start.1 = (bf16[512,256]{1,0:T(8,128)(2,1)S(1)}, bf16[512,256]{1,0:T(8,128)(2,1)S(1)}, u32[]{:S(2)}, u32[]{:S(2)}) collective-permute-start(bf16[512,256]{1,0:T(8,128)(2,1)S(1)} %get-tuple-element.25), channel_id=1, source_target_pairs={{0,2},{2,0},{1,3},{3,1},{4,6},{6,4},{5,7},{7,5},{8,10},{10,8},{9,1... | collective-permute-start | bytes 786440 | tf_op jit(solution)/shard_map/ppermute | solution.py:305
  22.2 1.5 %collective-permute-start.2 = (bf16[384,256]{1,0:T(8,128)(2,1)S(1)}, bf16[384,256]{1,0:T(8,128)(2,1)S(1)}, u32[]{:S(2)}, u32[]{:S(2)}) collective-permute-start(bf16[384,256]{1,0:T(8,128)(2,1)S(1)} %merge.2), channel_id=1, source_target_pairs={{0,1},{1,0},{2,3},{3,2},{4,5},{5,4},{6,7},{7,6},{8,9},{9,8},{10,11... | collective-permute-start | bytes 589832 | tf_op jit(solution)/shard_map/ppermute | solution.py:305
  23.8 17.7 %copy-start.2 = (bf16[256,256]{1,0:T(8,128)(2,1)S(1)}, bf16[256,256]{1,0:T(8,128)(2,1)}, u32[]{:S(2)}) copy-start(bf16[256,256]{1,0:T(8,128)(2,1)} %neigh_two_ref.1) | copy-start | bytes 393220
  23.8 17.7 %copy-start.8 = (f32[256]{0:T(256)S(1)}, f32[256]{0:T(256)}, u32[]{:S(2)}) copy-start(f32[256]{0:T(256)} %bias_ref.3) | copy-start | bytes 3076
  25.9 1.9 %collective-permute-start.3 = (bf16[896,256]{1,0:T(8,128)(2,1)S(1)}, bf16[896,256]{1,0:T(8,128)(2,1)S(1)}, u32[]{:S(2)}, u32[]{:S(2)}) collective-permute-start(bf16[896,256]{1,0:T(8,128)(2,1)S(1)} %get-tuple-element.29), channel_id=1, source_target_pairs={{0,1},{1,0},{2,3},{3,2},{4,5},{5,4},{6,7},{7,6},{8,9},{9,8},{10,11... | collective-permute-start | bytes 1376264 | tf_op jit(solution)/shard_map/ppermute | solution.py:305
  28.0 11.9 %collective-permute-start.4 = (bf16[512,256]{1,0:T(8,128)(2,1)S(1)}, bf16[512,256]{1,0:T(8,128)(2,1)S(1)}, u32[]{:S(2)}, u32[]{:S(2)}) collective-permute-start(bf16[512,256]{1,0:T(8,128)(2,1)S(1)} %get-tuple-element.33), channel_id=1, source_target_pairs={{0,2},{2,0},{1,3},{3,1},{4,6},{6,4},{5,7},{7,5},{8,10},{10,8},{9,1... | collective-permute-start | bytes 786440 | tf_op jit(solution)/shard_map/ppermute | solution.py:305
  39.9 1.5 %collective-permute-start.5 = (bf16[384,256]{1,0:T(8,128)(2,1)S(1)}, bf16[384,256]{1,0:T(8,128)(2,1)S(1)}, u32[]{:S(2)}, u32[]{:S(2)}) collective-permute-start(bf16[384,256]{1,0:T(8,128)(2,1)S(1)} %merge.3), channel_id=1, source_target_pairs={{0,1},{1,0},{2,3},{3,2},{4,5},{5,4},{6,7},{7,6},{8,9},{9,8},{10,11... | collective-permute-start | bytes 589832 | tf_op jit(solution)/shard_map/ppermute | solution.py:305

commit v4 on v3

--- a/solution.py
+++ b/solution.py
@@ -139,53 +139,93 @@
 
 
 def core_sum_kernel(
-    chips, hosts, keep_ref, came_ref, value_ref, picked_ref, mine_ref, msg_ref, *rest
+    chips, keep_ref, came_ref, value_ref, picked_ref, mine_ref, far_ref, *rest
 ):
-    to_refs, total = rest[:-1], rest[-1]
+    small_refs, big_refs, total = rest[: chips - 1], rest[chips - 1 : -1], rest[-1]
     rows = value_ref.shape[0]
     far = picked_ref.shape[0]
-    send = far // hosts
     each = rows + far
     chip = lax.axis_index("chip")
     total[...] = keep_ref[...].astype(F32) + came_ref[: chips * each, :].astype(F32)
-    mine_ref[...] = total[pl.ds(pl.multiple_of(chip * each, 8), rows), :]
-    for k, ref in enumerate(to_refs):
+    low = pl.multiple_of(chip * each, 8)
+    mine_ref[...] = total[pl.ds(low, rows), :]
+    far_ref[...] = total[pl.ds(low + rows, far), :]
+    for k in range(chips - 1):
         other = lax.rem(chip + k + 1, chips)
-        ref[:rows, :] = total[pl.ds(pl.multiple_of(other * each, 8), rows), :].astype(BF16)
-        ref[rows:, :] = value_ref[...]
-    picked = picked_ref[...].astype(F32)
-    for g in range(hosts):
-        for x in range(chips):
-            low = x * each + rows + g * send
-            both = jnp.concatenate(
-                [picked[g * send : (g + 1) * send], total[low : low + send, :]], 0
-            )
-            msg_ref[g * chips + x] = both.astype(BF16)
-
-
-def halo_part(recv_ref, hosts, chips, part):
-    send = recv_ref.shape[1] // 2
-    low = part * send
-    blocks = [
-        recv_ref[g * chips + x].astype(F32)[low : low + send]
-        for x in range(chips)
-        for g in range(hosts)
-    ]
-    return jnp.concatenate(blocks, 0).astype(BF16)
-
-
-def merge_kernel(chips, hosts, recv_ref, *refs):
-    came, out_ref = refs[:-1], refs[-1]
+        low = pl.multiple_of(other * each, 8)
+        small_refs[k][:far, :] = total[pl.ds(low + rows, far), :].astype(BF16)
+        small_refs[k][far:, :] = picked_ref[...]
+        big_refs[k][:rows, :] = total[pl.ds(low, rows), :].astype(BF16)
+        big_refs[k][rows:, :] = value_ref[...]
+
+
+def halves(hosts, bit):
+    stay = [r for r in range(hosts) if not r & bit]
+    return stay, [r for r in range(hosts) if r & bit]
+
+
+def deal_kernel(chips, hosts, picked_ref, far_ref, *refs):
+    came, (stay_ref, go_ref, buf) = refs[: chips - 1], refs[chips - 1 :]
+    far = far_ref.shape[0]
+    send = far // hosts
+    chip, me = lax.axis_index("chip"), lax.axis_index("hst")
+
+    def put(x, value):
+        buf[pl.ds(pl.multiple_of(x * far, far), far), :] = value
+
+    total = far_ref[...]
+    put(chip, picked_ref[...].astype(F32))
+    for k, ref in enumerate(came):
+        total = total + ref[:far, :].astype(F32)
+        put(lax.rem(chip - k - 1 + chips, chips), ref[far:, :].astype(F32))
+    buf[chips * far :, :] = total
+    for blocks, ref in zip(halves(hosts, 1), (stay_ref, go_ref)):
+        parts = []
+        for r in blocks:
+            host = lax.bitwise_xor(me, r)
+            for x in range(chips + 1):
+                parts.append(buf[pl.ds(pl.multiple_of(x * far + host * send, send), send), :])
+        ref[...] = jnp.concatenate(parts, 0).astype(BF16)
+
+
+def regroup(hosts, bit, stay_ref, came_ref):
+    size = stay_ref.shape[0] // (hosts // 2)
+    out = {}
+    for blocks, ref in zip(halves(hosts, bit), (stay_ref, came_ref)):
+        value = ref[...].astype(F32)
+        for i, r in enumerate(blocks):
+            out[r] = value[i * size : (i + 1) * size]
+    return out
+
+
+def pass_kernel(hosts, bit, stay_ref, came_ref, stay_out, go_out):
+    held = regroup(hosts, bit, stay_ref, came_ref)
+    for blocks, ref in zip(halves(hosts, 2 * bit), (stay_out, go_out)):
+        ref[...] = jnp.concatenate([held[r] for r in blocks], 0).astype(BF16)
+
+
+def merge_kernel(chips, hosts, stay_ref, came_ref, *refs):
+    came, (out_ref, back_ref, buf) = refs[: chips - 1], refs[chips - 1 :]
     rows = came[0].shape[0] // 2
+    far = back_ref.shape[0]
+    send = far // hosts
+    held = regroup(hosts, hosts // 2, stay_ref, came_ref)
+    me = lax.axis_index("hst")
+    for r, value in held.items():
+        host = lax.bitwise_xor(me, r)
+        for x in range(chips + 1):
+            low = pl.multiple_of(x * far + host * send, send)
+            buf[pl.ds(low, send), :] = value[x * send : (x + 1) * send]
     for k, ref in enumerate(came):
         out_ref[k * rows : (k + 1) * rows, :] = ref[rows:, :]
-    out_ref[len(came) * rows :, :] = halo_part(recv_ref, hosts, chips, 0)
-
-
-def gather_sources(chips, hosts, value, came_ref, chip_refs, recv_ref, shared_ref, space):
+    out_ref[len(came) * rows :, :] = buf[: chips * far, :].astype(BF16)
+    back_ref[...] = buf[chips * far :, :].astype(BF16)
+
+
+def gather_sources(chips, value, came_ref, chip_refs, here_ref, shared_ref, space):
     rows = value.shape[0]
     chip, core = lax.axis_index("chip"), lax.axis_index("core")
-    far_rows = recv_ref.shape[0] // chips * recv_ref.shape[1] // 2
+    far = (here_ref.shape[0] - (chips - 1) * rows) // chips
 
     def put(x, side, block):
         low = pl.multiple_of((x * CORES + side) * rows, rows)
@@ -198,26 +238,23 @@
         put(x, core, ref[rows:, :])
         put(x, 1 - core, shared_ref[k * rows : (k + 1) * rows, :])
     base = chips * CORES * rows
-    here = halo_part(recv_ref, hosts, chips, 0)
-    there = shared_ref[(chips - 1) * rows :, :]
     for x in range(chips):
-        for side, block in ((core, here), (1 - core, there)):
-            low = pl.multiple_of(base + (x * CORES + side) * far_rows, far_rows)
-            space[pl.ds(low, far_rows), :] = block[x * far_rows : (x + 1) * far_rows]
-
-
-def spread_total(pick, chips, hosts, mine_ref, chip_refs, recv_ref):
+        at = (chips - 1) * rows + x * far
+        for side, ref in ((core, here_ref), (1 - core, shared_ref)):
+            low = pl.multiple_of(base + (x * CORES + side) * far, far)
+            space[pl.ds(low, far), :] = ref[at : at + far, :]
+
+
+def spread_total(pick, mine_ref, chip_refs, back_ref):
     total = mine_ref[...]
     rows = total.shape[0]
     for ref in chip_refs:
         total = total + ref[:rows, :].astype(F32)
-    back = halo_part(recv_ref, hosts, chips, 1)
-    return total + dot_tn(jnp.concatenate([pick] * chips, 0), back)
+    return total + dot_tn(pick, back_ref[...])
 
 
 def middle_kernel(
     chips,
-    hosts,
     send_ref,
     adj_ref,
     adj_t_ref,
@@ -229,7 +266,8 @@
     self_two_ref,
     mine_ref,
     came_ref,
-    recv_ref,
+    here_ref,
+    back_ref,
     shared_ref,
     *refs,
 ):
@@ -239,7 +277,7 @@
     far = send_ref.shape[2] * send_ref.shape[3]
     pick = pick_matrix(send_ref, rows)
     gather_sources(
-        chips, hosts, features_ref[...], came_ref, chip_refs, recv_ref, shared_ref, space
+        chips, features_ref[...], came_ref, chip_refs, here_ref, shared_ref, space
     )
     agg = dot(adj_ref[...], space[...]).astype(BF16)
     pre = dot(features_ref[...], self_one_ref[...])
@@ -249,7 +287,7 @@
     hidden_ref[...] = hidden
     picked_ref[...] = dot(pick, hidden).astype(BF16)
     grad = dot_nt(cot_ref[...], self_two_ref[...])
-    grad = grad + spread_total(pick, chips, hosts, mine_ref, chip_refs, recv_ref)
+    grad = grad + spread_total(pick, mine_ref, chip_refs, back_ref)
     grad_pre = (grad * sigmoid * (1.0 + pre * (1.0 - sigmoid))).astype(BF16)
     grad_pre_ref[...] = grad_pre
     u = dot_nt(grad_pre, neigh_one_ref[...]).astype(BF16)
@@ -258,7 +296,6 @@
 
 def last_kernel(
     chips,
-    hosts,
     send_ref,
     adj_ref,
     hidden_ref,
@@ -269,7 +306,8 @@
     bias_ref,
     mine_ref,
     came_ref,
-    recv_ref,
+    here_ref,
+    back_ref,
     shared_ref,
     *refs,
 ):
@@ -278,14 +316,14 @@
     rows = hidden_ref.shape[0]
     pick = pick_matrix(send_ref, rows)
     gather_sources(
-        chips, hosts, hidden_ref[...], came_ref, chip_refs, recv_ref, shared_ref, space
+        chips, hidden_ref[...], came_ref, chip_refs, here_ref, shared_ref, space
     )
     agg = dot(adj_ref[...], space[...]).astype(BF16)
     result = dot(hidden_ref[...], self_two_ref[...])
     result = result + dot(agg, neigh_two_ref[...]) + bias_ref[...].reshape(1, -1)
     output_ref[...] = result.astype(BF16)
     grad = dot_nt(grad_pre_ref[...], self_one_ref[...])
-    grad_ref[...] = grad + spread_total(pick, chips, hosts, mine_ref, chip_refs, recv_ref)
+    grad_ref[...] = grad + spread_total(pick, mine_ref, chip_refs, back_ref)
 
 
 def call(kernel, name, out_shape, in_specs, args, scratch=(), limit=32):
@@ -303,6 +341,11 @@
 def shift(value, axis, k):
     size = lax.axis_size(axis)
     return lax.ppermute(value, axis, [(i, (i + k) % size) for i in range(size)])
+
+
+def flip(value, axis, bit):
+    size = lax.axis_size(axis)
+    return lax.ppermute(value, axis, [(i, i ^ bit) for i in range(size)])
 
 
 def shape(rows, width, kind=BF16):
@@ -339,29 +382,47 @@
 
     def exchange(keep, give, value, picked):
         came = shift(give, "core", 1)
-        mine, msg, *to = call(
-            functools.partial(core_sum_kernel, chips, hosts),
+        mine, far_sum, *to = call(
+            functools.partial(core_sum_kernel, chips),
             "core_sum",
-            (
-                shape(rows, width, F32),
-                jax.ShapeDtypeStruct((hosts * chips, 2 * send, width), BF16),
-            )
+            (shape(rows, width, F32), shape(far, width, F32))
+            + (shape(2 * far, width),) * (chips - 1)
             + (shape(2 * rows, width),) * (chips - 1),
             [VMEM] * 4,
             (keep, came, value, picked),
             [pltpu.VMEM(keep_shape.shape, F32)],
         )
-        terms = [shift(block, "chip", k + 1) for k, block in enumerate(to)]
-        recv = lax.all_to_all(msg, ("hst", "chip"), split_axis=0, concat_axis=0, tiled=True)
-        merged = call(
+        small = [shift(block, "chip", k + 1) for k, block in enumerate(to[: chips - 1])]
+        small, big = lax.optimization_barrier((small, to[chips - 1 :]))
+        block_buf = pltpu.VMEM(((chips + 1) * far, width), F32)
+        half = (shape((chips + 1) * far // 2, width),) * 2
+        stay, go = call(
+            functools.partial(deal_kernel, chips, hosts),
+            "deal",
+            half,
+            [VMEM] * (1 + chips),
+            (picked, far_sum, *small),
+            [block_buf],
+        )
+        terms = [shift(block, "chip", k + 1) for k, block in enumerate(big)]
+        bit = 1
+        got = flip(go, "hst", bit)
+        while 2 * bit < hosts:
+            stay, go = call(
+                functools.partial(pass_kernel, hosts, bit), "pass_on", half, [VMEM] * 2, (stay, got)
+            )
+            bit *= 2
+            got = flip(go, "hst", bit)
+        here, back = call(
             functools.partial(merge_kernel, chips, hosts),
             "merge",
-            shape((chips - 1) * rows + chips * far, width),
-            [VMEM] * chips,
-            (recv, *terms),
+            (shape((chips - 1) * rows + chips * far, width), shape(far, width)),
+            [VMEM] * (1 + chips),
+            (stay, got, *terms),
+            [block_buf],
         )
-        shared = shift(merged, "core", 1)
-        return mine, came, recv, shared, *terms
+        shared = shift(here, "core", 1)
+        return mine, came, here, back, shared, *terms
 
     adj, adj_t, keep, give, picked = call(
         functools.partial(prep_kernel, chips),
@@ -397,10 +458,10 @@
     )
     came = exchange(keep, give, features, picked)
     hidden, grad_pre, keep, give, picked = call(
-        functools.partial(middle_kernel, chips, hosts),
+        functools.partial(middle_kernel, chips),
         "middle",
         (rows_shape, rows_shape, keep_shape, give_shape, picked_shape),
-        [SMEM] + [VMEM] * (11 + chips),
+        [SMEM] + [VMEM] * (12 + chips),
         (
             send_list,
             adj,
@@ -417,10 +478,10 @@
     )
     came = exchange(keep, give, hidden, picked)
     return call(
-        functools.partial(last_kernel, chips, hosts),
+        functools.partial(last_kernel, chips),
         "last",
         (rows_shape, shape(rows, width, F32)),
-        [SMEM] + [VMEM] * (10 + chips),
+        [SMEM] + [VMEM] * (11 + chips),
         (
             send_list,
             adj,

time: 43.8 us -> 54.8 us (1.25)
  blocking collectives: 24.3 us -> 0 us
  waiting for transfers between devices: 5.98 us -> 26.4 us
  starting transfers between devices: 4.94 us -> 19.7 us
    all_to_all x2 -> x0, blocking collectives: 24.3 us -> none  [exchange(): lax.all_to_all(msg, ('hst', 'chip'), split_axis=0, concat_axis=0, tiled=T...]
    ppermute x0 -> x6, waiting for transfers between devices: none -> 14.3 us  [flip(): return lax.ppermute(value, axis, [(i, i ^ bit) for i in range(size)])]
    ppermute x0 -> x6, starting transfers between devices: none -> 12.9 us  [flip(): return lax.ppermute(value, axis, [(i, i ^ bit) for i in range(size)])]
    ppermute x6 -> x8, waiting for transfers between devices: 5.98 us -> 12.1 us  [shift(): return lax.ppermute(value, axis, [(i, (i + k) % size) for i in range(size)])]
    ppermute x6 -> x8, starting transfers between devices: 4.94 us -> 6.75 us  [shift(): return lax.ppermute(value, axis, [(i, (i + k) % size) for i in range(size)])]
    pallas_call x7 -> x13, Pallas kernels: 7.53 us -> 7.7 us  [call(): pl.pallas_call(kernel, out_shape=out_shape, in_specs=in_specs, out_specs=...]
  transfers between devices with their start and end apart: 6 -> 14, of which waited for: 4 -> 12; matrix products, arithmetic and copies ran while one was open for 0% -> 0% of each run, Pallas kernels for 0% -> 0%
where the time goes in v4:
time: 54.8 us; the launch traced here: 54.7 us
  waiting for transfers between devices  26.4 us (48%)
  starting transfers between devices  19.7 us (36%)
  Pallas kernels  7.7 us (14%)
  between operations  0.82 us (1%)
    ppermute x6, waiting for transfers between devices, flip(): return lax.ppermute(value, axis, [(i, i ^ bit) for i in range(size)])  14.3 us
    ppermute x6, starting transfers between devices, flip(): return lax.ppermute(value, axis, [(i, i ^ bit) for i in range(size)])  12.9 us
    ppermute x8, waiting for transfers between devices, shift(): return lax.ppermute(value, axis, [(i, (i + k) % size) for i in range(size)])  12.1 us
    pallas_call x13, Pallas kernels, call(): pl.pallas_call(kernel, out_shape=out_shape, in_specs=in_specs, out_specs=...  7.7 us
    ppermute x8, starting transfers between devices, shift(): return lax.ppermute(value, axis, [(i, (i + k) % size) for i in range(size)])  6.75 us
  transfers between devices with their start and end apart: 14, of which 12 were waited for; matrix products, arithmetic and copies ran while one was open for 0% of the time, Pallas kernels for 0%

profile of v4, /device:TPU:0, one launch (start us, length us, event | category | flops | bytes accessed | tf_op | source)
XLA Modules:
  0.0 54.7 jit_solution(1705362915319932353)
XLA Ops:
  0.7 2.9 %prep.1 = (bf16[256,1280]{1,0:T(8,128)(2,1)S(1)}, bf16[1280,256]{1,0:T(8,128)(2,1)S(1)}, bf16[640,256]{1,0:T(8,128)(2,1)S(1)}, bf16[896,256]{1,0:T(8,128)(2,1)S(1)}, bf16[64,256]{1,0:T(8,128)(2,1)S(1)}) custom-call(s32[64]{0:T(128)} %dst_hbm.1, s32[64]{0:T(128)} %src_hbm.1, s32[64]{0:T(128)} %rows_hbm.1, s32[1,1,8,8]{3,2,1,0:T(8,128)} %send_ref.3, ...), custom_call_target="tpu_custom_call" | custom-call | tf_op jit(solution)/shard_map/prep/pallas_call | solution.py:330
  3.6 0.5 collective-permute-start
  4.1 1.4 %collective-permute-done.came_ref = bf16[896,256]{1,0:T(8,128)(2,1)S(1)} collective-permute-done((bf16[896,256]{1,0:T(8,128)(2,1)S(1)}, bf16[896,256]{1,0:T(8,128)(2,1)S(1)}, u32[]{:S(2)}, u32[]{:S(2)}) %collective-permute-start) | collective-permute-done | bytes 458784 | tf_op jit(solution)/shard_map/ppermute | solution.py:343
  5.6 0.2 core_sum.2
  5.8 2.9 %collective-permute-start.1 = (bf16[128,256]{1,0:T(8,128)(2,1)S(1)}, bf16[128,256]{1,0:T(8,128)(2,1)S(1)}, u32[]{:S(2)}, u32[]{:S(2)}) collective-permute-start(bf16[128,256]{1,0:T(8,128)(2,1)S(1)} %get-tuple-element.47), channel_id=1, source_target_pairs={{0,2},{2,0},{1,3},{3,1},{4,6},{6,4},{5,7},{7,5},{8,10},{10,8},{9,1... | collective-permute-start | bytes 196616 | tf_op jit(solution)/shard_map/ppermute | solution.py:343
  8.7 2.4 %collective-permute-done.1.refs_0_ = bf16[128,256]{1,0:T(8,128)(2,1)S(1)} collective-permute-done((bf16[128,256]{1,0:T(8,128)(2,1)S(1)}, bf16[128,256]{1,0:T(8,128)(2,1)S(1)}, u32[]{:S(2)}, u32[]{:S(2)}) %collective-permute-start.1) | collective-permute-done | bytes 65568 | tf_op jit(solution)/shard_map/ppermute | solution.py:343
  11.1 1.9 %collective-permute-start.5 = (bf16[512,256]{1,0:T(8,128)(2,1)S(1)}, bf16[512,256]{1,0:T(8,128)(2,1)S(1)}, u32[]{:S(2)}, u32[]{:S(2)}) collective-permute-start(bf16[512,256]{1,0:T(8,128)(2,1)S(1)} %get-tuple-element.56), channel_id=1, source_target_pairs={{0,2},{2,0},{1,3},{3,1},{4,6},{6,4},{5,7},{7,5},{8,10},{10,8},{9,1... | collective-permute-start | bytes 786440 | tf_op jit(solution)/shard_map/ppermute | solution.py:343
  13.0 1.6 %collective-permute-start.2 = (bf16[96,256]{1,0:T(8,128)(2,1)S(1)}, bf16[96,256]{1,0:T(8,128)(2,1)S(1)}, u32[]{:S(2)}, u32[]{:S(2)}) collective-permute-start(bf16[96,256]{1,0:T(8,128)(2,1)S(1)} %get-tuple-element.51), channel_id=1, source_target_pairs={{0,4},{4,0},{8,12},{12,8},{16,20},{20,16},{24,28},{28,24},{1,5},{5... | collective-permute-start | bytes 147464 | tf_op jit(solution)/shard_map/ppermute | solution.py:348
  14.6 2.6 %collective-permute-done.2.came_ref = bf16[96,256]{1,0:T(8,128)(2,1)S(1)} collective-permute-done((bf16[96,256]{1,0:T(8,128)(2,1)S(1)}, bf16[96,256]{1,0:T(8,128)(2,1)S(1)}, u32[]{:S(2)}, u32[]{:S(2)}) %collective-permute-start.2) | collective-permute-done | bytes 49184 | tf_op jit(solution)/shard_map/ppermute | solution.py:348
  17.1 1.6 %collective-permute-start.3 = (bf16[96,256]{1,0:T(8,128)(2,1)S(1)}, bf16[96,256]{1,0:T(8,128)(2,1)S(1)}, u32[]{:S(2)}, u32[]{:S(2)}) collective-permute-start(bf16[96,256]{1,0:T(8,128)(2,1)S(1)} %get-tuple-element.53), channel_id=1, source_target_pairs={{0,8},{4,12},{8,0},{12,4},{16,24},{20,28},{24,16},{28,20},{1,9},{5... | collective-permute-start | bytes 147464 | tf_op jit(solution)/shard_map/ppermute | solution.py:348
  18.8 2.5 %collective-permute-done.3.came_ref = bf16[96,256]{1,0:T(8,128)(2,1)S(1)} collective-permute-done((bf16[96,256]{1,0:T(8,128)(2,1)S(1)}, bf16[96,256]{1,0:T(8,128)(2,1)S(1)}, u32[]{:S(2)}, u32[]{:S(2)}) %collective-permute-start.3) | collective-permute-done | bytes 49184 | tf_op jit(solution)/shard_map/ppermute | solution.py:348
  21.3 3.0 %collective-permute-start.4 = (bf16[96,256]{1,0:T(8,128)(2,1)S(1)}, bf16[96,256]{1,0:T(8,128)(2,1)S(1)}, u32[]{:S(2)}, u32[]{:S(2)}) collective-permute-start(bf16[96,256]{1,0:T(8,128)(2,1)S(1)} %get-tuple-element.55), channel_id=1, source_target_pairs={{0,16},{4,20},{8,24},{12,28},{16,0},{20,4},{24,8},{28,12},{1,17},{... | collective-permute-start | bytes 147464 | tf_op jit(solution)/shard_map/ppermute | solution.py:348
  24.3 2.1 %collective-permute-done.4.came_ref = bf16[96,256]{1,0:T(8,128)(2,1)S(1)} collective-permute-done((bf16[96,256]{1,0:T(8,128)(2,1)S(1)}, bf16[96,256]{1,0:T(8,128)(2,1)S(1)}, u32[]{:S(2)}, u32[]{:S(2)}) %collective-permute-start.4) | collective-permute-done | bytes 49184 | tf_op jit(solution)/shard_map/ppermute | solution.py:348
  26.4 0.1 collective-permute-start.6
  26.5 1.4 %collective-permute-done.6.shared_ref = bf16[384,256]{1,0:T(8,128)(2,1)S(1)} collective-permute-done((bf16[384,256]{1,0:T(8,128)(2,1)S(1)}, bf16[384,256]{1,0:T(8,128)(2,1)S(1)}, u32[]{:S(2)}, u32[]{:S(2)}) %collective-permute-start.6) | collective-permute-done | bytes 196640 | tf_op jit(solution)/shard_map/ppermute | solution.py:343
  28.0 0.0 copy-start.2
  28.0 2.1 %middle.1 = (bf16[256,256]{1,0:T(8,128)(2,1)S(1)}, bf16[256,256]{1,0:T(8,128)(2,1)S(1)}, bf16[640,256]{1,0:T(8,128)(2,1)S(1)}, bf16[896,256]{1,0:T(8,128)(2,1)S(1)}, bf16[64,256]{1,0:T(8,128)(2,1)S(1)}) custom-call(s32[1,1,8,8]{3,2,1,0:T(8,128)S(1)} %copy-done.6, bf16[256,1280]{1,0:T(8,128)(2,1)S(1)} %get-tuple-element.40.adj_ref, ...), custom_call_target="tpu_custom_call" | custom-call | tf_op jit(solution)/shard_map/middle/pallas_call | solution.py:330
  30.1 0.2 collective-permute-start.7
  30.3 1.7 %collective-permute-done.7.came_ref = bf16[896,256]{1,0:T(8,128)(2,1)S(1)} collective-permute-done((bf16[896,256]{1,0:T(8,128)(2,1)S(1)}, bf16[896,256]{1,0:T(8,128)(2,1)S(1)}, u32[]{:S(2)}, u32[]{:S(2)}) %collective-permute-start.7) | collective-permute-done | bytes 458784 | tf_op jit(solution)/shard_map/ppermute | solution.py:343
  32.0 0.2 core_sum.3
  32.2 0.6 %collective-permute-start.8 = (bf16[128,256]{1,0:T(8,128)(2,1)S(1)}, bf16[128,256]{1,0:T(8,128)(2,1)S(1)}, u32[]{:S(2)}, u32[]{:S(2)}) collective-permute-start(bf16[128,256]{1,0:T(8,128)(2,1)S(1)} %get-tuple-element.66), channel_id=1, source_target_pairs={{0,2},{2,0},{1,3},{3,1},{4,6},{6,4},{5,7},{7,5},{8,10},{10,8},{9,1... | collective-permute-start | bytes 196616 | tf_op jit(solution)/shard_map/ppermute | solution.py:343
  32.8 3.8 %collective-permute-done.8.refs_0_ = bf16[128,256]{1,0:T(8,128)(2,1)S(1)} collective-permute-done((bf16[128,256]{1,0:T(8,128)(2,1)S(1)}, bf16[128,256]{1,0:T(8,128)(2,1)S(1)}, u32[]{:S(2)}, u32[]{:S(2)}) %collective-permute-start.8) | collective-permute-done | bytes 65568 | tf_op jit(solution)/shard_map/ppermute | solution.py:343
  36.5 0.5 collective-permute-start.12
  37.1 1.6 %collective-permute-start.9 = (bf16[96,256]{1,0:T(8,128)(2,1)S(1)}, bf16[96,256]{1,0:T(8,128)(2,1)S(1)}, u32[]{:S(2)}, u32[]{:S(2)}) collective-permute-start(bf16[96,256]{1,0:T(8,128)(2,1)S(1)} %get-tuple-element.70), channel_id=1, source_target_pairs={{0,4},{4,0},{8,12},{12,8},{16,20},{20,16},{24,28},{28,24},{1,5},{5... | collective-permute-start | bytes 147464 | tf_op jit(solution)/shard_map/ppermute | solution.py:348
  38.7 2.5 %collective-permute-done.9.came_ref = bf16[96,256]{1,0:T(8,128)(2,1)S(1)} collective-permute-done((bf16[96,256]{1,0:T(8,128)(2,1)S(1)}, bf16[96,256]{1,0:T(8,128)(2,1)S(1)}, u32[]{:S(2)}, u32[]{:S(2)}) %collective-permute-start.9) | collective-permute-done | bytes 49184 | tf_op jit(solution)/shard_map/ppermute | solution.py:348
  41.2 1.7 %collective-permute-start.10 = (bf16[96,256]{1,0:T(8,128)(2,1)S(1)}, bf16[96,256]{1,0:T(8,128)(2,1)S(1)}, u32[]{:S(2)}, u32[]{:S(2)}) collective-permute-start(bf16[96,256]{1,0:T(8,128)(2,1)S(1)} %get-tuple-element.72), channel_id=1, source_target_pairs={{0,8},{4,12},{8,0},{12,4},{16,24},{20,28},{24,16},{28,20},{1,9},{5... | collective-permute-start | bytes 147464 | tf_op jit(solution)/shard_map/ppermute | solution.py:348
  42.9 2.5 %collective-permute-done.10.came_ref = bf16[96,256]{1,0:T(8,128)(2,1)S(1)} collective-permute-done((bf16[96,256]{1,0:T(8,128)(2,1)S(1)}, bf16[96,256]{1,0:T(8,128)(2,1)S(1)}, u32[]{:S(2)}, u32[]{:S(2)}) %collective-permute-start.10) | collective-permute-done | bytes 49184 | tf_op jit(solution)/shard_map/ppermute | solution.py:348
  45.4 3.5 %collective-permute-start.11 = (bf16[96,256]{1,0:T(8,128)(2,1)S(1)}, bf16[96,256]{1,0:T(8,128)(2,1)S(1)}, u32[]{:S(2)}, u32[]{:S(2)}) collective-permute-start(bf16[96,256]{1,0:T(8,128)(2,1)S(1)} %get-tuple-element.74), channel_id=1, source_target_pairs={{0,16},{4,20},{8,24},{12,28},{16,0},{20,4},{24,8},{28,12},{1,17},{... | collective-permute-start | bytes 147464 | tf_op jit(solution)/shard_map/ppermute | solution.py:348
  48.9 2.1 %collective-permute-done.11.came_ref = bf16[96,256]{1,0:T(8,128)(2,1)S(1)} collective-permute-done((bf16[96,256]{1,0:T(8,128)(2,1)S(1)}, bf16[96,256]{1,0:T(8,128)(2,1)S(1)}, u32[]{:S(2)}, u32[]{:S(2)}) %collective-permute-start.11) | collective-permute-done | bytes 49184 | tf_op jit(solution)/shard_map/ppermute | solution.py:348
  51.0 0.1 collective-permute-start.13
  51.1 1.4 %collective-permute-done.13.shared_ref = bf16[384,256]{1,0:T(8,128)(2,1)S(1)} collective-permute-done((bf16[384,256]{1,0:T(8,128)(2,1)S(1)}, bf16[384,256]{1,0:T(8,128)(2,1)S(1)}, u32[]{:S(2)}, u32[]{:S(2)}) %collective-permute-start.13) | collective-permute-done | bytes 196640 | tf_op jit(solution)/shard_map/ppermute | solution.py:343
  52.5 2.1 %last.1 = (bf16[256,256]{1,0:T(8,128)(2,1)}, f32[256,256]{1,0:T(8,128)}) custom-call(s32[1,1,8,8]{3,2,1,0:T(8,128)S(1)} %copy-done.6, bf16[256,1280]{1,0:T(8,128)(2,1)S(1)} %get-tuple-element.40.adj_ref, bf16[256,256]{1,0:T(8,128)(2,1)S(1)} %get-tuple-element.59.value_ref.hidden_ref, bf16[256,256]{1,0:T(8,128)(2,1)S(1)} %get-tuple-element.60.grad_pre_ref, ...), custom_call_target="tpu_custom_call" | custom-call | tf_op jit(solution)/shard_map/last/pallas_call | solution.py:330
  (27 shorter events, 0.2 us)
Async XLA Ops:
  0.6 27.3 %copy-start.6 = (s32[1,1,8,8]{3,2,1,0:T(8,128)S(1)}, s32[1,1,8,8]{3,2,1,0:T(8,128)}, u32[]{:S(2)}) copy-start(s32[1,1,8,8]{3,2,1,0:T(8,128)} %send_ref.3) | copy-start | bytes 772
  0.6 4.9 %copy-start = (bf16[256,256]{1,0:T(8,128)(2,1)S(1)}, bf16[256,256]{1,0:T(8,128)(2,1)}, u32[]{:S(2)}) copy-start(bf16[256,256]{1,0:T(8,128)(2,1)} %features_ref.1) | copy-start | bytes 393220
  0.7 27.3 %copy-start.1 = (bf16[256,256]{1,0:T(8,128)(2,1)S(1)}, bf16[256,256]{1,0:T(8,128)(2,1)}, u32[]{:S(2)}) copy-start(bf16[256,256]{1,0:T(8,128)(2,1)} %cot_ref.1) | copy-start | bytes 393220
  0.7 27.3 %copy-start.4 = (bf16[256,256]{1,0:T(8,128)(2,1)S(1)}, bf16[256,256]{1,0:T(8,128)(2,1)}, u32[]{:S(2)}) copy-start(bf16[256,256]{1,0:T(8,128)(2,1)} %self_two_ref.3) | copy-start | bytes 393220
  0.7 27.3 %copy-start.3 = (bf16[256,256]{1,0:T(8,128)(2,1)S(1)}, bf16[256,256]{1,0:T(8,128)(2,1)}, u32[]{:S(2)}) copy-start(bf16[256,256]{1,0:T(8,128)(2,1)} %self_one_ref.3) | copy-start | bytes 393220
  0.7 27.3 %copy-start.8 = (f32[256]{0:T(256)S(1)}, f32[256]{0:T(256)}, u32[]{:S(2)}) copy-start(f32[256]{0:T(256)} %bias_ref.2) | copy-start | bytes 3076
  0.7 27.3 %copy-start.5 = (bf16[256,256]{1,0:T(8,128)(2,1)S(1)}, bf16[256,256]{1,0:T(8,128)(2,1)}, u32[]{:S(2)}) copy-start(bf16[256,256]{1,0:T(8,128)(2,1)} %neigh_one_ref.1) | copy-start | bytes 393220
  3.6 2.0 %collective-permute-start = (bf16[896,256]{1,0:T(8,128)(2,1)S(1)}, bf16[896,256]{1,0:T(8,128)(2,1)S(1)}, u32[]{:S(2)}, u32[]{:S(2)}) collective-permute-start(bf16[896,256]{1,0:T(8,128)(2,1)S(1)} %get-tuple-element.43), channel_id=1, source_target_pairs={{0,1},{1,0},{2,3},{3,2},{4,5},{5,4},{6,7},{7,6},{8,9},{9,8},{10,11... | collective-permute-start | bytes 1376264 | tf_op jit(solution)/shard_map/ppermute | solution.py:343
  5.8 5.3 %collective-permute-start.1 = (bf16[128,256]{1,0:T(8,128)(2,1)S(1)}, bf16[128,256]{1,0:T(8,128)(2,1)S(1)}, u32[]{:S(2)}, u32[]{:S(2)}) collective-permute-start(bf16[128,256]{1,0:T(8,128)(2,1)S(1)} %get-tuple-element.47), channel_id=1, source_target_pairs={{0,2},{2,0},{1,3},{3,1},{4,6},{6,4},{5,7},{7,5},{8,10},{10,8},{9,1... | collective-permute-start | bytes 196616 | tf_op jit(solution)/shard_map/ppermute | solution.py:343
  11.1 15.3 %collective-permute-start.5 = (bf16[512,256]{1,0:T(8,128)(2,1)S(1)}, bf16[512,256]{1,0:T(8,128)(2,1)S(1)}, u32[]{:S(2)}, u32[]{:S(2)}) collective-permute-start(bf16[512,256]{1,0:T(8,128)(2,1)S(1)} %get-tuple-element.56), channel_id=1, source_target_pairs={{0,2},{2,0},{1,3},{3,1},{4,6},{6,4},{5,7},{7,5},{8,10},{10,8},{9,1... | collective-permute-start | bytes 786440 | tf_op jit(solution)/shard_map/ppermute | solution.py:343
  13.0 4.2 %collective-permute-start.2 = (bf16[96,256]{1,0:T(8,128)(2,1)S(1)}, bf16[96,256]{1,0:T(8,128)(2,1)S(1)}, u32[]{:S(2)}, u32[]{:S(2)}) collective-permute-start(bf16[96,256]{1,0:T(8,128)(2,1)S(1)} %get-tuple-element.51), channel_id=1, source_target_pairs={{0,4},{4,0},{8,12},{12,8},{16,20},{20,16},{24,28},{28,24},{1,5},{5... | collective-permute-start | bytes 147464 | tf_op jit(solution)/shard_map/ppermute | solution.py:348
  17.1 4.2 %collective-permute-start.3 = (bf16[96,256]{1,0:T(8,128)(2,1)S(1)}, bf16[96,256]{1,0:T(8,128)(2,1)S(1)}, u32[]{:S(2)}, u32[]{:S(2)}) collective-permute-start(bf16[96,256]{1,0:T(8,128)(2,1)S(1)} %get-tuple-element.53), channel_id=1, source_target_pairs={{0,8},{4,12},{8,0},{12,4},{16,24},{20,28},{24,16},{28,20},{1,9},{5... | collective-permute-start | bytes 147464 | tf_op jit(solution)/shard_map/ppermute | solution.py:348
  21.3 5.1 %collective-permute-start.4 = (bf16[96,256]{1,0:T(8,128)(2,1)S(1)}, bf16[96,256]{1,0:T(8,128)(2,1)S(1)}, u32[]{:S(2)}, u32[]{:S(2)}) collective-permute-start(bf16[96,256]{1,0:T(8,128)(2,1)S(1)} %get-tuple-element.55), channel_id=1, source_target_pairs={{0,16},{4,20},{8,24},{12,28},{16,0},{20,4},{24,8},{28,12},{1,17},{... | collective-permute-start | bytes 147464 | tf_op jit(solution)/shard_map/ppermute | solution.py:348
  26.4 1.5 %collective-permute-start.6 = (bf16[384,256]{1,0:T(8,128)(2,1)S(1)}, bf16[384,256]{1,0:T(8,128)(2,1)S(1)}, u32[]{:S(2)}, u32[]{:S(2)}) collective-permute-start(bf16[384,256]{1,0:T(8,128)(2,1)S(1)} %get-tuple-element.57.here_ref), channel_id=1, source_target_pairs={{0,1},{1,0},{2,3},{3,2},{4,5},{5,4},{6,7},{7,6},{8,9},{9,8},{10,11... | collective-permute-start | bytes 589832 | tf_op jit(solution)/shard_map/ppermute | solution.py:343
  28.0 24.5 %copy-start.2 = (bf16[256,256]{1,0:T(8,128)(2,1)S(1)}, bf16[256,256]{1,0:T(8,128)(2,1)}, u32[]{:S(2)}) copy-start(bf16[256,256]{1,0:T(8,128)(2,1)} %neigh_two_ref.1) | copy-start | bytes 393220
  28.0 24.5 %copy-start.7 = (f32[256]{0:T(256)S(1)}, f32[256]{0:T(256)}, u32[]{:S(2)}) copy-start(f32[256]{0:T(256)} %bias_ref.3) | copy-start | bytes 3076
  30.1 1.9 %collective-permute-start.7 = (bf16[896,256]{1,0:T(8,128)(2,1)S(1)}, bf16[896,256]{1,0:T(8,128)(2,1)S(1)}, u32[]{:S(2)}, u32[]{:S(2)}) collective-permute-start(bf16[896,256]{1,0:T(8,128)(2,1)S(1)} %get-tuple-element.62), channel_id=1, source_target_pairs={{0,1},{1,0},{2,3},{3,2},{4,5},{5,4},{6,7},{7,6},{8,9},{9,8},{10,11... | collective-permute-start | bytes 1376264 | tf_op jit(solution)/shard_map/ppermute | solution.py:343
  32.2 4.3 %collective-permute-start.8 = (bf16[128,256]{1,0:T(8,128)(2,1)S(1)}, bf16[128,256]{1,0:T(8,128)(2,1)S(1)}, u32[]{:S(2)}, u32[]{:S(2)}) collective-permute-start(bf16[128,256]{1,0:T(8,128)(2,1)S(1)} %get-tuple-element.66), channel_id=1, source_target_pairs={{0,2},{2,0},{1,3},{3,1},{4,6},{6,4},{5,7},{7,5},{8,10},{10,8},{9,1... | collective-permute-start | bytes 196616 | tf_op jit(solution)/shard_map/ppermute | solution.py:343
  36.5 14.4 %collective-permute-start.12 = (bf16[512,256]{1,0:T(8,128)(2,1)S(1)}, bf16[512,256]{1,0:T(8,128)(2,1)S(1)}, u32[]{:S(2)}, u32[]{:S(2)}) collective-permute-start(bf16[512,256]{1,0:T(8,128)(2,1)S(1)} %get-tuple-element.75), channel_id=1, source_target_pairs={{0,2},{2,0},{1,3},{3,1},{4,6},{6,4},{5,7},{7,5},{8,10},{10,8},{9,1... | collective-permute-start | bytes 786440 | tf_op jit(solution)/shard_map/ppermute | solution.py:343
  37.1 4.2 %collective-permute-start.9 = (bf16[96,256]{1,0:T(8,128)(2,1)S(1)}, bf16[96,256]{1,0:T(8,128)(2,1)S(1)}, u32[]{:S(2)}, u32[]{:S(2)}) collective-permute-start(bf16[96,256]{1,0:T(8,128)(2,1)S(1)} %get-tuple-element.70), channel_id=1, source_target_pairs={{0,4},{4,0},{8,12},{12,8},{16,20},{20,16},{24,28},{28,24},{1,5},{5... | collective-permute-start | bytes 147464 | tf_op jit(solution)/shard_map/ppermute | solution.py:348
  41.2 4.2 %collective-permute-start.10 = (bf16[96,256]{1,0:T(8,128)(2,1)S(1)}, bf16[96,256]{1,0:T(8,128)(2,1)S(1)}, u32[]{:S(2)}, u32[]{:S(2)}) collective-permute-start(bf16[96,256]{1,0:T(8,128)(2,1)S(1)} %get-tuple-element.72), channel_id=1, source_target_pairs={{0,8},{4,12},{8,0},{12,4},{16,24},{20,28},{24,16},{28,20},{1,9},{5... | collective-permute-start | bytes 147464 | tf_op jit(solution)/shard_map/ppermute | solution.py:348
  45.4 5.5 %collective-permute-start.11 = (bf16[96,256]{1,0:T(8,128)(2,1)S(1)}, bf16[96,256]{1,0:T(8,128)(2,1)S(1)}, u32[]{:S(2)}, u32[]{:S(2)}) collective-permute-start(bf16[96,256]{1,0:T(8,128)(2,1)S(1)} %get-tuple-element.74), channel_id=1, source_target_pairs={{0,16},{4,20},{8,24},{12,28},{16,0},{20,4},{24,8},{28,12},{1,17},{... | collective-permute-start | bytes 147464 | tf_op jit(solution)/shard_map/ppermute | solution.py:348
  51.0 1.5 %collective-permute-start.13 = (bf16[384,256]{1,0:T(8,128)(2,1)S(1)}, bf16[384,256]{1,0:T(8,128)(2,1)S(1)}, u32[]{:S(2)}, u32[]{:S(2)}) collective-permute-start(bf16[384,256]{1,0:T(8,128)(2,1)S(1)} %get-tuple-element.76.here_ref), channel_id=1, source_target_pairs={{0,1},{1,0},{2,3},{3,2},{4,5},{5,4},{6,7},{7,6},{8,9},{9,8},{10,11... | collective-permute-start | bytes 589832 | tf_op jit(solution)/shard_map/ppermute | solution.py:343

commit v5 on v3

--- a/solution.py
+++ b/solution.py
@@ -14,7 +14,6 @@
 CORES = 2
 
 VMEM = pl.BlockSpec(memory_space=pltpu.VMEM)
-SMEM = pl.BlockSpec(memory_space=pltpu.SMEM)
 HBM = pl.BlockSpec(memory_space=pltpu.HBM)
 
 
@@ -74,6 +73,7 @@
     keep_ref,
     give_ref,
     picked_ref,
+    pick_ref,
     dst_ref,
     src_ref,
     rows_ref,
@@ -114,7 +114,8 @@
     u = dot_nt(cot_ref[...], neigh_two_ref[...]).astype(BF16)
     copies[2].wait()
     copies[3].wait()
-    picked_ref[...] = dot(pick_matrix(send_ref, rows), features_ref[...]).astype(BF16)
+    pick_ref[...] = pick_matrix(send_ref, rows)
+    picked_ref[...] = dot(pick_ref[...], features_ref[...]).astype(BF16)
     for copy in copies[4:7]:
         copy.wait()
     place = lax.broadcasted_iota(jnp.int32, (blk, blk), 0)
@@ -182,113 +183,96 @@
     out_ref[len(came) * rows :, :] = halo_part(recv_ref, hosts, chips, 0)
 
 
-def gather_sources(chips, hosts, value, came_ref, chip_refs, recv_ref, shared_ref, space):
+def early_kernel(
+    chips, adj_ref, value_ref, came_ref, self_ref, bias_ref, up_ref, weight_ref, mine_ref,
+    agg_ref, direct_ref, grad_ref,
+):
+    value = value_ref[...]
     rows = value.shape[0]
     chip, core = lax.axis_index("chip"), lax.axis_index("core")
-    far_rows = recv_ref.shape[0] // chips * recv_ref.shape[1] // 2
-
-    def put(x, side, block):
-        low = pl.multiple_of((x * CORES + side) * rows, rows)
-        space[pl.ds(low, rows), :] = block
-
-    put(chip, core, value)
-    put(chip, 1 - core, came_ref[came_ref.shape[0] - rows :, :])
-    for k, ref in enumerate(chip_refs):
+    there = came_ref[came_ref.shape[0] - rows :, :]
+    total = 0.0
+    for side, block in ((core, value), (1 - core, there)):
+        low = pl.multiple_of((chip * CORES + side) * rows, rows)
+        total = total + dot(adj_ref[:, pl.ds(low, rows)], block)
+    agg_ref[...] = total
+    direct_ref[...] = dot(value, self_ref[...]) + bias_ref[...].reshape(1, -1)
+    grad_ref[...] = dot_nt(up_ref[...], weight_ref[...]) + mine_ref[...]
+
+
+def mid_kernel(chips, hosts, adj_ref, agg_ref, part_ref, pick_ref, recv_ref, *refs):
+    came, (agg_out, grad_ref) = refs[: chips - 1], refs[chips - 1 :]
+    rows = part_ref.shape[0]
+    chip, core = lax.axis_index("chip"), lax.axis_index("core")
+    agg, grad = agg_ref[...], part_ref[...]
+    for k, ref in enumerate(came):
+        grad = grad + ref[:rows, :].astype(F32)
         x = lax.rem(chip - k - 1 + chips, chips)
-        put(x, core, ref[rows:, :])
-        put(x, 1 - core, shared_ref[k * rows : (k + 1) * rows, :])
-    base = chips * CORES * rows
-    here = halo_part(recv_ref, hosts, chips, 0)
-    there = shared_ref[(chips - 1) * rows :, :]
+        low = pl.multiple_of((x * CORES + core) * rows, rows)
+        agg = agg + dot(adj_ref[:, pl.ds(low, rows)], ref[rows:, :])
+    back = halo_part(recv_ref, hosts, chips, 1)
+    grad_ref[...] = grad + dot_tn(jnp.concatenate([pick_ref[...]] * chips, 0), back)
+    agg_out[...] = agg
+
+
+def full_aggregate(chips, adj_ref, agg_ref, here_ref, shared_ref, halo):
+    rows = agg_ref.shape[0]
+    far = halo.shape[0] // (chips * CORES)
+    chip, core = lax.axis_index("chip"), lax.axis_index("core")
+    at = (chips - 1) * rows
     for x in range(chips):
-        for side, block in ((core, here), (1 - core, there)):
-            low = pl.multiple_of(base + (x * CORES + side) * far_rows, far_rows)
-            space[pl.ds(low, far_rows), :] = block[x * far_rows : (x + 1) * far_rows]
-
-
-def spread_total(pick, chips, hosts, mine_ref, chip_refs, recv_ref):
-    total = mine_ref[...]
-    rows = total.shape[0]
-    for ref in chip_refs:
-        total = total + ref[:rows, :].astype(F32)
-    back = halo_part(recv_ref, hosts, chips, 1)
-    return total + dot_tn(jnp.concatenate([pick] * chips, 0), back)
+        for side, ref in ((core, here_ref), (1 - core, shared_ref)):
+            low = pl.multiple_of((x * CORES + side) * far, far)
+            halo[pl.ds(low, far), :] = ref[at + x * far : at + (x + 1) * far, :]
+    agg = agg_ref[...]
+    for k in range(chips - 1):
+        x = lax.rem(chip - k - 1 + chips, chips)
+        low = pl.multiple_of((x * CORES + 1 - core) * rows, rows)
+        agg = agg + dot(adj_ref[:, pl.ds(low, rows)], shared_ref[k * rows : (k + 1) * rows, :])
+    return agg + dot(adj_ref[:, chips * CORES * rows :], halo[...])
 
 
 def middle_kernel(
     chips,
-    hosts,
-    send_ref,
     adj_ref,
     adj_t_ref,
-    features_ref,
-    cot_ref,
-    self_one_ref,
+    agg_ref,
+    direct_ref,
+    grad_ref,
+    pick_ref,
+    here_ref,
+    shared_ref,
     neigh_one_ref,
-    bias_ref,
-    self_two_ref,
-    mine_ref,
-    came_ref,
-    recv_ref,
-    shared_ref,
-    *refs,
-):
-    chip_refs = refs[: chips - 1]
-    hidden_ref, grad_pre_ref, keep_ref, give_ref, picked_ref, space = refs[chips - 1 :]
-    rows = features_ref.shape[0]
-    far = send_ref.shape[2] * send_ref.shape[3]
-    pick = pick_matrix(send_ref, rows)
-    gather_sources(
-        chips, hosts, features_ref[...], came_ref, chip_refs, recv_ref, shared_ref, space
-    )
-    agg = dot(adj_ref[...], space[...]).astype(BF16)
-    pre = dot(features_ref[...], self_one_ref[...])
-    pre = pre + dot(agg, neigh_one_ref[...]) + bias_ref[...].reshape(1, -1)
+    hidden_ref,
+    grad_pre_ref,
+    keep_ref,
+    give_ref,
+    picked_ref,
+    halo,
+    whole,
+):
+    agg = full_aggregate(chips, adj_ref, agg_ref, here_ref, shared_ref, halo).astype(BF16)
+    pre = direct_ref[...] + dot(agg, neigh_one_ref[...])
     sigmoid = jax.nn.sigmoid(pre)
     hidden = (pre * sigmoid).astype(BF16)
     hidden_ref[...] = hidden
-    picked_ref[...] = dot(pick, hidden).astype(BF16)
-    grad = dot_nt(cot_ref[...], self_two_ref[...])
-    grad = grad + spread_total(pick, chips, hosts, mine_ref, chip_refs, recv_ref)
-    grad_pre = (grad * sigmoid * (1.0 + pre * (1.0 - sigmoid))).astype(BF16)
+    picked_ref[...] = dot(pick_ref[...], hidden).astype(BF16)
+    grad_pre = (grad_ref[...] * sigmoid * (1.0 + pre * (1.0 - sigmoid))).astype(BF16)
     grad_pre_ref[...] = grad_pre
     u = dot_nt(grad_pre, neigh_one_ref[...]).astype(BF16)
-    spread_parts(chips, far, adj_t_ref[...], u, hidden, space, keep_ref, give_ref)
+    spread_parts(
+        chips, pick_ref.shape[0], adj_t_ref[...], u, hidden, whole, keep_ref, give_ref
+    )
 
 
 def last_kernel(
-    chips,
-    hosts,
-    send_ref,
-    adj_ref,
-    hidden_ref,
-    grad_pre_ref,
-    self_one_ref,
-    self_two_ref,
-    neigh_two_ref,
-    bias_ref,
-    mine_ref,
-    came_ref,
-    recv_ref,
-    shared_ref,
-    *refs,
-):
-    chip_refs = refs[: chips - 1]
-    output_ref, grad_ref, space = refs[chips - 1 :]
-    rows = hidden_ref.shape[0]
-    pick = pick_matrix(send_ref, rows)
-    gather_sources(
-        chips, hosts, hidden_ref[...], came_ref, chip_refs, recv_ref, shared_ref, space
-    )
-    agg = dot(adj_ref[...], space[...]).astype(BF16)
-    result = dot(hidden_ref[...], self_two_ref[...])
-    result = result + dot(agg, neigh_two_ref[...]) + bias_ref[...].reshape(1, -1)
-    output_ref[...] = result.astype(BF16)
-    grad = dot_nt(grad_pre_ref[...], self_one_ref[...])
-    grad_ref[...] = grad + spread_total(pick, chips, hosts, mine_ref, chip_refs, recv_ref)
-
-
-def call(kernel, name, out_shape, in_specs, args, scratch=(), limit=32):
+    chips, adj_ref, agg_ref, direct_ref, here_ref, shared_ref, neigh_two_ref, output_ref, halo
+):
+    agg = full_aggregate(chips, adj_ref, agg_ref, here_ref, shared_ref, halo).astype(BF16)
+    output_ref[...] = (direct_ref[...] + dot(agg, neigh_two_ref[...])).astype(BF16)
+
+
+def call(kernel, name, out_shape, in_specs, args, scratch=(), limit=32, flops=0):
     return pl.pallas_call(
         kernel,
         out_shape=out_shape,
@@ -296,6 +280,9 @@
         out_specs=jax.tree.map(lambda _: VMEM, out_shape),
         scratch_shapes=scratch,
         compiler_params=pltpu.CompilerParams(vmem_limit_bytes=limit * MIB),
+        cost_estimate=pl.CostEstimate(
+            flops=flops, bytes_accessed=flops // 1024, transcendentals=0
+        ),
         name=name,
     )(*args)
 
@@ -337,15 +324,16 @@
     rows_shape = shape(rows, width)
     space = pltpu.VMEM((all_rows, width), BF16)
 
-    def exchange(keep, give, value, picked):
+    square = 2 * rows * width * width
+    halo = pltpu.VMEM((chips * CORES * far, width), BF16)
+    sum_shape = shape(rows, width, F32)
+
+    def exchange(adj, pick, keep, give, picked, value, self_weight, bias, up, weight):
         came = shift(give, "core", 1)
         mine, msg, *to = call(
             functools.partial(core_sum_kernel, chips, hosts),
             "core_sum",
-            (
-                shape(rows, width, F32),
-                jax.ShapeDtypeStruct((hosts * chips, 2 * send, width), BF16),
-            )
+            (sum_shape, jax.ShapeDtypeStruct((hosts * chips, 2 * send, width), BF16))
             + (shape(2 * rows, width),) * (chips - 1),
             [VMEM] * 4,
             (keep, came, value, picked),
@@ -353,20 +341,37 @@
         )
         terms = [shift(block, "chip", k + 1) for k, block in enumerate(to)]
         recv = lax.all_to_all(msg, ("hst", "chip"), split_axis=0, concat_axis=0, tiled=True)
-        merged = call(
+        agg, direct, grad = call(
+            functools.partial(early_kernel, chips),
+            "early",
+            (sum_shape,) * 3,
+            [VMEM] * 8,
+            (adj, value, came, self_weight, bias, up, weight, mine),
+            flops=4 * square,
+        )
+        here = call(
             functools.partial(merge_kernel, chips, hosts),
             "merge",
             shape((chips - 1) * rows + chips * far, width),
             [VMEM] * chips,
             (recv, *terms),
         )
-        shared = shift(merged, "core", 1)
-        return mine, came, recv, shared, *terms
-
-    adj, adj_t, keep, give, picked = call(
+        shared = shift(here, "core", 1)
+        agg, grad = call(
+            functools.partial(mid_kernel, chips, hosts),
+            "mid",
+            (sum_shape,) * 2,
+            [VMEM] * (4 + chips),
+            (adj, agg, grad, pick, recv, *terms),
+            flops=2 * square,
+        )
+        return agg, direct, grad, here, shared
+
+    adj, adj_t, keep, give, picked, pick = call(
         functools.partial(prep_kernel, chips),
         "prep",
-        (shape(rows, all_rows), shape(all_rows, rows), keep_shape, give_shape, picked_shape),
+        (shape(rows, all_rows), shape(all_rows, rows), keep_shape, give_shape)
+        + (picked_shape, shape(far, rows)),
         [HBM] * 8,
         [
             pltpu.with_memory_space_constraint(value, pltpu.HBM)
@@ -395,45 +400,31 @@
             pltpu.SemaphoreType.DMA((7 + CHUNKS,)),
         ],
     )
-    came = exchange(keep, give, features, picked)
+    agg, direct, grad, here, shared = exchange(
+        adj, pick, keep, give, picked, features, self_one, bias_one, cotangent, self_two
+    )
     hidden, grad_pre, keep, give, picked = call(
-        functools.partial(middle_kernel, chips, hosts),
+        functools.partial(middle_kernel, chips),
         "middle",
         (rows_shape, rows_shape, keep_shape, give_shape, picked_shape),
-        [SMEM] + [VMEM] * (11 + chips),
-        (
-            send_list,
-            adj,
-            adj_t,
-            features,
-            cotangent,
-            self_one,
-            neigh_one,
-            bias_one,
-            self_two,
-            *came,
-        ),
-        [space],
-    )
-    came = exchange(keep, give, hidden, picked)
-    return call(
-        functools.partial(last_kernel, chips, hosts),
+        [VMEM] * 9,
+        (adj, adj_t, agg, direct, grad, pick, here, shared, neigh_one),
+        [halo, space],
+        flops=9 * square,
+    )
+    agg, direct, grad, here, shared = exchange(
+        adj, pick, keep, give, picked, hidden, self_two, bias_two, grad_pre, self_one
+    )
+    output = call(
+        functools.partial(last_kernel, chips),
         "last",
-        (rows_shape, shape(rows, width, F32)),
-        [SMEM] + [VMEM] * (10 + chips),
-        (
-            send_list,
-            adj,
-            hidden,
-            grad_pre,
-            self_one,
-            self_two,
-            neigh_two,
-            bias_two,
-            *came,
-        ),
-        [space],
-    )
+        rows_shape,
+        [VMEM] * 6,
+        (adj, agg, direct, here, shared, neigh_two),
+        [halo],
+        flops=3 * square,
+    )
+    return output, grad
 
 
 def solution(mesh):

time: 43.8 us -> 41.5 us (0.947)
  waiting for transfers between devices: 5.98 us -> 4.07 us
  Pallas kernels: 7.53 us -> 7.09 us
    ppermute x6, waiting for transfers between devices: 5.98 us -> 4.07 us  [shift(): return lax.ppermute(value, axis, [(i, (i + k) % size) for i in range(size)])]
    pallas_call x7 -> x11, Pallas kernels: 7.53 us -> 7.09 us  [call(): pl.pallas_call(kernel, out_shape=out_shape, in_specs=in_specs, out_specs=...]
  transfers between devices with their start and end apart: 6 -> 6, of which waited for: 4 -> 4; matrix products, arithmetic and copies ran while one was open for 0% -> 0% of each run, Pallas kernels for 0% -> 4%
where the time goes in v5:
time: 41.5 us; the launch traced here: 41.2 us
  blocking collectives  24.3 us (59%)
  Pallas kernels  7.09 us (17%)
  starting transfers between devices  4.97 us (12%)
  waiting for transfers between devices  4.07 us (10%)
  between operations  0.78 us (2%)
    all_to_all x2, blocking collectives, exchange(): lax.all_to_all(msg, ('hst', 'chip'), split_axis=0, concat_axis=0, tiled=T...  24.3 us
    pallas_call x11, Pallas kernels, call(): pl.pallas_call(kernel, out_shape=out_shape, in_specs=in_specs, out_specs=...  7.09 us
    ppermute x6, starting transfers between devices, shift(): return lax.ppermute(value, axis, [(i, (i + k) % size) for i in range(size)])  4.97 us
    ppermute x6, waiting for transfers between devices, shift(): return lax.ppermute(value, axis, [(i, (i + k) % size) for i in range(size)])  4.07 us
  transfers between devices with their start and end apart: 6, of which 4 were waited for; matrix products, arithmetic and copies ran while one was open for 0% of the time, Pallas kernels for 4%

profile of v5, /device:TPU:0, one launch (start us, length us, event | category | flops | bytes accessed | tf_op | source)
XLA Modules:
  0.0 41.2 jit_solution(14657416221997900217)
XLA Ops:
  0.6 0.0 copy-start
  0.6 0.0 copy-start.2
  0.7 0.0 copy-start.4
  0.7 0.0 copy-start.3
  0.7 0.0 copy-start.6
  0.7 2.9 %prep.1 = (bf16[256,1280]{1,0:T(8,128)(2,1)S(1)}, bf16[1280,256]{1,0:T(8,128)(2,1)S(1)}, bf16[640,256]{1,0:T(8,128)(2,1)S(1)}, bf16[896,256]{1,0:T(8,128)(2,1)S(...) custom-call(s32[64]{0:T(128)} %dst_hbm.1, s32[64]{0:T(128)} %src_hbm.1, s32[64]{0:T(128)} %rows_hbm.1, ...), custom_call_target="tpu_custom_call" | custom-call | tf_op jit(solution)/shard_map/prep/pallas_call | solution.py:276
  3.6 0.5 %collective-permute-start = (bf16[896,256]{1,0:T(8,128)(2,1)S(1)}, bf16[896,256]{1,0:T(8,128)(2,1)S(1)}, u32[]{:S(2)}, u32[]{:S(2)}) collective-permute-start(bf16[896,256]{1,0:T(8,128)(2,1)S(1)} %get-tuple-element.31), channel_id=1, source_target_pairs={{0,1},{1,0},{2,3},{3,2},{4,5},{5,4},{6,7},{7,6},{8,9},{9,8},{10,11... | collective-permute-start | bytes 1376264 | tf_op jit(solution)/shard_map/ppermute | solution.py:292
  4.1 1.4 %collective-permute-done.came_ref = bf16[896,256]{1,0:T(8,128)(2,1)S(1)} collective-permute-done((bf16[896,256]{1,0:T(8,128)(2,1)S(1)}, bf16[896,256]{1,0:T(8,128)(2,1)S(1)}, u32[]{:S(2)}, u32[]{:S(2)}) %collective-permute-start) | collective-permute-done | bytes 458784 | tf_op jit(solution)/shard_map/ppermute | solution.py:292
  5.5 0.0 copy-done
  5.6 0.2 core_sum.2
  5.7 2.9 %collective-permute-start.1 = (bf16[512,256]{1,0:T(8,128)(2,1)S(1)}, bf16[512,256]{1,0:T(8,128)(2,1)S(1)}, u32[]{:S(2)}, u32[]{:S(2)}) collective-permute-start(bf16[512,256]{1,0:T(8,128)(2,1)S(1)} %get-tuple-element.39), channel_id=1, source_target_pairs={{0,2},{2,0},{1,3},{3,1},{4,6},{6,4},{5,7},{7,5},{8,10},{10,8},{9,1... | collective-permute-start | bytes 786440 | tf_op jit(solution)/shard_map/ppermute | solution.py:292
  8.6 13.5 %all_to_all.10.recv_ref = bf16[16,16,256]{2,1,0:T(8,128)(2,1)S(1)} all-to-all(bf16[16,16,256]{2,1,0:T(8,128)(2,1)S(1)} %get-tuple-element.38), channel_id=1, replica_groups=mesh['hst'=8,'chip'=2,'core'=2] {'hst','chip'}, dimensions={0} | all-to-all | bytes 262144 | tf_op jit(solution)/shard_map/all_to_all | solution.py:343
  22.2 0.0 collective-permute-done.1.refs_0_
  22.2 0.1 collective-permute-start.2
  22.3 0.0 copy-done.2
  22.3 0.0 copy-done.4
  22.3 0.0 copy-done.3
  22.3 0.3 early.2
  22.6 0.2 mid.2
  22.9 0.8 %collective-permute-done.2.shared_ref = bf16[384,256]{1,0:T(8,128)(2,1)S(1)} collective-permute-done((bf16[384,256]{1,0:T(8,128)(2,1)S(1)}, bf16[384,256]{1,0:T(8,128)(2,1)S(1)}, u32[]{:S(2)}, u32[]{:S(2)}) %collective-permute-start.2) | collective-permute-done | bytes 196640 | tf_op jit(solution)/shard_map/ppermute | solution.py:292
  23.7 1.0 %middle.1 = (bf16[256,256]{1,0:T(8,128)(2,1)S(1)}, bf16[256,256]{1,0:T(8,128)(2,1)S(1)}, bf16[640,256]{1,0:T(8,128)(2,1)S(1)}, bf16[896,256]{1,0:T(8,128)(2,1)S(1)}, bf16[64,256]{1,0:T(8,128)(2,1)S(1)}) custom-call(bf16[256,1280]{1,0:T(8,128)(2,1)S(1)} %get-tuple-element.29.adj_ref, bf16[1280,256]{1,0:T(8,128)(2,1)S(1)} %get-tuple-element.30.adj_t_ref, ...), custom_call_target="tpu_custom_call" | custom-call | flops 301989888 | bytes 294912 | tf_op jit(solution)/shard_map/middle/pallas_call | solution.py:276
  24.7 0.2 collective-permute-start.3
  24.9 1.7 %collective-permute-done.3.came_ref = bf16[896,256]{1,0:T(8,128)(2,1)S(1)} collective-permute-done((bf16[896,256]{1,0:T(8,128)(2,1)S(1)}, bf16[896,256]{1,0:T(8,128)(2,1)S(1)}, u32[]{:S(2)}, u32[]{:S(2)}) %collective-permute-start.3) | collective-permute-done | bytes 458784 | tf_op jit(solution)/shard_map/ppermute | solution.py:292
  26.6 0.2 core_sum.3
  26.7 1.2 %collective-permute-start.4 = (bf16[512,256]{1,0:T(8,128)(2,1)S(1)}, bf16[512,256]{1,0:T(8,128)(2,1)S(1)}, u32[]{:S(2)}, u32[]{:S(2)}) collective-permute-start(bf16[512,256]{1,0:T(8,128)(2,1)S(1)} %get-tuple-element.52), channel_id=1, source_target_pairs={{0,2},{2,0},{1,3},{3,1},{4,6},{6,4},{5,7},{7,5},{8,10},{10,8},{9,1... | collective-permute-start | bytes 786440 | tf_op jit(solution)/shard_map/ppermute | solution.py:292
  27.9 10.8 %all_to_all.11.recv_ref = bf16[16,16,256]{2,1,0:T(8,128)(2,1)S(1)} all-to-all(bf16[16,16,256]{2,1,0:T(8,128)(2,1)S(1)} %get-tuple-element.51), channel_id=1, replica_groups=mesh['hst'=8,'chip'=2,'core'=2] {'hst','chip'}, dimensions={0} | all-to-all | bytes 262144 | tf_op jit(solution)/shard_map/all_to_all | solution.py:343
  38.7 0.0 collective-permute-done.4.refs_0_
  38.7 0.1 collective-permute-start.5
  38.8 0.3 early.3
  39.1 0.9 %mid.3 = (f32[256,256]{1,0:T(8,128)S(1)}, f32[256,256]{1,0:T(8,128)}) custom-call(bf16[256,1280]{1,0:T(8,128)(2,1)S(1)} %get-tuple-element.29.adj_ref, f32[256,256]{1,0:T(8,128)S(1)} %get-tuple-element.49.agg_ref, f32[256,256]{1,0:T(8,128)S(1)} %get-tuple-element.50.part_ref, bf16[64,256]{1,0:T(8,128)(2,1)S(1)} %get-tuple-element.37.pick_ref, ...), custom_call_target="tpu_custom_call" | custom-call | flops 67108864 | bytes 65536 | tf_op jit(solution)/shard_map/mid/pallas_call | solution.py:276
  40.0 0.1 collective-permute-done.5.shared_ref
  40.2 1.0 %last.1 = bf16[256,256]{1,0:T(8,128)(2,1)} custom-call(bf16[256,1280]{1,0:T(8,128)(2,1)S(1)} %get-tuple-element.29.adj_ref, f32[256,256]{1,0:T(8,128)S(1)} %get-tuple-element.53.agg_ref, f32[256,256]{1,0:T(8,128)S(1)} %get-tuple-element.54.direct_ref, bf16[384,256]{1,0:T(8,128)(2,1)S(1)} %merge.3.here_ref, ...), custom_call_target="tpu_custom_call" | custom-call | flops 100663296 | bytes 98304 | tf_op jit(solution)/shard_map/last/pallas_call | solution.py:276
  (9 shorter events, 0.0 us)
Async XLA Ops:
  0.6 4.9 %copy-start = (bf16[256,256]{1,0:T(8,128)(2,1)S(1)}, bf16[256,256]{1,0:T(8,128)(2,1)}, u32[]{:S(2)}) copy-start(bf16[256,256]{1,0:T(8,128)(2,1)} %value_ref.3) | copy-start | bytes 393220
  0.6 21.6 %copy-start.2 = (bf16[256,256]{1,0:T(8,128)(2,1)S(1)}, bf16[256,256]{1,0:T(8,128)(2,1)}, u32[]{:S(2)}) copy-start(bf16[256,256]{1,0:T(8,128)(2,1)} %up_ref.1) | copy-start | bytes 393220
  0.7 21.6 %copy-start.4 = (bf16[256,256]{1,0:T(8,128)(2,1)S(1)}, bf16[256,256]{1,0:T(8,128)(2,1)}, u32[]{:S(2)}) copy-start(bf16[256,256]{1,0:T(8,128)(2,1)} %self_ref.3) | copy-start | bytes 393220
  0.7 21.6 %copy-start.3 = (bf16[256,256]{1,0:T(8,128)(2,1)S(1)}, bf16[256,256]{1,0:T(8,128)(2,1)}, u32[]{:S(2)}) copy-start(bf16[256,256]{1,0:T(8,128)(2,1)} %weight_ref.3) | copy-start | bytes 393220
  0.7 21.6 %copy-start.6 = (f32[256]{0:T(256)S(1)}, f32[256]{0:T(256)}, u32[]{:S(2)}) copy-start(f32[256]{0:T(256)} %bias_ref.2) | copy-start | bytes 3076
  3.6 2.0 %collective-permute-start = (bf16[896,256]{1,0:T(8,128)(2,1)S(1)}, bf16[896,256]{1,0:T(8,128)(2,1)S(1)}, u32[]{:S(2)}, u32[]{:S(2)}) collective-permute-start(bf16[896,256]{1,0:T(8,128)(2,1)S(1)} %get-tuple-element.31), channel_id=1, source_target_pairs={{0,1},{1,0},{2,3},{3,2},{4,5},{5,4},{6,7},{7,6},{8,9},{9,8},{10,11... | collective-permute-start | bytes 1376264 | tf_op jit(solution)/shard_map/ppermute | solution.py:292
  5.7 16.5 %collective-permute-start.1 = (bf16[512,256]{1,0:T(8,128)(2,1)S(1)}, bf16[512,256]{1,0:T(8,128)(2,1)S(1)}, u32[]{:S(2)}, u32[]{:S(2)}) collective-permute-start(bf16[512,256]{1,0:T(8,128)(2,1)S(1)} %get-tuple-element.39), channel_id=1, source_target_pairs={{0,2},{2,0},{1,3},{3,1},{4,6},{6,4},{5,7},{7,5},{8,10},{10,8},{9,1... | collective-permute-start | bytes 786440 | tf_op jit(solution)/shard_map/ppermute | solution.py:292
  22.2 1.5 %copy-start.5 = (bf16[256,256]{1,0:T(8,128)(2,1)S(1)}, bf16[256,256]{1,0:T(8,128)(2,1)}, u32[]{:S(2)}) copy-start(bf16[256,256]{1,0:T(8,128)(2,1)} %neigh_one_ref.1) | copy-start | bytes 393220
  22.2 1.5 %collective-permute-start.2 = (bf16[384,256]{1,0:T(8,128)(2,1)S(1)}, bf16[384,256]{1,0:T(8,128)(2,1)S(1)}, u32[]{:S(2)}, u32[]{:S(2)}) collective-permute-start(bf16[384,256]{1,0:T(8,128)(2,1)S(1)} %merge.2.here_ref), channel_id=1, source_target_pairs={{0,1},{1,0},{2,3},{3,2},{4,5},{5,4},{6,7},{7,6},{8,9},{9,8},{10,11... | collective-permute-start | bytes 589832 | tf_op jit(solution)/shard_map/ppermute | solution.py:292
  23.7 15.1 %copy-start.7 = (f32[256]{0:T(256)S(1)}, f32[256]{0:T(256)}, u32[]{:S(2)}) copy-start(f32[256]{0:T(256)} %bias_ref.3) | copy-start | bytes 3076
  24.7 1.9 %collective-permute-start.3 = (bf16[896,256]{1,0:T(8,128)(2,1)S(1)}, bf16[896,256]{1,0:T(8,128)(2,1)S(1)}, u32[]{:S(2)}, u32[]{:S(2)}) collective-permute-start(bf16[896,256]{1,0:T(8,128)(2,1)S(1)} %get-tuple-element.44), channel_id=1, source_target_pairs={{0,1},{1,0},{2,3},{3,2},{4,5},{5,4},{6,7},{7,6},{8,9},{9,8},{10,11... | collective-permute-start | bytes 1376264 | tf_op jit(solution)/shard_map/ppermute | solution.py:292
  26.7 11.9 %collective-permute-start.4 = (bf16[512,256]{1,0:T(8,128)(2,1)S(1)}, bf16[512,256]{1,0:T(8,128)(2,1)S(1)}, u32[]{:S(2)}, u32[]{:S(2)}) collective-permute-start(bf16[512,256]{1,0:T(8,128)(2,1)S(1)} %get-tuple-element.52), channel_id=1, source_target_pairs={{0,2},{2,0},{1,3},{3,1},{4,6},{6,4},{5,7},{7,5},{8,10},{10,8},{9,1... | collective-permute-start | bytes 786440 | tf_op jit(solution)/shard_map/ppermute | solution.py:292
  38.7 1.5 %copy-start.1 = (bf16[256,256]{1,0:T(8,128)(2,1)S(1)}, bf16[256,256]{1,0:T(8,128)(2,1)}, u32[]{:S(2)}) copy-start(bf16[256,256]{1,0:T(8,128)(2,1)} %neigh_two_ref.1) | copy-start | bytes 393220
  38.7 1.5 %collective-permute-start.5 = (bf16[384,256]{1,0:T(8,128)(2,1)S(1)}, bf16[384,256]{1,0:T(8,128)(2,1)S(1)}, u32[]{:S(2)}, u32[]{:S(2)}) collective-permute-start(bf16[384,256]{1,0:T(8,128)(2,1)S(1)} %merge.3.here_ref), channel_id=1, source_target_pairs={{0,1},{1,0},{2,3},{3,2},{4,5},{5,4},{6,7},{7,6},{8,9},{9,8},{10,11... | collective-permute-start | bytes 589832 | tf_op jit(solution)/shard_map/ppermute | solution.py:292

commit v6 on v5

--- a/solution.py
+++ b/solution.py
@@ -11,6 +11,7 @@
 BF16 = jnp.bfloat16
 MIB = 1024 * 1024
 CHUNKS = 8
+PARTS = 4
 CORES = 2
 
 VMEM = pl.BlockSpec(memory_space=pltpu.VMEM)
@@ -82,9 +83,9 @@
     features_ref,
     cot_ref,
     neigh_two_ref,
-    acc,
     whole,
     sems,
+    *accs,
 ):
     tiles, blk = tile_buf.shape[0], tile_buf.shape[1]
     each = tiles // CHUNKS
@@ -106,9 +107,11 @@
         copy.start()
     rows = features_ref.shape[0]
     bpd = rows // blk
-    sources = acc.shape[0] // bpd
+    sources = accs[0].shape[0] // bpd
     far = send_ref.shape[2] * send_ref.shape[3]
-    acc[...] = jnp.zeros_like(acc)
+    part = accs[0].shape[1]
+    for acc in accs:
+        acc[...] = jnp.zeros_like(acc)
     copies[0].wait()
     copies[1].wait()
     u = dot_nt(cot_ref[...], neigh_two_ref[...]).astype(BF16)
@@ -118,20 +121,21 @@
     picked_ref[...] = dot(pick_ref[...], features_ref[...]).astype(BF16)
     for copy in copies[4:7]:
         copy.wait()
-    place = lax.broadcasted_iota(jnp.int32, (blk, blk), 0)
+    place = lax.broadcasted_iota(jnp.int32, (part, blk), 0)
     for c in range(CHUNKS):
         copies[7 + c].wait()
 
         def add(t, carry):
             slot = dst_ref[t] * sources + src_ref[t]
-            live = jnp.where(place < rows_ref[t], tile_buf[t].astype(F32), 0.0)
-            acc[slot] = acc[slot] + live
+            for i, acc in enumerate(accs):
+                value = tile_buf[t, i * part : (i + 1) * part, :].astype(F32)
+                acc[slot] += jnp.where(place < rows_ref[t] - i * part, value, 0.0)
             return carry
 
         lax.fori_loop(c * each, (c + 1) * each, add, 0, unroll=True)
     for b in range(bpd):
         for j in range(sources):
-            block = acc[b * sources + j].astype(BF16)
+            block = jnp.concatenate([acc[b * sources + j] for acc in accs], 0).astype(BF16)
             adj_ref[b * blk : (b + 1) * blk, j * blk : (j + 1) * blk] = block
             adj_t_ref[j * blk : (j + 1) * blk, b * blk : (b + 1) * blk] = block.T
     spread_parts(
@@ -140,10 +144,10 @@
 
 
 def core_sum_kernel(
-    chips, hosts, keep_ref, came_ref, value_ref, picked_ref, mine_ref, msg_ref, *rest
+    chips, hosts, keep_ref, came_ref, picked_ref, mine_ref, msg_ref, *rest
 ):
     to_refs, total = rest[:-1], rest[-1]
-    rows = value_ref.shape[0]
+    rows = mine_ref.shape[0]
     far = picked_ref.shape[0]
     send = far // hosts
     each = rows + far
@@ -152,8 +156,7 @@
     mine_ref[...] = total[pl.ds(pl.multiple_of(chip * each, 8), rows), :]
     for k, ref in enumerate(to_refs):
         other = lax.rem(chip + k + 1, chips)
-        ref[:rows, :] = total[pl.ds(pl.multiple_of(other * each, 8), rows), :].astype(BF16)
-        ref[rows:, :] = value_ref[...]
+        ref[...] = total[pl.ds(pl.multiple_of(other * each, 8), rows), :].astype(BF16)
     picked = picked_ref[...].astype(F32)
     for g in range(hosts):
         for x in range(chips):
@@ -175,16 +178,20 @@
     return jnp.concatenate(blocks, 0).astype(BF16)
 
 
-def merge_kernel(chips, hosts, recv_ref, *refs):
-    came, out_ref = refs[:-1], refs[-1]
-    rows = came[0].shape[0] // 2
+def merge_kernel(chips, hosts, recv_ref, mine_ref, *refs):
+    terms, came, (out_ref, sum_ref) = refs[: chips - 1], refs[chips - 1 : -2], refs[-2:]
+    rows = came[0].shape[0]
+    total = mine_ref[...]
+    for ref in terms:
+        total = total + ref[...].astype(F32)
+    sum_ref[...] = total
     for k, ref in enumerate(came):
-        out_ref[k * rows : (k + 1) * rows, :] = ref[rows:, :]
+        out_ref[k * rows : (k + 1) * rows, :] = ref[...]
     out_ref[len(came) * rows :, :] = halo_part(recv_ref, hosts, chips, 0)
 
 
 def early_kernel(
-    chips, adj_ref, value_ref, came_ref, self_ref, bias_ref, up_ref, weight_ref, mine_ref,
+    chips, adj_ref, value_ref, came_ref, self_ref, bias_ref, up_ref, weight_ref,
     agg_ref, direct_ref, grad_ref,
 ):
     value = value_ref[...]
@@ -197,19 +204,18 @@
         total = total + dot(adj_ref[:, pl.ds(low, rows)], block)
     agg_ref[...] = total
     direct_ref[...] = dot(value, self_ref[...]) + bias_ref[...].reshape(1, -1)
-    grad_ref[...] = dot_nt(up_ref[...], weight_ref[...]) + mine_ref[...]
-
-
-def mid_kernel(chips, hosts, adj_ref, agg_ref, part_ref, pick_ref, recv_ref, *refs):
-    came, (agg_out, grad_ref) = refs[: chips - 1], refs[chips - 1 :]
+    grad_ref[...] = dot_nt(up_ref[...], weight_ref[...])
+
+
+def mid_kernel(chips, hosts, adj_ref, agg_ref, part_ref, sum_ref, pick_ref, recv_ref, *refs):
+    came, (agg_out, grad_ref) = refs[:-2], refs[-2:]
     rows = part_ref.shape[0]
     chip, core = lax.axis_index("chip"), lax.axis_index("core")
-    agg, grad = agg_ref[...], part_ref[...]
+    agg, grad = agg_ref[...], part_ref[...] + sum_ref[...]
     for k, ref in enumerate(came):
-        grad = grad + ref[:rows, :].astype(F32)
         x = lax.rem(chip - k - 1 + chips, chips)
         low = pl.multiple_of((x * CORES + core) * rows, rows)
-        agg = agg + dot(adj_ref[:, pl.ds(low, rows)], ref[rows:, :])
+        agg = agg + dot(adj_ref[:, pl.ds(low, rows)], ref[...])
     back = halo_part(recv_ref, hosts, chips, 1)
     grad_ref[...] = grad + dot_tn(jnp.concatenate([pick_ref[...]] * chips, 0), back)
     agg_out[...] = agg
@@ -330,13 +336,14 @@
 
     def exchange(adj, pick, keep, give, picked, value, self_weight, bias, up, weight):
         came = shift(give, "core", 1)
+        moved = [shift(value, "chip", k) for k in range(1, chips)]
         mine, msg, *to = call(
             functools.partial(core_sum_kernel, chips, hosts),
             "core_sum",
             (sum_shape, jax.ShapeDtypeStruct((hosts * chips, 2 * send, width), BF16))
-            + (shape(2 * rows, width),) * (chips - 1),
-            [VMEM] * 4,
-            (keep, came, value, picked),
+            + (rows_shape,) * (chips - 1),
+            [VMEM] * 3,
+            (keep, came, picked),
             [pltpu.VMEM(keep_shape.shape, F32)],
         )
         terms = [shift(block, "chip", k + 1) for k, block in enumerate(to)]
@@ -345,24 +352,24 @@
             functools.partial(early_kernel, chips),
             "early",
             (sum_shape,) * 3,
-            [VMEM] * 8,
-            (adj, value, came, self_weight, bias, up, weight, mine),
+            [VMEM] * 7,
+            (adj, value, came, self_weight, bias, up, weight),
             flops=4 * square,
         )
-        here = call(
+        here, total = call(
             functools.partial(merge_kernel, chips, hosts),
             "merge",
-            shape((chips - 1) * rows + chips * far, width),
-            [VMEM] * chips,
-            (recv, *terms),
+            (shape((chips - 1) * rows + chips * far, width), sum_shape),
+            [VMEM] * (2 * chips),
+            (recv, mine, *terms, *moved),
         )
         shared = shift(here, "core", 1)
         agg, grad = call(
             functools.partial(mid_kernel, chips, hosts),
             "mid",
             (sum_shape,) * 2,
-            [VMEM] * (4 + chips),
-            (adj, agg, grad, pick, recv, *terms),
+            [VMEM] * (5 + chips),
+            (adj, agg, grad, total, pick, recv, *moved),
             flops=2 * square,
         )
         return agg, direct, grad, here, shared
@@ -395,10 +402,10 @@
             pltpu.VMEM(features.shape, BF16),
             pltpu.VMEM(cotangent.shape, BF16),
             pltpu.VMEM(neigh_two.shape, BF16),
-            pltpu.VMEM(((rows // blk) * (all_rows // blk), blk, blk), F32),
             space,
             pltpu.SemaphoreType.DMA((7 + CHUNKS,)),
-        ],
+        ]
+        + [pltpu.VMEM(((rows // blk) * (all_rows // blk), blk // PARTS, blk), F32)] * PARTS,
     )
     agg, direct, grad, here, shared = exchange(
         adj, pick, keep, give, picked, features, self_one, bias_one, cotangent, self_two

time: 41.5 us -> 48.2 us (1.16)
  blocking collectives: 24.3 us -> 0 us
  waiting for transfers between devices: 4.07 us -> 19.1 us
  starting transfers between devices: 4.97 us -> 19.6 us
  Pallas kernels: 7.09 us -> 8.27 us
    all_to_all x2 -> x0, blocking collectives: 24.3 us -> none  [exchange(): lax.all_to_all(msg, ('hst', 'chip'), split_axis=0, concat_axis=0, tiled=T...]
    ppermute x6 -> x8, waiting for transfers between devices: 4.07 us -> 19.1 us  [shift(): return lax.ppermute(value, axis, [(i, (i + k) % size) for i in range(size)])]
    all_to_all x0 -> x2, starting transfers between devices: none -> 14.6 us  [exchange(): lax.all_to_all(msg, ('hst', 'chip'), split_axis=0, concat_axis=0, tiled=T...]
    pallas_call x11, Pallas kernels: 7.09 us -> 8.27 us  [call(): pl.pallas_call(kernel, out_shape=out_shape, in_specs=in_specs, out_specs=...]
    ppermute x6 -> x8, starting transfers between devices: 4.97 us -> 5.08 us  [shift(): return lax.ppermute(value, axis, [(i, (i + k) % size) for i in range(size)])]
  transfers between devices with their start and end apart: 6 -> 10, of which waited for: 4 -> 8; matrix products, arithmetic and copies ran while one was open for 0% -> 0% of each run, Pallas kernels for 4% -> 4%
where the time goes in v6:
time: 48.2 us; the launch traced here: 47.8 us
  starting transfers between devices  19.6 us (41%)
  waiting for transfers between devices  19.1 us (40%)
  Pallas kernels  8.27 us (17%)
  between operations  0.8 us (2%)
    ppermute x8, waiting for transfers between devices, shift(): return lax.ppermute(value, axis, [(i, (i + k) % size) for i in range(size)])  19.1 us
    all_to_all x2, starting transfers between devices, exchange(): lax.all_to_all(msg, ('hst', 'chip'), split_axis=0, concat_axis=0, tiled=T...  14.6 us
    pallas_call x11, Pallas kernels, call(): pl.pallas_call(kernel, out_shape=out_shape, in_specs=in_specs, out_specs=...  8.27 us
    ppermute x8, starting transfers between devices, shift(): return lax.ppermute(value, axis, [(i, (i + k) % size) for i in range(size)])  5.08 us
  transfers between devices with their start and end apart: 10, of which 8 were waited for; matrix products, arithmetic and copies ran while one was open for 0% of the time, Pallas kernels for 4%

profile of v6, /device:TPU:0, one launch (start us, length us, event | category | flops | bytes accessed | tf_op | source)
XLA Modules:
  0.0 47.8 jit_solution(12652515684329715512)
XLA Ops:
  0.6 0.0 copy-start.1
  0.6 0.0 copy-start.2
  0.7 0.0 copy-start.4
  0.7 2.8 %prep.1 = (bf16[256,1280]{1,0:T(8,128)(2,1)S(1)}, bf16[1280,256]{1,0:T(8,128)(2,1)S(1)}, bf16[640,256]{1,0:T(8,128)(2,1)S(1)}, bf16[896,256]{1,0:T(8,128)(2,1)S(...) custom-call(s32[64]{0:T(128)} %dst_hbm.1, s32[64]{0:T(128)} %src_hbm.1, s32[64]{0:T(128)} %rows_hbm.1, ...), custom_call_target="tpu_custom_call" | custom-call | tf_op jit(solution)/shard_map/prep/pallas_call | solution.py:282
  3.5 0.5 %collective-permute-start = (bf16[896,256]{1,0:T(8,128)(2,1)S(1)}, bf16[896,256]{1,0:T(8,128)(2,1)S(1)}, u32[]{:S(2)}, u32[]{:S(2)}) collective-permute-start(bf16[896,256]{1,0:T(8,128)(2,1)S(1)} %get-tuple-element.35), channel_id=1, source_target_pairs={{0,1},{1,0},{2,3},{3,2},{4,5},{5,4},{6,7},{7,6},{8,9},{9,8},{10,11... | collective-permute-start | bytes 1376264 | tf_op jit(solution)/shard_map/ppermute | solution.py:298
  4.0 1.4 %collective-permute-done.came_ref = bf16[896,256]{1,0:T(8,128)(2,1)S(1)} collective-permute-done((bf16[896,256]{1,0:T(8,128)(2,1)S(1)}, bf16[896,256]{1,0:T(8,128)(2,1)S(1)}, u32[]{:S(2)}, u32[]{:S(2)}) %collective-permute-start) | collective-permute-done | bytes 458784 | tf_op jit(solution)/shard_map/ppermute | solution.py:298
  5.5 0.8 %core_sum.2 = (f32[256,256]{1,0:T(8,128)S(1)}, bf16[16,16,256]{2,1,0:T(8,128)(2,1)}, bf16[256,256]{1,0:T(8,128)(2,1)S(1)}) custom-call(bf16[640,256]{1,0:T(8,128)(2,1)S(1)} %get-tuple-element.38.keep_ref, bf16[896,256]{1,0:T(8,128)(2,1)S(1)} %collective-permute-done.came_ref, bf16[64,256]{1,0:T(8,128)(2,1)S(1)} %get-tuple-element.39.picked_ref), custom_call_target="tpu_custom_call" | custom-call | tf_op jit(solution)/shard_map/core_sum/pallas_call | solution.py:282
  6.2 8.4 %all-to-all-start = ((bf16[16,16,256]{2,1,0:T(8,128)(2,1)}), bf16[16,16,256]{2,1,0:T(8,128)(2,1)S(1)}, u32[]{:S(2)}, u32[]{:S(2)}) async-start(bf16[16,16,256]{2,1,0:T(8,128)(2,1)} %get-tuple-element.40), calls=%async_computation | async-start | bytes 262144 | tf_op jit(solution)/shard_map/all_to_all | solution.py:350
  14.6 2.0 %collective-permute-start.2 = (bf16[256,256]{1,0:T(8,128)(2,1)S(1)}, bf16[256,256]{1,0:T(8,128)(2,1)S(1)}, u32[]{:S(2)}, u32[]{:S(2)}) collective-permute-start(bf16[256,256]{1,0:T(8,128)(2,1)S(1)} %copy-done.1), channel_id=1, source_target_pairs={{0,2},{2,0},{1,3},{3,1},{4,6},{6,4},{5,7},{7,5},{8,10},{10,8},{9,1... | collective-permute-start | bytes 393224 | tf_op jit(solution)/shard_map/ppermute | solution.py:298
  16.6 0.1 collective-permute-start.1
  16.7 5.8 %collective-permute-done.2.refs_1_.refs_0_ = bf16[256,256]{1,0:T(8,128)(2,1)S(1)} collective-permute-done((bf16[256,256]{1,0:T(8,128)(2,1)S(1)}, bf16[256,256]{1,0:T(8,128)(2,1)S(1)}, u32[]{:S(2)}, u32[]{:S(2)}) %collective-permute-start.2) | collective-permute-done | bytes 131104 | tf_op jit(solution)/shard_map/ppermute | solution.py:298
  22.5 1.7 %collective-permute-done.1.refs_0_ = bf16[256,256]{1,0:T(8,128)(2,1)S(1)} collective-permute-done((bf16[256,256]{1,0:T(8,128)(2,1)S(1)}, bf16[256,256]{1,0:T(8,128)(2,1)S(1)}, u32[]{:S(2)}, u32[]{:S(2)}) %collective-permute-start.1) | collective-permute-done | bytes 131104 | tf_op jit(solution)/shard_map/ppermute | solution.py:298
  24.2 0.0 all-to-all-done.recv_ref
  24.2 0.1 collective-permute-start.3
  24.4 0.3 early.2
  24.7 0.2 mid.2
  24.9 0.8 %collective-permute-done.3.shared_ref = bf16[384,256]{1,0:T(8,128)(2,1)S(1)} collective-permute-done((bf16[384,256]{1,0:T(8,128)(2,1)S(1)}, bf16[384,256]{1,0:T(8,128)(2,1)S(1)}, u32[]{:S(2)}, u32[]{:S(2)}) %collective-permute-start.3) | collective-permute-done | bytes 196640 | tf_op jit(solution)/shard_map/ppermute | solution.py:298
  25.8 1.0 %middle.1 = (bf16[256,256]{1,0:T(8,128)(2,1)S(1)}, bf16[256,256]{1,0:T(8,128)(2,1)S(1)}, bf16[640,256]{1,0:T(8,128)(2,1)S(1)}, bf16[896,256]{1,0:T(8,128)(2,1)S(1)}, bf16[64,256]{1,0:T(8,128)(2,1)S(1)}) custom-call(bf16[256,1280]{1,0:T(8,128)(2,1)S(1)} %get-tuple-element.33.adj_ref, bf16[1280,256]{1,0:T(8,128)(2,1)S(1)} %get-tuple-element.34.adj_t_ref, ...), custom_call_target="tpu_custom_call" | custom-call | flops 301989888 | bytes 294912 | tf_op jit(solution)/shard_map/middle/pallas_call | solution.py:282
  26.7 0.2 collective-permute-start.4
  27.0 1.6 %collective-permute-done.4.came_ref = bf16[896,256]{1,0:T(8,128)(2,1)S(1)} collective-permute-done((bf16[896,256]{1,0:T(8,128)(2,1)S(1)}, bf16[896,256]{1,0:T(8,128)(2,1)S(1)}, u32[]{:S(2)}, u32[]{:S(2)}) %collective-permute-start.4) | collective-permute-done | bytes 458784 | tf_op jit(solution)/shard_map/ppermute | solution.py:298
  28.6 0.8 %core_sum.3 = (f32[256,256]{1,0:T(8,128)S(1)}, bf16[16,16,256]{2,1,0:T(8,128)(2,1)}, bf16[256,256]{1,0:T(8,128)(2,1)S(1)}) custom-call(bf16[640,256]{1,0:T(8,128)(2,1)S(1)} %get-tuple-element.54.keep_ref, bf16[896,256]{1,0:T(8,128)(2,1)S(1)} %collective-permute-done.4.came_ref, bf16[64,256]{1,0:T(8,128)(2,1)S(1)} %get-tuple-element.55.picked_ref), custom_call_target="tpu_custom_call" | custom-call | tf_op jit(solution)/shard_map/core_sum/pallas_call | solution.py:282
  29.4 6.2 %all-to-all-start.1 = ((bf16[16,16,256]{2,1,0:T(8,128)(2,1)}), bf16[16,16,256]{2,1,0:T(8,128)(2,1)S(1)}, u32[]{:S(2)}, u32[]{:S(2)}) async-start(bf16[16,16,256]{2,1,0:T(8,128)(2,1)} %get-tuple-element.56), calls=%async_computation.1 | async-start | bytes 262144 | tf_op jit(solution)/shard_map/all_to_all | solution.py:350
  35.6 1.9 %collective-permute-start.6 = (bf16[256,256]{1,0:T(8,128)(2,1)S(1)}, bf16[256,256]{1,0:T(8,128)(2,1)S(1)}, u32[]{:S(2)}, u32[]{:S(2)}) collective-permute-start(bf16[256,256]{1,0:T(8,128)(2,1)S(1)} %get-tuple-element.49.value_ref), channel_id=1, source_target_pairs={{0,2},{2,0},{1,3},{3,1},{4,6},{6,4},{5,7},{7,5},{8,10},{10,8},{9,1... | collective-permute-start | bytes 393224 | tf_op jit(solution)/shard_map/ppermute | solution.py:298
  37.5 0.2 collective-permute-start.5
  37.7 5.8 %collective-permute-done.6.refs_1_.refs_0_ = bf16[256,256]{1,0:T(8,128)(2,1)S(1)} collective-permute-done((bf16[256,256]{1,0:T(8,128)(2,1)S(1)}, bf16[256,256]{1,0:T(8,128)(2,1)S(1)}, u32[]{:S(2)}, u32[]{:S(2)}) %collective-permute-start.6) | collective-permute-done | bytes 131104 | tf_op jit(solution)/shard_map/ppermute | solution.py:298
  43.5 1.7 %collective-permute-done.5.refs_0_ = bf16[256,256]{1,0:T(8,128)(2,1)S(1)} collective-permute-done((bf16[256,256]{1,0:T(8,128)(2,1)S(1)}, bf16[256,256]{1,0:T(8,128)(2,1)S(1)}, u32[]{:S(2)}, u32[]{:S(2)}) %collective-permute-start.5) | collective-permute-done | bytes 131104 | tf_op jit(solution)/shard_map/ppermute | solution.py:298
  45.2 0.0 all-to-all-done.1.recv_ref
  45.3 0.1 collective-permute-start.7
  45.3 0.3 early.3
  45.7 1.0 %mid.3 = (f32[256,256]{1,0:T(8,128)S(1)}, f32[256,256]{1,0:T(8,128)}) custom-call(bf16[256,1280]{1,0:T(8,128)(2,1)S(1)} %get-tuple-element.33.adj_ref, f32[256,256]{1,0:T(8,128)S(1)} %get-tuple-element.52.agg_ref, f32[256,256]{1,0:T(8,128)S(1)} %get-tuple-element.53.part_ref, f32[256,256]{1,0:T(8,128)S(1)} %get-tuple-element.59.sum_ref, ...), custom_call_target="tpu_custom_call" | custom-call | flops 67108864 | bytes 65536 | tf_op jit(solution)/shard_map/mid/pallas_call | solution.py:282
  46.6 0.1 collective-permute-done.7.shared_ref
  46.8 1.0 %last.1 = bf16[256,256]{1,0:T(8,128)(2,1)} custom-call(bf16[256,1280]{1,0:T(8,128)(2,1)S(1)} %get-tuple-element.33.adj_ref, f32[256,256]{1,0:T(8,128)S(1)} %get-tuple-element.60.agg_ref, f32[256,256]{1,0:T(8,128)S(1)} %get-tuple-element.61.direct_ref, bf16[384,256]{1,0:T(8,128)(2,1)S(1)} %get-tuple-element.62.here_ref, ...), custom_call_target="tpu_custom_call" | custom-call | flops 100663296 | bytes 98304 | tf_op jit(solution)/shard_map/last/pallas_call | solution.py:282
  (15 shorter events, 0.1 us)
Async XLA Ops:
  0.6 14.0 %copy-start.1 = (bf16[256,256]{1,0:T(8,128)(2,1)S(1)}, bf16[256,256]{1,0:T(8,128)(2,1)}, u32[]{:S(2)}) copy-start(bf16[256,256]{1,0:T(8,128)(2,1)} %value_ref.1) | copy-start | bytes 393220
  0.6 23.7 %copy-start.2 = (bf16[256,256]{1,0:T(8,128)(2,1)S(1)}, bf16[256,256]{1,0:T(8,128)(2,1)}, u32[]{:S(2)}) copy-start(bf16[256,256]{1,0:T(8,128)(2,1)} %up_ref.1) | copy-start | bytes 393220
  0.7 23.7 %copy-start.4 = (bf16[256,256]{1,0:T(8,128)(2,1)S(1)}, bf16[256,256]{1,0:T(8,128)(2,1)}, u32[]{:S(2)}) copy-start(bf16[256,256]{1,0:T(8,128)(2,1)} %self_ref.3) | copy-start | bytes 393220
  0.7 23.7 %copy-start.3 = (bf16[256,256]{1,0:T(8,128)(2,1)S(1)}, bf16[256,256]{1,0:T(8,128)(2,1)}, u32[]{:S(2)}) copy-start(bf16[256,256]{1,0:T(8,128)(2,1)} %weight_ref.3) | copy-start | bytes 393220
  0.7 23.7 %copy-start.6 = (f32[256]{0:T(256)S(1)}, f32[256]{0:T(256)}, u32[]{:S(2)}) copy-start(f32[256]{0:T(256)} %bias_ref.2) | copy-start | bytes 3076
  3.5 2.0 %collective-permute-start = (bf16[896,256]{1,0:T(8,128)(2,1)S(1)}, bf16[896,256]{1,0:T(8,128)(2,1)S(1)}, u32[]{:S(2)}, u32[]{:S(2)}) collective-permute-start(bf16[896,256]{1,0:T(8,128)(2,1)S(1)} %get-tuple-element.35), channel_id=1, source_target_pairs={{0,1},{1,0},{2,3},{3,2},{4,5},{5,4},{6,7},{7,6},{8,9},{9,8},{10,11... | collective-permute-start | bytes 1376264 | tf_op jit(solution)/shard_map/ppermute | solution.py:298
  6.2 19.5 %copy-start.5 = (bf16[256,256]{1,0:T(8,128)(2,1)S(1)}, bf16[256,256]{1,0:T(8,128)(2,1)}, u32[]{:S(2)}) copy-start(bf16[256,256]{1,0:T(8,128)(2,1)} %neigh_one_ref.1) | copy-start | bytes 393220
  6.2 17.9 %all-to-all-start = ((bf16[16,16,256]{2,1,0:T(8,128)(2,1)}), bf16[16,16,256]{2,1,0:T(8,128)(2,1)S(1)}, u32[]{:S(2)}, u32[]{:S(2)}) async-start(bf16[16,16,256]{2,1,0:T(8,128)(2,1)} %get-tuple-element.40), calls=%async_computation | async-start | bytes 262144 | tf_op jit(solution)/shard_map/all_to_all | solution.py:350
  14.6 7.9 %collective-permute-start.2 = (bf16[256,256]{1,0:T(8,128)(2,1)S(1)}, bf16[256,256]{1,0:T(8,128)(2,1)S(1)}, u32[]{:S(2)}, u32[]{:S(2)}) collective-permute-start(bf16[256,256]{1,0:T(8,128)(2,1)S(1)} %copy-done.1), channel_id=1, source_target_pairs={{0,2},{2,0},{1,3},{3,1},{4,6},{6,4},{5,7},{7,5},{8,10},{10,8},{9,1... | collective-permute-start | bytes 393224 | tf_op jit(solution)/shard_map/ppermute | solution.py:298
  16.6 7.6 %collective-permute-start.1 = (bf16[256,256]{1,0:T(8,128)(2,1)S(1)}, bf16[256,256]{1,0:T(8,128)(2,1)S(1)}, u32[]{:S(2)}, u32[]{:S(2)}) collective-permute-start(bf16[256,256]{1,0:T(8,128)(2,1)S(1)} %get-tuple-element.42), channel_id=1, source_target_pairs={{0,2},{2,0},{1,3},{3,1},{4,6},{6,4},{5,7},{7,5},{8,10},{10,8},{9,1... | collective-permute-start | bytes 393224 | tf_op jit(solution)/shard_map/ppermute | solution.py:298
  24.2 1.5 %collective-permute-start.3 = (bf16[384,256]{1,0:T(8,128)(2,1)S(1)}, bf16[384,256]{1,0:T(8,128)(2,1)S(1)}, u32[]{:S(2)}, u32[]{:S(2)}) collective-permute-start(bf16[384,256]{1,0:T(8,128)(2,1)S(1)} %get-tuple-element.48.here_ref), channel_id=1, source_target_pairs={{0,1},{1,0},{2,3},{3,2},{4,5},{5,4},{6,7},{7,6},{8,9},{9,8},{10,11... | collective-permute-start | bytes 589832 | tf_op jit(solution)/shard_map/ppermute | solution.py:298
  25.7 19.6 %copy-start.7 = (f32[256]{0:T(256)S(1)}, f32[256]{0:T(256)}, u32[]{:S(2)}) copy-start(f32[256]{0:T(256)} %bias_ref.3) | copy-start | bytes 3076
  26.7 1.9 %collective-permute-start.4 = (bf16[896,256]{1,0:T(8,128)(2,1)S(1)}, bf16[896,256]{1,0:T(8,128)(2,1)S(1)}, u32[]{:S(2)}, u32[]{:S(2)}) collective-permute-start(bf16[896,256]{1,0:T(8,128)(2,1)S(1)} %get-tuple-element.50), channel_id=1, source_target_pairs={{0,1},{1,0},{2,3},{3,2},{4,5},{5,4},{6,7},{7,6},{8,9},{9,8},{10,11... | collective-permute-start | bytes 1376264 | tf_op jit(solution)/shard_map/ppermute | solution.py:298
  29.4 17.4 %copy-start = (bf16[256,256]{1,0:T(8,128)(2,1)S(1)}, bf16[256,256]{1,0:T(8,128)(2,1)}, u32[]{:S(2)}) copy-start(bf16[256,256]{1,0:T(8,128)(2,1)} %neigh_two_ref.1) | copy-start | bytes 393220
  29.4 15.8 %all-to-all-start.1 = ((bf16[16,16,256]{2,1,0:T(8,128)(2,1)}), bf16[16,16,256]{2,1,0:T(8,128)(2,1)S(1)}, u32[]{:S(2)}, u32[]{:S(2)}) async-start(bf16[16,16,256]{2,1,0:T(8,128)(2,1)} %get-tuple-element.56), calls=%async_computation.1 | async-start | bytes 262144 | tf_op jit(solution)/shard_map/all_to_all | solution.py:350
  35.6 7.9 %collective-permute-start.6 = (bf16[256,256]{1,0:T(8,128)(2,1)S(1)}, bf16[256,256]{1,0:T(8,128)(2,1)S(1)}, u32[]{:S(2)}, u32[]{:S(2)}) collective-permute-start(bf16[256,256]{1,0:T(8,128)(2,1)S(1)} %get-tuple-element.49.value_ref), channel_id=1, source_target_pairs={{0,2},{2,0},{1,3},{3,1},{4,6},{6,4},{5,7},{7,5},{8,10},{10,8},{9,1... | collective-permute-start | bytes 393224 | tf_op jit(solution)/shard_map/ppermute | solution.py:298
  37.5 7.7 %collective-permute-start.5 = (bf16[256,256]{1,0:T(8,128)(2,1)S(1)}, bf16[256,256]{1,0:T(8,128)(2,1)S(1)}, u32[]{:S(2)}, u32[]{:S(2)}) collective-permute-start(bf16[256,256]{1,0:T(8,128)(2,1)S(1)} %get-tuple-element.58), channel_id=1, source_target_pairs={{0,2},{2,0},{1,3},{3,1},{4,6},{6,4},{5,7},{7,5},{8,10},{10,8},{9,1... | collective-permute-start | bytes 393224 | tf_op jit(solution)/shard_map/ppermute | solution.py:298
  45.3 1.5 %collective-permute-start.7 = (bf16[384,256]{1,0:T(8,128)(2,1)S(1)}, bf16[384,256]{1,0:T(8,128)(2,1)S(1)}, u32[]{:S(2)}, u32[]{:S(2)}) collective-permute-start(bf16[384,256]{1,0:T(8,128)(2,1)S(1)} %get-tuple-element.62.here_ref), channel_id=1, source_target_pairs={{0,1},{1,0},{2,3},{3,2},{4,5},{5,4},{6,7},{7,6},{8,9},{9,8},{10,11... | collective-permute-start | bytes 589832 | tf_op jit(solution)/shard_map/ppermute | solution.py:298

commit v7 on v6

v7 whole, which is shorter than its diff:
```python
import functools

import jax
import jax.numpy as jnp
from jax import lax
from jax.experimental import pallas as pl
from jax.experimental.pallas import tpu as pltpu
from jax.sharding import Mesh, PartitionSpec as P

F32 = jnp.float32
BF16 = jnp.bfloat16
MIB = 1024 * 1024
CHUNKS = 8
PARTS = 4
CORES = 2

VMEM = pl.BlockSpec(memory_space=pltpu.VMEM)
HBM = pl.BlockSpec(memory_space=pltpu.HBM)


def dot(a, b):
    return jnp.dot(a, b, preferred_element_type=F32)


def dot_nt(a, b):
    return lax.dot_general(a, b, (((1,), (1,)), ((), ())), preferred_element_type=F32)


def dot_tn(a, b):
    return lax.dot_general(a, b, (((0,), (0,)), ((), ())), preferred_element_type=F32)


def pick_matrix(send_ref, rows):
    hosts, send = send_ref.shape[2], send_ref.shape[3]
    place = lax.broadcasted_iota(jnp.int32, (send, rows), 0)
    column = lax.broadcasted_iota(jnp.int32, (send, rows), 1)
    parts = []
    for g in range(hosts):
        index = jnp.zeros((send, rows), jnp.int32)
        for s in range(send):
            index = jnp.where(place == s, send_ref[0, 0, g, s], index)
        parts.append(jnp.where(index == column, 1.0, 0.0).astype(F32))
    return jnp.concatenate(parts, 0).astype(BF16)


def column(chips, far, rows, side, whole_ref, out_ref):
    each = rows + far
    for x in range(chips):
        d = x * CORES + side
        low = pl.multiple_of(d * rows, rows)
        out_ref[x * each : x * each + rows, :] = whole_ref[pl.ds(low, rows), :]
        low = pl.multiple_of(chips * CORES * rows + d * far, far)
        out_ref[x * each + rows : (x + 1) * each, :] = whole_ref[pl.ds(low, far), :]


def prep_kernel(
    chips,
    dst_hbm,
    src_hbm,
    rows_hbm,
    send_hbm,
    tile_hbm,
    features_hbm,
    cot_hbm,
    neigh_two_hbm,
    adj_t_ref,
    give_ref,
    up_ref,
    picked_ref,
    pick_ref,
    dst_ref,
    src_ref,
    rows_ref,
    send_ref,
    tile_buf,
    features_ref,
    cot_ref,
    neigh_two_ref,
    col,
    sems,
    *accs,
):
    tiles, blk = tile_buf.shape[0], tile_buf.shape[1]
    each = tiles // CHUNKS
    pairs = [
        (cot_hbm, cot_ref),
        (neigh_two_hbm, neigh_two_ref),
        (features_hbm, features_ref),
        (send_hbm, send_ref),
        (dst_hbm, dst_ref),
        (src_hbm, src_ref),
        (rows_hbm, rows_ref),
    ]
    pairs += [
        (tile_hbm.at[pl.ds(c * each, each)], tile_buf.at[pl.ds(c * each, each)])
        for c in range(CHUNKS)
    ]
    copies = [pltpu.make_async_copy(a, b, sems.at[i]) for i, (a, b) in enumerate(pairs)]
    for copy in copies:
        copy.start()
    rows = features_ref.shape[0]
    bpd = rows // blk
    sources = accs[0].shape[0] // bpd
    part = accs[0].shape[1]
    far = send_ref.shape[2] * send_ref.shape[3]
    for acc in accs:
        acc[...] = jnp.zeros_like(acc)
    copies[0].wait()
    copies[1].wait()
    u = dot_nt(cot_ref[...], neigh_two_ref[...]).astype(BF16)
    up_ref[...] = u
    copies[2].wait()
    copies[3].wait()
    pick_ref[...] = pick_matrix(send_ref, rows)
    picked_ref[...] = dot(pick_ref[...], features_ref[...]).astype(BF16)
    give_ref[chips * (rows + far) :, :] = features_ref[...]
    for copy in copies[4:7]:
        copy.wait()
    place = lax.broadcasted_iota(jnp.int32, (part, blk), 0)
    for c in range(CHUNKS):
        copies[7 + c].wait()

        def add(t, carry):
            slot = dst_ref[t] * sources + src_ref[t]
            for i, acc in enumerate(accs):
                value = tile_buf[t, i * part : (i + 1) * part, :].astype(F32)
                acc[slot] += jnp.where(place < rows_ref[t] - i * part, value, 0.0)
            return carry

        lax.fori_loop(c * each, (c + 1) * each, add, 0, unroll=True)
    for b in range(bpd):
        for j in range(sources):
            block = jnp.concatenate([acc[b * sources + j] for acc in accs], 0).astype(BF16)
            adj_t_ref[j * blk : (j + 1) * blk, b * blk : (b + 1) * blk] = block.T
    column(chips, far, rows, 1 - lax.axis_index("core"), adj_t_ref, col)
    give_ref[: chips * (rows + far), :] = dot(col[...], u).astype(BF16)


def rest_kernel(chips, adj_t_ref, up_ref, cot_ref, pick_ref, adj_ref, col_ref, keep_ref, lend_ref):
    far, rows = pick_ref.shape
    core = lax.axis_index("core")
    count = chips * (rows + far)
    column(chips, far, rows, core, adj_t_ref, col_ref)
    column(chips, far, rows, 1 - core, adj_t_ref, lend_ref)
    lend_ref[count : count + rows, :] = cot_ref[...]
    lend_ref[count + rows :, :] = pick_ref[...]
    keep_ref[...] = dot(col_ref[...], up_ref[...]).astype(BF16)
    for j in range(adj_t_ref.shape[0] // rows):
        adj_ref[:, j * rows : (j + 1) * rows] = adj_t_ref[j * rows : (j + 1) * rows, :].T


def deal(chips, hosts, total, picked, value, mine_ref, msg_ref, to_refs):
    rows = value.shape[0]
    far = picked.shape[0]
    send = far // hosts
    each = rows + far
    chip = lax.axis_index("chip")
    mine_ref[...] = total[pl.ds(pl.multiple_of(chip * each, 8), rows), :]
    for k, ref in enumerate(to_refs):
        other = lax.rem(chip + k + 1, chips)
        ref[:rows, :] = total[pl.ds(pl.multiple_of(other * each, 8), rows), :].astype(BF16)
        ref[rows:, :] = value
    for g in range(hosts):
        for x in range(chips):
            low = x * each + rows + g * send
            both = jnp.concatenate(
                [picked[g * send : (g + 1) * send], total[low : low + send, :]], 0
            )
            msg_ref[g * chips + x] = both.astype(BF16)


def core_sum_kernel(
    chips, hosts, keep_ref, came_ref, value_ref, picked_ref, mine_ref, msg_ref, *rest
):
    total = rest[-1]
    total[...] = keep_ref[...].astype(F32) + came_ref[: total.shape[0], :].astype(F32)
    picked = picked_ref[...].astype(F32)
    deal(chips, hosts, total, picked, value_ref[...], mine_ref, msg_ref, rest[:-1])


def halo_part(recv_ref, hosts, chips, part):
    send = recv_ref.shape[1] // 2
    low = part * send
    blocks = [
        recv_ref[g * chips + x].astype(F32)[low : low + send]
        for x in range(chips)
        for g in range(hosts)
    ]
    return jnp.concatenate(blocks, 0).astype(BF16)


def merge_kernel(chips, hosts, with_terms, recv_ref, mine_ref, *refs):
    came, (out_ref, sum_ref) = refs[: chips - 1], refs[chips - 1 :]
    rows = mine_ref.shape[0]
    total = mine_ref[...]
    for k, ref in enumerate(came):
        total = total + ref[:rows, :].astype(F32)
        out_ref[k * rows : (k + 1) * rows, :] = ref[rows:, :]
    sum_ref[...] = total
    low = len(came) * rows
    halo = halo_part(recv_ref, hosts, chips, 0)
    high = low + halo.shape[0]
    out_ref[low:high, :] = halo
    if with_terms:
        out_ref[high : high + rows, :] = total.astype(BF16)
        out_ref[high + rows :, :] = halo_part(recv_ref, hosts, chips, 1)


def own_chip(adj_refs, blocks):
    chip, core = lax.axis_index("chip"), lax.axis_index("core")
    rows = blocks[0].shape[0]
    parts = []
    for adj_ref in adj_refs:
        total = 0.0
        for side, block in ((core, blocks[0]), (1 - core, blocks[1])):
            low = pl.multiple_of((chip * CORES + side) * rows, rows)
            total = total + dot(adj_ref[:, pl.ds(low, rows)], block)
        parts.append(total)
    return jnp.concatenate(parts, 0)


def early_one_kernel(
    chips, adj_ref, adj_two_ref, value_ref, came_ref, self_ref, bias_ref, up_ref, lent_ref, weight_ref,
    agg_ref, direct_ref, grad_ref,
):
    value = value_ref[...]
    rows = value.shape[0]
    there = came_ref[came_ref.shape[0] - rows :, :]
    agg_ref[...] = own_chip((adj_ref, adj_two_ref), (value, there))
    both = jnp.concatenate([value, there], 0)
    direct_ref[...] = dot(both, self_ref[...]) + bias_ref[...].reshape(1, -1)
    count = came_ref.shape[0] - rows
    both = jnp.concatenate([up_ref[...], lent_ref[count : count + rows, :]], 0)
    grad_ref[...] = dot_nt(both, weight_ref[...])


def early_two_kernel(
    chips, adj_ref, value_ref, there_ref, self_ref, bias_ref, up_ref, weight_ref,
    agg_ref, direct_ref, grad_ref,
):
    value = value_ref[...]
    agg_ref[...] = own_chip((adj_ref,), (value, there_ref[...]))
    direct_ref[...] = dot(value, self_ref[...]) + bias_ref[...].reshape(1, -1)
    grad_ref[...] = dot_nt(up_ref[...], weight_ref[...])


def mid_kernel(chips, hosts, count, *refs):
    adj_refs, refs = refs[:count], refs[count:]
    agg_ref, part_ref, sum_ref, pick_ref, recv_ref = refs[:5]
    came, (agg_out, grad_ref) = refs[5:-2], refs[-2:]
    rows = sum_ref.shape[0]
    chip, core = lax.axis_index("chip"), lax.axis_index("core")
    for i, adj_ref in enumerate(adj_refs):
        agg = agg_ref[i * rows : (i + 1) * rows, :]
        for k, ref in enumerate(came):
            x = lax.rem(chip - k - 1 + chips, chips)
            low = pl.multiple_of((x * CORES + core) * rows, rows)
            agg = agg + dot(adj_ref[:, pl.ds(low, rows)], ref[rows:, :])
        agg_out[i * rows : (i + 1) * rows, :] = agg
    back = halo_part(recv_ref, hosts, chips, 1)
    grad = part_ref[:rows, :] + sum_ref[...]
    grad_ref[:rows, :] = grad + dot_tn(jnp.concatenate([pick_ref[...]] * chips, 0), back)
    if count > 1:
        grad_ref[rows:, :] = part_ref[rows:, :]


def full_aggregate(chips, far, adj_refs, agg_ref, here_ref, shared_ref, halo):
    rows = adj_refs[0].shape[0]
    chip, core = lax.axis_index("chip"), lax.axis_index("core")
    at = (chips - 1) * rows
    for x in range(chips):
        for side, ref in ((core, here_ref), (1 - core, shared_ref)):
            low = pl.multiple_of((x * CORES + side) * far, far)
            halo[pl.ds(low, far), :] = ref[at + x * far : at + (x + 1) * far, :]
    parts = []
    for i, adj_ref in enumerate(adj_refs):
        agg = agg_ref[i * rows : (i + 1) * rows, :]
        for k in range(chips - 1):
            x = lax.rem(chip - k - 1 + chips, chips)
            low = pl.multiple_of((x * CORES + 1 - core) * rows, rows)
            agg = agg + dot(adj_ref[:, pl.ds(low, rows)], shared_ref[k * rows : (k + 1) * rows, :])
        parts.append(agg + dot(adj_ref[:, chips * CORES * rows :], halo[...]))
    return jnp.concatenate(parts, 0).astype(BF16)


def middle_kernel(
    chips,
    hosts,
    adj_ref,
    adj_two_ref,
    col_ref,
    lent_ref,
    agg_ref,
    direct_ref,
    grad_ref,
    pick_ref,
    here_ref,
    shared_ref,
    neigh_one_ref,
    hidden_ref,
    there_ref,
    grad_pre_ref,
    mine_ref,
    msg_ref,
    *rest,
):
    to_refs, halo, total = rest[:-2], rest[-2], rest[-1]
    far, rows = pick_ref.shape
    count = total.shape[0]
    agg = full_aggregate(
        chips, far, (adj_ref, adj_two_ref), agg_ref, here_ref, shared_ref, halo
    )
    pre = direct_ref[...] + dot(agg, neigh_one_ref[...])
    sigmoid = jax.nn.sigmoid(pre)
    hidden = (pre * sigmoid).astype(BF16)
    hidden_ref[...] = hidden[:rows]
    there_ref[...] = hidden[rows:]
    low = (chips - 1) * rows + chips * far
    pick_two = lent_ref[count + rows :, :]
    add = shared_ref[low : low + rows, :].astype(F32)
    add = add + dot_tn(jnp.concatenate([pick_two] * chips, 0), shared_ref[low + rows :, :])
    grad = jnp.concatenate([grad_ref[:rows, :], grad_ref[rows:, :] + add], 0)
    grad_pre = (grad * sigmoid * (1.0 + pre * (1.0 - sigmoid))).astype(BF16)
    grad_pre_ref[...] = grad_pre[:rows]
    u = dot_nt(grad_pre, neigh_one_ref[...]).astype(BF16)
    total[...] = dot(col_ref[...], u[:rows]) + dot(lent_ref[:count, :], u[rows:])
    picked = dot(pick_ref[...], hidden[:rows])
    deal(chips, hosts, total, picked, hidden[:rows], mine_ref, msg_ref, to_refs)


def last_kernel(
    chips, far, adj_ref, agg_ref, direct_ref, here_ref, shared_ref, neigh_two_ref, output_ref, halo
):
    agg = full_aggregate(chips, far, (adj_ref,), agg_ref, here_ref, shared_ref, halo)
    output_ref[...] = (direct_ref[...] + dot(agg, neigh_two_ref[...])).astype(BF16)


def call(kernel, name, out_shape, in_specs, args, scratch=(), limit=32, flops=0):
    return pl.pallas_call(
        kernel,
        out_shape=out_shape,
        in_specs=in_specs,
        out_specs=jax.tree.map(lambda _: VMEM, out_shape),
        scratch_shapes=scratch,
        compiler_params=pltpu.CompilerParams(vmem_limit_bytes=limit * MIB),
        cost_estimate=pl.CostEstimate(
            flops=flops, bytes_accessed=flops // 1024, transcendentals=0
        ),
        name=name,
    )(*args)


def shift(value, axis, k):
    size = lax.axis_size(axis)
    return lax.ppermute(value, axis, [(i, (i + k) % size) for i in range(size)])


def shape(rows, width, kind=BF16):
    return jax.ShapeDtypeStruct((rows, width), kind)


def body(
    features,
    send_list,
    tile_dst,
    tile_src,
    tile_rows,
    tile_val,
    self_one,
    neigh_one,
    bias_one,
    self_two,
    neigh_two,
    bias_two,
    cotangent,
):
    chips = lax.axis_size("chip")
    hosts = lax.axis_size("hst")
    rows, width = features.shape
    tiles, blk = tile_val.shape[:2]
    send = send_list.shape[3]
    far = hosts * send
    all_rows = chips * CORES * (rows + far)
    count = chips * (rows + far)
    rows_shape = shape(rows, width)
    sum_shape = shape(rows, width, F32)
    both_shape = shape(CORES * rows, width, F32)
    square = 2 * rows * width * width
    halo = pltpu.VMEM((chips * CORES * far, width), BF16)
    total = pltpu.VMEM((count, width), F32)
    halo_rows = (chips - 1) * rows + chips * far
    dealt = (
        sum_shape,
        jax.ShapeDtypeStruct((hosts * chips, 2 * send, width), BF16),
    ) + (shape(2 * rows, width),) * (chips - 1)

    def across(mine, msg, to, with_terms):
        terms = [shift(block, "chip", k + 1) for k, block in enumerate(to)]
        recv = lax.all_to_all(msg, ("hst", "chip"), split_axis=0, concat_axis=0, tiled=True)
        here, summed = call(
            functools.partial(merge_kernel, chips, hosts, with_terms),
            "merge",
            (shape(halo_rows + (rows + chips * far) * with_terms, width), sum_shape),
            [VMEM] * (1 + chips),
            (recv, mine, *terms),
        )
        return terms, recv, here, summed, shift(here, "core", 1)

    adj_t, give, up, picked, pick = call(
        functools.partial(prep_kernel, chips),
        "prep",
        (
            shape(all_rows, rows),
            shape(count + rows, width),
            rows_shape,
            shape(far, width),
            shape(far, rows),
        ),
        [HBM] * 8,
        [
            pltpu.with_memory_space_constraint(value, pltpu.HBM)
            for value in (
                tile_dst,
                tile_src,
                tile_rows,
                send_list,
                tile_val,
                features,
                cotangent,
                neigh_two,
            )
        ],
        [
            pltpu.SMEM(tile_dst.shape, jnp.int32),
            pltpu.SMEM(tile_src.shape, jnp.int32),
            pltpu.SMEM(tile_rows.shape, jnp.int32),
            pltpu.SMEM(send_list.shape, jnp.int32),
            pltpu.VMEM(tile_val.shape, BF16),
            pltpu.VMEM(features.shape, BF16),
            pltpu.VMEM(cotangent.shape, BF16),
            pltpu.VMEM(neigh_two.shape, BF16),
            pltpu.VMEM((count, rows), BF16),
            pltpu.SemaphoreType.DMA((7 + CHUNKS,)),
        ]
        + [pltpu.VMEM(((rows // blk) * (all_rows // blk), blk // PARTS, blk), F32)] * PARTS,
    )
    came = shift(give, "core", 1)
    adj, col, keep, lend = call(
        functools.partial(rest_kernel, chips),
        "rest",
        (
            shape(rows, all_rows),
            shape(count, rows),
            shape(count, width),
            shape(count + rows + far, width),
        ),
        [VMEM] * 4,
        (adj_t, up, cotangent, pick),
        flops=3 * square,
    )
    adj_two = shift(adj, "core", 1)
    lent = shift(lend, "core", 1)
    mine, msg, *to = call(
        functools.partial(core_sum_kernel, chips, hosts),
        "core_sum",
        dealt,
        [VMEM] * 4,
        (keep, came, features, picked),
        [total],
    )
    terms, recv, here, summed, shared = across(mine, msg, to, 1)
    agg, direct, grad = call(
        functools.partial(early_one_kernel, chips),
        "early_one",
        (both_shape,) * 3,
        [VMEM] * 9,
        (adj, adj_two, features, came, self_one, bias_one, cotangent, lent, self_two),
        flops=8 * square,
    )
    agg, grad = call(
        functools.partial(mid_kernel, chips, hosts, 2),
        "mid_one",
        (both_shape,) * 2,
        [VMEM] * (6 + chips),
        (adj, adj_two, agg, grad, summed, pick, recv, *terms),
        flops=3 * square,
    )
    hidden, there, grad_pre, mine, msg, *to = call(
        functools.partial(middle_kernel, chips, hosts),
        "middle",
        (rows_shape,) * 3 + dealt,
        [VMEM] * 11,
        (adj, adj_two, col, lent, agg, direct, grad, pick, here, shared, neigh_one),
        [halo, total],
        flops=12 * square,
    )
    terms, recv, here, summed, shared = across(mine, msg, to, 0)
    agg, direct, grad = call(
        functools.partial(early_two_kernel, chips),
        "early_two",
        (sum_shape,) * 3,
        [VMEM] * 7,
        (adj, hidden, there, self_two, bias_two, grad_pre, self_one),
        flops=4 * square,
    )
    agg, grad = call(
        functools.partial(mid_kernel, chips, hosts, 1),
        "mid_two",
        (sum_shape,) * 2,
        [VMEM] * (5 + chips),
        (adj, agg, grad, summed, pick, recv, *terms),
        flops=2 * square,
    )
    output = call(
        functools.partial(last_kernel, chips, far),
        "last",
        rows_shape,
        [VMEM] * 6,
        (adj, agg, direct, here, shared, neigh_two),
        [halo],
        flops=3 * square,
    )
    return output, grad


def solution(mesh):
    hosts, devs = mesh.devices.shape
    mesh = Mesh(mesh.devices.reshape(hosts, devs // CORES, CORES), ("hst", "chip", "core"))
    dev = ("chip", "core")
    every = ("hst", "chip", "core")
    return jax.shard_map(
        body,
        mesh=mesh,
        in_specs=(
            P(every, None),
            P("hst", dev, None, None),
            P(every),
            P(every),
            P(every),
            P(every, None, None),
            P(),
            P(),
            P(),
            P(),
            P(),
            P(),
            P(every, None),
        ),
        out_specs=(P(every, None), P(every, None)),
        check_vma=False,
    )
```

time: 48.2 us -> 42.3 us (0.88)
  blocking collectives: 0 us -> 10.8 us
  waiting for transfers between devices: 19.1 us -> 9.12 us
  starting transfers between devices: 19.6 us -> 10.7 us
  local copies, waits for them, and re-layouts: 0.03 us -> 2.47 us
    ppermute x8 -> x7, waiting for transfers between devices: 19.1 us -> 1.39 us  [shift(): return lax.ppermute(value, axis, [(i, (i + k) % size) for i in range(size)])]
    all_to_all x0 -> x1, blocking collectives: none -> 10.8 us  [across(): lax.all_to_all(msg, ('hst', 'chip'), split_axis=0, concat_axis=0, tiled=T...]
    all_to_all x2 -> x1, starting transfers between devices: 14.6 us -> 5.94 us  [across(): lax.all_to_all(msg, ('hst', 'chip'), split_axis=0, concat_axis=0, tiled=T...]
    all_to_all x2 -> x1, waiting for transfers between devices: 0.01 us -> 7.72 us  [across(): lax.all_to_all(msg, ('hst', 'chip'), split_axis=0, concat_axis=0, tiled=T...]
    unnamed x16 -> x22, local copies, waits for them, and re-layouts: 0.03 us -> 2.47 us
    ppermute x8 -> x7, starting transfers between devices: 5.08 us -> 4.8 us  [shift(): return lax.ppermute(value, axis, [(i, (i + k) % size) for i in range(size)])]
  transfers between devices with their start and end apart: 10 -> 8, of which waited for: 8 -> 4; matrix products, arithmetic and copies ran while one was open for 0% -> 0% of each run, Pallas kernels for 4% -> 8%
where the time goes in v7:
time: 42.3 us; the launch traced here: 42.1 us
  blocking collectives  10.8 us (26%)
  starting transfers between devices  10.7 us (25%)
  waiting for transfers between devices  9.12 us (22%)
  Pallas kernels  8.11 us (19%)
  local copies, waits for them, and re-layouts  2.47 us (6%)
  between operations  0.84 us (2%)
    all_to_all x1, blocking collectives, across(): lax.all_to_all(msg, ('hst', 'chip'), split_axis=0, concat_axis=0, tiled=T...  10.8 us
    pallas_call x11, Pallas kernels, call(): pl.pallas_call(kernel, out_shape=out_shape, in_specs=in_specs, out_specs=...  8.11 us
    all_to_all x1, waiting for transfers between devices, across(): lax.all_to_all(msg, ('hst', 'chip'), split_axis=0, concat_axis=0, tiled=T...  7.72 us
    all_to_all x1, starting transfers between devices, across(): lax.all_to_all(msg, ('hst', 'chip'), split_axis=0, concat_axis=0, tiled=T...  5.94 us
    ppermute x7, starting transfers between devices, shift(): return lax.ppermute(value, axis, [(i, (i + k) % size) for i in range(size)])  4.8 us
    unnamed x22, local copies, waits for them, and re-layouts  2.47 us
    ppermute x7, waiting for transfers between devices, shift(): return lax.ppermute(value, axis, [(i, (i + k) % size) for i in range(size)])  1.39 us
  transfers between devices with their start and end apart: 8, of which 4 were waited for; matrix products, arithmetic and copies ran while one was open for 0% of the time, Pallas kernels for 8%

profile of v7, /device:TPU:0, one launch (start us, length us, event | category | flops | bytes accessed | tf_op | source)
XLA Modules:
  0.0 42.1 jit_solution(6370090965182858607)
XLA Ops:
  0.7 2.7 %prep.1 = (bf16[1280,256]{1,0:T(8,128)(2,1)S(1)}, bf16[896,256]{1,0:T(8,128)(2,1)S(1)}, bf16[256,256]{1,0:T(8,128)(2,1)S(1)}, bf16[64,256]{1,0:T(8,128)(2,1)S(1)}, bf16[64,256]{1,0:T(8,128)(2,1)S(1)}) custom-call(s32[64]{0:T(128)} %dst_hbm.1, s32[64]{0:T(128)} %src_hbm.1, s32[64]{0:T(128)} %rows_hbm.1, s32[1,1,8,8]{3,2,1,0:T(8,128)} %send_hbm.1, ...), custom_call_target="tpu_custom_call" | custom-call | tf_op jit(solution)/shard_map/prep/pallas_call | solution.py:339
  3.4 0.5 %collective-permute-start.2 = (bf16[896,256]{1,0:T(8,128)(2,1)S(1)}, bf16[896,256]{1,0:T(8,128)(2,1)S(1)}, u32[]{:S(2)}, u32[]{:S(2)}) collective-permute-start(bf16[896,256]{1,0:T(8,128)(2,1)S(1)} %get-tuple-element.40), channel_id=1, source_target_pairs={{0,1},{1,0},{2,3},{3,2},{4,5},{5,4},{6,7},{7,6},{8,9},{9,8},{10,11... | collective-permute-start | bytes 1376264 | tf_op jit(solution)/shard_map/ppermute | solution.py:355
  3.9 0.3 rest.1
  4.2 0.8 %copy-done.10 = bf16[960,256]{1,0:T(8,128)(2,1)} copy-done((bf16[960,256]{1,0:T(8,128)(2,1)}, bf16[960,256]{1,0:T(8,128)(2,1)S(1)}, u32[]{:S(2)}) %copy-start.10) | copy-done | bytes 491544
  5.0 0.1 collective-permute-start
  5.0 0.3 collective-permute-done.2.came_ref
  5.3 0.9 %core_sum.1 = (f32[256,256]{1,0:T(8,128)S(1)}, bf16[16,16,256]{2,1,0:T(8,128)(2,1)}, bf16[512,256]{1,0:T(8,128)(2,1)}) custom-call(bf16[640,256]{1,0:T(8,128)(2,1)S(1)} %get-tuple-element.43.keep_ref, bf16[896,256]{1,0:T(8,128)(2,1)S(1)} %collective-permute-done.2.came_ref, bf16[256,256]{1,0:T(8,128)(2,1)S(1)} %copy-done, ...), custom_call_target="tpu_custom_call" | custom-call | tf_op jit(solution)/shard_map/core_sum/pallas_call | solution.py:339
  6.2 0.7 %copy-done.5 = f32[256,256]{1,0:T(8,128)} copy-done((f32[256,256]{1,0:T(8,128)}, f32[256,256]{1,0:T(8,128)S(1)}, u32[]{:S(2)}) %copy-start.5) | copy-done | bytes 262168
  6.9 2.9 %collective-permute-start.3 = (bf16[512,256]{1,0:T(8,128)(2,1)}, bf16[512,256]{1,0:T(8,128)(2,1)S(1)}, u32[]{:S(2)}, u32[]{:S(2)}) collective-permute-start(bf16[512,256]{1,0:T(8,128)(2,1)} %get-tuple-element.47), channel_id=1, source_target_pairs={{0,2},{2,0},{1,3},{3,1},{4,6},{6,4},{5,7},{7,5},{8,10},{10,8},{9,1... | collective-permute-start | bytes 786440 | tf_op jit(solution)/shard_map/ppermute | solution.py:355
  9.8 5.9 %all-to-all-start = ((bf16[16,16,256]{2,1,0:T(8,128)(2,1)}), bf16[16,16,256]{2,1,0:T(8,128)(2,1)S(1)}, u32[]{:S(2)}, u32[]{:S(2)}) async-start(bf16[16,16,256]{2,1,0:T(8,128)(2,1)} %get-tuple-element.45), calls=%async_computation | async-start | bytes 262144 | tf_op jit(solution)/shard_map/all_to_all | solution.py:399
  15.7 0.1 collective-permute-start.1
  15.8 7.7 %all-to-all-done.recv_ref.refs_6_ = bf16[16,16,256]{2,1,0:T(8,128)(2,1)S(1)} async-done(((bf16[16,16,256]{2,1,0:T(8,128)(2,1)}), bf16[16,16,256]{2,1,0:T(8,128)(2,1)S(1)}, u32[]{:S(2)}, u32[]{:S(2)}) %all-to-all-start) | async-done | bytes 131104 | tf_op jit(solution)/shard_map/all_to_all | solution.py:399
  23.5 0.0 collective-permute-done.3.refs_0_.refs_7_
  23.6 0.9 %copy-done.6 = f32[256,256]{1,0:T(8,128)S(1)} copy-done((f32[256,256]{1,0:T(8,128)S(1)}, f32[256,256]{1,0:T(8,128)}, u32[]{:S(2)}) %copy-start.6) | copy-done | bytes 262168
  24.5 0.1 merge.2
  24.6 0.1 collective-permute-start.4
  24.6 0.0 collective-permute-done.1.lent_ref
  24.7 0.0 collective-permute-done.adj_two_ref.refs_1_
  24.7 0.4 %early_one.1 = (f32[512,256]{1,0:T(8,128)S(1)}, f32[512,256]{1,0:T(8,128)S(1)}, f32[512,256]{1,0:T(8,128)S(1)}) custom-call(bf16[256,1280]{1,0:T(8,128)(2,1)S(1)} %get-tuple-element.37.adj_ref.refs_0_, bf16[256,1280]{1,0:T(8,128)(2,1)S(1)} %collective-permute-done.adj_two_ref.refs_1_, bf16[256,256]{1,0:T(8,128)(2,1)S(1)} %copy-done, ...), custom_call_target="tpu_custom_call" | custom-call | flops 268435456 | bytes 262144 | tf_op jit(solution)/shard_map/early_one/pallas_call | solution.py:339
  25.1 0.0 copy-start.7
  25.2 0.3 mid_one.1
  25.4 0.9 %collective-permute-done.4.shared_ref = bf16[768,256]{1,0:T(8,128)(2,1)S(1)} collective-permute-done((bf16[768,256]{1,0:T(8,128)(2,1)S(1)}, bf16[768,256]{1,0:T(8,128)(2,1)S(1)}, u32[]{:S(2)}, u32[]{:S(2)}) %collective-permute-start.4) | collective-permute-done | bytes 393248 | tf_op jit(solution)/shard_map/ppermute | solution.py:355
  26.4 1.1 %middle.1 = (bf16[256,256]{1,0:T(8,128)(2,1)S(1)}, bf16[256,256]{1,0:T(8,128)(2,1)S(1)}, bf16[256,256]{1,0:T(8,128)(2,1)S(1)}, f32[256,256]{1,0:T(8,128)S(1)}, b...) custom-call(bf16[256,1280]{1,0:T(8,128)(2,1)S(1)} %get-tuple-element.37.adj_ref.refs_0_, ...), custom_call_target="tpu_custom_call" | custom-call | flops 402653184 | bytes 393216 | tf_op jit(solution)/shard_map/middle/pallas_call | solution.py:339
  27.5 0.0 copy-start.2
  27.5 1.2 %collective-permute-start.5 = (bf16[512,256]{1,0:T(8,128)(2,1)S(1)}, bf16[512,256]{1,0:T(8,128)(2,1)S(1)}, u32[]{:S(2)}, u32[]{:S(2)}) collective-permute-start(bf16[512,256]{1,0:T(8,128)(2,1)S(1)} %get-tuple-element.60), channel_id=1, source_target_pairs={{0,2},{2,0},{1,3},{3,1},{4,6},{6,4},{5,7},{7,5},{8,10},{10,8},{9,1... | collective-permute-start | bytes 786440 | tf_op jit(solution)/shard_map/ppermute | solution.py:355
  28.7 10.8 %all_to_all.10.recv_ref.refs_5_ = bf16[16,16,256]{2,1,0:T(8,128)(2,1)S(1)} all-to-all(bf16[16,16,256]{2,1,0:T(8,128)(2,1)S(1)} %get-tuple-element.58), channel_id=1, replica_groups=mesh['hst'=8,'chip'=2,'core'=2] {'hst','chip'}, dimensions={0} | all-to-all | bytes 262144 | tf_op jit(solution)/shard_map/all_to_all | solution.py:399
  39.5 0.0 collective-permute-done.5.refs_0_.refs_6_
  39.5 0.1 collective-permute-start.6
  39.6 0.3 early_two.1
  39.9 1.0 %mid_two.1 = (f32[256,256]{1,0:T(8,128)S(1)}, f32[256,256]{1,0:T(8,128)}) custom-call(bf16[256,1280]{1,0:T(8,128)(2,1)S(1)} %get-tuple-element.37.adj_ref.refs_0_, f32[256,256]{1,0:T(8,128)S(1)} %get-tuple-element.56.refs_1_, f32[256,256]{1,0:T(8,128)S(1)} %get-tuple-element.57.refs_2_, f32[256,256]{1,0:T(8,128)S(1)} %get-tuple-element.61.refs_3_, ...), custom_call_target="tpu_custom_call" | custom-call | flops 67108864 | bytes 65536 | tf_op jit(solution)/shard_map/mid_two/pallas_call | solution.py:339
  40.9 0.1 collective-permute-done.6.shared_ref
  41.0 1.0 %last.1 = bf16[256,256]{1,0:T(8,128)(2,1)} custom-call(bf16[256,1280]{1,0:T(8,128)(2,1)S(1)} %get-tuple-element.37.adj_ref.refs_0_, f32[256,256]{1,0:T(8,128)S(1)} %get-tuple-element.62.agg_ref, f32[256,256]{1,0:T(8,128)S(1)} %get-tuple-element.63.direct_ref, bf16[384,256]{1,0:T(8,128)(2,1)S(1)} %get-tuple-element.64.here_ref, ...), custom_call_target="tpu_custom_call" | custom-call | flops 100663296 | bytes 98304 | tf_op jit(solution)/shard_map/last/pallas_call | solution.py:339
  (18 shorter events, 0.1 us)
Async XLA Ops:
  0.6 4.7 %copy-start = (bf16[256,256]{1,0:T(8,128)(2,1)S(1)}, bf16[256,256]{1,0:T(8,128)(2,1)}, u32[]{:S(2)}) copy-start(bf16[256,256]{1,0:T(8,128)(2,1)} %value_ref.3) | copy-start | bytes 393220
  0.6 3.2 %copy-start.1 = (bf16[256,256]{1,0:T(8,128)(2,1)S(1)}, bf16[256,256]{1,0:T(8,128)(2,1)}, u32[]{:S(2)}) copy-start(bf16[256,256]{1,0:T(8,128)(2,1)} %up_ref.1) | copy-start | bytes 393220
  0.7 24.0 %copy-start.3 = (bf16[256,256]{1,0:T(8,128)(2,1)S(1)}, bf16[256,256]{1,0:T(8,128)(2,1)}, u32[]{:S(2)}) copy-start(bf16[256,256]{1,0:T(8,128)(2,1)} %weight_ref.3) | copy-start | bytes 393220
  0.7 24.0 %copy-start.8 = (f32[256]{0:T(256)S(1)}, f32[256]{0:T(256)}, u32[]{:S(2)}) copy-start(f32[256]{0:T(256)} %bias_ref.2) | copy-start | bytes 3076
  0.7 24.0 %copy-start.4 = (bf16[256,256]{1,0:T(8,128)(2,1)S(1)}, bf16[256,256]{1,0:T(8,128)(2,1)}, u32[]{:S(2)}) copy-start(bf16[256,256]{1,0:T(8,128)(2,1)} %self_ref.3) | copy-start | bytes 393220
  3.4 2.0 %collective-permute-start.2 = (bf16[896,256]{1,0:T(8,128)(2,1)S(1)}, bf16[896,256]{1,0:T(8,128)(2,1)S(1)}, u32[]{:S(2)}, u32[]{:S(2)}) collective-permute-start(bf16[896,256]{1,0:T(8,128)(2,1)S(1)} %get-tuple-element.40), channel_id=1, source_target_pairs={{0,1},{1,0},{2,3},{3,2},{4,5},{5,4},{6,7},{7,6},{8,9},{9,8},{10,11... | collective-permute-start | bytes 1376264 | tf_op jit(solution)/shard_map/ppermute | solution.py:355
  4.2 0.8 %copy-start.10 = (bf16[960,256]{1,0:T(8,128)(2,1)}, bf16[960,256]{1,0:T(8,128)(2,1)S(1)}, u32[]{:S(2)}) copy-start(bf16[960,256]{1,0:T(8,128)(2,1)S(1)} %get-tuple-element.39) | copy-start | bytes 1474564
  5.0 19.7 %collective-permute-start = (bf16[256,1280]{1,0:T(8,128)(2,1)S(1)}, bf16[256,1280]{1,0:T(8,128)(2,1)S(1)}, u32[]{:S(2)}, u32[]{:S(2)}) collective-permute-start(bf16[256,1280]{1,0:T(8,128)(2,1)S(1)} %get-tuple-element.37.adj_ref.refs_0_), channel_id=1, source_target_pairs={{0,1},{1,0},{2,3},{3,2},{4,5},{5,4},{6,7},{7,6},{8,9},{9,8},{10,11... | collective-permute-start | bytes 1966088 | tf_op jit(solution)/shard_map/ppermute | solution.py:355
  6.2 0.7 %copy-start.5 = (f32[256,256]{1,0:T(8,128)}, f32[256,256]{1,0:T(8,128)S(1)}, u32[]{:S(2)}) copy-start(f32[256,256]{1,0:T(8,128)S(1)} %get-tuple-element.46.mine_ref) | copy-start | bytes 786436
  6.9 16.6 %collective-permute-start.3 = (bf16[512,256]{1,0:T(8,128)(2,1)}, bf16[512,256]{1,0:T(8,128)(2,1)S(1)}, u32[]{:S(2)}, u32[]{:S(2)}) collective-permute-start(bf16[512,256]{1,0:T(8,128)(2,1)} %get-tuple-element.47), channel_id=1, source_target_pairs={{0,2},{2,0},{1,3},{3,1},{4,6},{6,4},{5,7},{7,5},{8,10},{10,8},{9,1... | collective-permute-start | bytes 786440 | tf_op jit(solution)/shard_map/ppermute | solution.py:355
  9.8 13.8 %all-to-all-start = ((bf16[16,16,256]{2,1,0:T(8,128)(2,1)}), bf16[16,16,256]{2,1,0:T(8,128)(2,1)S(1)}, u32[]{:S(2)}, u32[]{:S(2)}) async-start(bf16[16,16,256]{2,1,0:T(8,128)(2,1)} %get-tuple-element.45), calls=%async_computation | async-start | bytes 262144 | tf_op jit(solution)/shard_map/all_to_all | solution.py:399
  15.7 8.9 %collective-permute-start.1 = (bf16[960,256]{1,0:T(8,128)(2,1)}, bf16[960,256]{1,0:T(8,128)(2,1)S(1)}, u32[]{:S(2)}, u32[]{:S(2)}) collective-permute-start(bf16[960,256]{1,0:T(8,128)(2,1)} %copy-done.10), channel_id=1, source_target_pairs={{0,1},{1,0},{2,3},{3,2},{4,5},{5,4},{6,7},{7,6},{8,9},{9,8},{10,11... | collective-permute-start | bytes 1474568 | tf_op jit(solution)/shard_map/ppermute | solution.py:355
  23.6 1.0 %copy-start.6 = (f32[256,256]{1,0:T(8,128)S(1)}, f32[256,256]{1,0:T(8,128)}, u32[]{:S(2)}) copy-start(f32[256,256]{1,0:T(8,128)} %copy-done.5) | copy-start | bytes 786436
  24.6 1.8 %collective-permute-start.4 = (bf16[768,256]{1,0:T(8,128)(2,1)S(1)}, bf16[768,256]{1,0:T(8,128)(2,1)S(1)}, u32[]{:S(2)}, u32[]{:S(2)}) collective-permute-start(bf16[768,256]{1,0:T(8,128)(2,1)S(1)} %get-tuple-element.52.here_ref), channel_id=1, source_target_pairs={{0,1},{1,0},{2,3},{3,2},{4,5},{5,4},{6,7},{7,6},{8,9},{9,8},{10,11... | collective-permute-start | bytes 1179656 | tf_op jit(solution)/shard_map/ppermute | solution.py:355
  25.1 1.2 %copy-start.7 = (bf16[256,256]{1,0:T(8,128)(2,1)S(1)}, bf16[256,256]{1,0:T(8,128)(2,1)}, u32[]{:S(2)}) copy-start(bf16[256,256]{1,0:T(8,128)(2,1)} %neigh_one_ref.1) | copy-start | bytes 393220
  26.4 13.2 %copy-start.9 = (f32[256]{0:T(256)S(1)}, f32[256]{0:T(256)}, u32[]{:S(2)}) copy-start(f32[256]{0:T(256)} %bias_ref.3) | copy-start | bytes 3076
  27.5 13.5 %copy-start.2 = (bf16[256,256]{1,0:T(8,128)(2,1)S(1)}, bf16[256,256]{1,0:T(8,128)(2,1)}, u32[]{:S(2)}) copy-start(bf16[256,256]{1,0:T(8,128)(2,1)} %neigh_two_ref.1) | copy-start | bytes 393220
  27.5 11.9 %collective-permute-start.5 = (bf16[512,256]{1,0:T(8,128)(2,1)S(1)}, bf16[512,256]{1,0:T(8,128)(2,1)S(1)}, u32[]{:S(2)}, u32[]{:S(2)}) collective-permute-start(bf16[512,256]{1,0:T(8,128)(2,1)S(1)} %get-tuple-element.60), channel_id=1, source_target_pairs={{0,2},{2,0},{1,3},{3,1},{4,6},{6,4},{5,7},{7,5},{8,10},{10,8},{9,1... | collective-permute-start | bytes 786440 | tf_op jit(solution)/shard_map/ppermute | solution.py:355
  39.5 1.5 %collective-permute-start.6 = (bf16[384,256]{1,0:T(8,128)(2,1)S(1)}, bf16[384,256]{1,0:T(8,128)(2,1)S(1)}, u32[]{:S(2)}, u32[]{:S(2)}) collective-permute-start(bf16[384,256]{1,0:T(8,128)(2,1)S(1)} %get-tuple-element.64.here_ref), channel_id=1, source_target_pairs={{0,1},{1,0},{2,3},{3,2},{4,5},{5,4},{6,7},{7,6},{8,9},{9,8},{10,11... | collective-permute-start | bytes 589832 | tf_op jit(solution)/shard_map/ppermute | solution.py:355

commit v8 on v7

--- a/solution.py
+++ b/solution.py
@@ -43,14 +43,15 @@
     return jnp.concatenate(parts, 0).astype(BF16)
 
 
-def column(chips, far, rows, side, whole_ref, out_ref):
+def column(chips, far, rows, side, whole_ref, out_ref, base):
     each = rows + far
     for x in range(chips):
         d = x * CORES + side
         low = pl.multiple_of(d * rows, rows)
-        out_ref[x * each : x * each + rows, :] = whole_ref[pl.ds(low, rows), :]
+        at = base + x * each
+        out_ref[at : at + rows, :] = whole_ref[pl.ds(low, rows), :]
         low = pl.multiple_of(chips * CORES * rows + d * far, far)
-        out_ref[x * each + rows : (x + 1) * each, :] = whole_ref[pl.ds(low, far), :]
+        out_ref[at + rows : at + each, :] = whole_ref[pl.ds(low, far), :]
 
 
 def prep_kernel(
@@ -132,21 +133,25 @@
         for j in range(sources):
             block = jnp.concatenate([acc[b * sources + j] for acc in accs], 0).astype(BF16)
             adj_t_ref[j * blk : (j + 1) * blk, b * blk : (b + 1) * blk] = block.T
-    column(chips, far, rows, 1 - lax.axis_index("core"), adj_t_ref, col)
+    column(chips, far, rows, 1 - lax.axis_index("core"), adj_t_ref, col, 0)
     give_ref[: chips * (rows + far), :] = dot(col[...], u).astype(BF16)
 
 
 def rest_kernel(chips, adj_t_ref, up_ref, cot_ref, pick_ref, adj_ref, col_ref, keep_ref, lend_ref):
     far, rows = pick_ref.shape
     core = lax.axis_index("core")
+    all_rows = adj_t_ref.shape[0]
     count = chips * (rows + far)
-    column(chips, far, rows, core, adj_t_ref, col_ref)
-    column(chips, far, rows, 1 - core, adj_t_ref, lend_ref)
-    lend_ref[count : count + rows, :] = cot_ref[...]
-    lend_ref[count + rows :, :] = pick_ref[...]
+    for j in range(all_rows // rows):
+        block = adj_t_ref[j * rows : (j + 1) * rows, :].T
+        adj_ref[j * rows : (j + 1) * rows, :] = block
+        lend_ref[j * rows : (j + 1) * rows, :] = block
+    column(chips, far, rows, core, adj_t_ref, col_ref, 0)
+    column(chips, far, rows, 1 - core, adj_t_ref, lend_ref, all_rows)
+    low = all_rows + count
+    lend_ref[low : low + rows, :] = cot_ref[...]
+    lend_ref[low + rows :, :] = pick_ref[...]
     keep_ref[...] = dot(col_ref[...], up_ref[...]).astype(BF16)
-    for j in range(adj_t_ref.shape[0] // rows):
-        adj_ref[:, j * rows : (j + 1) * rows] = adj_t_ref[j * rows : (j + 1) * rows, :].T
 
 
 def deal(chips, hosts, total, picked, value, mine_ref, msg_ref, to_refs):
@@ -214,23 +219,24 @@
         total = 0.0
         for side, block in ((core, blocks[0]), (1 - core, blocks[1])):
             low = pl.multiple_of((chip * CORES + side) * rows, rows)
-            total = total + dot(adj_ref[:, pl.ds(low, rows)], block)
+            total = total + dot(adj_ref[pl.ds(low, rows), :], block)
         parts.append(total)
     return jnp.concatenate(parts, 0)
 
 
 def early_one_kernel(
-    chips, adj_ref, adj_two_ref, value_ref, came_ref, self_ref, bias_ref, up_ref, lent_ref, weight_ref,
+    chips, adj_ref, lent_ref, value_ref, came_ref, self_ref, bias_ref, up_ref, weight_ref,
     agg_ref, direct_ref, grad_ref,
 ):
     value = value_ref[...]
     rows = value.shape[0]
     there = came_ref[came_ref.shape[0] - rows :, :]
-    agg_ref[...] = own_chip((adj_ref, adj_two_ref), (value, there))
+    agg_ref[...] = own_chip((adj_ref, lent_ref), (value, there))
     both = jnp.concatenate([value, there], 0)
     direct_ref[...] = dot(both, self_ref[...]) + bias_ref[...].reshape(1, -1)
     count = came_ref.shape[0] - rows
-    both = jnp.concatenate([up_ref[...], lent_ref[count : count + rows, :]], 0)
+    high = lent_ref.shape[0] - (count // chips - rows)
+    both = jnp.concatenate([up_ref[...], lent_ref[high - rows : high, :]], 0)
     grad_ref[...] = dot_nt(both, weight_ref[...])
 
 
@@ -255,7 +261,7 @@
         for k, ref in enumerate(came):
             x = lax.rem(chip - k - 1 + chips, chips)
             low = pl.multiple_of((x * CORES + core) * rows, rows)
-            agg = agg + dot(adj_ref[:, pl.ds(low, rows)], ref[rows:, :])
+            agg = agg + dot(adj_ref[pl.ds(low, rows), :], ref[rows:, :])
         agg_out[i * rows : (i + 1) * rows, :] = agg
     back = halo_part(recv_ref, hosts, chips, 1)
     grad = part_ref[:rows, :] + sum_ref[...]
@@ -264,8 +270,7 @@
         grad_ref[rows:, :] = part_ref[rows:, :]
 
 
-def full_aggregate(chips, far, adj_refs, agg_ref, here_ref, shared_ref, halo):
-    rows = adj_refs[0].shape[0]
+def full_aggregate(chips, far, rows, adj_refs, agg_ref, here_ref, shared_ref, halo):
     chip, core = lax.axis_index("chip"), lax.axis_index("core")
     at = (chips - 1) * rows
     for x in range(chips):
@@ -278,8 +283,11 @@
         for k in range(chips - 1):
             x = lax.rem(chip - k - 1 + chips, chips)
             low = pl.multiple_of((x * CORES + 1 - core) * rows, rows)
-            agg = agg + dot(adj_ref[:, pl.ds(low, rows)], shared_ref[k * rows : (k + 1) * rows, :])
-        parts.append(agg + dot(adj_ref[:, chips * CORES * rows :], halo[...]))
+            agg = agg + dot(adj_ref[pl.ds(low, rows), :], shared_ref[k * rows : (k + 1) * rows, :])
+        for j in range(halo.shape[0] // rows):
+            low = chips * CORES * rows + j * rows
+            agg = agg + dot(adj_ref[low : low + rows, :], halo[j * rows : (j + 1) * rows, :])
+        parts.append(agg)
     return jnp.concatenate(parts, 0).astype(BF16)
 
 
@@ -287,9 +295,8 @@
     chips,
     hosts,
     adj_ref,
-    adj_two_ref,
+    lent_ref,
     col_ref,
-    lent_ref,
     agg_ref,
     direct_ref,
     grad_ref,
@@ -308,7 +315,7 @@
     far, rows = pick_ref.shape
     count = total.shape[0]
     agg = full_aggregate(
-        chips, far, (adj_ref, adj_two_ref), agg_ref, here_ref, shared_ref, halo
+        chips, far, rows, (adj_ref, lent_ref), agg_ref, here_ref, shared_ref, halo
     )
     pre = direct_ref[...] + dot(agg, neigh_one_ref[...])
     sigmoid = jax.nn.sigmoid(pre)
@@ -316,14 +323,17 @@
     hidden_ref[...] = hidden[:rows]
     there_ref[...] = hidden[rows:]
     low = (chips - 1) * rows + chips * far
-    pick_two = lent_ref[count + rows :, :]
+    base = lent_ref.shape[0] - far - rows - count
+    pick_two = lent_ref[base + count + rows :, :]
     add = shared_ref[low : low + rows, :].astype(F32)
     add = add + dot_tn(jnp.concatenate([pick_two] * chips, 0), shared_ref[low + rows :, :])
     grad = jnp.concatenate([grad_ref[:rows, :], grad_ref[rows:, :] + add], 0)
     grad_pre = (grad * sigmoid * (1.0 + pre * (1.0 - sigmoid))).astype(BF16)
     grad_pre_ref[...] = grad_pre[:rows]
     u = dot_nt(grad_pre, neigh_one_ref[...]).astype(BF16)
-    total[...] = dot(col_ref[...], u[:rows]) + dot(lent_ref[:count, :], u[rows:])
+    total[...] = dot(col_ref[...], u[:rows]) + dot(
+        lent_ref[base : base + count, :], u[rows:]
+    )
     picked = dot(pick_ref[...], hidden[:rows])
     deal(chips, hosts, total, picked, hidden[:rows], mine_ref, msg_ref, to_refs)
 
@@ -331,7 +341,8 @@
 def last_kernel(
     chips, far, adj_ref, agg_ref, direct_ref, here_ref, shared_ref, neigh_two_ref, output_ref, halo
 ):
-    agg = full_aggregate(chips, far, (adj_ref,), agg_ref, here_ref, shared_ref, halo)
+    rows = agg_ref.shape[0]
+    agg = full_aggregate(chips, far, rows, (adj_ref,), agg_ref, here_ref, shared_ref, halo)
     output_ref[...] = (direct_ref[...] + dot(agg, neigh_two_ref[...])).astype(BF16)
 
 
@@ -449,16 +460,16 @@
         functools.partial(rest_kernel, chips),
         "rest",
         (
-            shape(rows, all_rows),
+            shape(all_rows, rows),
             shape(count, rows),
             shape(count, width),
-            shape(count + rows + far, width),
+            shape(all_rows + count + rows + far, width),
         ),
         [VMEM] * 4,
         (adj_t, up, cotangent, pick),
         flops=3 * square,
     )
-    adj_two = shift(adj, "core", 1)
+    came, lend = lax.optimization_barrier((came, lend))
     lent = shift(lend, "core", 1)
     mine, msg, *to = call(
         functools.partial(core_sum_kernel, chips, hosts),
@@ -473,8 +484,8 @@
         functools.partial(early_one_kernel, chips),
         "early_one",
         (both_shape,) * 3,
-        [VMEM] * 9,
-        (adj, adj_two, features, came, self_one, bias_one, cotangent, lent, self_two),
+        [VMEM] * 8,
+        (adj, lent, features, came, self_one, bias_one, cotangent, self_two),
         flops=8 * square,
     )
     agg, grad = call(
@@ -482,15 +493,15 @@
         "mid_one",
         (both_shape,) * 2,
         [VMEM] * (6 + chips),
-        (adj, adj_two, agg, grad, summed, pick, recv, *terms),
+        (adj, lent, agg, grad, summed, pick, recv, *terms),
         flops=3 * square,
     )
     hidden, there, grad_pre, mine, msg, *to = call(
         functools.partial(middle_kernel, chips, hosts),
         "middle",
         (rows_shape,) * 3 + dealt,
-        [VMEM] * 11,
-        (adj, adj_two, col, lent, agg, direct, grad, pick, here, shared, neigh_one),
+        [VMEM] * 10,
+        (adj, lent, col, agg, direct, grad, pick, here, shared, neigh_one),
         [halo, total],
         flops=12 * square,
     )

time: 42.3 us -> 40.1 us (0.948)
  blocking collectives: 10.8 us -> 24.5 us
  waiting for transfers between devices: 9.12 us -> 2.22 us
  starting transfers between devices: 10.7 us -> 4.9 us
  local copies, waits for them, and re-layouts: 2.47 us -> 0.04 us
  Pallas kernels: 8.11 us -> 7.35 us
    all_to_all x1 -> x2, blocking collectives: 10.8 us -> 24.5 us  [across(): lax.all_to_all(msg, ('hst', 'chip'), split_axis=0, concat_axis=0, tiled=T...]
    all_to_all x1 -> x0, waiting for transfers between devices: 7.72 us -> none  [across(): lax.all_to_all(msg, ('hst', 'chip'), split_axis=0, concat_axis=0, tiled=T...]
    all_to_all x1 -> x0, starting transfers between devices: 5.94 us -> none  [across(): lax.all_to_all(msg, ('hst', 'chip'), split_axis=0, concat_axis=0, tiled=T...]
    unnamed x22 -> x16, local copies, waits for them, and re-layouts: 2.47 us -> 0.04 us
    ppermute x7 -> x6, waiting for transfers between devices: 1.39 us -> 2.22 us  [shift(): return lax.ppermute(value, axis, [(i, (i + k) % size) for i in range(size)])]
    pallas_call x11, Pallas kernels: 8.11 us -> 7.35 us  [call(): pl.pallas_call(kernel, out_shape=out_shape, in_specs=in_specs, out_specs=...]
    ppermute x7 -> x6, starting transfers between devices: 4.8 us -> 4.9 us  [shift(): return lax.ppermute(value, axis, [(i, (i + k) % size) for i in range(size)])]
  transfers between devices with their start and end apart: 8 -> 6, of which waited for: 4 -> 3; matrix products, arithmetic and copies ran while one was open for 0% -> 0% of each run, Pallas kernels for 8% -> 6%
where the time goes in v8:
time: 40.1 us; the launch traced here: 39.9 us
  blocking collectives  24.5 us (61%)
  Pallas kernels  7.35 us (18%)
  starting transfers between devices  4.9 us (12%)
  waiting for transfers between devices  2.22 us (6%)
  between operations  0.81 us (2%)
    all_to_all x2, blocking collectives, across(): lax.all_to_all(msg, ('hst', 'chip'), split_axis=0, concat_axis=0, tiled=T...  24.5 us
    pallas_call x11, Pallas kernels, call(): pl.pallas_call(kernel, out_shape=out_shape, in_specs=in_specs, out_specs=...  7.35 us
    ppermute x6, starting transfers between devices, shift(): return lax.ppermute(value, axis, [(i, (i + k) % size) for i in range(size)])  4.9 us
    ppermute x6, waiting for transfers between devices, shift(): return lax.ppermute(value, axis, [(i, (i + k) % size) for i in range(size)])  2.22 us
  transfers between devices with their start and end apart: 6, of which 3 were waited for; matrix products, arithmetic and copies ran while one was open for 0% of the time, Pallas kernels for 6%

profile of v8, /device:TPU:0, one launch (start us, length us, event | category | flops | bytes accessed | tf_op | source)
XLA Modules:
  0.0 39.9 jit_solution(4830730476572521909)
XLA Ops:
  0.6 0.0 copy-start
  0.6 0.0 copy-start.1
  0.7 2.7 %prep.1 = (bf16[1280,256]{1,0:T(8,128)(2,1)S(1)}, bf16[896,256]{1,0:T(8,128)(2,1)S(1)}, bf16[256,256]{1,0:T(8,128)(2,1)S(1)}, bf16[64,256]{1,0:T(8,128)(2,1)S(1)}, bf16[64,256]{1,0:T(8,128)(2,1)S(1)}) custom-call(s32[64]{0:T(128)} %dst_hbm.1, s32[64]{0:T(128)} %src_hbm.1, s32[64]{0:T(128)} %rows_hbm.1, s32[1,1,8,8]{3,2,1,0:T(8,128)} %send_hbm.1, ...), custom_call_target="tpu_custom_call" | custom-call | tf_op jit(solution)/shard_map/prep/pallas_call | solution.py:350
  3.3 0.5 %collective-permute-start = (bf16[896,256]{1,0:T(8,128)(2,1)S(1)}, bf16[896,256]{1,0:T(8,128)(2,1)S(1)}, u32[]{:S(2)}, u32[]{:S(2)}) collective-permute-start(bf16[896,256]{1,0:T(8,128)(2,1)S(1)} %get-tuple-element.40), channel_id=1, source_target_pairs={{0,1},{1,0},{2,3},{3,2},{4,5},{5,4},{6,7},{7,6},{8,9},{9,8},{10,11... | collective-permute-start | bytes 1376264 | tf_op jit(solution)/shard_map/ppermute | solution.py:366
  3.8 0.3 rest.1
  4.1 0.0 copy-start.3
  4.1 0.0 copy-start.4
  4.1 0.0 copy-start.6
  4.2 1.1 %collective-permute-done.came_ref = bf16[896,256]{1,0:T(8,128)(2,1)S(1)} collective-permute-done((bf16[896,256]{1,0:T(8,128)(2,1)S(1)}, bf16[896,256]{1,0:T(8,128)(2,1)S(1)}, u32[]{:S(2)}, u32[]{:S(2)}) %collective-permute-start) | collective-permute-done | bytes 458784 | tf_op jit(solution)/shard_map/ppermute | solution.py:366
  5.3 0.4 collective-permute-start.1
  5.7 0.2 core_sum.1
  5.8 2.7 %collective-permute-start.2 = (bf16[512,256]{1,0:T(8,128)(2,1)S(1)}, bf16[512,256]{1,0:T(8,128)(2,1)S(1)}, u32[]{:S(2)}, u32[]{:S(2)}) collective-permute-start(bf16[512,256]{1,0:T(8,128)(2,1)S(1)} %get-tuple-element.51), channel_id=1, source_target_pairs={{0,2},{2,0},{1,3},{3,1},{4,6},{6,4},{5,7},{7,5},{8,10},{10,8},{9,1... | collective-permute-start | bytes 786440 | tf_op jit(solution)/shard_map/ppermute | solution.py:366
  8.5 13.5 %all_to_all.10.recv_ref.refs_6_ = bf16[16,16,256]{2,1,0:T(8,128)(2,1)S(1)} all-to-all(bf16[16,16,256]{2,1,0:T(8,128)(2,1)S(1)} %get-tuple-element.49), channel_id=1, replica_groups=mesh['hst'=8,'chip'=2,'core'=2] {'hst','chip'}, dimensions={0} | all-to-all | bytes 262144 | tf_op jit(solution)/shard_map/all_to_all | solution.py:410
  22.1 0.0 collective-permute-done.2.refs_0_.refs_7_
  22.1 0.1 merge.2
  22.1 0.1 collective-permute-start.3
  22.2 0.0 collective-permute-done.1.lent_ref.refs_1_
  22.3 0.4 %early_one.1 = (f32[512,256]{1,0:T(8,128)S(1)}, f32[512,256]{1,0:T(8,128)S(1)}, f32[512,256]{1,0:T(8,128)S(1)}) custom-call(bf16[1280,256]{1,0:T(8,128)(2,1)S(1)} %get-tuple-element.39.adj_ref.refs_0_, bf16[2240,256]{1,0:T(8,128)(2,1)S(1)} %collective-permute-done.1.lent_ref.refs_1_, bf16[256,256]{1,0:T(8,128)(2,1)S(1)} %copy-done, ...), custom_call_target="tpu_custom_call" | custom-call | flops 268435456 | bytes 262144 | tf_op jit(solution)/shard_map/early_one/pallas_call | solution.py:350
  22.7 0.0 copy-start.5
  22.7 0.3 mid_one.1
  23.0 0.9 %collective-permute-done.3.shared_ref = bf16[768,256]{1,0:T(8,128)(2,1)S(1)} collective-permute-done((bf16[768,256]{1,0:T(8,128)(2,1)S(1)}, bf16[768,256]{1,0:T(8,128)(2,1)S(1)}, u32[]{:S(2)}, u32[]{:S(2)}) %collective-permute-start.3) | collective-permute-done | bytes 393248 | tf_op jit(solution)/shard_map/ppermute | solution.py:366
  23.9 1.2 %middle.1 = (bf16[256,256]{1,0:T(8,128)(2,1)S(1)}, bf16[256,256]{1,0:T(8,128)(2,1)S(1)}, bf16[256,256]{1,0:T(8,128)(2,1)S(1)}, f32[256,256]{1,0:T(8,128)S(1)}, b...) custom-call(bf16[1280,256]{1,0:T(8,128)(2,1)S(1)} %get-tuple-element.39.adj_ref.refs_0_, ...), custom_call_target="tpu_custom_call" | custom-call | flops 402653184 | bytes 393216 | tf_op jit(solution)/shard_map/middle/pallas_call | solution.py:350
  25.1 1.2 %collective-permute-start.4 = (bf16[512,256]{1,0:T(8,128)(2,1)S(1)}, bf16[512,256]{1,0:T(8,128)(2,1)S(1)}, u32[]{:S(2)}, u32[]{:S(2)}) collective-permute-start(bf16[512,256]{1,0:T(8,128)(2,1)S(1)} %get-tuple-element.64), channel_id=1, source_target_pairs={{0,2},{2,0},{1,3},{3,1},{4,6},{6,4},{5,7},{7,5},{8,10},{10,8},{9,1... | collective-permute-start | bytes 786440 | tf_op jit(solution)/shard_map/ppermute | solution.py:366
  26.3 11.0 %all_to_all.11.recv_ref.refs_5_ = bf16[16,16,256]{2,1,0:T(8,128)(2,1)S(1)} all-to-all(bf16[16,16,256]{2,1,0:T(8,128)(2,1)S(1)} %get-tuple-element.62), channel_id=1, replica_groups=mesh['hst'=8,'chip'=2,'core'=2] {'hst','chip'}, dimensions={0} | all-to-all | bytes 262144 | tf_op jit(solution)/shard_map/all_to_all | solution.py:410
  37.3 0.0 collective-permute-done.4.refs_0_.refs_6_
  37.3 0.1 collective-permute-start.5
  37.4 0.0 copy-done.7
  37.4 0.3 early_two.1
  37.7 0.0 copy-start.2
  37.7 0.9 %mid_two.1 = (f32[256,256]{1,0:T(8,128)S(1)}, f32[256,256]{1,0:T(8,128)}) custom-call(bf16[1280,256]{1,0:T(8,128)(2,1)S(1)} %get-tuple-element.39.adj_ref.refs_0_, f32[256,256]{1,0:T(8,128)S(1)} %get-tuple-element.60.refs_1_, f32[256,256]{1,0:T(8,128)S(1)} %get-tuple-element.61.refs_2_, f32[256,256]{1,0:T(8,128)S(1)} %get-tuple-element.65.refs_3_, ...), custom_call_target="tpu_custom_call" | custom-call | flops 67108864 | bytes 65536 | tf_op jit(solution)/shard_map/mid_two/pallas_call | solution.py:350
  38.7 0.1 collective-permute-done.5.shared_ref
  38.8 1.0 %last.1 = bf16[256,256]{1,0:T(8,128)(2,1)} custom-call(bf16[1280,256]{1,0:T(8,128)(2,1)S(1)} %get-tuple-element.39.adj_ref.refs_0_, f32[256,256]{1,0:T(8,128)S(1)} %get-tuple-element.66.agg_ref, f32[256,256]{1,0:T(8,128)S(1)} %get-tuple-element.67.direct_ref, bf16[384,256]{1,0:T(8,128)(2,1)S(1)} %get-tuple-element.68.here_ref, ...), custom_call_target="tpu_custom_call" | custom-call | flops 100663296 | bytes 98304 | tf_op jit(solution)/shard_map/last/pallas_call | solution.py:350
  (9 shorter events, 0.1 us)
Async XLA Ops:
  0.6 5.0 %copy-start = (bf16[256,256]{1,0:T(8,128)(2,1)S(1)}, bf16[256,256]{1,0:T(8,128)(2,1)}, u32[]{:S(2)}) copy-start(bf16[256,256]{1,0:T(8,128)(2,1)} %value_ref.3) | copy-start | bytes 393220
  0.6 3.2 %copy-start.1 = (bf16[256,256]{1,0:T(8,128)(2,1)S(1)}, bf16[256,256]{1,0:T(8,128)(2,1)}, u32[]{:S(2)}) copy-start(bf16[256,256]{1,0:T(8,128)(2,1)} %up_ref.1) | copy-start | bytes 393220
  3.3 2.0 %collective-permute-start = (bf16[896,256]{1,0:T(8,128)(2,1)S(1)}, bf16[896,256]{1,0:T(8,128)(2,1)S(1)}, u32[]{:S(2)}, u32[]{:S(2)}) collective-permute-start(bf16[896,256]{1,0:T(8,128)(2,1)S(1)} %get-tuple-element.40), channel_id=1, source_target_pairs={{0,1},{1,0},{2,3},{3,2},{4,5},{5,4},{6,7},{7,6},{8,9},{9,8},{10,11... | collective-permute-start | bytes 1376264 | tf_op jit(solution)/shard_map/ppermute | solution.py:366
  4.1 18.1 %copy-start.3 = (bf16[256,256]{1,0:T(8,128)(2,1)S(1)}, bf16[256,256]{1,0:T(8,128)(2,1)}, u32[]{:S(2)}) copy-start(bf16[256,256]{1,0:T(8,128)(2,1)} %weight_ref.3) | copy-start | bytes 393220
  4.1 18.1 %copy-start.4 = (bf16[256,256]{1,0:T(8,128)(2,1)S(1)}, bf16[256,256]{1,0:T(8,128)(2,1)}, u32[]{:S(2)}) copy-start(bf16[256,256]{1,0:T(8,128)(2,1)} %self_ref.3) | copy-start | bytes 393220
  4.1 18.1 %copy-start.6 = (f32[256]{0:T(256)S(1)}, f32[256]{0:T(256)}, u32[]{:S(2)}) copy-start(f32[256]{0:T(256)} %bias_ref.2) | copy-start | bytes 3076
  5.3 16.9 %collective-permute-start.1 = (bf16[2240,256]{1,0:T(8,128)(2,1)S(1)}, bf16[2240,256]{1,0:T(8,128)(2,1)S(1)}, u32[]{:S(2)}, u32[]{:S(2)}) collective-permute-start(bf16[2240,256]{1,0:T(8,128)(2,1)S(1)} %get-tuple-element.42), channel_id=1, source_target_pairs={{0,1},{1,0},{2,3},{3,2},{4,5},{5,4},{6,7},{7,6},{8,9},{9,8},{10,11... | collective-permute-start | bytes 3440648 | tf_op jit(solution)/shard_map/ppermute | solution.py:366
  5.8 16.2 %collective-permute-start.2 = (bf16[512,256]{1,0:T(8,128)(2,1)S(1)}, bf16[512,256]{1,0:T(8,128)(2,1)S(1)}, u32[]{:S(2)}, u32[]{:S(2)}) collective-permute-start(bf16[512,256]{1,0:T(8,128)(2,1)S(1)} %get-tuple-element.51), channel_id=1, source_target_pairs={{0,2},{2,0},{1,3},{3,1},{4,6},{6,4},{5,7},{7,5},{8,10},{10,8},{9,1... | collective-permute-start | bytes 786440 | tf_op jit(solution)/shard_map/ppermute | solution.py:366
  22.1 1.8 %collective-permute-start.3 = (bf16[768,256]{1,0:T(8,128)(2,1)S(1)}, bf16[768,256]{1,0:T(8,128)(2,1)S(1)}, u32[]{:S(2)}, u32[]{:S(2)}) collective-permute-start(bf16[768,256]{1,0:T(8,128)(2,1)S(1)} %get-tuple-element.56.here_ref), channel_id=1, source_target_pairs={{0,1},{1,0},{2,3},{3,2},{4,5},{5,4},{6,7},{7,6},{8,9},{9,8},{10,11... | collective-permute-start | bytes 1179656 | tf_op jit(solution)/shard_map/ppermute | solution.py:366
  22.7 1.2 %copy-start.5 = (bf16[256,256]{1,0:T(8,128)(2,1)S(1)}, bf16[256,256]{1,0:T(8,128)(2,1)}, u32[]{:S(2)}) copy-start(bf16[256,256]{1,0:T(8,128)(2,1)} %neigh_one_ref.1) | copy-start | bytes 393220
  23.9 13.5 %copy-start.7 = (f32[256]{0:T(256)S(1)}, f32[256]{0:T(256)}, u32[]{:S(2)}) copy-start(f32[256]{0:T(256)} %bias_ref.3) | copy-start | bytes 3076
  25.1 12.2 %collective-permute-start.4 = (bf16[512,256]{1,0:T(8,128)(2,1)S(1)}, bf16[512,256]{1,0:T(8,128)(2,1)S(1)}, u32[]{:S(2)}, u32[]{:S(2)}) collective-permute-start(bf16[512,256]{1,0:T(8,128)(2,1)S(1)} %get-tuple-element.64), channel_id=1, source_target_pairs={{0,2},{2,0},{1,3},{3,1},{4,6},{6,4},{5,7},{7,5},{8,10},{10,8},{9,1... | collective-permute-start | bytes 786440 | tf_op jit(solution)/shard_map/ppermute | solution.py:366
  37.3 1.5 %collective-permute-start.5 = (bf16[384,256]{1,0:T(8,128)(2,1)S(1)}, bf16[384,256]{1,0:T(8,128)(2,1)S(1)}, u32[]{:S(2)}, u32[]{:S(2)}) collective-permute-start(bf16[384,256]{1,0:T(8,128)(2,1)S(1)} %get-tuple-element.68.here_ref), channel_id=1, source_target_pairs={{0,1},{1,0},{2,3},{3,2},{4,5},{5,4},{6,7},{7,6},{8,9},{9,8},{10,11... | collective-permute-start | bytes 589832 | tf_op jit(solution)/shard_map/ppermute | solution.py:366
  37.7 1.1 %copy-start.2 = (bf16[256,256]{1,0:T(8,128)(2,1)S(1)}, bf16[256,256]{1,0:T(8,128)(2,1)}, u32[]{:S(2)}) copy-start(bf16[256,256]{1,0:T(8,128)(2,1)} %neigh_two_ref.1) | copy-start | bytes 393220

commit v9 on v8

--- a/solution.py
+++ b/solution.py
@@ -43,15 +43,17 @@
     return jnp.concatenate(parts, 0).astype(BF16)
 
 
-def column(chips, far, rows, side, whole_ref, out_ref, base):
+def column(chips, far, rows, side, adj_ref, far_t, out_ref):
     each = rows + far
+    own_rows = chips * CORES * rows
+    for j in range(far_t.shape[0] // rows):
+        low = own_rows + j * rows
+        far_t[j * rows : (j + 1) * rows, :] = adj_ref[low : low + rows, :].T
     for x in range(chips):
         d = x * CORES + side
-        low = pl.multiple_of(d * rows, rows)
-        at = base + x * each
-        out_ref[at : at + rows, :] = whole_ref[pl.ds(low, rows), :]
-        low = pl.multiple_of(chips * CORES * rows + d * far, far)
-        out_ref[at + rows : at + each, :] = whole_ref[pl.ds(low, far), :]
+        at = x * each
+        out_ref[at : at + rows, :] = adj_ref[pl.ds(pl.multiple_of(d * rows, rows), rows), :].T
+        out_ref[at + rows : at + each, :] = far_t[pl.ds(pl.multiple_of(d * far, far), far), :]
 
 
 def prep_kernel(
@@ -64,7 +66,7 @@
     features_hbm,
     cot_hbm,
     neigh_two_hbm,
-    adj_t_ref,
+    adj_ref,
     give_ref,
     up_ref,
     picked_ref,
@@ -77,6 +79,7 @@
     features_ref,
     cot_ref,
     neigh_two_ref,
+    far_t,
     col,
     sems,
     *accs,
@@ -114,7 +117,6 @@
     copies[3].wait()
     pick_ref[...] = pick_matrix(send_ref, rows)
     picked_ref[...] = dot(pick_ref[...], features_ref[...]).astype(BF16)
-    give_ref[chips * (rows + far) :, :] = features_ref[...]
     for copy in copies[4:7]:
         copy.wait()
     place = lax.broadcasted_iota(jnp.int32, (part, blk), 0)
@@ -132,26 +134,24 @@
     for b in range(bpd):
         for j in range(sources):
             block = jnp.concatenate([acc[b * sources + j] for acc in accs], 0).astype(BF16)
-            adj_t_ref[j * blk : (j + 1) * blk, b * blk : (b + 1) * blk] = block.T
-    column(chips, far, rows, 1 - lax.axis_index("core"), adj_t_ref, col, 0)
-    give_ref[: chips * (rows + far), :] = dot(col[...], u).astype(BF16)
-
-
-def rest_kernel(chips, adj_t_ref, up_ref, cot_ref, pick_ref, adj_ref, col_ref, keep_ref, lend_ref):
-    far, rows = pick_ref.shape
-    core = lax.axis_index("core")
-    all_rows = adj_t_ref.shape[0]
-    count = chips * (rows + far)
-    for j in range(all_rows // rows):
-        block = adj_t_ref[j * rows : (j + 1) * rows, :].T
-        adj_ref[j * rows : (j + 1) * rows, :] = block
-        lend_ref[j * rows : (j + 1) * rows, :] = block
-    column(chips, far, rows, core, adj_t_ref, col_ref, 0)
-    column(chips, far, rows, 1 - core, adj_t_ref, lend_ref, all_rows)
-    low = all_rows + count
+            low = j // bpd * rows + b * blk
+            left = j % bpd * blk
+            adj_ref[low : low + blk, left : left + blk] = block
+    column(chips, far, rows, 1 - lax.axis_index("core"), adj_ref, far_t, col)
+    give_ref[...] = dot(col[...], u).astype(BF16)
+
+
+def rest_kernel(
+    chips, adj_ref, up_ref, cot_ref, value_ref, col_ref, keep_ref, lend_ref, far_t
+):
+    rows = up_ref.shape[0]
+    far = col_ref.shape[0] // chips - rows
+    column(chips, far, rows, lax.axis_index("core"), adj_ref, far_t, col_ref)
+    keep_ref[...] = dot(col_ref[...], up_ref[...]).astype(BF16)
+    low = adj_ref.shape[0]
+    lend_ref[:low, :] = adj_ref[...]
     lend_ref[low : low + rows, :] = cot_ref[...]
-    lend_ref[low + rows :, :] = pick_ref[...]
-    keep_ref[...] = dot(col_ref[...], up_ref[...]).astype(BF16)
+    lend_ref[low + rows :, :] = value_ref[...]
 
 
 def deal(chips, hosts, total, picked, value, mine_ref, msg_ref, to_refs):
@@ -178,7 +178,7 @@
     chips, hosts, keep_ref, came_ref, value_ref, picked_ref, mine_ref, msg_ref, *rest
 ):
     total = rest[-1]
-    total[...] = keep_ref[...].astype(F32) + came_ref[: total.shape[0], :].astype(F32)
+    total[...] = keep_ref[...].astype(F32) + came_ref[...].astype(F32)
     picked = picked_ref[...].astype(F32)
     deal(chips, hosts, total, picked, value_ref[...], mine_ref, msg_ref, rest[:-1])
 
@@ -194,21 +194,27 @@
     return jnp.concatenate(blocks, 0).astype(BF16)
 
 
-def merge_kernel(chips, hosts, with_terms, recv_ref, mine_ref, *refs):
+def merge_kernel(chips, hosts, with_terms, recv_ref, mine_ref, pick_ref, *refs):
     came, (out_ref, sum_ref) = refs[: chips - 1], refs[chips - 1 :]
     rows = mine_ref.shape[0]
     total = mine_ref[...]
     for k, ref in enumerate(came):
         total = total + ref[:rows, :].astype(F32)
         out_ref[k * rows : (k + 1) * rows, :] = ref[rows:, :]
+    if with_terms:
+        total = total + returned(pick_ref, recv_ref, hosts, chips)
     sum_ref[...] = total
     low = len(came) * rows
     halo = halo_part(recv_ref, hosts, chips, 0)
     high = low + halo.shape[0]
     out_ref[low:high, :] = halo
     if with_terms:
-        out_ref[high : high + rows, :] = total.astype(BF16)
-        out_ref[high + rows :, :] = halo_part(recv_ref, hosts, chips, 1)
+        out_ref[high:, :] = total.astype(BF16)
+
+
+def returned(pick_ref, recv_ref, hosts, chips):
+    back = halo_part(recv_ref, hosts, chips, 1)
+    return dot_tn(jnp.concatenate([pick_ref[...]] * chips, 0), back)
 
 
 def own_chip(adj_refs, blocks):
@@ -225,19 +231,20 @@
 
 
 def early_one_kernel(
-    chips, adj_ref, lent_ref, value_ref, came_ref, self_ref, bias_ref, up_ref, weight_ref,
-    agg_ref, direct_ref, grad_ref,
+    chips, adj_ref, lent_ref, value_ref, self_ref, bias_ref, up_ref, weight_ref,
+    agg_ref, direct_ref, grad_ref, col_ref, far_t,
 ):
     value = value_ref[...]
     rows = value.shape[0]
-    there = came_ref[came_ref.shape[0] - rows :, :]
+    low = adj_ref.shape[0]
+    there = lent_ref[low + rows :, :]
     agg_ref[...] = own_chip((adj_ref, lent_ref), (value, there))
     both = jnp.concatenate([value, there], 0)
     direct_ref[...] = dot(both, self_ref[...]) + bias_ref[...].reshape(1, -1)
-    count = came_ref.shape[0] - rows
-    high = lent_ref.shape[0] - (count // chips - rows)
-    both = jnp.concatenate([up_ref[...], lent_ref[high - rows : high, :]], 0)
+    both = jnp.concatenate([up_ref[...], lent_ref[low : low + rows, :]], 0)
     grad_ref[...] = dot_nt(both, weight_ref[...])
+    far = col_ref.shape[0] // chips - rows
+    column(chips, far, rows, lax.axis_index("core"), lent_ref, far_t, col_ref)
 
 
 def early_two_kernel(
@@ -263,11 +270,12 @@
             low = pl.multiple_of((x * CORES + core) * rows, rows)
             agg = agg + dot(adj_ref[pl.ds(low, rows), :], ref[rows:, :])
         agg_out[i * rows : (i + 1) * rows, :] = agg
-    back = halo_part(recv_ref, hosts, chips, 1)
-    grad = part_ref[:rows, :] + sum_ref[...]
-    grad_ref[:rows, :] = grad + dot_tn(jnp.concatenate([pick_ref[...]] * chips, 0), back)
     if count > 1:
+        grad_ref[:rows, :] = part_ref[:rows, :] + sum_ref[...]
         grad_ref[rows:, :] = part_ref[rows:, :]
+    else:
+        grad = part_ref[...] + sum_ref[...]
+        grad_ref[...] = grad + returned(pick_ref, recv_ref, hosts, chips)
 
 
 def full_aggregate(chips, far, rows, adj_refs, agg_ref, here_ref, shared_ref, halo):
@@ -297,6 +305,7 @@
     adj_ref,
     lent_ref,
     col_ref,
+    col_two_ref,
     agg_ref,
     direct_ref,
     grad_ref,
@@ -313,7 +322,6 @@
 ):
     to_refs, halo, total = rest[:-2], rest[-2], rest[-1]
     far, rows = pick_ref.shape
-    count = total.shape[0]
     agg = full_aggregate(
         chips, far, rows, (adj_ref, lent_ref), agg_ref, here_ref, shared_ref, halo
     )
@@ -323,17 +331,12 @@
     hidden_ref[...] = hidden[:rows]
     there_ref[...] = hidden[rows:]
     low = (chips - 1) * rows + chips * far
-    base = lent_ref.shape[0] - far - rows - count
-    pick_two = lent_ref[base + count + rows :, :]
-    add = shared_ref[low : low + rows, :].astype(F32)
-    add = add + dot_tn(jnp.concatenate([pick_two] * chips, 0), shared_ref[low + rows :, :])
+    add = shared_ref[low:, :].astype(F32)
     grad = jnp.concatenate([grad_ref[:rows, :], grad_ref[rows:, :] + add], 0)
     grad_pre = (grad * sigmoid * (1.0 + pre * (1.0 - sigmoid))).astype(BF16)
     grad_pre_ref[...] = grad_pre[:rows]
     u = dot_nt(grad_pre, neigh_one_ref[...]).astype(BF16)
-    total[...] = dot(col_ref[...], u[:rows]) + dot(
-        lent_ref[base : base + count, :], u[rows:]
-    )
+    total[...] = dot(col_ref[...], u[:rows]) + dot(col_two_ref[...], u[rows:])
     picked = dot(pick_ref[...], hidden[:rows])
     deal(chips, hosts, total, picked, hidden[:rows], mine_ref, msg_ref, to_refs)
 
@@ -411,18 +414,19 @@
         here, summed = call(
             functools.partial(merge_kernel, chips, hosts, with_terms),
             "merge",
-            (shape(halo_rows + (rows + chips * far) * with_terms, width), sum_shape),
-            [VMEM] * (1 + chips),
-            (recv, mine, *terms),
+            (shape(halo_rows + rows * with_terms, width), sum_shape),
+            [VMEM] * (2 + chips),
+            (recv, mine, pick, *terms),
         )
         return terms, recv, here, summed, shift(here, "core", 1)
 
-    adj_t, give, up, picked, pick = call(
+    far_t = pltpu.VMEM((chips * CORES * far, rows), BF16)
+    adj, give, up, picked, pick = call(
         functools.partial(prep_kernel, chips),
         "prep",
         (
             shape(all_rows, rows),
-            shape(count + rows, width),
+            shape(count, width),
             rows_shape,
             shape(far, width),
             shape(far, rows),
@@ -450,26 +454,22 @@
             pltpu.VMEM(features.shape, BF16),
             pltpu.VMEM(cotangent.shape, BF16),
             pltpu.VMEM(neigh_two.shape, BF16),
+            far_t,
             pltpu.VMEM((count, rows), BF16),
             pltpu.SemaphoreType.DMA((7 + CHUNKS,)),
         ]
         + [pltpu.VMEM(((rows // blk) * (all_rows // blk), blk // PARTS, blk), F32)] * PARTS,
     )
     came = shift(give, "core", 1)
-    adj, col, keep, lend = call(
+    col, keep, lend = call(
         functools.partial(rest_kernel, chips),
         "rest",
-        (
-            shape(all_rows, rows),
-            shape(count, rows),
-            shape(count, width),
-            shape(all_rows + count + rows + far, width),
-        ),
+        (shape(count, rows), shape(count, width), shape(all_rows + 2 * rows, width)),
         [VMEM] * 4,
-        (adj_t, up, cotangent, pick),
+        (adj, up, cotangent, features),
+        [far_t],
         flops=3 * square,
     )
-    came, lend = lax.optimization_barrier((came, lend))
     lent = shift(lend, "core", 1)
     mine, msg, *to = call(
         functools.partial(core_sum_kernel, chips, hosts),
@@ -478,14 +478,16 @@
         [VMEM] * 4,
         (keep, came, features, picked),
         [total],
+        flops=60 * square,
     )
     terms, recv, here, summed, shared = across(mine, msg, to, 1)
-    agg, direct, grad = call(
+    agg, direct, grad, col_two = call(
         functools.partial(early_one_kernel, chips),
         "early_one",
-        (both_shape,) * 3,
-        [VMEM] * 8,
-        (adj, lent, features, came, self_one, bias_one, cotangent, self_two),
+        (both_shape,) * 3 + (shape(count, rows),),
+        [VMEM] * 7,
+        (adj, lent, features, self_one, bias_one, cotangent, self_two),
+        [far_t],
         flops=8 * square,
     )
     agg, grad = call(
@@ -500,8 +502,8 @@
         functools.partial(middle_kernel, chips, hosts),
         "middle",
         (rows_shape,) * 3 + dealt,
-        [VMEM] * 10,
-        (adj, lent, col, agg, direct, grad, pick, here, shared, neigh_one),
+        [VMEM] * 11,
+        (adj, lent, col, col_two, agg, direct, grad, pick, here, shared, neigh_one),
         [halo, total],
         flops=12 * square,
     )

time: 40.1 us -> 39.5 us (0.985)
  transfers between devices with their start and end apart: 6 -> 6, of which waited for: 3 -> 3; matrix products, arithmetic and copies ran while one was open for 0% -> 0% of each run, Pallas kernels for 6% -> 7%
where the time goes in v9:
time: 39.5 us; the launch traced here: 39.2 us
  blocking collectives  24.3 us (62%)
  Pallas kernels  7.41 us (19%)
  starting transfers between devices  4.88 us (12%)
  waiting for transfers between devices  1.83 us (5%)
  between operations  0.79 us (2%)
    all_to_all x2, blocking collectives, across(): lax.all_to_all(msg, ('hst', 'chip'), split_axis=0, concat_axis=0, tiled=T...  24.3 us
    pallas_call x11, Pallas kernels, call(): pl.pallas_call(kernel, out_shape=out_shape, in_specs=in_specs, out_specs=...  7.41 us
    ppermute x6, starting transfers between devices, shift(): return lax.ppermute(value, axis, [(i, (i + k) % size) for i in range(size)])  4.88 us
    ppermute x6, waiting for transfers between devices, shift(): return lax.ppermute(value, axis, [(i, (i + k) % size) for i in range(size)])  1.83 us
  transfers between devices with their start and end apart: 6, of which 3 were waited for; matrix products, arithmetic and copies ran while one was open for 0% of the time, Pallas kernels for 7%

profile of v9, /device:TPU:0, one launch (start us, length us, event | category | flops | bytes accessed | tf_op | source)
XLA Modules:
  0.0 39.2 jit_solution(14091072231296702506)
XLA Ops:
  0.6 0.0 copy-start
  0.6 0.0 copy-start.1
  0.7 2.6 %prep.1 = (bf16[1280,256]{1,0:T(8,128)(2,1)S(1)}, bf16[640,256]{1,0:T(8,128)(2,1)S(1)}, bf16[256,256]{1,0:T(8,128)(2,1)S(1)}, bf16[64,256]{1,0:T(8,128)(2,1)S(1)}, bf16[64,256]{1,0:T(8,128)(2,1)S(1)}) custom-call(s32[64]{0:T(128)} %dst_hbm.1, s32[64]{0:T(128)} %src_hbm.1, s32[64]{0:T(128)} %rows_hbm.1, s32[1,1,8,8]{3,2,1,0:T(8,128)} %send_hbm.1, ...), custom_call_target="tpu_custom_call" | custom-call | tf_op jit(solution)/shard_map/prep/pallas_call | solution.py:353
  3.3 0.5 %collective-permute-start.1 = (bf16[640,256]{1,0:T(8,128)(2,1)S(1)}, bf16[640,256]{1,0:T(8,128)(2,1)S(1)}, u32[]{:S(2)}, u32[]{:S(2)}) collective-permute-start(bf16[640,256]{1,0:T(8,128)(2,1)S(1)} %get-tuple-element.42), channel_id=1, source_target_pairs={{0,1},{1,0},{2,3},{3,2},{4,5},{5,4},{6,7},{7,6},{8,9},{9,8},{10,11... | collective-permute-start | bytes 983048 | tf_op jit(solution)/shard_map/ppermute | solution.py:369
  3.8 0.0 copy-done
  3.8 0.0 copy-done.1
  3.8 0.3 rest.1
  4.1 0.1 collective-permute-start
  4.3 0.8 %collective-permute-done.1.came_ref = bf16[640,256]{1,0:T(8,128)(2,1)S(1)} collective-permute-done((bf16[640,256]{1,0:T(8,128)(2,1)S(1)}, bf16[640,256]{1,0:T(8,128)(2,1)S(1)}, u32[]{:S(2)}, u32[]{:S(2)}) %collective-permute-start.1) | collective-permute-done | bytes 327712 | tf_op jit(solution)/shard_map/ppermute | solution.py:369
  5.1 0.2 core_sum.1
  5.2 2.9 %collective-permute-start.2 = (bf16[512,256]{1,0:T(8,128)(2,1)S(1)}, bf16[512,256]{1,0:T(8,128)(2,1)S(1)}, u32[]{:S(2)}, u32[]{:S(2)}) collective-permute-start(bf16[512,256]{1,0:T(8,128)(2,1)S(1)} %get-tuple-element.47), channel_id=1, source_target_pairs={{0,2},{2,0},{1,3},{3,1},{4,6},{6,4},{5,7},{7,5},{8,10},{10,8},{9,1... | collective-permute-start | bytes 786440 | tf_op jit(solution)/shard_map/ppermute | solution.py:369
  8.2 13.5 %all_to_all.10.recv_ref.refs_6_ = bf16[16,16,256]{2,1,0:T(8,128)(2,1)S(1)} all-to-all(bf16[16,16,256]{2,1,0:T(8,128)(2,1)S(1)} %get-tuple-element.44), channel_id=1, replica_groups=mesh['hst'=8,'chip'=2,'core'=2] {'hst','chip'}, dimensions={0} | all-to-all | bytes 262144 | tf_op jit(solution)/shard_map/all_to_all | solution.py:413
  21.7 0.0 collective-permute-done.2.refs_0_.refs_7_
  21.7 0.2 merge.2
  21.9 0.1 collective-permute-start.3
  22.0 0.0 collective-permute-done.lent_ref.refs_1_
  22.0 0.0 copy-done.3
  22.1 0.4 %early_one.1 = (f32[512,256]{1,0:T(8,128)S(1)}, f32[512,256]{1,0:T(8,128)S(1)}, f32[512,256]{1,0:T(8,128)S(1)}, bf16[640,256]{1,0:T(8,128)(2,1)S(1)}) custom-call(bf16[1280,256]{1,0:T(8,128)(2,1)S(1)} %get-tuple-element.34.adj_ref.refs_0_, bf16[1792,256]{1,0:T(8,128)(2,1)S(1)} %collective-permute-done.lent_ref.refs_1_, bf16[256,256]{1,0:T(8,128)(2,1)S(1)} %copy-done, ...), custom_call_target="tpu_custom_call" | custom-call | flops 268435456 | bytes 262144 | tf_op jit(solution)/shard_map/early_one/pallas_call | solution.py:353
  22.5 0.0 copy-start.5
  22.5 0.2 mid_one.1
  22.8 0.9 %collective-permute-done.3.shared_ref = bf16[640,256]{1,0:T(8,128)(2,1)S(1)} collective-permute-done((bf16[640,256]{1,0:T(8,128)(2,1)S(1)}, bf16[640,256]{1,0:T(8,128)(2,1)S(1)}, u32[]{:S(2)}, u32[]{:S(2)}) %collective-permute-start.3) | collective-permute-done | bytes 327712 | tf_op jit(solution)/shard_map/ppermute | solution.py:369
  23.6 1.1 %middle.1 = (bf16[256,256]{1,0:T(8,128)(2,1)S(1)}, bf16[256,256]{1,0:T(8,128)(2,1)S(1)}, bf16[256,256]{1,0:T(8,128)(2,1)S(1)}, f32[256,256]{1,0:T(8,128)S(1)}, b...) custom-call(bf16[1280,256]{1,0:T(8,128)(2,1)S(1)} %get-tuple-element.34.adj_ref.refs_0_, ...), custom_call_target="tpu_custom_call" | custom-call | flops 402653184 | bytes 393216 | tf_op jit(solution)/shard_map/middle/pallas_call | solution.py:353
  24.7 0.0 copy-start.2
  24.7 1.2 %collective-permute-start.4 = (bf16[512,256]{1,0:T(8,128)(2,1)S(1)}, bf16[512,256]{1,0:T(8,128)(2,1)S(1)}, u32[]{:S(2)}, u32[]{:S(2)}) collective-permute-start(bf16[512,256]{1,0:T(8,128)(2,1)S(1)} %get-tuple-element.60), channel_id=1, source_target_pairs={{0,2},{2,0},{1,3},{3,1},{4,6},{6,4},{5,7},{7,5},{8,10},{10,8},{9,1... | collective-permute-start | bytes 786440 | tf_op jit(solution)/shard_map/ppermute | solution.py:369
  25.9 10.8 %all_to_all.11.recv_ref.refs_5_ = bf16[16,16,256]{2,1,0:T(8,128)(2,1)S(1)} all-to-all(bf16[16,16,256]{2,1,0:T(8,128)(2,1)S(1)} %get-tuple-element.58), channel_id=1, replica_groups=mesh['hst'=8,'chip'=2,'core'=2] {'hst','chip'}, dimensions={0} | all-to-all | bytes 262144 | tf_op jit(solution)/shard_map/all_to_all | solution.py:413
  36.7 0.0 collective-permute-done.4.refs_0_.refs_6_
  36.7 0.1 collective-permute-start.5
  36.8 0.3 early_two.1
  37.1 0.9 %mid_two.1 = (f32[256,256]{1,0:T(8,128)S(1)}, f32[256,256]{1,0:T(8,128)}) custom-call(bf16[1280,256]{1,0:T(8,128)(2,1)S(1)} %get-tuple-element.34.adj_ref.refs_0_, f32[256,256]{1,0:T(8,128)S(1)} %get-tuple-element.56.refs_1_, f32[256,256]{1,0:T(8,128)S(1)} %get-tuple-element.57.refs_2_, f32[256,256]{1,0:T(8,128)S(1)} %get-tuple-element.61.refs_3_, ...), custom_call_target="tpu_custom_call" | custom-call | flops 67108864 | bytes 65536 | tf_op jit(solution)/shard_map/mid_two/pallas_call | solution.py:353
  38.0 0.2 collective-permute-done.5.shared_ref
  38.2 0.0 copy-done.2
  38.2 1.0 %last.1 = bf16[256,256]{1,0:T(8,128)(2,1)} custom-call(bf16[1280,256]{1,0:T(8,128)(2,1)S(1)} %get-tuple-element.34.adj_ref.refs_0_, f32[256,256]{1,0:T(8,128)S(1)} %get-tuple-element.62.agg_ref, f32[256,256]{1,0:T(8,128)S(1)} %get-tuple-element.63.direct_ref, bf16[384,256]{1,0:T(8,128)(2,1)S(1)} %get-tuple-element.64.here_ref, ...), custom_call_target="tpu_custom_call" | custom-call | flops 100663296 | bytes 98304 | tf_op jit(solution)/shard_map/last/pallas_call | solution.py:353
  (9 shorter events, 0.1 us)
Async XLA Ops:
  0.6 3.2 %copy-start = (bf16[256,256]{1,0:T(8,128)(2,1)S(1)}, bf16[256,256]{1,0:T(8,128)(2,1)}, u32[]{:S(2)}) copy-start(bf16[256,256]{1,0:T(8,128)(2,1)} %value_ref.5) | copy-start | bytes 393220
  0.6 3.2 %copy-start.1 = (bf16[256,256]{1,0:T(8,128)(2,1)S(1)}, bf16[256,256]{1,0:T(8,128)(2,1)}, u32[]{:S(2)}) copy-start(bf16[256,256]{1,0:T(8,128)(2,1)} %up_ref.1) | copy-start | bytes 393220
  3.3 1.8 %collective-permute-start.1 = (bf16[640,256]{1,0:T(8,128)(2,1)S(1)}, bf16[640,256]{1,0:T(8,128)(2,1)S(1)}, u32[]{:S(2)}, u32[]{:S(2)}) collective-permute-start(bf16[640,256]{1,0:T(8,128)(2,1)S(1)} %get-tuple-element.42), channel_id=1, source_target_pairs={{0,1},{1,0},{2,3},{3,2},{4,5},{5,4},{6,7},{7,6},{8,9},{9,8},{10,11... | collective-permute-start | bytes 983048 | tf_op jit(solution)/shard_map/ppermute | solution.py:369
  4.1 17.9 %collective-permute-start = (bf16[1792,256]{1,0:T(8,128)(2,1)S(1)}, bf16[1792,256]{1,0:T(8,128)(2,1)S(1)}, u32[]{:S(2)}, u32[]{:S(2)}) collective-permute-start(bf16[1792,256]{1,0:T(8,128)(2,1)S(1)} %get-tuple-element.36), channel_id=1, source_target_pairs={{0,1},{1,0},{2,3},{3,2},{4,5},{5,4},{6,7},{7,6},{8,9},{9,8},{10,11... | collective-permute-start | bytes 2752520 | tf_op jit(solution)/shard_map/ppermute | solution.py:369
  5.1 17.0 %copy-start.3 = (bf16[256,256]{1,0:T(8,128)(2,1)S(1)}, bf16[256,256]{1,0:T(8,128)(2,1)}, u32[]{:S(2)}) copy-start(bf16[256,256]{1,0:T(8,128)(2,1)} %weight_ref.3) | copy-start | bytes 393220
  5.1 17.0 %copy-start.4 = (bf16[256,256]{1,0:T(8,128)(2,1)S(1)}, bf16[256,256]{1,0:T(8,128)(2,1)}, u32[]{:S(2)}) copy-start(bf16[256,256]{1,0:T(8,128)(2,1)} %self_ref.3) | copy-start | bytes 393220
  5.1 17.0 %copy-start.6 = (f32[256]{0:T(256)S(1)}, f32[256]{0:T(256)}, u32[]{:S(2)}) copy-start(f32[256]{0:T(256)} %bias_ref.2) | copy-start | bytes 3076
  5.2 16.5 %collective-permute-start.2 = (bf16[512,256]{1,0:T(8,128)(2,1)S(1)}, bf16[512,256]{1,0:T(8,128)(2,1)S(1)}, u32[]{:S(2)}, u32[]{:S(2)}) collective-permute-start(bf16[512,256]{1,0:T(8,128)(2,1)S(1)} %get-tuple-element.47), channel_id=1, source_target_pairs={{0,2},{2,0},{1,3},{3,1},{4,6},{6,4},{5,7},{7,5},{8,10},{10,8},{9,1... | collective-permute-start | bytes 786440 | tf_op jit(solution)/shard_map/ppermute | solution.py:369
  21.9 1.7 %collective-permute-start.3 = (bf16[640,256]{1,0:T(8,128)(2,1)S(1)}, bf16[640,256]{1,0:T(8,128)(2,1)S(1)}, u32[]{:S(2)}, u32[]{:S(2)}) collective-permute-start(bf16[640,256]{1,0:T(8,128)(2,1)S(1)} %get-tuple-element.52.here_ref), channel_id=1, source_target_pairs={{0,1},{1,0},{2,3},{3,2},{4,5},{5,4},{6,7},{7,6},{8,9},{9,8},{10,11... | collective-permute-start | bytes 983048 | tf_op jit(solution)/shard_map/ppermute | solution.py:369
  22.5 1.1 %copy-start.5 = (bf16[256,256]{1,0:T(8,128)(2,1)S(1)}, bf16[256,256]{1,0:T(8,128)(2,1)}, u32[]{:S(2)}) copy-start(bf16[256,256]{1,0:T(8,128)(2,1)} %neigh_one_ref.1) | copy-start | bytes 393220
  23.6 13.1 %copy-start.7 = (f32[256]{0:T(256)S(1)}, f32[256]{0:T(256)}, u32[]{:S(2)}) copy-start(f32[256]{0:T(256)} %bias_ref.3) | copy-start | bytes 3076
  24.7 13.5 %copy-start.2 = (bf16[256,256]{1,0:T(8,128)(2,1)S(1)}, bf16[256,256]{1,0:T(8,128)(2,1)}, u32[]{:S(2)}) copy-start(bf16[256,256]{1,0:T(8,128)(2,1)} %neigh_two_ref.1) | copy-start | bytes 393220
  24.7 11.9 %collective-permute-start.4 = (bf16[512,256]{1,0:T(8,128)(2,1)S(1)}, bf16[512,256]{1,0:T(8,128)(2,1)S(1)}, u32[]{:S(2)}, u32[]{:S(2)}) collective-permute-start(bf16[512,256]{1,0:T(8,128)(2,1)S(1)} %get-tuple-element.60), channel_id=1, source_target_pairs={{0,2},{2,0},{1,3},{3,1},{4,6},{6,4},{5,7},{7,5},{8,10},{10,8},{9,1... | collective-permute-start | bytes 786440 | tf_op jit(solution)/shard_map/ppermute | solution.py:369
  36.7 1.5 %collective-permute-start.5 = (bf16[384,256]{1,0:T(8,128)(2,1)S(1)}, bf16[384,256]{1,0:T(8,128)(2,1)S(1)}, u32[]{:S(2)}, u32[]{:S(2)}) collective-permute-start(bf16[384,256]{1,0:T(8,128)(2,1)S(1)} %get-tuple-element.64.here_ref), channel_id=1, source_target_pairs={{0,1},{1,0},{2,3},{3,2},{4,5},{5,4},{6,7},{7,6},{8,9},{9,8},{10,11... | collective-permute-start | bytes 589832 | tf_op jit(solution)/shard_map/ppermute | solution.py:369

commit v10 on v9

--- a/solution.py
+++ b/solution.py
@@ -12,6 +12,7 @@
 MIB = 1024 * 1024
 CHUNKS = 8
 PARTS = 4
+HALVES = 2
 CORES = 2
 
 VMEM = pl.BlockSpec(memory_space=pltpu.VMEM)
@@ -24,10 +25,6 @@
 
 def dot_nt(a, b):
     return lax.dot_general(a, b, (((1,), (1,)), ((), ())), preferred_element_type=F32)
-
-
-def dot_tn(a, b):
-    return lax.dot_general(a, b, (((0,), (0,)), ((), ())), preferred_element_type=F32)
 
 
 def pick_matrix(send_ref, rows):
@@ -86,19 +83,20 @@
 ):
     tiles, blk = tile_buf.shape[0], tile_buf.shape[1]
     each = tiles // CHUNKS
-    pairs = [
+    first = CHUNKS * 3 // 4
+    chunks = [
+        (tile_hbm.at[pl.ds(c * each, each)], tile_buf.at[pl.ds(c * each, each)])
+        for c in range(CHUNKS)
+    ]
+    pairs = [(dst_hbm, dst_ref), (src_hbm, src_ref), (rows_hbm, rows_ref)]
+    pairs += chunks[:first]
+    pairs += [
         (cot_hbm, cot_ref),
         (neigh_two_hbm, neigh_two_ref),
         (features_hbm, features_ref),
         (send_hbm, send_ref),
-        (dst_hbm, dst_ref),
-        (src_hbm, src_ref),
-        (rows_hbm, rows_ref),
     ]
-    pairs += [
-        (tile_hbm.at[pl.ds(c * each, each)], tile_buf.at[pl.ds(c * each, each)])
-        for c in range(CHUNKS)
-    ]
+    pairs += chunks[first:]
     copies = [pltpu.make_async_copy(a, b, sems.at[i]) for i, (a, b) in enumerate(pairs)]
     for copy in copies:
         copy.start()
@@ -109,27 +107,28 @@
     far = send_ref.shape[2] * send_ref.shape[3]
     for acc in accs:
         acc[...] = jnp.zeros_like(acc)
-    copies[0].wait()
-    copies[1].wait()
+    place = lax.broadcasted_iota(jnp.int32, (part, blk), 0)
+
+    def add(t, carry):
+        slot = dst_ref[t] * sources + src_ref[t]
+        for i, acc in enumerate(accs):
+            value = tile_buf[t, i * part : (i + 1) * part, :].astype(F32)
+            acc[slot] += jnp.where(place < rows_ref[t] - i * part, value, 0.0)
+        return carry
+
+    for copy in copies[:3]:
+        copy.wait()
+    for c in range(first):
+        copies[3 + c].wait()
+        lax.fori_loop(c * each, (c + 1) * each, add, 0, unroll=True)
+    for copy in copies[3 + first : 7 + first]:
+        copy.wait()
     u = dot_nt(cot_ref[...], neigh_two_ref[...]).astype(BF16)
     up_ref[...] = u
-    copies[2].wait()
-    copies[3].wait()
     pick_ref[...] = pick_matrix(send_ref, rows)
     picked_ref[...] = dot(pick_ref[...], features_ref[...]).astype(BF16)
-    for copy in copies[4:7]:
-        copy.wait()
-    place = lax.broadcasted_iota(jnp.int32, (part, blk), 0)
-    for c in range(CHUNKS):
+    for c in range(first, CHUNKS):
         copies[7 + c].wait()
-
-        def add(t, carry):
-            slot = dst_ref[t] * sources + src_ref[t]
-            for i, acc in enumerate(accs):
-                value = tile_buf[t, i * part : (i + 1) * part, :].astype(F32)
-                acc[slot] += jnp.where(place < rows_ref[t] - i * part, value, 0.0)
-            return carry
-
         lax.fori_loop(c * each, (c + 1) * each, add, 0, unroll=True)
     for b in range(bpd):
         for j in range(sources):
@@ -142,7 +141,7 @@
 
 
 def rest_kernel(
-    chips, adj_ref, up_ref, cot_ref, value_ref, col_ref, keep_ref, lend_ref, far_t
+    chips, adj_ref, up_ref, cot_ref, value_ref, pick_ref, col_ref, keep_ref, lend_ref, place_ref, far_t
 ):
     rows = up_ref.shape[0]
     far = col_ref.shape[0] // chips - rows
@@ -152,6 +151,7 @@
     lend_ref[:low, :] = adj_ref[...]
     lend_ref[low : low + rows, :] = cot_ref[...]
     lend_ref[low + rows :, :] = value_ref[...]
+    place_ref[...] = jnp.concatenate([pick_ref[...]] * chips, 0).T
 
 
 def deal(chips, hosts, total, picked, value, mine_ref, msg_ref, to_refs):
@@ -194,7 +194,7 @@
     return jnp.concatenate(blocks, 0).astype(BF16)
 
 
-def merge_kernel(chips, hosts, with_terms, recv_ref, mine_ref, pick_ref, *refs):
+def merge_kernel(chips, hosts, with_terms, recv_ref, mine_ref, place_ref, *refs):
     came, (out_ref, sum_ref) = refs[: chips - 1], refs[chips - 1 :]
     rows = mine_ref.shape[0]
     total = mine_ref[...]
@@ -202,7 +202,7 @@
         total = total + ref[:rows, :].astype(F32)
         out_ref[k * rows : (k + 1) * rows, :] = ref[rows:, :]
     if with_terms:
-        total = total + returned(pick_ref, recv_ref, hosts, chips)
+        total = total + returned(place_ref, recv_ref, hosts, chips)
     sum_ref[...] = total
     low = len(came) * rows
     halo = halo_part(recv_ref, hosts, chips, 0)
@@ -212,9 +212,8 @@
         out_ref[high:, :] = total.astype(BF16)
 
 
-def returned(pick_ref, recv_ref, hosts, chips):
-    back = halo_part(recv_ref, hosts, chips, 1)
-    return dot_tn(jnp.concatenate([pick_ref[...]] * chips, 0), back)
+def returned(place_ref, recv_ref, hosts, chips):
+    return dot(place_ref[...], halo_part(recv_ref, hosts, chips, 1))
 
 
 def own_chip(adj_refs, blocks):
@@ -259,7 +258,7 @@
 
 def mid_kernel(chips, hosts, count, *refs):
     adj_refs, refs = refs[:count], refs[count:]
-    agg_ref, part_ref, sum_ref, pick_ref, recv_ref = refs[:5]
+    agg_ref, part_ref, sum_ref, place_ref, recv_ref = refs[:5]
     came, (agg_out, grad_ref) = refs[5:-2], refs[-2:]
     rows = sum_ref.shape[0]
     chip, core = lax.axis_index("chip"), lax.axis_index("core")
@@ -275,28 +274,28 @@
         grad_ref[rows:, :] = part_ref[rows:, :]
     else:
         grad = part_ref[...] + sum_ref[...]
-        grad_ref[...] = grad + returned(pick_ref, recv_ref, hosts, chips)
-
-
-def full_aggregate(chips, far, rows, adj_refs, agg_ref, here_ref, shared_ref, halo):
-    chip, core = lax.axis_index("chip"), lax.axis_index("core")
+        grad_ref[...] = grad + returned(place_ref, recv_ref, hosts, chips)
+
+
+def put_halo(chips, far, rows, here_ref, shared_ref, halo):
+    core = lax.axis_index("core")
     at = (chips - 1) * rows
     for x in range(chips):
         for side, ref in ((core, here_ref), (1 - core, shared_ref)):
             low = pl.multiple_of((x * CORES + side) * far, far)
             halo[pl.ds(low, far), :] = ref[at + x * far : at + (x + 1) * far, :]
-    parts = []
-    for i, adj_ref in enumerate(adj_refs):
-        agg = agg_ref[i * rows : (i + 1) * rows, :]
-        for k in range(chips - 1):
-            x = lax.rem(chip - k - 1 + chips, chips)
-            low = pl.multiple_of((x * CORES + 1 - core) * rows, rows)
-            agg = agg + dot(adj_ref[pl.ds(low, rows), :], shared_ref[k * rows : (k + 1) * rows, :])
-        for j in range(halo.shape[0] // rows):
-            low = chips * CORES * rows + j * rows
-            agg = agg + dot(adj_ref[low : low + rows, :], halo[j * rows : (j + 1) * rows, :])
-        parts.append(agg)
-    return jnp.concatenate(parts, 0).astype(BF16)
+
+
+def add_far(chips, rows, adj_ref, start, size, agg, shared_ref, halo):
+    chip, core = lax.axis_index("chip"), lax.axis_index("core")
+    for k in range(chips - 1):
+        x = lax.rem(chip - k - 1 + chips, chips)
+        low = pl.multiple_of((x * CORES + 1 - core) * rows + start, size)
+        agg = agg + dot(adj_ref[pl.ds(low, size), :], shared_ref[k * rows : (k + 1) * rows, :])
+    for j in range(halo.shape[0] // rows):
+        low = chips * CORES * rows + j * rows + start
+        agg = agg + dot(adj_ref[low : low + size, :], halo[j * rows : (j + 1) * rows, :])
+    return agg
 
 
 def middle_kernel(
@@ -322,9 +321,14 @@
 ):
     to_refs, halo, total = rest[:-2], rest[-2], rest[-1]
     far, rows = pick_ref.shape
-    agg = full_aggregate(
-        chips, far, rows, (adj_ref, lent_ref), agg_ref, here_ref, shared_ref, halo
-    )
+    put_halo(chips, far, rows, here_ref, shared_ref, halo)
+    parts = [
+        add_far(
+            chips, rows, ref, 0, rows, agg_ref[i * rows : (i + 1) * rows, :], shared_ref, halo
+        )
+        for i, ref in enumerate((adj_ref, lent_ref))
+    ]
+    agg = jnp.concatenate(parts, 0).astype(BF16)
     pre = direct_ref[...] + dot(agg, neigh_one_ref[...])
     sigmoid = jax.nn.sigmoid(pre)
     hidden = (pre * sigmoid).astype(BF16)
@@ -342,19 +346,42 @@
 
 
 def last_kernel(
-    chips, far, adj_ref, agg_ref, direct_ref, here_ref, shared_ref, neigh_two_ref, output_ref, halo
+    chips,
+    far,
+    adj_ref,
+    agg_ref,
+    direct_ref,
+    here_ref,
+    shared_ref,
+    neigh_two_ref,
+    output_hbm,
+    halo,
+    out,
+    sems,
 ):
     rows = agg_ref.shape[0]
-    agg = full_aggregate(chips, far, rows, (adj_ref,), agg_ref, here_ref, shared_ref, halo)
-    output_ref[...] = (direct_ref[...] + dot(agg, neigh_two_ref[...])).astype(BF16)
-
-
-def call(kernel, name, out_shape, in_specs, args, scratch=(), limit=32, flops=0):
+    halves = out.shape[0]
+    each = rows // halves
+    put_halo(chips, far, rows, here_ref, shared_ref, halo)
+    copies = []
+    for i in range(halves):
+        part = pl.ds(i * each, each)
+        agg = add_far(
+            chips, rows, adj_ref, i * each, each, agg_ref[part, :], shared_ref, halo
+        ).astype(BF16)
+        out[i] = (direct_ref[part, :] + dot(agg, neigh_two_ref[...])).astype(BF16)
+        copies.append(pltpu.make_async_copy(out.at[i], output_hbm.at[part], sems.at[i]))
+        copies[-1].start()
+    for copy in copies:
+        copy.wait()
+
+
+def call(kernel, name, out_shape, in_specs, args, scratch=(), limit=32, flops=0, out_space=pltpu.VMEM):
     return pl.pallas_call(
         kernel,
         out_shape=out_shape,
         in_specs=in_specs,
-        out_specs=jax.tree.map(lambda _: VMEM, out_shape),
+        out_specs=jax.tree.map(lambda _: pl.BlockSpec(memory_space=out_space), out_shape),
         scratch_shapes=scratch,
         compiler_params=pltpu.CompilerParams(vmem_limit_bytes=limit * MIB),
         cost_estimate=pl.CostEstimate(
@@ -416,7 +443,7 @@
             "merge",
             (shape(halo_rows + rows * with_terms, width), sum_shape),
             [VMEM] * (2 + chips),
-            (recv, mine, pick, *terms),
+            (recv, mine, place, *terms),
         )
         return terms, recv, here, summed, shift(here, "core", 1)
 
@@ -461,12 +488,17 @@
         + [pltpu.VMEM(((rows // blk) * (all_rows // blk), blk // PARTS, blk), F32)] * PARTS,
     )
     came = shift(give, "core", 1)
-    col, keep, lend = call(
+    col, keep, lend, place = call(
         functools.partial(rest_kernel, chips),
         "rest",
-        (shape(count, rows), shape(count, width), shape(all_rows + 2 * rows, width)),
-        [VMEM] * 4,
-        (adj, up, cotangent, features),
+        (
+            shape(count, rows),
+            shape(count, width),
+            shape(all_rows + 2 * rows, width),
+            shape(rows, chips * far),
+        ),
+        [VMEM] * 5,
+        (adj, up, cotangent, features, pick),
         [far_t],
         flops=3 * square,
     )
@@ -495,7 +527,7 @@
         "mid_one",
         (both_shape,) * 2,
         [VMEM] * (6 + chips),
-        (adj, lent, agg, grad, summed, pick, recv, *terms),
+        (adj, lent, agg, grad, summed, place, recv, *terms),
         flops=3 * square,
     )
     hidden, there, grad_pre, mine, msg, *to = call(
@@ -521,7 +553,7 @@
         "mid_two",
         (sum_shape,) * 2,
         [VMEM] * (5 + chips),
-        (adj, agg, grad, summed, pick, recv, *terms),
+        (adj, agg, grad, summed, place, recv, *terms),
         flops=2 * square,
     )
     output = call(
@@ -530,8 +562,13 @@
         rows_shape,
         [VMEM] * 6,
         (adj, agg, direct, here, shared, neigh_two),
-        [halo],
+        [
+            halo,
+            pltpu.VMEM((HALVES, rows // HALVES, width), BF16),
+            pltpu.SemaphoreType.DMA((HALVES,)),
+        ],
         flops=3 * square,
+        out_space=pl.ANY,
     )
     return output, grad
 

time: 39.5 us -> 39.5 us (level)
  no operation moved by 1% of the time
where the time goes in v10:
time: 39.5 us; the launch traced here: 39.3 us
  blocking collectives  24.4 us (62%)
  Pallas kernels  7.32 us (19%)
  starting transfers between devices  4.86 us (12%)
  waiting for transfers between devices  1.86 us (5%)
  between operations  0.78 us (2%)
    all_to_all x2, blocking collectives, across(): lax.all_to_all(msg, ('hst', 'chip'), split_axis=0, concat_axis=0, tiled=T...  24.4 us
    pallas_call x11, Pallas kernels, call(): pl.pallas_call(kernel, out_shape=out_shape, in_specs=in_specs, out_specs=...  7.32 us
    ppermute x6, starting transfers between devices, shift(): return lax.ppermute(value, axis, [(i, (i + k) % size) for i in range(size)])  4.86 us
    ppermute x6, waiting for transfers between devices, shift(): return lax.ppermute(value, axis, [(i, (i + k) % size) for i in range(size)])  1.86 us
  transfers between devices with their start and end apart: 6, of which 3 were waited for; matrix products, arithmetic and copies ran while one was open for 0% of the time, Pallas kernels for 7%

profile of v10, /device:TPU:0, one launch (start us, length us, event | category | flops | bytes accessed | tf_op | source)
XLA Modules:
  0.0 39.3 jit_solution(3440114172748799323)
XLA Ops:
  0.6 0.0 copy-start
  0.6 0.0 copy-start.1
  0.7 2.5 %prep.1 = (bf16[1280,256]{1,0:T(8,128)(2,1)S(1)}, bf16[640,256]{1,0:T(8,128)(2,1)S(1)}, bf16[256,256]{1,0:T(8,128)(2,1)S(1)}, bf16[64,256]{1,0:T(8,128)(2,1)S(1)}, bf16[64,256]{1,0:T(8,128)(2,1)S(1)}) custom-call(s32[64]{0:T(128)} %dst_hbm.1, s32[64]{0:T(128)} %src_hbm.1, s32[64]{0:T(128)} %rows_hbm.1, s32[1,1,8,8]{3,2,1,0:T(8,128)} %send_hbm.1, ...), custom_call_target="tpu_custom_call" | custom-call | tf_op jit(solution)/shard_map/prep/pallas_call | solution.py:380
  3.1 0.5 %collective-permute-start.1 = (bf16[640,256]{1,0:T(8,128)(2,1)S(1)}, bf16[640,256]{1,0:T(8,128)(2,1)S(1)}, u32[]{:S(2)}, u32[]{:S(2)}) collective-permute-start(bf16[640,256]{1,0:T(8,128)(2,1)S(1)} %get-tuple-element.44), channel_id=1, source_target_pairs={{0,1},{1,0},{2,3},{3,2},{4,5},{5,4},{6,7},{7,6},{8,9},{9,8},{10,11... | collective-permute-start | bytes 983048 | tf_op jit(solution)/shard_map/ppermute | solution.py:396
  3.6 0.0 copy-done
  3.6 0.0 copy-done.1
  3.7 0.3 rest.1
  4.0 0.1 collective-permute-start
  4.1 0.8 %collective-permute-done.1.came_ref = bf16[640,256]{1,0:T(8,128)(2,1)S(1)} collective-permute-done((bf16[640,256]{1,0:T(8,128)(2,1)S(1)}, bf16[640,256]{1,0:T(8,128)(2,1)S(1)}, u32[]{:S(2)}, u32[]{:S(2)}) %collective-permute-start.1) | collective-permute-done | bytes 327712 | tf_op jit(solution)/shard_map/ppermute | solution.py:396
  4.9 0.2 core_sum.1
  5.1 2.9 %collective-permute-start.2 = (bf16[512,256]{1,0:T(8,128)(2,1)S(1)}, bf16[512,256]{1,0:T(8,128)(2,1)S(1)}, u32[]{:S(2)}, u32[]{:S(2)}) collective-permute-start(bf16[512,256]{1,0:T(8,128)(2,1)S(1)} %get-tuple-element.49), channel_id=1, source_target_pairs={{0,2},{2,0},{1,3},{3,1},{4,6},{6,4},{5,7},{7,5},{8,10},{10,8},{9,1... | collective-permute-start | bytes 786440 | tf_op jit(solution)/shard_map/ppermute | solution.py:396
  8.0 13.5 %all_to_all.10.recv_ref.refs_6_ = bf16[16,16,256]{2,1,0:T(8,128)(2,1)S(1)} all-to-all(bf16[16,16,256]{2,1,0:T(8,128)(2,1)S(1)} %get-tuple-element.46), channel_id=1, replica_groups=mesh['hst'=8,'chip'=2,'core'=2] {'hst','chip'}, dimensions={0} | all-to-all | bytes 262144 | tf_op jit(solution)/shard_map/all_to_all | solution.py:440
  21.5 0.0 collective-permute-done.2.refs_0_.refs_7_
  21.5 0.2 merge.2
  21.7 0.1 collective-permute-start.3
  21.8 0.0 collective-permute-done.lent_ref.refs_1_
  21.8 0.0 copy-done.3
  21.8 0.0 copy-done.4
  21.8 0.0 copy-done.6
  21.8 0.4 %early_one.1 = (f32[512,256]{1,0:T(8,128)S(1)}, f32[512,256]{1,0:T(8,128)S(1)}, f32[512,256]{1,0:T(8,128)S(1)}, bf16[640,256]{1,0:T(8,128)(2,1)S(1)}) custom-call(bf16[1280,256]{1,0:T(8,128)(2,1)S(1)} %get-tuple-element.35.adj_ref.refs_0_, bf16[1792,256]{1,0:T(8,128)(2,1)S(1)} %collective-permute-done.lent_ref.refs_1_, bf16[256,256]{1,0:T(8,128)(2,1)S(1)} %copy-done, ...), custom_call_target="tpu_custom_call" | custom-call | flops 268435456 | bytes 262144 | tf_op jit(solution)/shard_map/early_one/pallas_call | solution.py:380
  22.3 0.0 copy-start.5
  22.3 0.2 mid_one.1
  22.5 0.9 %collective-permute-done.3.shared_ref = bf16[640,256]{1,0:T(8,128)(2,1)S(1)} collective-permute-done((bf16[640,256]{1,0:T(8,128)(2,1)S(1)}, bf16[640,256]{1,0:T(8,128)(2,1)S(1)}, u32[]{:S(2)}, u32[]{:S(2)}) %collective-permute-start.3) | collective-permute-done | bytes 327712 | tf_op jit(solution)/shard_map/ppermute | solution.py:396
  23.4 1.1 %middle.1 = (bf16[256,256]{1,0:T(8,128)(2,1)S(1)}, bf16[256,256]{1,0:T(8,128)(2,1)S(1)}, bf16[256,256]{1,0:T(8,128)(2,1)S(1)}, f32[256,256]{1,0:T(8,128)S(1)}, b...) custom-call(bf16[1280,256]{1,0:T(8,128)(2,1)S(1)} %get-tuple-element.35.adj_ref.refs_0_, ...), custom_call_target="tpu_custom_call" | custom-call | flops 402653184 | bytes 393216 | tf_op jit(solution)/shard_map/middle/pallas_call | solution.py:380
  24.5 1.2 %collective-permute-start.4 = (bf16[512,256]{1,0:T(8,128)(2,1)S(1)}, bf16[512,256]{1,0:T(8,128)(2,1)S(1)}, u32[]{:S(2)}, u32[]{:S(2)}) collective-permute-start(bf16[512,256]{1,0:T(8,128)(2,1)S(1)} %get-tuple-element.62), channel_id=1, source_target_pairs={{0,2},{2,0},{1,3},{3,1},{4,6},{6,4},{5,7},{7,5},{8,10},{10,8},{9,1... | collective-permute-start | bytes 786440 | tf_op jit(solution)/shard_map/ppermute | solution.py:396
  25.6 10.9 %all_to_all.11.recv_ref.refs_5_ = bf16[16,16,256]{2,1,0:T(8,128)(2,1)S(1)} all-to-all(bf16[16,16,256]{2,1,0:T(8,128)(2,1)S(1)} %get-tuple-element.60), channel_id=1, replica_groups=mesh['hst'=8,'chip'=2,'core'=2] {'hst','chip'}, dimensions={0} | all-to-all | bytes 262144 | tf_op jit(solution)/shard_map/all_to_all | solution.py:440
  36.6 0.0 collective-permute-done.4.refs_0_.refs_6_
  36.6 0.1 collective-permute-start.5
  36.7 0.3 early_two.1
  37.0 0.9 %mid_two.1 = (f32[256,256]{1,0:T(8,128)S(1)}, f32[256,256]{1,0:T(8,128)}) custom-call(bf16[1280,256]{1,0:T(8,128)(2,1)S(1)} %get-tuple-element.35.adj_ref.refs_0_, f32[256,256]{1,0:T(8,128)S(1)} %get-tuple-element.58.refs_1_, f32[256,256]{1,0:T(8,128)S(1)} %get-tuple-element.59.refs_2_, f32[256,256]{1,0:T(8,128)S(1)} %get-tuple-element.63.refs_3_, ...), custom_call_target="tpu_custom_call" | custom-call | flops 67108864 | bytes 65536 | tf_op jit(solution)/shard_map/mid_two/pallas_call | solution.py:380
  37.9 0.2 collective-permute-done.5.shared_ref
  38.1 1.2 %last.1 = bf16[256,256]{1,0:T(8,128)(2,1)} custom-call(bf16[1280,256]{1,0:T(8,128)(2,1)S(1)} %get-tuple-element.35.adj_ref.refs_0_, f32[256,256]{1,0:T(8,128)S(1)} %get-tuple-element.64.agg_ref, f32[256,256]{1,0:T(8,128)S(1)} %get-tuple-element.65.direct_ref, bf16[384,256]{1,0:T(8,128)(2,1)S(1)} %get-tuple-element.66.here_ref, ...), custom_call_target="tpu_custom_call" | custom-call | flops 100663296 | bytes 98304 | tf_op jit(solution)/shard_map/last/pallas_call | solution.py:380
  (9 shorter events, 0.1 us)
Async XLA Ops:
  0.6 3.0 %copy-start = (bf16[256,256]{1,0:T(8,128)(2,1)S(1)}, bf16[256,256]{1,0:T(8,128)(2,1)}, u32[]{:S(2)}) copy-start(bf16[256,256]{1,0:T(8,128)(2,1)} %value_ref.5) | copy-start | bytes 393220
  0.6 3.0 %copy-start.1 = (bf16[256,256]{1,0:T(8,128)(2,1)S(1)}, bf16[256,256]{1,0:T(8,128)(2,1)}, u32[]{:S(2)}) copy-start(bf16[256,256]{1,0:T(8,128)(2,1)} %up_ref.1) | copy-start | bytes 393220
  3.1 1.8 %collective-permute-start.1 = (bf16[640,256]{1,0:T(8,128)(2,1)S(1)}, bf16[640,256]{1,0:T(8,128)(2,1)S(1)}, u32[]{:S(2)}, u32[]{:S(2)}) collective-permute-start(bf16[640,256]{1,0:T(8,128)(2,1)S(1)} %get-tuple-element.44), channel_id=1, source_target_pairs={{0,1},{1,0},{2,3},{3,2},{4,5},{5,4},{6,7},{7,6},{8,9},{9,8},{10,11... | collective-permute-start | bytes 983048 | tf_op jit(solution)/shard_map/ppermute | solution.py:396
  4.0 17.8 %collective-permute-start = (bf16[1792,256]{1,0:T(8,128)(2,1)S(1)}, bf16[1792,256]{1,0:T(8,128)(2,1)S(1)}, u32[]{:S(2)}, u32[]{:S(2)}) collective-permute-start(bf16[1792,256]{1,0:T(8,128)(2,1)S(1)} %get-tuple-element.38), channel_id=1, source_target_pairs={{0,1},{1,0},{2,3},{3,2},{4,5},{5,4},{6,7},{7,6},{8,9},{9,8},{10,11... | collective-permute-start | bytes 2752520 | tf_op jit(solution)/shard_map/ppermute | solution.py:396
  4.9 16.9 %copy-start.3 = (bf16[256,256]{1,0:T(8,128)(2,1)S(1)}, bf16[256,256]{1,0:T(8,128)(2,1)}, u32[]{:S(2)}) copy-start(bf16[256,256]{1,0:T(8,128)(2,1)} %weight_ref.3) | copy-start | bytes 393220
  4.9 16.9 %copy-start.4 = (bf16[256,256]{1,0:T(8,128)(2,1)S(1)}, bf16[256,256]{1,0:T(8,128)(2,1)}, u32[]{:S(2)}) copy-start(bf16[256,256]{1,0:T(8,128)(2,1)} %self_ref.3) | copy-start | bytes 393220
  4.9 16.9 %copy-start.6 = (f32[256]{0:T(256)S(1)}, f32[256]{0:T(256)}, u32[]{:S(2)}) copy-start(f32[256]{0:T(256)} %bias_ref.2) | copy-start | bytes 3076
  5.1 16.5 %collective-permute-start.2 = (bf16[512,256]{1,0:T(8,128)(2,1)S(1)}, bf16[512,256]{1,0:T(8,128)(2,1)S(1)}, u32[]{:S(2)}, u32[]{:S(2)}) collective-permute-start(bf16[512,256]{1,0:T(8,128)(2,1)S(1)} %get-tuple-element.49), channel_id=1, source_target_pairs={{0,2},{2,0},{1,3},{3,1},{4,6},{6,4},{5,7},{7,5},{8,10},{10,8},{9,1... | collective-permute-start | bytes 786440 | tf_op jit(solution)/shard_map/ppermute | solution.py:396
  21.7 1.7 %collective-permute-start.3 = (bf16[640,256]{1,0:T(8,128)(2,1)S(1)}, bf16[640,256]{1,0:T(8,128)(2,1)S(1)}, u32[]{:S(2)}, u32[]{:S(2)}) collective-permute-start(bf16[640,256]{1,0:T(8,128)(2,1)S(1)} %get-tuple-element.54.here_ref), channel_id=1, source_target_pairs={{0,1},{1,0},{2,3},{3,2},{4,5},{5,4},{6,7},{7,6},{8,9},{9,8},{10,11... | collective-permute-start | bytes 983048 | tf_op jit(solution)/shard_map/ppermute | solution.py:396
  22.3 1.1 %copy-start.5 = (bf16[256,256]{1,0:T(8,128)(2,1)S(1)}, bf16[256,256]{1,0:T(8,128)(2,1)}, u32[]{:S(2)}) copy-start(bf16[256,256]{1,0:T(8,128)(2,1)} %neigh_one_ref.1) | copy-start | bytes 393220
  23.4 13.3 %copy-start.7 = (f32[256]{0:T(256)S(1)}, f32[256]{0:T(256)}, u32[]{:S(2)}) copy-start(f32[256]{0:T(256)} %bias_ref.3) | copy-start | bytes 3076
  24.5 12.1 %collective-permute-start.4 = (bf16[512,256]{1,0:T(8,128)(2,1)S(1)}, bf16[512,256]{1,0:T(8,128)(2,1)S(1)}, u32[]{:S(2)}, u32[]{:S(2)}) collective-permute-start(bf16[512,256]{1,0:T(8,128)(2,1)S(1)} %get-tuple-element.62), channel_id=1, source_target_pairs={{0,2},{2,0},{1,3},{3,1},{4,6},{6,4},{5,7},{7,5},{8,10},{10,8},{9,1... | collective-permute-start | bytes 786440 | tf_op jit(solution)/shard_map/ppermute | solution.py:396
  25.6 12.5 %copy-start.2 = (bf16[256,256]{1,0:T(8,128)(2,1)S(1)}, bf16[256,256]{1,0:T(8,128)(2,1)}, u32[]{:S(2)}) copy-start(bf16[256,256]{1,0:T(8,128)(2,1)} %neigh_two_ref.1) | copy-start | bytes 393220
  36.6 1.5 %collective-permute-start.5 = (bf16[384,256]{1,0:T(8,128)(2,1)S(1)}, bf16[384,256]{1,0:T(8,128)(2,1)S(1)}, u32[]{:S(2)}, u32[]{:S(2)}) collective-permute-start(bf16[384,256]{1,0:T(8,128)(2,1)S(1)} %get-tuple-element.66.here_ref), channel_id=1, source_target_pairs={{0,1},{1,0},{2,3},{3,2},{4,5},{5,4},{6,7},{7,6},{8,9},{9,8},{10,11... | collective-permute-start | bytes 589832 | tf_op jit(solution)/shard_map/ppermute | solution.py:396

commit v11 on v10

--- a/solution.py
+++ b/solution.py
@@ -12,7 +12,6 @@
 MIB = 1024 * 1024
 CHUNKS = 8
 PARTS = 4
-HALVES = 2
 CORES = 2
 
 VMEM = pl.BlockSpec(memory_space=pltpu.VMEM)
@@ -41,14 +40,15 @@
 
 
 def column(chips, far, rows, side, adj_ref, far_t, out_ref):
+    chip = lax.axis_index("chip")
     each = rows + far
     own_rows = chips * CORES * rows
     for j in range(far_t.shape[0] // rows):
         low = own_rows + j * rows
         far_t[j * rows : (j + 1) * rows, :] = adj_ref[low : low + rows, :].T
-    for x in range(chips):
-        d = x * CORES + side
-        at = x * each
+    for k in range(chips):
+        d = lax.rem(chip + k, chips) * CORES + side
+        at = k * each
         out_ref[at : at + rows, :] = adj_ref[pl.ds(pl.multiple_of(d * rows, rows), rows), :].T
         out_ref[at + rows : at + each, :] = far_t[pl.ds(pl.multiple_of(d * far, far), far), :]
 
@@ -160,27 +160,25 @@
     send = far // hosts
     each = rows + far
     chip = lax.axis_index("chip")
-    mine_ref[...] = total[pl.ds(pl.multiple_of(chip * each, 8), rows), :]
-    for k, ref in enumerate(to_refs):
-        other = lax.rem(chip + k + 1, chips)
-        ref[:rows, :] = total[pl.ds(pl.multiple_of(other * each, 8), rows), :].astype(BF16)
-        ref[rows:, :] = value
-    for g in range(hosts):
-        for x in range(chips):
-            low = x * each + rows + g * send
-            both = jnp.concatenate(
-                [picked[g * send : (g + 1) * send], total[low : low + send, :]], 0
-            )
-            msg_ref[g * chips + x] = both.astype(BF16)
+    mine_ref[...] = total[:rows]
+    for k in range(chips):
+        low = k * each + rows
+        if k > 0:
+            to_refs[k - 1][:rows, :] = total[k * each : low].astype(BF16)
+            to_refs[k - 1][rows:, :] = value
+        x = lax.rem(chip + k, chips)
+        for g in range(hosts):
+            at = low + g * send
+            both = [picked[g * send : (g + 1) * send], total[at : at + send]]
+            msg_ref[g * chips + x] = jnp.concatenate(both, 0).astype(BF16)
 
 
 def core_sum_kernel(
     chips, hosts, keep_ref, came_ref, value_ref, picked_ref, mine_ref, msg_ref, *rest
 ):
-    total = rest[-1]
-    total[...] = keep_ref[...].astype(F32) + came_ref[...].astype(F32)
+    total = keep_ref[...].astype(F32) + came_ref[...].astype(F32)
     picked = picked_ref[...].astype(F32)
-    deal(chips, hosts, total, picked, value_ref[...], mine_ref, msg_ref, rest[:-1])
+    deal(chips, hosts, total, picked, value_ref[...], mine_ref, msg_ref, rest)
 
 
 def halo_part(recv_ref, hosts, chips, part):
@@ -194,22 +192,20 @@
     return jnp.concatenate(blocks, 0).astype(BF16)
 
 
-def merge_kernel(chips, hosts, with_terms, recv_ref, mine_ref, place_ref, *refs):
+def merge_kernel(chips, hosts, recv_ref, mine_ref, place_ref, *refs):
     came, (out_ref, sum_ref) = refs[: chips - 1], refs[chips - 1 :]
     rows = mine_ref.shape[0]
     total = mine_ref[...]
     for k, ref in enumerate(came):
         total = total + ref[:rows, :].astype(F32)
         out_ref[k * rows : (k + 1) * rows, :] = ref[rows:, :]
-    if with_terms:
-        total = total + returned(place_ref, recv_ref, hosts, chips)
+    total = total + returned(place_ref, recv_ref, hosts, chips)
     sum_ref[...] = total
     low = len(came) * rows
     halo = halo_part(recv_ref, hosts, chips, 0)
     high = low + halo.shape[0]
     out_ref[low:high, :] = halo
-    if with_terms:
-        out_ref[high:, :] = total.astype(BF16)
+    out_ref[high:, :] = total.astype(BF16)
 
 
 def returned(place_ref, recv_ref, hosts, chips):
@@ -246,35 +242,61 @@
     column(chips, far, rows, lax.axis_index("core"), lent_ref, far_t, col_ref)
 
 
-def early_two_kernel(
-    chips, adj_ref, value_ref, there_ref, self_ref, bias_ref, up_ref, weight_ref,
-    agg_ref, direct_ref, grad_ref,
-):
-    value = value_ref[...]
-    agg_ref[...] = own_chip((adj_ref,), (value, there_ref[...]))
-    direct_ref[...] = dot(value, self_ref[...]) + bias_ref[...].reshape(1, -1)
-    grad_ref[...] = dot_nt(up_ref[...], weight_ref[...])
-
-
-def mid_kernel(chips, hosts, count, *refs):
-    adj_refs, refs = refs[:count], refs[count:]
-    agg_ref, part_ref, sum_ref, place_ref, recv_ref = refs[:5]
-    came, (agg_out, grad_ref) = refs[5:-2], refs[-2:]
+def mid_kernel(chips, adj_ref, lent_ref, agg_ref, part_ref, sum_ref, *refs):
+    came, (agg_out, grad_ref) = refs[:-2], refs[-2:]
     rows = sum_ref.shape[0]
     chip, core = lax.axis_index("chip"), lax.axis_index("core")
-    for i, adj_ref in enumerate(adj_refs):
+    for i, ref in enumerate((adj_ref, lent_ref)):
         agg = agg_ref[i * rows : (i + 1) * rows, :]
-        for k, ref in enumerate(came):
+        for k, block in enumerate(came):
             x = lax.rem(chip - k - 1 + chips, chips)
             low = pl.multiple_of((x * CORES + core) * rows, rows)
-            agg = agg + dot(adj_ref[pl.ds(low, rows), :], ref[rows:, :])
+            agg = agg + dot(ref[pl.ds(low, rows), :], block[rows:, :])
         agg_out[i * rows : (i + 1) * rows, :] = agg
-    if count > 1:
-        grad_ref[:rows, :] = part_ref[:rows, :] + sum_ref[...]
-        grad_ref[rows:, :] = part_ref[rows:, :]
-    else:
-        grad = part_ref[...] + sum_ref[...]
-        grad_ref[...] = grad + returned(place_ref, recv_ref, hosts, chips)
+    grad_ref[:rows, :] = part_ref[:rows, :] + sum_ref[...]
+    grad_ref[rows:, :] = part_ref[rows:, :]
+
+
+def column_product(chips, hosts, adj_ref, value_ref, came, recv_ref, neigh_ref, halo):
+    rows = value_ref.shape[0]
+    far = halo.shape[0] // (chips * CORES)
+    chip, core = lax.axis_index("chip"), lax.axis_index("core")
+    low = pl.multiple_of((chip * CORES + core) * rows, rows)
+    agg = dot(adj_ref[pl.ds(low, rows), :], value_ref[...])
+    for k, block in enumerate(came):
+        x = lax.rem(chip - k - 1 + chips, chips)
+        low = pl.multiple_of((x * CORES + core) * rows, rows)
+        agg = agg + dot(adj_ref[pl.ds(low, rows), :], block[rows:, :])
+    rows_here = halo_part(recv_ref, hosts, chips, 0)
+    halo[...] = jnp.zeros_like(halo)
+    for x in range(chips):
+        low = pl.multiple_of((x * CORES + core) * far, far)
+        halo[pl.ds(low, far), :] = rows_here[x * far : (x + 1) * far]
+    for j in range(halo.shape[0] // rows):
+        low = (chips * CORES + j) * rows
+        agg = agg + dot(adj_ref[low : low + rows, :], halo[j * rows : (j + 1) * rows, :])
+    return dot(agg.astype(BF16), neigh_ref[...])
+
+
+def there_kernel(chips, hosts, lent_ref, value_ref, recv_ref, neigh_ref, *refs):
+    came, out_ref, halo = refs[:-2], refs[-2], refs[-1]
+    out_ref[...] = column_product(
+        chips, hosts, lent_ref, value_ref, came, recv_ref, neigh_ref, halo
+    ).astype(BF16)
+
+
+def here_kernel(
+    chips, hosts, adj_ref, value_ref, recv_ref, neigh_ref, self_ref, bias_ref, up_ref, weight_ref,
+    mine_ref, place_ref, *refs
+):
+    came, out_ref, grad_ref, halo = refs[:-3], refs[-3], refs[-2], refs[-1]
+    rows = mine_ref.shape[0]
+    grad = dot_nt(up_ref[...], weight_ref[...]) + mine_ref[...]
+    for block in came:
+        grad = grad + block[:rows, :].astype(F32)
+    grad_ref[...] = grad + returned(place_ref, recv_ref, hosts, chips)
+    out = column_product(chips, hosts, adj_ref, value_ref, came, recv_ref, neigh_ref, halo)
+    out_ref[...] = out + dot(value_ref[...], self_ref[...]) + bias_ref[...].reshape(1, -1)
 
 
 def put_halo(chips, far, rows, here_ref, shared_ref, halo):
@@ -313,13 +335,12 @@
     shared_ref,
     neigh_one_ref,
     hidden_ref,
-    there_ref,
     grad_pre_ref,
     mine_ref,
     msg_ref,
     *rest,
 ):
-    to_refs, halo, total = rest[:-2], rest[-2], rest[-1]
+    to_refs, halo = rest[:-1], rest[-1]
     far, rows = pick_ref.shape
     put_halo(chips, far, rows, here_ref, shared_ref, halo)
     parts = [
@@ -333,55 +354,27 @@
     sigmoid = jax.nn.sigmoid(pre)
     hidden = (pre * sigmoid).astype(BF16)
     hidden_ref[...] = hidden[:rows]
-    there_ref[...] = hidden[rows:]
     low = (chips - 1) * rows + chips * far
     add = shared_ref[low:, :].astype(F32)
     grad = jnp.concatenate([grad_ref[:rows, :], grad_ref[rows:, :] + add], 0)
     grad_pre = (grad * sigmoid * (1.0 + pre * (1.0 - sigmoid))).astype(BF16)
     grad_pre_ref[...] = grad_pre[:rows]
     u = dot_nt(grad_pre, neigh_one_ref[...]).astype(BF16)
-    total[...] = dot(col_ref[...], u[:rows]) + dot(col_two_ref[...], u[rows:])
+    total = dot(col_ref[...], u[:rows]) + dot(col_two_ref[...], u[rows:])
     picked = dot(pick_ref[...], hidden[:rows])
     deal(chips, hosts, total, picked, hidden[:rows], mine_ref, msg_ref, to_refs)
 
 
-def last_kernel(
-    chips,
-    far,
-    adj_ref,
-    agg_ref,
-    direct_ref,
-    here_ref,
-    shared_ref,
-    neigh_two_ref,
-    output_hbm,
-    halo,
-    out,
-    sems,
-):
-    rows = agg_ref.shape[0]
-    halves = out.shape[0]
-    each = rows // halves
-    put_halo(chips, far, rows, here_ref, shared_ref, halo)
-    copies = []
-    for i in range(halves):
-        part = pl.ds(i * each, each)
-        agg = add_far(
-            chips, rows, adj_ref, i * each, each, agg_ref[part, :], shared_ref, halo
-        ).astype(BF16)
-        out[i] = (direct_ref[part, :] + dot(agg, neigh_two_ref[...])).astype(BF16)
-        copies.append(pltpu.make_async_copy(out.at[i], output_hbm.at[part], sems.at[i]))
-        copies[-1].start()
-    for copy in copies:
-        copy.wait()
-
-
-def call(kernel, name, out_shape, in_specs, args, scratch=(), limit=32, flops=0, out_space=pltpu.VMEM):
+def last_kernel(here_ref, there_ref, output_ref):
+    output_ref[...] = (here_ref[...] + there_ref[...].astype(F32)).astype(BF16)
+
+
+def call(kernel, name, out_shape, in_specs, args, scratch=(), limit=32, flops=0):
     return pl.pallas_call(
         kernel,
         out_shape=out_shape,
         in_specs=in_specs,
-        out_specs=jax.tree.map(lambda _: pl.BlockSpec(memory_space=out_space), out_shape),
+        out_specs=jax.tree.map(lambda _: VMEM, out_shape),
         scratch_shapes=scratch,
         compiler_params=pltpu.CompilerParams(vmem_limit_bytes=limit * MIB),
         cost_estimate=pl.CostEstimate(
@@ -428,24 +421,16 @@
     both_shape = shape(CORES * rows, width, F32)
     square = 2 * rows * width * width
     halo = pltpu.VMEM((chips * CORES * far, width), BF16)
-    total = pltpu.VMEM((count, width), F32)
     halo_rows = (chips - 1) * rows + chips * far
     dealt = (
         sum_shape,
         jax.ShapeDtypeStruct((hosts * chips, 2 * send, width), BF16),
     ) + (shape(2 * rows, width),) * (chips - 1)
 
-    def across(mine, msg, to, with_terms):
+    def across(msg, to):
         terms = [shift(block, "chip", k + 1) for k, block in enumerate(to)]
         recv = lax.all_to_all(msg, ("hst", "chip"), split_axis=0, concat_axis=0, tiled=True)
-        here, summed = call(
-            functools.partial(merge_kernel, chips, hosts, with_terms),
-            "merge",
-            (shape(halo_rows + rows * with_terms, width), sum_shape),
-            [VMEM] * (2 + chips),
-            (recv, mine, place, *terms),
-        )
-        return terms, recv, here, summed, shift(here, "core", 1)
+        return terms, recv
 
     far_t = pltpu.VMEM((chips * CORES * far, rows), BF16)
     adj, give, up, picked, pick = call(
@@ -509,10 +494,17 @@
         dealt,
         [VMEM] * 4,
         (keep, came, features, picked),
-        [total],
         flops=60 * square,
     )
-    terms, recv, here, summed, shared = across(mine, msg, to, 1)
+    terms, recv = across(msg, to)
+    here, summed = call(
+        functools.partial(merge_kernel, chips, hosts),
+        "merge",
+        (shape(halo_rows + rows, width), sum_shape),
+        [VMEM] * (2 + chips),
+        (recv, mine, place, *terms),
+    )
+    shared = shift(here, "core", 1)
     agg, direct, grad, col_two = call(
         functools.partial(early_one_kernel, chips),
         "early_one",
@@ -523,53 +515,54 @@
         flops=8 * square,
     )
     agg, grad = call(
-        functools.partial(mid_kernel, chips, hosts, 2),
-        "mid_one",
+        functools.partial(mid_kernel, chips),
+        "mid",
         (both_shape,) * 2,
-        [VMEM] * (6 + chips),
-        (adj, lent, agg, grad, summed, place, recv, *terms),
+        [VMEM] * (4 + chips),
+        (adj, lent, agg, grad, summed, *terms),
         flops=3 * square,
     )
-    hidden, there, grad_pre, mine, msg, *to = call(
+    hidden, grad_pre, mine, msg, *to = call(
         functools.partial(middle_kernel, chips, hosts),
         "middle",
-        (rows_shape,) * 3 + dealt,
+        (rows_shape,) * 2 + dealt,
         [VMEM] * 11,
         (adj, lent, col, col_two, agg, direct, grad, pick, here, shared, neigh_one),
-        [halo, total],
+        [halo],
         flops=12 * square,
     )
-    terms, recv, here, summed, shared = across(mine, msg, to, 0)
-    agg, direct, grad = call(
-        functools.partial(early_two_kernel, chips),
-        "early_two",
-        (sum_shape,) * 3,
-        [VMEM] * 7,
-        (adj, hidden, there, self_two, bias_two, grad_pre, self_one),
-        flops=4 * square,
-    )
-    agg, grad = call(
-        functools.partial(mid_kernel, chips, hosts, 1),
-        "mid_two",
+    terms, recv = across(msg, to)
+    there = call(
+        functools.partial(there_kernel, chips, hosts),
+        "there",
+        rows_shape,
+        [VMEM] * (3 + chips),
+        (lent, hidden, recv, neigh_two, *terms),
+        [halo],
+    )
+    shared = shift(there, "core", 1)
+    here, grad = call(
+        functools.partial(here_kernel, chips, hosts),
+        "here",
         (sum_shape,) * 2,
-        [VMEM] * (5 + chips),
-        (adj, agg, grad, summed, place, recv, *terms),
-        flops=2 * square,
-    )
-    output = call(
-        functools.partial(last_kernel, chips, far),
-        "last",
-        rows_shape,
-        [VMEM] * 6,
-        (adj, agg, direct, here, shared, neigh_two),
-        [
-            halo,
-            pltpu.VMEM((HALVES, rows // HALVES, width), BF16),
-            pltpu.SemaphoreType.DMA((HALVES,)),
-        ],
-        flops=3 * square,
-        out_space=pl.ANY,
-    )
+        [VMEM] * (9 + chips),
+        (
+            adj,
+            hidden,
+            recv,
+            neigh_two,
+            self_two,
+            bias_two,
+            grad_pre,
+            self_one,
+            mine,
+            place,
+            *terms,
+        ),
+        [halo],
+        flops=7 * square,
+    )
+    output = call(last_kernel, "last", rows_shape, [VMEM] * 2, (here, shared))
     return output, grad
 
 

time: 39.5 us -> 39 us (0.987)
  Pallas kernels: 7.32 us -> 6.79 us
    pallas_call x11 -> x10, Pallas kernels: 7.32 us -> 6.79 us  [call(): pl.pallas_call(kernel, out_shape=out_shape, in_specs=in_specs, out_specs=...]
  transfers between devices with their start and end apart: 6 -> 6, of which waited for: 3 -> 3; matrix products, arithmetic and copies ran while one was open for 0% -> 0% of each run, Pallas kernels for 7% -> 6%
where the time goes in v11:
time: 39 us; the launch traced here: 38.8 us
  blocking collectives  24.3 us (62%)
  Pallas kernels  6.79 us (17%)
  starting transfers between devices  4.85 us (12%)
  waiting for transfers between devices  2.03 us (5%)
  between operations  0.77 us (2%)
    all_to_all x2, blocking collectives, across(): lax.all_to_all(msg, ('hst', 'chip'), split_axis=0, concat_axis=0, tiled=T...  24.3 us
    pallas_call x10, Pallas kernels, call(): pl.pallas_call(kernel, out_shape=out_shape, in_specs=in_specs, out_specs=...  6.79 us
    ppermute x6, starting transfers between devices, shift(): return lax.ppermute(value, axis, [(i, (i + k) % size) for i in range(size)])  4.85 us
    ppermute x6, waiting for transfers between devices, shift(): return lax.ppermute(value, axis, [(i, (i + k) % size) for i in range(size)])  2.03 us
  transfers between devices with their start and end apart: 6, of which 3 were waited for; matrix products, arithmetic and copies ran while one was open for 0% of the time, Pallas kernels for 6%

profile of v11, /device:TPU:0, one launch (start us, length us, event | category | flops | bytes accessed | tf_op | source)
XLA Modules:
  0.0 38.8 jit_solution(187322921456196602)
XLA Ops:
  0.6 0.0 copy-start.1
  0.6 0.0 copy-start.2
  0.7 2.5 %prep.1 = (bf16[1280,256]{1,0:T(8,128)(2,1)S(1)}, bf16[640,256]{1,0:T(8,128)(2,1)S(1)}, bf16[256,256]{1,0:T(8,128)(2,1)S(1)}, bf16[64,256]{1,0:T(8,128)(2,1)S(1)}, bf16[64,256]{1,0:T(8,128)(2,1)S(1)}) custom-call(s32[64]{0:T(128)} %dst_hbm.1, s32[64]{0:T(128)} %src_hbm.1, s32[64]{0:T(128)} %rows_hbm.1, s32[1,1,8,8]{3,2,1,0:T(8,128)} %send_hbm.1, ...), custom_call_target="tpu_custom_call" | custom-call | tf_op jit(solution)/shard_map/prep/pallas_call | solution.py:373
  3.2 0.5 %collective-permute-start.1 = (bf16[640,256]{1,0:T(8,128)(2,1)S(1)}, bf16[640,256]{1,0:T(8,128)(2,1)S(1)}, u32[]{:S(2)}, u32[]{:S(2)}) collective-permute-start(bf16[640,256]{1,0:T(8,128)(2,1)S(1)} %get-tuple-element.38), channel_id=1, source_target_pairs={{0,1},{1,0},{2,3},{3,2},{4,5},{5,4},{6,7},{7,6},{8,9},{9,8},{10,11... | collective-permute-start | bytes 983048 | tf_op jit(solution)/shard_map/ppermute | solution.py:389
  3.7 0.0 copy-done.1
  3.7 0.3 rest.1
  4.0 0.1 collective-permute-start
  4.1 0.8 %collective-permute-done.1.came_ref = bf16[640,256]{1,0:T(8,128)(2,1)S(1)} collective-permute-done((bf16[640,256]{1,0:T(8,128)(2,1)S(1)}, bf16[640,256]{1,0:T(8,128)(2,1)S(1)}, u32[]{:S(2)}, u32[]{:S(2)}) %collective-permute-start.1) | collective-permute-done | bytes 327712 | tf_op jit(solution)/shard_map/ppermute | solution.py:389
  4.9 0.1 core_sum.1
  5.0 2.9 %collective-permute-start.2 = (bf16[512,256]{1,0:T(8,128)(2,1)S(1)}, bf16[512,256]{1,0:T(8,128)(2,1)S(1)}, u32[]{:S(2)}, u32[]{:S(2)}) collective-permute-start(bf16[512,256]{1,0:T(8,128)(2,1)S(1)} %get-tuple-element.43), channel_id=1, source_target_pairs={{0,2},{2,0},{1,3},{3,1},{4,6},{6,4},{5,7},{7,5},{8,10},{10,8},{9,1... | collective-permute-start | bytes 786440 | tf_op jit(solution)/shard_map/ppermute | solution.py:389
  7.9 13.5 %all_to_all.10.recv_ref = bf16[16,16,256]{2,1,0:T(8,128)(2,1)S(1)} all-to-all(bf16[16,16,256]{2,1,0:T(8,128)(2,1)S(1)} %get-tuple-element.40), channel_id=1, replica_groups=mesh['hst'=8,'chip'=2,'core'=2] {'hst','chip'}, dimensions={0} | all-to-all | bytes 262144 | tf_op jit(solution)/shard_map/all_to_all | solution.py:432
  21.5 0.0 collective-permute-done.2.refs_0_
  21.5 0.2 merge.1
  21.6 0.1 collective-permute-start.3
  21.7 0.0 collective-permute-done.lent_ref
  21.7 0.0 copy-done.3
  21.7 0.0 copy-done.4
  21.8 0.0 copy-done.7
  21.8 0.4 %early_one.1 = (f32[512,256]{1,0:T(8,128)S(1)}, f32[512,256]{1,0:T(8,128)S(1)}, f32[512,256]{1,0:T(8,128)S(1)}, bf16[640,256]{1,0:T(8,128)(2,1)S(1)}) custom-call(bf16[1280,256]{1,0:T(8,128)(2,1)S(1)} %get-tuple-element.29.adj_ref, bf16[1792,256]{1,0:T(8,128)(2,1)S(1)} %collective-permute-done.lent_ref, bf16[256,256]{1,0:T(8,128)(2,1)S(1)} %copy-done.1, ...), custom_call_target="tpu_custom_call" | custom-call | flops 268435456 | bytes 262144 | tf_op jit(solution)/shard_map/early_one/pallas_call | solution.py:373
  22.2 0.0 copy-start.5
  22.2 0.2 mid.1
  22.5 0.9 %collective-permute-done.3.shared_ref = bf16[640,256]{1,0:T(8,128)(2,1)S(1)} collective-permute-done((bf16[640,256]{1,0:T(8,128)(2,1)S(1)}, bf16[640,256]{1,0:T(8,128)(2,1)S(1)}, u32[]{:S(2)}, u32[]{:S(2)}) %collective-permute-start.3) | collective-permute-done | bytes 327712 | tf_op jit(solution)/shard_map/ppermute | solution.py:389
  23.4 1.0 %middle.1 = (bf16[256,256]{1,0:T(8,128)(2,1)S(1)}, bf16[256,256]{1,0:T(8,128)(2,1)S(1)}, f32[256,256]{1,0:T(8,128)S(1)}, bf16[16,16,256]{2,1,0:T(8,128)(2,1)S(1)}, bf16[512,256]{1,0:T(8,128)(2,1)S(1)}) custom-call(bf16[1280,256]{1,0:T(8,128)(2,1)S(1)} %get-tuple-element.29.adj_ref, bf16[1792,256]{1,0:T(8,128)(2,1)S(1)} %collective-permute-done.lent_ref, ...), custom_call_target="tpu_custom_call" | custom-call | flops 402653184 | bytes 393216 | tf_op jit(solution)/shard_map/middle/pallas_call | solution.py:373
  24.3 1.1 %collective-permute-start.4 = (bf16[512,256]{1,0:T(8,128)(2,1)S(1)}, bf16[512,256]{1,0:T(8,128)(2,1)S(1)}, u32[]{:S(2)}, u32[]{:S(2)}) collective-permute-start(bf16[512,256]{1,0:T(8,128)(2,1)S(1)} %get-tuple-element.53), channel_id=1, source_target_pairs={{0,2},{2,0},{1,3},{3,1},{4,6},{6,4},{5,7},{7,5},{8,10},{10,8},{9,1... | collective-permute-start | bytes 786440 | tf_op jit(solution)/shard_map/ppermute | solution.py:389
  25.5 10.8 %all_to_all.11.recv_ref = bf16[16,16,256]{2,1,0:T(8,128)(2,1)S(1)} all-to-all(bf16[16,16,256]{2,1,0:T(8,128)(2,1)S(1)} %get-tuple-element.50), channel_id=1, replica_groups=mesh['hst'=8,'chip'=2,'core'=2] {'hst','chip'}, dimensions={0} | all-to-all | bytes 262144 | tf_op jit(solution)/shard_map/all_to_all | solution.py:432
  36.3 0.0 collective-permute-done.4.refs_0_
  36.3 0.4 %there.1 = bf16[256,256]{1,0:T(8,128)(2,1)S(1)} custom-call(bf16[1792,256]{1,0:T(8,128)(2,1)S(1)} %collective-permute-done.lent_ref, bf16[256,256]{1,0:T(8,128)(2,1)S(1)} %get-tuple-element.49.value_ref, bf16[16,16,256]{2,1,0:T(8,128)(2,1)S(1)} %all_to_all.11.recv_ref, bf16[256,256]{1,0:T(8,128)(2,1)S(1)} %copy-done, ...), custom_call_target="tpu_custom_call" | custom-call | tf_op jit(solution)/shard_map/there/pallas_call | solution.py:373
  36.7 0.1 collective-permute-start.5
  36.8 0.0 copy-done.6
  36.8 1.0 %here.1 = (f32[256,256]{1,0:T(8,128)S(1)}, f32[256,256]{1,0:T(8,128)}) custom-call(bf16[1280,256]{1,0:T(8,128)(2,1)S(1)} %get-tuple-element.29.adj_ref, bf16[256,256]{1,0:T(8,128)(2,1)S(1)} %get-tuple-element.49.value_ref, bf16[16,16,256]{2,1,0:T(8,128)(2,1)S(1)} %all_to_all.11.recv_ref, bf16[256,256]{1,0:T(8,128)(2,1)S(1)} %copy-done, ...), custom_call_target="tpu_custom_call" | custom-call | flops 234881024 | bytes 229376 | tf_op jit(solution)/shard_map/here/pallas_call | solution.py:373
  37.8 0.3 collective-permute-done.5.there_ref
  38.1 0.7 %last.1 = bf16[256,256]{1,0:T(8,128)(2,1)} custom-call(f32[256,256]{1,0:T(8,128)S(1)} %get-tuple-element.54.here_ref, bf16[256,256]{1,0:T(8,128)(2,1)S(1)} %collective-permute-done.5.there_ref), custom_call_target="tpu_custom_call" | custom-call | tf_op jit(solution)/shard_map/last/pallas_call | solution.py:373
  (8 shorter events, 0.0 us)
Async XLA Ops:
  0.6 3.0 %copy-start.1 = (bf16[256,256]{1,0:T(8,128)(2,1)S(1)}, bf16[256,256]{1,0:T(8,128)(2,1)}, u32[]{:S(2)}) copy-start(bf16[256,256]{1,0:T(8,128)(2,1)} %value_ref.5) | copy-start | bytes 393220
  0.6 3.0 %copy-start.2 = (bf16[256,256]{1,0:T(8,128)(2,1)S(1)}, bf16[256,256]{1,0:T(8,128)(2,1)}, u32[]{:S(2)}) copy-start(bf16[256,256]{1,0:T(8,128)(2,1)} %up_ref.1) | copy-start | bytes 393220
  3.2 1.8 %collective-permute-start.1 = (bf16[640,256]{1,0:T(8,128)(2,1)S(1)}, bf16[640,256]{1,0:T(8,128)(2,1)S(1)}, u32[]{:S(2)}, u32[]{:S(2)}) collective-permute-start(bf16[640,256]{1,0:T(8,128)(2,1)S(1)} %get-tuple-element.38), channel_id=1, source_target_pairs={{0,1},{1,0},{2,3},{3,2},{4,5},{5,4},{6,7},{7,6},{8,9},{9,8},{10,11... | collective-permute-start | bytes 983048 | tf_op jit(solution)/shard_map/ppermute | solution.py:389
  4.0 17.7 %collective-permute-start = (bf16[1792,256]{1,0:T(8,128)(2,1)S(1)}, bf16[1792,256]{1,0:T(8,128)(2,1)S(1)}, u32[]{:S(2)}, u32[]{:S(2)}) collective-permute-start(bf16[1792,256]{1,0:T(8,128)(2,1)S(1)} %get-tuple-element.32), channel_id=1, source_target_pairs={{0,1},{1,0},{2,3},{3,2},{4,5},{5,4},{6,7},{7,6},{8,9},{9,8},{10,11... | collective-permute-start | bytes 2752520 | tf_op jit(solution)/shard_map/ppermute | solution.py:389
  4.9 16.8 %copy-start.3 = (bf16[256,256]{1,0:T(8,128)(2,1)S(1)}, bf16[256,256]{1,0:T(8,128)(2,1)}, u32[]{:S(2)}) copy-start(bf16[256,256]{1,0:T(8,128)(2,1)} %weight_ref.3) | copy-start | bytes 393220
  4.9 16.8 %copy-start.4 = (bf16[256,256]{1,0:T(8,128)(2,1)S(1)}, bf16[256,256]{1,0:T(8,128)(2,1)}, u32[]{:S(2)}) copy-start(bf16[256,256]{1,0:T(8,128)(2,1)} %self_ref.3) | copy-start | bytes 393220
  4.9 16.8 %copy-start.7 = (f32[256]{0:T(256)S(1)}, f32[256]{0:T(256)}, u32[]{:S(2)}) copy-start(f32[256]{0:T(256)} %bias_ref.2) | copy-start | bytes 3076
  5.0 16.5 %collective-permute-start.2 = (bf16[512,256]{1,0:T(8,128)(2,1)S(1)}, bf16[512,256]{1,0:T(8,128)(2,1)S(1)}, u32[]{:S(2)}, u32[]{:S(2)}) collective-permute-start(bf16[512,256]{1,0:T(8,128)(2,1)S(1)} %get-tuple-element.43), channel_id=1, source_target_pairs={{0,2},{2,0},{1,3},{3,1},{4,6},{6,4},{5,7},{7,5},{8,10},{10,8},{9,1... | collective-permute-start | bytes 786440 | tf_op jit(solution)/shard_map/ppermute | solution.py:389
  21.6 1.7 %collective-permute-start.3 = (bf16[640,256]{1,0:T(8,128)(2,1)S(1)}, bf16[640,256]{1,0:T(8,128)(2,1)S(1)}, u32[]{:S(2)}, u32[]{:S(2)}) collective-permute-start(bf16[640,256]{1,0:T(8,128)(2,1)S(1)} %get-tuple-element.48.here_ref), channel_id=1, source_target_pairs={{0,1},{1,0},{2,3},{3,2},{4,5},{5,4},{6,7},{7,6},{8,9},{9,8},{10,11... | collective-permute-start | bytes 983048 | tf_op jit(solution)/shard_map/ppermute | solution.py:389
  22.2 1.1 %copy-start.5 = (bf16[256,256]{1,0:T(8,128)(2,1)S(1)}, bf16[256,256]{1,0:T(8,128)(2,1)}, u32[]{:S(2)}) copy-start(bf16[256,256]{1,0:T(8,128)(2,1)} %neigh_one_ref.1) | copy-start | bytes 393220
  23.3 12.9 %copy-start = (bf16[256,256]{1,0:T(8,128)(2,1)S(1)}, bf16[256,256]{1,0:T(8,128)(2,1)}, u32[]{:S(2)}) copy-start(bf16[256,256]{1,0:T(8,128)(2,1)} %neigh_ref.3) | copy-start | bytes 393220
  23.3 13.4 %copy-start.6 = (f32[256]{0:T(256)S(1)}, f32[256]{0:T(256)}, u32[]{:S(2)}) copy-start(f32[256]{0:T(256)} %bias_ref.3) | copy-start | bytes 3076
  24.3 11.9 %collective-permute-start.4 = (bf16[512,256]{1,0:T(8,128)(2,1)S(1)}, bf16[512,256]{1,0:T(8,128)(2,1)S(1)}, u32[]{:S(2)}, u32[]{:S(2)}) collective-permute-start(bf16[512,256]{1,0:T(8,128)(2,1)S(1)} %get-tuple-element.53), channel_id=1, source_target_pairs={{0,2},{2,0},{1,3},{3,1},{4,6},{6,4},{5,7},{7,5},{8,10},{10,8},{9,1... | collective-permute-start | bytes 786440 | tf_op jit(solution)/shard_map/ppermute | solution.py:389
  36.7 1.4 %collective-permute-start.5 = (bf16[256,256]{1,0:T(8,128)(2,1)S(1)}, bf16[256,256]{1,0:T(8,128)(2,1)S(1)}, u32[]{:S(2)}, u32[]{:S(2)}) collective-permute-start(bf16[256,256]{1,0:T(8,128)(2,1)S(1)} %there.1), channel_id=1, source_target_pairs={{0,1},{1,0},{2,3},{3,2},{4,5},{5,4},{6,7},{7,6},{8,9},{9,8},{10,11... | collective-permute-start | bytes 393224 | tf_op jit(solution)/shard_map/ppermute | solution.py:389

commit v12 on v11

--- a/solution.py
+++ b/solution.py
@@ -170,7 +170,7 @@
         for g in range(hosts):
             at = low + g * send
             both = [picked[g * send : (g + 1) * send], total[at : at + send]]
-            msg_ref[g * chips + x] = jnp.concatenate(both, 0).astype(BF16)
+            msg_ref[x * hosts + g] = jnp.concatenate(both, 0).astype(BF16)
 
 
 def core_sum_kernel(
@@ -185,7 +185,7 @@
     send = recv_ref.shape[1] // 2
     low = part * send
     blocks = [
-        recv_ref[g * chips + x].astype(F32)[low : low + send]
+        recv_ref[x * hosts + g].astype(F32)[low : low + send]
         for x in range(chips)
         for g in range(hosts)
     ]
@@ -212,16 +212,30 @@
     return dot(place_ref[...], halo_part(recv_ref, hosts, chips, 1))
 
 
+def joint(pairs):
+    left = jnp.concatenate([a for a, _ in pairs], 1)
+    return dot(left, jnp.concatenate([b for _, b in pairs], 0))
+
+
+def square_of(adj_ref, x, side, rows):
+    return adj_ref[pl.ds(pl.multiple_of((x * CORES + side) * rows, rows), rows), :]
+
+
+def far_pairs(chips, rows, adj_ref, halo):
+    base = chips * CORES * rows
+    return [
+        (adj_ref[base + low : base + low + rows, :], halo[low : low + rows, :])
+        for low in range(0, halo.shape[0], rows)
+    ]
+
+
 def own_chip(adj_refs, blocks):
     chip, core = lax.axis_index("chip"), lax.axis_index("core")
     rows = blocks[0].shape[0]
-    parts = []
-    for adj_ref in adj_refs:
-        total = 0.0
-        for side, block in ((core, blocks[0]), (1 - core, blocks[1])):
-            low = pl.multiple_of((chip * CORES + side) * rows, rows)
-            total = total + dot(adj_ref[pl.ds(low, rows), :], block)
-        parts.append(total)
+    parts = [
+        joint([(square_of(ref, chip, s, rows), b) for s, b in zip((core, 1 - core), blocks)])
+        for ref in adj_refs
+    ]
     return jnp.concatenate(parts, 0)
 
 
@@ -261,20 +275,16 @@
     rows = value_ref.shape[0]
     far = halo.shape[0] // (chips * CORES)
     chip, core = lax.axis_index("chip"), lax.axis_index("core")
-    low = pl.multiple_of((chip * CORES + core) * rows, rows)
-    agg = dot(adj_ref[pl.ds(low, rows), :], value_ref[...])
+    pairs = [(square_of(adj_ref, chip, core, rows), value_ref[...])]
     for k, block in enumerate(came):
         x = lax.rem(chip - k - 1 + chips, chips)
-        low = pl.multiple_of((x * CORES + core) * rows, rows)
-        agg = agg + dot(adj_ref[pl.ds(low, rows), :], block[rows:, :])
+        pairs.append((square_of(adj_ref, x, core, rows), block[rows:, :]))
     rows_here = halo_part(recv_ref, hosts, chips, 0)
     halo[...] = jnp.zeros_like(halo)
     for x in range(chips):
         low = pl.multiple_of((x * CORES + core) * far, far)
         halo[pl.ds(low, far), :] = rows_here[x * far : (x + 1) * far]
-    for j in range(halo.shape[0] // rows):
-        low = (chips * CORES + j) * rows
-        agg = agg + dot(adj_ref[low : low + rows, :], halo[j * rows : (j + 1) * rows, :])
+    agg = joint(pairs + far_pairs(chips, rows, adj_ref, halo))
     return dot(agg.astype(BF16), neigh_ref[...])
 
 
@@ -308,16 +318,14 @@
             halo[pl.ds(low, far), :] = ref[at + x * far : at + (x + 1) * far, :]
 
 
-def add_far(chips, rows, adj_ref, start, size, agg, shared_ref, halo):
+def add_far(chips, rows, adj_ref, agg, shared_ref, halo):
     chip, core = lax.axis_index("chip"), lax.axis_index("core")
+    pairs = []
     for k in range(chips - 1):
         x = lax.rem(chip - k - 1 + chips, chips)
-        low = pl.multiple_of((x * CORES + 1 - core) * rows + start, size)
-        agg = agg + dot(adj_ref[pl.ds(low, size), :], shared_ref[k * rows : (k + 1) * rows, :])
-    for j in range(halo.shape[0] // rows):
-        low = chips * CORES * rows + j * rows + start
-        agg = agg + dot(adj_ref[low : low + size, :], halo[j * rows : (j + 1) * rows, :])
-    return agg
+        block = shared_ref[k * rows : (k + 1) * rows, :]
+        pairs.append((square_of(adj_ref, x, 1 - core, rows), block))
+    return agg + joint(pairs + far_pairs(chips, rows, adj_ref, halo))
 
 
 def middle_kernel(
@@ -344,9 +352,7 @@
     far, rows = pick_ref.shape
     put_halo(chips, far, rows, here_ref, shared_ref, halo)
     parts = [
-        add_far(
-            chips, rows, ref, 0, rows, agg_ref[i * rows : (i + 1) * rows, :], shared_ref, halo
-        )
+        add_far(chips, rows, ref, agg_ref[i * rows : (i + 1) * rows, :], shared_ref, halo)
         for i, ref in enumerate((adj_ref, lent_ref))
     ]
     agg = jnp.concatenate(parts, 0).astype(BF16)
@@ -360,7 +366,7 @@
     grad_pre = (grad * sigmoid * (1.0 + pre * (1.0 - sigmoid))).astype(BF16)
     grad_pre_ref[...] = grad_pre[:rows]
     u = dot_nt(grad_pre, neigh_one_ref[...]).astype(BF16)
-    total = dot(col_ref[...], u[:rows]) + dot(col_two_ref[...], u[rows:])
+    total = joint([(col_ref[...], u[:rows]), (col_two_ref[...], u[rows:])])
     picked = dot(pick_ref[...], hidden[:rows])
     deal(chips, hosts, total, picked, hidden[:rows], mine_ref, msg_ref, to_refs)
 
@@ -429,7 +435,7 @@
 
     def across(msg, to):
         terms = [shift(block, "chip", k + 1) for k, block in enumerate(to)]
-        recv = lax.all_to_all(msg, ("hst", "chip"), split_axis=0, concat_axis=0, tiled=True)
+        recv = lax.all_to_all(msg, ("chip", "hst"), split_axis=0, concat_axis=0, tiled=True)
         return terms, recv
 
     far_t = pltpu.VMEM((chips * CORES * far, rows), BF16)

time: 39 us -> 38.9 us (level)
  no operation moved by 1% of the time
where the time goes in v12:
time: 38.9 us; the launch traced here: 38.7 us
  blocking collectives  24.5 us (63%)
  Pallas kernels  6.79 us (17%)
  starting transfers between devices  4.59 us (12%)
  waiting for transfers between devices  2.02 us (5%)
  between operations  0.78 us (2%)
    all_to_all x2, blocking collectives, across(): lax.all_to_all(msg, ('chip', 'hst'), split_axis=0, concat_axis=0, tiled=T...  24.5 us
    pallas_call x10, Pallas kernels, call(): pl.pallas_call(kernel, out_shape=out_shape, in_specs=in_specs, out_specs=...  6.79 us
    ppermute x6, starting transfers between devices, shift(): return lax.ppermute(value, axis, [(i, (i + k) % size) for i in range(size)])  4.59 us
    ppermute x6, waiting for transfers between devices, shift(): return lax.ppermute(value, axis, [(i, (i + k) % size) for i in range(size)])  2.02 us
  transfers between devices with their start and end apart: 6, of which 3 were waited for; matrix products, arithmetic and copies ran while one was open for 0% of the time, Pallas kernels for 6%

profile of v12, /device:TPU:0, one launch (start us, length us, event | category | flops | bytes accessed | tf_op | source)
XLA Modules:
  0.0 38.7 jit_solution(1477754236581632583)
XLA Ops:
  0.6 0.0 copy-start.1
  0.6 0.0 copy-start.2
  0.7 2.5 %prep.1 = (bf16[1280,256]{1,0:T(8,128)(2,1)S(1)}, bf16[640,256]{1,0:T(8,128)(2,1)S(1)}, bf16[256,256]{1,0:T(8,128)(2,1)S(1)}, bf16[64,256]{1,0:T(8,128)(2,1)S(1)}, bf16[64,256]{1,0:T(8,128)(2,1)S(1)}) custom-call(s32[64]{0:T(128)} %dst_hbm.1, s32[64]{0:T(128)} %src_hbm.1, s32[64]{0:T(128)} %rows_hbm.1, s32[1,1,8,8]{3,2,1,0:T(8,128)} %send_hbm.1, ...), custom_call_target="tpu_custom_call" | custom-call | tf_op jit(solution)/shard_map/prep/pallas_call | solution.py:379
  3.2 0.5 %collective-permute-start.1 = (bf16[640,256]{1,0:T(8,128)(2,1)S(1)}, bf16[640,256]{1,0:T(8,128)(2,1)S(1)}, u32[]{:S(2)}, u32[]{:S(2)}) collective-permute-start(bf16[640,256]{1,0:T(8,128)(2,1)S(1)} %get-tuple-element.38), channel_id=1, source_target_pairs={{0,1},{1,0},{2,3},{3,2},{4,5},{5,4},{6,7},{7,6},{8,9},{9,8},{10,11... | collective-permute-start | bytes 983048 | tf_op jit(solution)/shard_map/ppermute | solution.py:395
  3.7 0.0 copy-done.1
  3.7 0.0 copy-done.2
  3.7 0.3 rest.1
  4.0 0.1 collective-permute-start
  4.1 0.8 %collective-permute-done.1.came_ref = bf16[640,256]{1,0:T(8,128)(2,1)S(1)} collective-permute-done((bf16[640,256]{1,0:T(8,128)(2,1)S(1)}, bf16[640,256]{1,0:T(8,128)(2,1)S(1)}, u32[]{:S(2)}, u32[]{:S(2)}) %collective-permute-start.1) | collective-permute-done | bytes 327712 | tf_op jit(solution)/shard_map/ppermute | solution.py:395
  4.9 0.1 core_sum.1
  5.0 2.9 %collective-permute-start.2 = (bf16[512,256]{1,0:T(8,128)(2,1)S(1)}, bf16[512,256]{1,0:T(8,128)(2,1)S(1)}, u32[]{:S(2)}, u32[]{:S(2)}) collective-permute-start(bf16[512,256]{1,0:T(8,128)(2,1)S(1)} %get-tuple-element.43), channel_id=1, source_target_pairs={{0,2},{2,0},{1,3},{3,1},{4,6},{6,4},{5,7},{7,5},{8,10},{10,8},{9,1... | collective-permute-start | bytes 786440 | tf_op jit(solution)/shard_map/ppermute | solution.py:395
  7.9 13.5 %all_to_all.10.recv_ref = bf16[16,16,256]{2,1,0:T(8,128)(2,1)S(1)} all-to-all(bf16[16,16,256]{2,1,0:T(8,128)(2,1)S(1)} %get-tuple-element.40), channel_id=1, replica_groups=mesh['hst'=8,'chip'=2,'core'=2] {'chip','hst'}, dimensions={0} | all-to-all | bytes 262144 | tf_op jit(solution)/shard_map/all_to_all | solution.py:438
  21.5 0.0 collective-permute-done.2.refs_0_
  21.5 0.2 merge.1
  21.6 0.1 collective-permute-start.3
  21.7 0.0 collective-permute-done.lent_ref
  21.7 0.0 copy-done.3
  21.7 0.0 copy-done.4
  21.8 0.0 copy-done.7
  21.8 0.4 %early_one.1 = (f32[512,256]{1,0:T(8,128)S(1)}, f32[512,256]{1,0:T(8,128)S(1)}, f32[512,256]{1,0:T(8,128)S(1)}, bf16[640,256]{1,0:T(8,128)(2,1)S(1)}) custom-call(bf16[1280,256]{1,0:T(8,128)(2,1)S(1)} %get-tuple-element.29.adj_ref, bf16[1792,256]{1,0:T(8,128)(2,1)S(1)} %collective-permute-done.lent_ref, bf16[256,256]{1,0:T(8,128)(2,1)S(1)} %copy-done.1, ...), custom_call_target="tpu_custom_call" | custom-call | flops 268435456 | bytes 262144 | tf_op jit(solution)/shard_map/early_one/pallas_call | solution.py:379
  22.2 0.0 copy-start.5
  22.2 0.2 mid.1
  22.5 0.9 %collective-permute-done.3.shared_ref = bf16[640,256]{1,0:T(8,128)(2,1)S(1)} collective-permute-done((bf16[640,256]{1,0:T(8,128)(2,1)S(1)}, bf16[640,256]{1,0:T(8,128)(2,1)S(1)}, u32[]{:S(2)}, u32[]{:S(2)}) %collective-permute-start.3) | collective-permute-done | bytes 327712 | tf_op jit(solution)/shard_map/ppermute | solution.py:395
  23.4 1.0 %middle.1 = (bf16[256,256]{1,0:T(8,128)(2,1)S(1)}, bf16[256,256]{1,0:T(8,128)(2,1)S(1)}, f32[256,256]{1,0:T(8,128)S(1)}, bf16[16,16,256]{2,1,0:T(8,128)(2,1)S(1)}, bf16[512,256]{1,0:T(8,128)(2,1)S(1)}) custom-call(bf16[1280,256]{1,0:T(8,128)(2,1)S(1)} %get-tuple-element.29.adj_ref, bf16[1792,256]{1,0:T(8,128)(2,1)S(1)} %collective-permute-done.lent_ref, ...), custom_call_target="tpu_custom_call" | custom-call | flops 402653184 | bytes 393216 | tf_op jit(solution)/shard_map/middle/pallas_call | solution.py:379
  24.3 0.9 %collective-permute-start.4 = (bf16[512,256]{1,0:T(8,128)(2,1)S(1)}, bf16[512,256]{1,0:T(8,128)(2,1)S(1)}, u32[]{:S(2)}, u32[]{:S(2)}) collective-permute-start(bf16[512,256]{1,0:T(8,128)(2,1)S(1)} %get-tuple-element.53), channel_id=1, source_target_pairs={{0,2},{2,0},{1,3},{3,1},{4,6},{6,4},{5,7},{7,5},{8,10},{10,8},{9,1... | collective-permute-start | bytes 786440 | tf_op jit(solution)/shard_map/ppermute | solution.py:395
  25.2 11.0 %all_to_all.11.recv_ref = bf16[16,16,256]{2,1,0:T(8,128)(2,1)S(1)} all-to-all(bf16[16,16,256]{2,1,0:T(8,128)(2,1)S(1)} %get-tuple-element.50), channel_id=1, replica_groups=mesh['hst'=8,'chip'=2,'core'=2] {'chip','hst'}, dimensions={0} | all-to-all | bytes 262144 | tf_op jit(solution)/shard_map/all_to_all | solution.py:438
  36.2 0.0 collective-permute-done.4.refs_0_
  36.2 0.4 %there.1 = bf16[256,256]{1,0:T(8,128)(2,1)S(1)} custom-call(bf16[1792,256]{1,0:T(8,128)(2,1)S(1)} %collective-permute-done.lent_ref, bf16[256,256]{1,0:T(8,128)(2,1)S(1)} %get-tuple-element.49.value_ref, bf16[16,16,256]{2,1,0:T(8,128)(2,1)S(1)} %all_to_all.11.recv_ref, bf16[256,256]{1,0:T(8,128)(2,1)S(1)} %copy-done, ...), custom_call_target="tpu_custom_call" | custom-call | tf_op jit(solution)/shard_map/there/pallas_call | solution.py:379
  36.6 0.1 collective-permute-start.5
  36.7 1.0 %here.1 = (f32[256,256]{1,0:T(8,128)S(1)}, f32[256,256]{1,0:T(8,128)}) custom-call(bf16[1280,256]{1,0:T(8,128)(2,1)S(1)} %get-tuple-element.29.adj_ref, bf16[256,256]{1,0:T(8,128)(2,1)S(1)} %get-tuple-element.49.value_ref, bf16[16,16,256]{2,1,0:T(8,128)(2,1)S(1)} %all_to_all.11.recv_ref, bf16[256,256]{1,0:T(8,128)(2,1)S(1)} %copy-done, ...), custom_call_target="tpu_custom_call" | custom-call | flops 234881024 | bytes 229376 | tf_op jit(solution)/shard_map/here/pallas_call | solution.py:379
  37.7 0.3 collective-permute-done.5.there_ref
  38.0 0.7 %last.1 = bf16[256,256]{1,0:T(8,128)(2,1)} custom-call(f32[256,256]{1,0:T(8,128)S(1)} %get-tuple-element.54.here_ref, bf16[256,256]{1,0:T(8,128)(2,1)S(1)} %collective-permute-done.5.there_ref), custom_call_target="tpu_custom_call" | custom-call | tf_op jit(solution)/shard_map/last/pallas_call | solution.py:379
  (8 shorter events, 0.0 us)
Async XLA Ops:
  0.6 3.0 %copy-start.1 = (bf16[256,256]{1,0:T(8,128)(2,1)S(1)}, bf16[256,256]{1,0:T(8,128)(2,1)}, u32[]{:S(2)}) copy-start(bf16[256,256]{1,0:T(8,128)(2,1)} %value_ref.5) | copy-start | bytes 393220
  0.6 3.0 %copy-start.2 = (bf16[256,256]{1,0:T(8,128)(2,1)S(1)}, bf16[256,256]{1,0:T(8,128)(2,1)}, u32[]{:S(2)}) copy-start(bf16[256,256]{1,0:T(8,128)(2,1)} %up_ref.1) | copy-start | bytes 393220
  3.2 1.8 %collective-permute-start.1 = (bf16[640,256]{1,0:T(8,128)(2,1)S(1)}, bf16[640,256]{1,0:T(8,128)(2,1)S(1)}, u32[]{:S(2)}, u32[]{:S(2)}) collective-permute-start(bf16[640,256]{1,0:T(8,128)(2,1)S(1)} %get-tuple-element.38), channel_id=1, source_target_pairs={{0,1},{1,0},{2,3},{3,2},{4,5},{5,4},{6,7},{7,6},{8,9},{9,8},{10,11... | collective-permute-start | bytes 983048 | tf_op jit(solution)/shard_map/ppermute | solution.py:395
  4.0 17.7 %collective-permute-start = (bf16[1792,256]{1,0:T(8,128)(2,1)S(1)}, bf16[1792,256]{1,0:T(8,128)(2,1)S(1)}, u32[]{:S(2)}, u32[]{:S(2)}) collective-permute-start(bf16[1792,256]{1,0:T(8,128)(2,1)S(1)} %get-tuple-element.32), channel_id=1, source_target_pairs={{0,1},{1,0},{2,3},{3,2},{4,5},{5,4},{6,7},{7,6},{8,9},{9,8},{10,11... | collective-permute-start | bytes 2752520 | tf_op jit(solution)/shard_map/ppermute | solution.py:395
  4.9 16.8 %copy-start.3 = (bf16[256,256]{1,0:T(8,128)(2,1)S(1)}, bf16[256,256]{1,0:T(8,128)(2,1)}, u32[]{:S(2)}) copy-start(bf16[256,256]{1,0:T(8,128)(2,1)} %weight_ref.3) | copy-start | bytes 393220
  4.9 16.8 %copy-start.4 = (bf16[256,256]{1,0:T(8,128)(2,1)S(1)}, bf16[256,256]{1,0:T(8,128)(2,1)}, u32[]{:S(2)}) copy-start(bf16[256,256]{1,0:T(8,128)(2,1)} %self_ref.3) | copy-start | bytes 393220
  4.9 16.8 %copy-start.7 = (f32[256]{0:T(256)S(1)}, f32[256]{0:T(256)}, u32[]{:S(2)}) copy-start(f32[256]{0:T(256)} %bias_ref.2) | copy-start | bytes 3076
  5.0 16.5 %collective-permute-start.2 = (bf16[512,256]{1,0:T(8,128)(2,1)S(1)}, bf16[512,256]{1,0:T(8,128)(2,1)S(1)}, u32[]{:S(2)}, u32[]{:S(2)}) collective-permute-start(bf16[512,256]{1,0:T(8,128)(2,1)S(1)} %get-tuple-element.43), channel_id=1, source_target_pairs={{0,2},{2,0},{1,3},{3,1},{4,6},{6,4},{5,7},{7,5},{8,10},{10,8},{9,1... | collective-permute-start | bytes 786440 | tf_op jit(solution)/shard_map/ppermute | solution.py:395
  21.6 1.7 %collective-permute-start.3 = (bf16[640,256]{1,0:T(8,128)(2,1)S(1)}, bf16[640,256]{1,0:T(8,128)(2,1)S(1)}, u32[]{:S(2)}, u32[]{:S(2)}) collective-permute-start(bf16[640,256]{1,0:T(8,128)(2,1)S(1)} %get-tuple-element.48.here_ref), channel_id=1, source_target_pairs={{0,1},{1,0},{2,3},{3,2},{4,5},{5,4},{6,7},{7,6},{8,9},{9,8},{10,11... | collective-permute-start | bytes 983048 | tf_op jit(solution)/shard_map/ppermute | solution.py:395
  22.2 1.1 %copy-start.5 = (bf16[256,256]{1,0:T(8,128)(2,1)S(1)}, bf16[256,256]{1,0:T(8,128)(2,1)}, u32[]{:S(2)}) copy-start(bf16[256,256]{1,0:T(8,128)(2,1)} %neigh_one_ref.1) | copy-start | bytes 393220
  23.3 12.8 %copy-start = (bf16[256,256]{1,0:T(8,128)(2,1)S(1)}, bf16[256,256]{1,0:T(8,128)(2,1)}, u32[]{:S(2)}) copy-start(bf16[256,256]{1,0:T(8,128)(2,1)} %neigh_ref.3) | copy-start | bytes 393220
  23.4 13.3 %copy-start.6 = (f32[256]{0:T(256)S(1)}, f32[256]{0:T(256)}, u32[]{:S(2)}) copy-start(f32[256]{0:T(256)} %bias_ref.3) | copy-start | bytes 3076
  24.3 11.9 %collective-permute-start.4 = (bf16[512,256]{1,0:T(8,128)(2,1)S(1)}, bf16[512,256]{1,0:T(8,128)(2,1)S(1)}, u32[]{:S(2)}, u32[]{:S(2)}) collective-permute-start(bf16[512,256]{1,0:T(8,128)(2,1)S(1)} %get-tuple-element.53), channel_id=1, source_target_pairs={{0,2},{2,0},{1,3},{3,1},{4,6},{6,4},{5,7},{7,5},{8,10},{10,8},{9,1... | collective-permute-start | bytes 786440 | tf_op jit(solution)/shard_map/ppermute | solution.py:395
  36.6 1.4 %collective-permute-start.5 = (bf16[256,256]{1,0:T(8,128)(2,1)S(1)}, bf16[256,256]{1,0:T(8,128)(2,1)S(1)}, u32[]{:S(2)}, u32[]{:S(2)}) collective-permute-start(bf16[256,256]{1,0:T(8,128)(2,1)S(1)} %there.1), channel_id=1, source_target_pairs={{0,1},{1,0},{2,3},{3,2},{4,5},{5,4},{6,7},{7,6},{8,9},{9,8},{10,11... | collective-permute-start | bytes 393224 | tf_op jit(solution)/shard_map/ppermute | solution.py:395

commit v13 on v12

--- a/solution.py
+++ b/solution.py
@@ -63,24 +63,27 @@
     features_hbm,
     cot_hbm,
     neigh_two_hbm,
-    adj_ref,
     give_ref,
     up_ref,
     picked_ref,
     pick_ref,
-    dst_ref,
-    src_ref,
-    rows_ref,
-    send_ref,
-    tile_buf,
-    features_ref,
-    cot_ref,
-    neigh_two_ref,
-    far_t,
-    col,
-    sems,
-    *accs,
+    *rest,
 ):
+    accs, rest = rest[:PARTS], rest[PARTS:]
+    (
+        dst_ref,
+        src_ref,
+        rows_ref,
+        send_ref,
+        tile_buf,
+        features_ref,
+        cot_ref,
+        neigh_two_ref,
+        square,
+        far_t,
+        col,
+        sems,
+    ) = rest
     tiles, blk = tile_buf.shape[0], tile_buf.shape[1]
     each = tiles // CHUNKS
     first = CHUNKS * 3 // 4
@@ -130,20 +133,38 @@
     for c in range(first, CHUNKS):
         copies[7 + c].wait()
         lax.fori_loop(c * each, (c + 1) * each, add, 0, unroll=True)
+    chip, side = lax.axis_index("chip"), 1 - lax.axis_index("core")
+    base = chips * CORES
+    for j in range(far_t.shape[0] // rows):
+        put_square(accs, bpd, base + j, square, 0)
+        far_t[j * rows : (j + 1) * rows, :] = square[...].T
+    for k in range(chips):
+        d = lax.rem(chip + k, chips) * CORES + side
+        at = k * (rows + far)
+        put_square(accs, bpd, d, square, 0)
+        col[at : at + rows, :] = square[...].T
+        low = pl.multiple_of(d * far, far)
+        col[at + rows : at + rows + far, :] = far_t[pl.ds(low, far), :]
+    give_ref[...] = dot(col[...], u).astype(BF16)
+
+
+def put_square(accs, bpd, d, out_ref, base):
+    sources = accs[0].shape[0] // bpd
+    part, blk = accs[0].shape[1:]
     for b in range(bpd):
-        for j in range(sources):
-            block = jnp.concatenate([acc[b * sources + j] for acc in accs], 0).astype(BF16)
-            low = j // bpd * rows + b * blk
-            left = j % bpd * blk
-            adj_ref[low : low + blk, left : left + blk] = block
-    column(chips, far, rows, 1 - lax.axis_index("core"), adj_ref, far_t, col)
-    give_ref[...] = dot(col[...], u).astype(BF16)
-
-
-def rest_kernel(
-    chips, adj_ref, up_ref, cot_ref, value_ref, pick_ref, col_ref, keep_ref, lend_ref, place_ref, far_t
-):
+        for j in range(bpd):
+            for i, acc in enumerate(accs):
+                low = base + b * blk + i * part
+                value = acc[b * sources + d * bpd + j].astype(BF16)
+                out_ref[low : low + part, j * blk : (j + 1) * blk] = value
+
+
+def rest_kernel(chips, up_ref, cot_ref, value_ref, pick_ref, *refs):
+    accs, (adj_ref, col_ref, keep_ref, lend_ref, place_ref, far_t) = refs[:PARTS], refs[PARTS:]
     rows = up_ref.shape[0]
+    bpd = rows // accs[0].shape[2]
+    for d in range(adj_ref.shape[0] // rows):
+        put_square(accs, bpd, d, adj_ref, d * rows)
     far = col_ref.shape[0] // chips - rows
     column(chips, far, rows, lax.axis_index("core"), adj_ref, far_t, col_ref)
     keep_ref[...] = dot(col_ref[...], up_ref[...]).astype(BF16)
@@ -358,8 +379,8 @@
     agg = jnp.concatenate(parts, 0).astype(BF16)
     pre = direct_ref[...] + dot(agg, neigh_one_ref[...])
     sigmoid = jax.nn.sigmoid(pre)
-    hidden = (pre * sigmoid).astype(BF16)
-    hidden_ref[...] = hidden[:rows]
+    hidden = (pre[:rows] * sigmoid[:rows]).astype(BF16)
+    hidden_ref[...] = hidden
     low = (chips - 1) * rows + chips * far
     add = shared_ref[low:, :].astype(F32)
     grad = jnp.concatenate([grad_ref[:rows, :], grad_ref[rows:, :] + add], 0)
@@ -367,8 +388,8 @@
     grad_pre_ref[...] = grad_pre[:rows]
     u = dot_nt(grad_pre, neigh_one_ref[...]).astype(BF16)
     total = joint([(col_ref[...], u[:rows]), (col_two_ref[...], u[rows:])])
-    picked = dot(pick_ref[...], hidden[:rows])
-    deal(chips, hosts, total, picked, hidden[:rows], mine_ref, msg_ref, to_refs)
+    picked = dot(pick_ref[...], hidden)
+    deal(chips, hosts, total, picked, hidden, mine_ref, msg_ref, to_refs)
 
 
 def last_kernel(here_ref, there_ref, output_ref):
@@ -439,16 +460,11 @@
         return terms, recv
 
     far_t = pltpu.VMEM((chips * CORES * far, rows), BF16)
-    adj, give, up, picked, pick = call(
+    sums = jax.ShapeDtypeStruct(((rows // blk) * (all_rows // blk), blk // PARTS, blk), F32)
+    give, up, picked, pick, *sums = call(
         functools.partial(prep_kernel, chips),
         "prep",
-        (
-            shape(all_rows, rows),
-            shape(count, width),
-            rows_shape,
-            shape(far, width),
-            shape(far, rows),
-        ),
+        (shape(count, width), rows_shape, shape(far, width), shape(far, rows)) + (sums,) * PARTS,
         [HBM] * 8,
         [
             pltpu.with_memory_space_constraint(value, pltpu.HBM)
@@ -472,24 +488,25 @@
             pltpu.VMEM(features.shape, BF16),
             pltpu.VMEM(cotangent.shape, BF16),
             pltpu.VMEM(neigh_two.shape, BF16),
+            pltpu.VMEM((rows, rows), BF16),
             far_t,
             pltpu.VMEM((count, rows), BF16),
             pltpu.SemaphoreType.DMA((7 + CHUNKS,)),
-        ]
-        + [pltpu.VMEM(((rows // blk) * (all_rows // blk), blk // PARTS, blk), F32)] * PARTS,
+        ],
     )
     came = shift(give, "core", 1)
-    col, keep, lend, place = call(
+    adj, col, keep, lend, place = call(
         functools.partial(rest_kernel, chips),
         "rest",
         (
+            shape(all_rows, rows),
             shape(count, rows),
             shape(count, width),
             shape(all_rows + 2 * rows, width),
             shape(rows, chips * far),
         ),
-        [VMEM] * 5,
-        (adj, up, cotangent, features, pick),
+        [VMEM] * (4 + PARTS),
+        (up, cotangent, features, pick, *sums),
         [far_t],
         flops=3 * square,
     )

time: 38.9 us -> 38.9 us (level)
  no operation moved by 1% of the time
where the time goes in v13:
time: 38.9 us; the launch traced here: 38.7 us
  blocking collectives  24.5 us (63%)
  Pallas kernels  6.92 us (18%)
  starting transfers between devices  4.6 us (12%)
  waiting for transfers between devices  1.85 us (5%)
  between operations  0.78 us (2%)
    all_to_all x2, blocking collectives, across(): lax.all_to_all(msg, ('chip', 'hst'), split_axis=0, concat_axis=0, tiled=T...  24.5 us
    pallas_call x10, Pallas kernels, call(): pl.pallas_call(kernel, out_shape=out_shape, in_specs=in_specs, out_specs=...  6.92 us
    ppermute x6, starting transfers between devices, shift(): return lax.ppermute(value, axis, [(i, (i + k) % size) for i in range(size)])  4.6 us
    ppermute x6, waiting for transfers between devices, shift(): return lax.ppermute(value, axis, [(i, (i + k) % size) for i in range(size)])  1.85 us
  transfers between devices with their start and end apart: 6, of which 3 were waited for; matrix products, arithmetic and copies ran while one was open for 0% of the time, Pallas kernels for 6%

profile of v13, /device:TPU:0, one launch (start us, length us, event | category | flops | bytes accessed | tf_op | source)
XLA Modules:
  0.0 38.7 jit_solution(4908411592868922635)
XLA Ops:
  0.6 0.0 copy-start.1
  0.6 0.0 copy-start.2
  0.7 2.4 %prep.1 = (bf16[640,256]{1,0:T(8,128)(2,1)S(1)}, bf16[256,256]{1,0:T(8,128)(2,1)S(1)}, bf16[64,256]{1,0:T(8,128)(2,1)S(1)}, bf16[64,256]{1,0:T(8,128)(2,1)S(1)},...) custom-call(s32[64]{0:T(128)} %dst_hbm.1, ...), custom_call_target="tpu_custom_call" | custom-call | tf_op jit(solution)/shard_map/prep/pallas_call | solution.py:400
  3.1 0.5 %collective-permute-start.1 = (bf16[640,256]{1,0:T(8,128)(2,1)S(1)}, bf16[640,256]{1,0:T(8,128)(2,1)S(1)}, u32[]{:S(2)}, u32[]{:S(2)}) collective-permute-start(bf16[640,256]{1,0:T(8,128)(2,1)S(1)} %get-tuple-element.46), channel_id=1, source_target_pairs={{0,1},{1,0},{2,3},{3,2},{4,5},{5,4},{6,7},{7,6},{8,9},{9,8},{10,11... | collective-permute-start | bytes 983048 | tf_op jit(solution)/shard_map/ppermute | solution.py:416
  3.6 0.0 copy-done.1
  3.6 0.0 copy-done.2
  3.6 0.5 %rest.1 = (bf16[1280,256]{1,0:T(8,128)(2,1)S(1)}, bf16[640,256]{1,0:T(8,128)(2,1)S(1)}, bf16[640,256]{1,0:T(8,128)(2,1)S(1)}, bf16[1792,256]{1,0:T(8,128)(2,1)S(1)}, bf16[256,128]{1,0:T(8,128)(2,1)S(1)}) custom-call(bf16[256,256]{1,0:T(8,128)(2,1)S(1)} %get-tuple-element.33.up_ref, bf16[256,256]{1,0:T(8,128)(2,1)S(1)} %copy-done.2, ...), custom_call_target="tpu_custom_call" | custom-call | flops 100663296 | bytes 98304 | tf_op jit(solution)/shard_map/rest/pallas_call | solution.py:400
  4.1 0.1 collective-permute-start
  4.3 0.6 %collective-permute-done.1.came_ref = bf16[640,256]{1,0:T(8,128)(2,1)S(1)} collective-permute-done((bf16[640,256]{1,0:T(8,128)(2,1)S(1)}, bf16[640,256]{1,0:T(8,128)(2,1)S(1)}, u32[]{:S(2)}, u32[]{:S(2)}) %collective-permute-start.1) | collective-permute-done | bytes 327712 | tf_op jit(solution)/shard_map/ppermute | solution.py:416
  4.9 0.1 core_sum.1
  5.0 2.9 %collective-permute-start.2 = (bf16[512,256]{1,0:T(8,128)(2,1)S(1)}, bf16[512,256]{1,0:T(8,128)(2,1)S(1)}, u32[]{:S(2)}, u32[]{:S(2)}) collective-permute-start(bf16[512,256]{1,0:T(8,128)(2,1)S(1)} %get-tuple-element.51), channel_id=1, source_target_pairs={{0,2},{2,0},{1,3},{3,1},{4,6},{6,4},{5,7},{7,5},{8,10},{10,8},{9,1... | collective-permute-start | bytes 786440 | tf_op jit(solution)/shard_map/ppermute | solution.py:416
  7.9 13.5 %all_to_all.10.recv_ref = bf16[16,16,256]{2,1,0:T(8,128)(2,1)S(1)} all-to-all(bf16[16,16,256]{2,1,0:T(8,128)(2,1)S(1)} %get-tuple-element.48), channel_id=1, replica_groups=mesh['hst'=8,'chip'=2,'core'=2] {'chip','hst'}, dimensions={0} | all-to-all | bytes 262144 | tf_op jit(solution)/shard_map/all_to_all | solution.py:459
  21.4 0.0 collective-permute-done.2.refs_0_
  21.4 0.2 merge.1
  21.6 0.1 collective-permute-start.3
  21.7 0.0 collective-permute-done.lent_ref
  21.7 0.0 copy-done.3
  21.7 0.0 copy-done.4
  21.7 0.4 %early_one.1 = (f32[512,256]{1,0:T(8,128)S(1)}, f32[512,256]{1,0:T(8,128)S(1)}, f32[512,256]{1,0:T(8,128)S(1)}, bf16[640,256]{1,0:T(8,128)(2,1)S(1)}) custom-call(bf16[1280,256]{1,0:T(8,128)(2,1)S(1)} %get-tuple-element.39.adj_ref, bf16[1792,256]{1,0:T(8,128)(2,1)S(1)} %collective-permute-done.lent_ref, bf16[256,256]{1,0:T(8,128)(2,1)S(1)} %copy-done.1, ...), custom_call_target="tpu_custom_call" | custom-call | flops 268435456 | bytes 262144 | tf_op jit(solution)/shard_map/early_one/pallas_call | solution.py:400
  22.2 0.0 copy-start.5
  22.2 0.2 mid.1
  22.4 0.9 %collective-permute-done.3.shared_ref = bf16[640,256]{1,0:T(8,128)(2,1)S(1)} collective-permute-done((bf16[640,256]{1,0:T(8,128)(2,1)S(1)}, bf16[640,256]{1,0:T(8,128)(2,1)S(1)}, u32[]{:S(2)}, u32[]{:S(2)}) %collective-permute-start.3) | collective-permute-done | bytes 327712 | tf_op jit(solution)/shard_map/ppermute | solution.py:416
  23.3 1.0 %middle.1 = (bf16[256,256]{1,0:T(8,128)(2,1)S(1)}, bf16[256,256]{1,0:T(8,128)(2,1)S(1)}, f32[256,256]{1,0:T(8,128)S(1)}, bf16[16,16,256]{2,1,0:T(8,128)(2,1)S(1)}, bf16[512,256]{1,0:T(8,128)(2,1)S(1)}) custom-call(bf16[1280,256]{1,0:T(8,128)(2,1)S(1)} %get-tuple-element.39.adj_ref, bf16[1792,256]{1,0:T(8,128)(2,1)S(1)} %collective-permute-done.lent_ref, ...), custom_call_target="tpu_custom_call" | custom-call | flops 402653184 | bytes 393216 | tf_op jit(solution)/shard_map/middle/pallas_call | solution.py:400
  24.3 0.9 %collective-permute-start.4 = (bf16[512,256]{1,0:T(8,128)(2,1)S(1)}, bf16[512,256]{1,0:T(8,128)(2,1)S(1)}, u32[]{:S(2)}, u32[]{:S(2)}) collective-permute-start(bf16[512,256]{1,0:T(8,128)(2,1)S(1)} %get-tuple-element.61), channel_id=1, source_target_pairs={{0,2},{2,0},{1,3},{3,1},{4,6},{6,4},{5,7},{7,5},{8,10},{10,8},{9,1... | collective-permute-start | bytes 786440 | tf_op jit(solution)/shard_map/ppermute | solution.py:416
  25.2 11.0 %all_to_all.11.recv_ref = bf16[16,16,256]{2,1,0:T(8,128)(2,1)S(1)} all-to-all(bf16[16,16,256]{2,1,0:T(8,128)(2,1)S(1)} %get-tuple-element.58), channel_id=1, replica_groups=mesh['hst'=8,'chip'=2,'core'=2] {'chip','hst'}, dimensions={0} | all-to-all | bytes 262144 | tf_op jit(solution)/shard_map/all_to_all | solution.py:459
  36.1 0.0 collective-permute-done.4.refs_0_
  36.2 0.4 %there.1 = bf16[256,256]{1,0:T(8,128)(2,1)S(1)} custom-call(bf16[1792,256]{1,0:T(8,128)(2,1)S(1)} %collective-permute-done.lent_ref, bf16[256,256]{1,0:T(8,128)(2,1)S(1)} %get-tuple-element.57.value_ref, bf16[16,16,256]{2,1,0:T(8,128)(2,1)S(1)} %all_to_all.11.recv_ref, bf16[256,256]{1,0:T(8,128)(2,1)S(1)} %copy-done, ...), custom_call_target="tpu_custom_call" | custom-call | tf_op jit(solution)/shard_map/there/pallas_call | solution.py:400
  36.6 0.1 collective-permute-start.5
  36.7 0.0 copy-done.6
  36.7 1.0 %here.1 = (f32[256,256]{1,0:T(8,128)S(1)}, f32[256,256]{1,0:T(8,128)}) custom-call(bf16[1280,256]{1,0:T(8,128)(2,1)S(1)} %get-tuple-element.39.adj_ref, bf16[256,256]{1,0:T(8,128)(2,1)S(1)} %get-tuple-element.57.value_ref, bf16[16,16,256]{2,1,0:T(8,128)(2,1)S(1)} %all_to_all.11.recv_ref, bf16[256,256]{1,0:T(8,128)(2,1)S(1)} %copy-done, ...), custom_call_target="tpu_custom_call" | custom-call | flops 234881024 | bytes 229376 | tf_op jit(solution)/shard_map/here/pallas_call | solution.py:400
  37.6 0.3 collective-permute-done.5.there_ref
  38.0 0.7 %last.1 = bf16[256,256]{1,0:T(8,128)(2,1)} custom-call(f32[256,256]{1,0:T(8,128)S(1)} %get-tuple-element.62.here_ref, bf16[256,256]{1,0:T(8,128)(2,1)S(1)} %collective-permute-done.5.there_ref), custom_call_target="tpu_custom_call" | custom-call | tf_op jit(solution)/shard_map/last/pallas_call | solution.py:400
  (8 shorter events, 0.0 us)
Async XLA Ops:
  0.6 3.0 %copy-start.1 = (bf16[256,256]{1,0:T(8,128)(2,1)S(1)}, bf16[256,256]{1,0:T(8,128)(2,1)}, u32[]{:S(2)}) copy-start(bf16[256,256]{1,0:T(8,128)(2,1)} %value_ref.5) | copy-start | bytes 393220
  0.6 3.0 %copy-start.2 = (bf16[256,256]{1,0:T(8,128)(2,1)S(1)}, bf16[256,256]{1,0:T(8,128)(2,1)}, u32[]{:S(2)}) copy-start(bf16[256,256]{1,0:T(8,128)(2,1)} %up_ref.1) | copy-start | bytes 393220
  3.1 1.8 %collective-permute-start.1 = (bf16[640,256]{1,0:T(8,128)(2,1)S(1)}, bf16[640,256]{1,0:T(8,128)(2,1)S(1)}, u32[]{:S(2)}, u32[]{:S(2)}) collective-permute-start(bf16[640,256]{1,0:T(8,128)(2,1)S(1)} %get-tuple-element.46), channel_id=1, source_target_pairs={{0,1},{1,0},{2,3},{3,2},{4,5},{5,4},{6,7},{7,6},{8,9},{9,8},{10,11... | collective-permute-start | bytes 983048 | tf_op jit(solution)/shard_map/ppermute | solution.py:416
  4.1 17.6 %collective-permute-start = (bf16[1792,256]{1,0:T(8,128)(2,1)S(1)}, bf16[1792,256]{1,0:T(8,128)(2,1)S(1)}, u32[]{:S(2)}, u32[]{:S(2)}) collective-permute-start(bf16[1792,256]{1,0:T(8,128)(2,1)S(1)} %get-tuple-element.40), channel_id=1, source_target_pairs={{0,1},{1,0},{2,3},{3,2},{4,5},{5,4},{6,7},{7,6},{8,9},{9,8},{10,11... | collective-permute-start | bytes 2752520 | tf_op jit(solution)/shard_map/ppermute | solution.py:416
  4.9 16.8 %copy-start.3 = (bf16[256,256]{1,0:T(8,128)(2,1)S(1)}, bf16[256,256]{1,0:T(8,128)(2,1)}, u32[]{:S(2)}) copy-start(bf16[256,256]{1,0:T(8,128)(2,1)} %weight_ref.3) | copy-start | bytes 393220
  4.9 16.8 %copy-start.4 = (bf16[256,256]{1,0:T(8,128)(2,1)S(1)}, bf16[256,256]{1,0:T(8,128)(2,1)}, u32[]{:S(2)}) copy-start(bf16[256,256]{1,0:T(8,128)(2,1)} %self_ref.3) | copy-start | bytes 393220
  4.9 16.8 %copy-start.7 = (f32[256]{0:T(256)S(1)}, f32[256]{0:T(256)}, u32[]{:S(2)}) copy-start(f32[256]{0:T(256)} %bias_ref.2) | copy-start | bytes 3076
  5.0 16.5 %collective-permute-start.2 = (bf16[512,256]{1,0:T(8,128)(2,1)S(1)}, bf16[512,256]{1,0:T(8,128)(2,1)S(1)}, u32[]{:S(2)}, u32[]{:S(2)}) collective-permute-start(bf16[512,256]{1,0:T(8,128)(2,1)S(1)} %get-tuple-element.51), channel_id=1, source_target_pairs={{0,2},{2,0},{1,3},{3,1},{4,6},{6,4},{5,7},{7,5},{8,10},{10,8},{9,1... | collective-permute-start | bytes 786440 | tf_op jit(solution)/shard_map/ppermute | solution.py:416
  21.6 1.7 %collective-permute-start.3 = (bf16[640,256]{1,0:T(8,128)(2,1)S(1)}, bf16[640,256]{1,0:T(8,128)(2,1)S(1)}, u32[]{:S(2)}, u32[]{:S(2)}) collective-permute-start(bf16[640,256]{1,0:T(8,128)(2,1)S(1)} %get-tuple-element.56.here_ref), channel_id=1, source_target_pairs={{0,1},{1,0},{2,3},{3,2},{4,5},{5,4},{6,7},{7,6},{8,9},{9,8},{10,11... | collective-permute-start | bytes 983048 | tf_op jit(solution)/shard_map/ppermute | solution.py:416
  22.2 1.1 %copy-start.5 = (bf16[256,256]{1,0:T(8,128)(2,1)S(1)}, bf16[256,256]{1,0:T(8,128)(2,1)}, u32[]{:S(2)}) copy-start(bf16[256,256]{1,0:T(8,128)(2,1)} %neigh_one_ref.1) | copy-start | bytes 393220
  23.3 12.8 %copy-start = (bf16[256,256]{1,0:T(8,128)(2,1)S(1)}, bf16[256,256]{1,0:T(8,128)(2,1)}, u32[]{:S(2)}) copy-start(bf16[256,256]{1,0:T(8,128)(2,1)} %neigh_ref.3) | copy-start | bytes 393220
  23.3 13.3 %copy-start.6 = (f32[256]{0:T(256)S(1)}, f32[256]{0:T(256)}, u32[]{:S(2)}) copy-start(f32[256]{0:T(256)} %bias_ref.3) | copy-start | bytes 3076
  24.3 11.9 %collective-permute-start.4 = (bf16[512,256]{1,0:T(8,128)(2,1)S(1)}, bf16[512,256]{1,0:T(8,128)(2,1)S(1)}, u32[]{:S(2)}, u32[]{:S(2)}) collective-permute-start(bf16[512,256]{1,0:T(8,128)(2,1)S(1)} %get-tuple-element.61), channel_id=1, source_target_pairs={{0,2},{2,0},{1,3},{3,1},{4,6},{6,4},{5,7},{7,5},{8,10},{10,8},{9,1... | collective-permute-start | bytes 786440 | tf_op jit(solution)/shard_map/ppermute | solution.py:416
  36.6 1.4 %collective-permute-start.5 = (bf16[256,256]{1,0:T(8,128)(2,1)S(1)}, bf16[256,256]{1,0:T(8,128)(2,1)S(1)}, u32[]{:S(2)}, u32[]{:S(2)}) collective-permute-start(bf16[256,256]{1,0:T(8,128)(2,1)S(1)} %there.1), channel_id=1, source_target_pairs={{0,1},{1,0},{2,3},{3,2},{4,5},{5,4},{6,7},{7,6},{8,9},{9,8},{10,11... | collective-permute-start | bytes 393224 | tf_op jit(solution)/shard_map/ppermute | solution.py:416

commit v14 on v13

--- a/solution.py
+++ b/solution.py
@@ -10,7 +10,7 @@
 F32 = jnp.float32
 BF16 = jnp.bfloat16
 MIB = 1024 * 1024
-CHUNKS = 8
+CHUNKS = 4
 PARTS = 4
 CORES = 2
 

time: 38.9 us -> 38.9 us (level)
  no operation moved by 1% of the time
where the time goes in v14:
time: 38.9 us; the launch traced here: 38.7 us
  blocking collectives  24.5 us (63%)
  Pallas kernels  6.95 us (18%)
  starting transfers between devices  4.59 us (12%)
  waiting for transfers between devices  1.86 us (5%)
  between operations  0.78 us (2%)
    all_to_all x2, blocking collectives, across(): lax.all_to_all(msg, ('chip', 'hst'), split_axis=0, concat_axis=0, tiled=T...  24.5 us
    pallas_call x10, Pallas kernels, call(): pl.pallas_call(kernel, out_shape=out_shape, in_specs=in_specs, out_specs=...  6.95 us
    ppermute x6, starting transfers between devices, shift(): return lax.ppermute(value, axis, [(i, (i + k) % size) for i in range(size)])  4.59 us
    ppermute x6, waiting for transfers between devices, shift(): return lax.ppermute(value, axis, [(i, (i + k) % size) for i in range(size)])  1.86 us
  transfers between devices with their start and end apart: 6, of which 3 were waited for; matrix products, arithmetic and copies ran while one was open for 0% of the time, Pallas kernels for 6%

profile of v14, /device:TPU:0, one launch (start us, length us, event | category | flops | bytes accessed | tf_op | source)
XLA Modules:
  0.0 38.7 jit_solution(1021792336390264123)
XLA Ops:
  0.6 0.0 copy-start.1
  0.6 0.0 copy-start.2
  0.7 2.5 %prep.1 = (bf16[640,256]{1,0:T(8,128)(2,1)S(1)}, bf16[256,256]{1,0:T(8,128)(2,1)S(1)}, bf16[64,256]{1,0:T(8,128)(2,1)S(1)}, bf16[64,256]{1,0:T(8,128)(2,1)S(1)},...) custom-call(s32[64]{0:T(128)} %dst_hbm.1, ...), custom_call_target="tpu_custom_call" | custom-call | tf_op jit(solution)/shard_map/prep/pallas_call | solution.py:400
  3.1 0.5 %collective-permute-start.1 = (bf16[640,256]{1,0:T(8,128)(2,1)S(1)}, bf16[640,256]{1,0:T(8,128)(2,1)S(1)}, u32[]{:S(2)}, u32[]{:S(2)}) collective-permute-start(bf16[640,256]{1,0:T(8,128)(2,1)S(1)} %get-tuple-element.46), channel_id=1, source_target_pairs={{0,1},{1,0},{2,3},{3,2},{4,5},{5,4},{6,7},{7,6},{8,9},{9,8},{10,11... | collective-permute-start | bytes 983048 | tf_op jit(solution)/shard_map/ppermute | solution.py:416
  3.7 0.0 copy-done.1
  3.7 0.0 copy-done.2
  3.7 0.5 %rest.1 = (bf16[1280,256]{1,0:T(8,128)(2,1)S(1)}, bf16[640,256]{1,0:T(8,128)(2,1)S(1)}, bf16[640,256]{1,0:T(8,128)(2,1)S(1)}, bf16[1792,256]{1,0:T(8,128)(2,1)S(1)}, bf16[256,128]{1,0:T(8,128)(2,1)S(1)}) custom-call(bf16[256,256]{1,0:T(8,128)(2,1)S(1)} %get-tuple-element.33.up_ref, bf16[256,256]{1,0:T(8,128)(2,1)S(1)} %copy-done.2, ...), custom_call_target="tpu_custom_call" | custom-call | flops 100663296 | bytes 98304 | tf_op jit(solution)/shard_map/rest/pallas_call | solution.py:400
  4.2 0.1 collective-permute-start
  4.3 0.6 %collective-permute-done.1.came_ref = bf16[640,256]{1,0:T(8,128)(2,1)S(1)} collective-permute-done((bf16[640,256]{1,0:T(8,128)(2,1)S(1)}, bf16[640,256]{1,0:T(8,128)(2,1)S(1)}, u32[]{:S(2)}, u32[]{:S(2)}) %collective-permute-start.1) | collective-permute-done | bytes 327712 | tf_op jit(solution)/shard_map/ppermute | solution.py:416
  4.9 0.1 core_sum.1
  5.0 2.9 %collective-permute-start.2 = (bf16[512,256]{1,0:T(8,128)(2,1)S(1)}, bf16[512,256]{1,0:T(8,128)(2,1)S(1)}, u32[]{:S(2)}, u32[]{:S(2)}) collective-permute-start(bf16[512,256]{1,0:T(8,128)(2,1)S(1)} %get-tuple-element.51), channel_id=1, source_target_pairs={{0,2},{2,0},{1,3},{3,1},{4,6},{6,4},{5,7},{7,5},{8,10},{10,8},{9,1... | collective-permute-start | bytes 786440 | tf_op jit(solution)/shard_map/ppermute | solution.py:416
  7.9 13.5 %all_to_all.10.recv_ref = bf16[16,16,256]{2,1,0:T(8,128)(2,1)S(1)} all-to-all(bf16[16,16,256]{2,1,0:T(8,128)(2,1)S(1)} %get-tuple-element.48), channel_id=1, replica_groups=mesh['hst'=8,'chip'=2,'core'=2] {'chip','hst'}, dimensions={0} | all-to-all | bytes 262144 | tf_op jit(solution)/shard_map/all_to_all | solution.py:459
  21.4 0.0 collective-permute-done.2.refs_0_
  21.5 0.2 merge.1
  21.6 0.1 collective-permute-start.3
  21.7 0.0 collective-permute-done.lent_ref
  21.7 0.0 copy-done.3
  21.7 0.0 copy-done.4
  21.8 0.4 %early_one.1 = (f32[512,256]{1,0:T(8,128)S(1)}, f32[512,256]{1,0:T(8,128)S(1)}, f32[512,256]{1,0:T(8,128)S(1)}, bf16[640,256]{1,0:T(8,128)(2,1)S(1)}) custom-call(bf16[1280,256]{1,0:T(8,128)(2,1)S(1)} %get-tuple-element.39.adj_ref, bf16[1792,256]{1,0:T(8,128)(2,1)S(1)} %collective-permute-done.lent_ref, bf16[256,256]{1,0:T(8,128)(2,1)S(1)} %copy-done.1, ...), custom_call_target="tpu_custom_call" | custom-call | flops 268435456 | bytes 262144 | tf_op jit(solution)/shard_map/early_one/pallas_call | solution.py:400
  22.2 0.0 copy-start.5
  22.2 0.2 mid.1
  22.5 0.9 %collective-permute-done.3.shared_ref = bf16[640,256]{1,0:T(8,128)(2,1)S(1)} collective-permute-done((bf16[640,256]{1,0:T(8,128)(2,1)S(1)}, bf16[640,256]{1,0:T(8,128)(2,1)S(1)}, u32[]{:S(2)}, u32[]{:S(2)}) %collective-permute-start.3) | collective-permute-done | bytes 327712 | tf_op jit(solution)/shard_map/ppermute | solution.py:416
  23.3 0.0 copy-done.5
  23.3 1.0 %middle.1 = (bf16[256,256]{1,0:T(8,128)(2,1)S(1)}, bf16[256,256]{1,0:T(8,128)(2,1)S(1)}, f32[256,256]{1,0:T(8,128)S(1)}, bf16[16,16,256]{2,1,0:T(8,128)(2,1)S(1)}, bf16[512,256]{1,0:T(8,128)(2,1)S(1)}) custom-call(bf16[1280,256]{1,0:T(8,128)(2,1)S(1)} %get-tuple-element.39.adj_ref, bf16[1792,256]{1,0:T(8,128)(2,1)S(1)} %collective-permute-done.lent_ref, ...), custom_call_target="tpu_custom_call" | custom-call | flops 402653184 | bytes 393216 | tf_op jit(solution)/shard_map/middle/pallas_call | solution.py:400
  24.3 0.9 %collective-permute-start.4 = (bf16[512,256]{1,0:T(8,128)(2,1)S(1)}, bf16[512,256]{1,0:T(8,128)(2,1)S(1)}, u32[]{:S(2)}, u32[]{:S(2)}) collective-permute-start(bf16[512,256]{1,0:T(8,128)(2,1)S(1)} %get-tuple-element.61), channel_id=1, source_target_pairs={{0,2},{2,0},{1,3},{3,1},{4,6},{6,4},{5,7},{7,5},{8,10},{10,8},{9,1... | collective-permute-start | bytes 786440 | tf_op jit(solution)/shard_map/ppermute | solution.py:416
  25.2 11.0 %all_to_all.11.recv_ref = bf16[16,16,256]{2,1,0:T(8,128)(2,1)S(1)} all-to-all(bf16[16,16,256]{2,1,0:T(8,128)(2,1)S(1)} %get-tuple-element.58), channel_id=1, replica_groups=mesh['hst'=8,'chip'=2,'core'=2] {'chip','hst'}, dimensions={0} | all-to-all | bytes 262144 | tf_op jit(solution)/shard_map/all_to_all | solution.py:459
  36.2 0.0 collective-permute-done.4.refs_0_
  36.2 0.4 %there.1 = bf16[256,256]{1,0:T(8,128)(2,1)S(1)} custom-call(bf16[1792,256]{1,0:T(8,128)(2,1)S(1)} %collective-permute-done.lent_ref, bf16[256,256]{1,0:T(8,128)(2,1)S(1)} %get-tuple-element.57.value_ref, bf16[16,16,256]{2,1,0:T(8,128)(2,1)S(1)} %all_to_all.11.recv_ref, bf16[256,256]{1,0:T(8,128)(2,1)S(1)} %copy-done, ...), custom_call_target="tpu_custom_call" | custom-call | tf_op jit(solution)/shard_map/there/pallas_call | solution.py:400
  36.6 0.1 collective-permute-start.5
  36.7 1.0 %here.1 = (f32[256,256]{1,0:T(8,128)S(1)}, f32[256,256]{1,0:T(8,128)}) custom-call(bf16[1280,256]{1,0:T(8,128)(2,1)S(1)} %get-tuple-element.39.adj_ref, bf16[256,256]{1,0:T(8,128)(2,1)S(1)} %get-tuple-element.57.value_ref, bf16[16,16,256]{2,1,0:T(8,128)(2,1)S(1)} %all_to_all.11.recv_ref, bf16[256,256]{1,0:T(8,128)(2,1)S(1)} %copy-done, ...), custom_call_target="tpu_custom_call" | custom-call | flops 234881024 | bytes 229376 | tf_op jit(solution)/shard_map/here/pallas_call | solution.py:400
  37.7 0.3 collective-permute-done.5.there_ref
  38.0 0.7 %last.1 = bf16[256,256]{1,0:T(8,128)(2,1)} custom-call(f32[256,256]{1,0:T(8,128)S(1)} %get-tuple-element.62.here_ref, bf16[256,256]{1,0:T(8,128)(2,1)S(1)} %collective-permute-done.5.there_ref), custom_call_target="tpu_custom_call" | custom-call | tf_op jit(solution)/shard_map/last/pallas_call | solution.py:400
  (8 shorter events, 0.0 us)
Async XLA Ops:
  0.6 3.0 %copy-start.1 = (bf16[256,256]{1,0:T(8,128)(2,1)S(1)}, bf16[256,256]{1,0:T(8,128)(2,1)}, u32[]{:S(2)}) copy-start(bf16[256,256]{1,0:T(8,128)(2,1)} %value_ref.5) | copy-start | bytes 393220
  0.6 3.0 %copy-start.2 = (bf16[256,256]{1,0:T(8,128)(2,1)S(1)}, bf16[256,256]{1,0:T(8,128)(2,1)}, u32[]{:S(2)}) copy-start(bf16[256,256]{1,0:T(8,128)(2,1)} %up_ref.1) | copy-start | bytes 393220
  3.1 1.8 %collective-permute-start.1 = (bf16[640,256]{1,0:T(8,128)(2,1)S(1)}, bf16[640,256]{1,0:T(8,128)(2,1)S(1)}, u32[]{:S(2)}, u32[]{:S(2)}) collective-permute-start(bf16[640,256]{1,0:T(8,128)(2,1)S(1)} %get-tuple-element.46), channel_id=1, source_target_pairs={{0,1},{1,0},{2,3},{3,2},{4,5},{5,4},{6,7},{7,6},{8,9},{9,8},{10,11... | collective-permute-start | bytes 983048 | tf_op jit(solution)/shard_map/ppermute | solution.py:416
  4.2 17.5 %collective-permute-start = (bf16[1792,256]{1,0:T(8,128)(2,1)S(1)}, bf16[1792,256]{1,0:T(8,128)(2,1)S(1)}, u32[]{:S(2)}, u32[]{:S(2)}) collective-permute-start(bf16[1792,256]{1,0:T(8,128)(2,1)S(1)} %get-tuple-element.40), channel_id=1, source_target_pairs={{0,1},{1,0},{2,3},{3,2},{4,5},{5,4},{6,7},{7,6},{8,9},{9,8},{10,11... | collective-permute-start | bytes 2752520 | tf_op jit(solution)/shard_map/ppermute | solution.py:416
  4.9 16.8 %copy-start.3 = (bf16[256,256]{1,0:T(8,128)(2,1)S(1)}, bf16[256,256]{1,0:T(8,128)(2,1)}, u32[]{:S(2)}) copy-start(bf16[256,256]{1,0:T(8,128)(2,1)} %weight_ref.3) | copy-start | bytes 393220
  4.9 16.8 %copy-start.4 = (bf16[256,256]{1,0:T(8,128)(2,1)S(1)}, bf16[256,256]{1,0:T(8,128)(2,1)}, u32[]{:S(2)}) copy-start(bf16[256,256]{1,0:T(8,128)(2,1)} %self_ref.3) | copy-start | bytes 393220
  4.9 16.8 %copy-start.7 = (f32[256]{0:T(256)S(1)}, f32[256]{0:T(256)}, u32[]{:S(2)}) copy-start(f32[256]{0:T(256)} %bias_ref.2) | copy-start | bytes 3076
  5.0 16.4 %collective-permute-start.2 = (bf16[512,256]{1,0:T(8,128)(2,1)S(1)}, bf16[512,256]{1,0:T(8,128)(2,1)S(1)}, u32[]{:S(2)}, u32[]{:S(2)}) collective-permute-start(bf16[512,256]{1,0:T(8,128)(2,1)S(1)} %get-tuple-element.51), channel_id=1, source_target_pairs={{0,2},{2,0},{1,3},{3,1},{4,6},{6,4},{5,7},{7,5},{8,10},{10,8},{9,1... | collective-permute-start | bytes 786440 | tf_op jit(solution)/shard_map/ppermute | solution.py:416
  21.6 1.7 %collective-permute-start.3 = (bf16[640,256]{1,0:T(8,128)(2,1)S(1)}, bf16[640,256]{1,0:T(8,128)(2,1)S(1)}, u32[]{:S(2)}, u32[]{:S(2)}) collective-permute-start(bf16[640,256]{1,0:T(8,128)(2,1)S(1)} %get-tuple-element.56.here_ref), channel_id=1, source_target_pairs={{0,1},{1,0},{2,3},{3,2},{4,5},{5,4},{6,7},{7,6},{8,9},{9,8},{10,11... | collective-permute-start | bytes 983048 | tf_op jit(solution)/shard_map/ppermute | solution.py:416
  22.2 1.1 %copy-start.5 = (bf16[256,256]{1,0:T(8,128)(2,1)S(1)}, bf16[256,256]{1,0:T(8,128)(2,1)}, u32[]{:S(2)}) copy-start(bf16[256,256]{1,0:T(8,128)(2,1)} %neigh_one_ref.1) | copy-start | bytes 393220
  23.3 12.8 %copy-start = (bf16[256,256]{1,0:T(8,128)(2,1)S(1)}, bf16[256,256]{1,0:T(8,128)(2,1)}, u32[]{:S(2)}) copy-start(bf16[256,256]{1,0:T(8,128)(2,1)} %neigh_ref.3) | copy-start | bytes 393220
  23.3 13.3 %copy-start.6 = (f32[256]{0:T(256)S(1)}, f32[256]{0:T(256)}, u32[]{:S(2)}) copy-start(f32[256]{0:T(256)} %bias_ref.3) | copy-start | bytes 3076
  24.3 11.9 %collective-permute-start.4 = (bf16[512,256]{1,0:T(8,128)(2,1)S(1)}, bf16[512,256]{1,0:T(8,128)(2,1)S(1)}, u32[]{:S(2)}, u32[]{:S(2)}) collective-permute-start(bf16[512,256]{1,0:T(8,128)(2,1)S(1)} %get-tuple-element.61), channel_id=1, source_target_pairs={{0,2},{2,0},{1,3},{3,1},{4,6},{6,4},{5,7},{7,5},{8,10},{10,8},{9,1... | collective-permute-start | bytes 786440 | tf_op jit(solution)/shard_map/ppermute | solution.py:416
  36.6 1.4 %collective-permute-start.5 = (bf16[256,256]{1,0:T(8,128)(2,1)S(1)}, bf16[256,256]{1,0:T(8,128)(2,1)S(1)}, u32[]{:S(2)}, u32[]{:S(2)}) collective-permute-start(bf16[256,256]{1,0:T(8,128)(2,1)S(1)} %there.1), channel_id=1, source_target_pairs={{0,1},{1,0},{2,3},{3,2},{4,5},{5,4},{6,7},{7,6},{8,9},{9,8},{10,11... | collective-permute-start | bytes 393224 | tf_op jit(solution)/shard_map/ppermute | solution.py:416

commit v15 on v13

--- a/solution.py
+++ b/solution.py
@@ -180,7 +180,7 @@
     far = picked.shape[0]
     send = far // hosts
     each = rows + far
-    chip = lax.axis_index("chip")
+    chip, core = lax.axis_index("chip"), lax.axis_index("core")
     mine_ref[...] = total[:rows]
     for k in range(chips):
         low = k * each + rows
@@ -190,8 +190,9 @@
         x = lax.rem(chip + k, chips)
         for g in range(hosts):
             at = low + g * send
-            both = [picked[g * send : (g + 1) * send], total[at : at + send]]
-            msg_ref[x * hosts + g] = jnp.concatenate(both, 0).astype(BF16)
+            to = (x * hosts + g) * CORES
+            msg_ref[to + core] = total[at : at + send].astype(BF16)
+            msg_ref[to + 1 - core] = picked[g * send : (g + 1) * send].astype(BF16)
 
 
 def core_sum_kernel(
@@ -202,11 +203,9 @@
     deal(chips, hosts, total, picked, value_ref[...], mine_ref, msg_ref, rest)
 
 
-def halo_part(recv_ref, hosts, chips, part):
-    send = recv_ref.shape[1] // 2
-    low = part * send
+def received(recv_ref, hosts, chips, side):
     blocks = [
-        recv_ref[x * hosts + g].astype(F32)[low : low + send]
+        recv_ref[(x * hosts + g) * CORES + side].astype(F32)
         for x in range(chips)
         for g in range(hosts)
     ]
@@ -223,14 +222,14 @@
     total = total + returned(place_ref, recv_ref, hosts, chips)
     sum_ref[...] = total
     low = len(came) * rows
-    halo = halo_part(recv_ref, hosts, chips, 0)
+    halo = received(recv_ref, hosts, chips, 1 - lax.axis_index("core"))
     high = low + halo.shape[0]
     out_ref[low:high, :] = halo
     out_ref[high:, :] = total.astype(BF16)
 
 
 def returned(place_ref, recv_ref, hosts, chips):
-    return dot(place_ref[...], halo_part(recv_ref, hosts, chips, 1))
+    return dot(place_ref[...], received(recv_ref, hosts, chips, lax.axis_index("core")))
 
 
 def joint(pairs):
@@ -300,10 +299,10 @@
     for k, block in enumerate(came):
         x = lax.rem(chip - k - 1 + chips, chips)
         pairs.append((square_of(adj_ref, x, core, rows), block[rows:, :]))
-    rows_here = halo_part(recv_ref, hosts, chips, 0)
+    rows_here = received(recv_ref, hosts, chips, 1 - core)
     halo[...] = jnp.zeros_like(halo)
     for x in range(chips):
-        low = pl.multiple_of((x * CORES + core) * far, far)
+        low = pl.multiple_of((x * CORES + 1 - core) * far, far)
         halo[pl.ds(low, far), :] = rows_here[x * far : (x + 1) * far]
     agg = joint(pairs + far_pairs(chips, rows, adj_ref, halo))
     return dot(agg.astype(BF16), neigh_ref[...])
@@ -334,7 +333,7 @@
     core = lax.axis_index("core")
     at = (chips - 1) * rows
     for x in range(chips):
-        for side, ref in ((core, here_ref), (1 - core, shared_ref)):
+        for side, ref in ((1 - core, here_ref), (core, shared_ref)):
             low = pl.multiple_of((x * CORES + side) * far, far)
             halo[pl.ds(low, far), :] = ref[at + x * far : at + (x + 1) * far, :]
 
@@ -451,12 +450,12 @@
     halo_rows = (chips - 1) * rows + chips * far
     dealt = (
         sum_shape,
-        jax.ShapeDtypeStruct((hosts * chips, 2 * send, width), BF16),
+        jax.ShapeDtypeStruct((chips * hosts * CORES, send, width), BF16),
     ) + (shape(2 * rows, width),) * (chips - 1)
 
     def across(msg, to):
         terms = [shift(block, "chip", k + 1) for k, block in enumerate(to)]
-        recv = lax.all_to_all(msg, ("chip", "hst"), split_axis=0, concat_axis=0, tiled=True)
+        recv = lax.all_to_all(msg, ("chip", "hst", "core"), split_axis=0, concat_axis=0, tiled=True)
         return terms, recv
 
     far_t = pltpu.VMEM((chips * CORES * far, rows), BF16)

time: 38.9 us -> 37.9 us (0.974)
  blocking collectives: 24.5 us -> 23.5 us
  starting transfers between devices: 4.6 us -> 5.07 us
  waiting for transfers between devices: 1.85 us -> 1.38 us
    all_to_all x2, blocking collectives: 24.5 us -> 23.5 us  [across(): lax.all_to_all(msg, ('chip', 'hst', 'core'), split_axis=0, concat_axis=0,...]
    ppermute x6, starting transfers between devices: 4.6 us -> 5.07 us  [shift(): return lax.ppermute(value, axis, [(i, (i + k) % size) for i in range(size)])]
    ppermute x6, waiting for transfers between devices: 1.85 us -> 1.38 us  [shift(): return lax.ppermute(value, axis, [(i, (i + k) % size) for i in range(size)])]
where the time goes in v15:
time: 37.9 us; the launch traced here: 37.7 us
  blocking collectives  23.5 us (62%)
  Pallas kernels  6.95 us (18%)
  starting transfers between devices  5.07 us (13%)
  waiting for transfers between devices  1.38 us (4%)
  between operations  0.73 us (2%)
    all_to_all x2, blocking collectives, across(): lax.all_to_all(msg, ('chip', 'hst', 'core'), split_axis=0, concat_axis=0,...  23.5 us
    pallas_call x10, Pallas kernels, call(): pl.pallas_call(kernel, out_shape=out_shape, in_specs=in_specs, out_specs=...  6.95 us
    ppermute x6, starting transfers between devices, shift(): return lax.ppermute(value, axis, [(i, (i + k) % size) for i in range(size)])  5.07 us
    ppermute x6, waiting for transfers between devices, shift(): return lax.ppermute(value, axis, [(i, (i + k) % size) for i in range(size)])  1.38 us
  transfers between devices with their start and end apart: 6, of which 3 were waited for; matrix products, arithmetic and copies ran while one was open for 0% of the time, Pallas kernels for 6%

profile of v15, /device:TPU:0, one launch (start us, length us, event | category | flops | bytes accessed | tf_op | source)
XLA Modules:
  0.0 37.7 jit_solution(10795167107873105840)
XLA Ops:
  0.6 0.0 copy-start.1
  0.6 0.0 copy-start.2
  0.7 2.5 %prep.1 = (bf16[640,256]{1,0:T(8,128)(2,1)S(1)}, bf16[256,256]{1,0:T(8,128)(2,1)S(1)}, bf16[64,256]{1,0:T(8,128)(2,1)S(1)}, bf16[64,256]{1,0:T(8,128)(2,1)S(1)},...) custom-call(s32[64]{0:T(128)} %dst_hbm.1, ...), custom_call_target="tpu_custom_call" | custom-call | tf_op jit(solution)/shard_map/prep/pallas_call | solution.py:399
  3.1 0.5 %collective-permute-start.1 = (bf16[640,256]{1,0:T(8,128)(2,1)S(1)}, bf16[640,256]{1,0:T(8,128)(2,1)S(1)}, u32[]{:S(2)}, u32[]{:S(2)}) collective-permute-start(bf16[640,256]{1,0:T(8,128)(2,1)S(1)} %get-tuple-element.46), channel_id=1, source_target_pairs={{0,1},{1,0},{2,3},{3,2},{4,5},{5,4},{6,7},{7,6},{8,9},{9,8},{10,11... | collective-permute-start | bytes 983048 | tf_op jit(solution)/shard_map/ppermute | solution.py:415
  3.6 0.0 copy-done.1
  3.6 0.0 copy-done.2
  3.6 0.5 %rest.1 = (bf16[1280,256]{1,0:T(8,128)(2,1)S(1)}, bf16[640,256]{1,0:T(8,128)(2,1)S(1)}, bf16[640,256]{1,0:T(8,128)(2,1)S(1)}, bf16[1792,256]{1,0:T(8,128)(2,1)S(1)}, bf16[256,128]{1,0:T(8,128)(2,1)S(1)}) custom-call(bf16[256,256]{1,0:T(8,128)(2,1)S(1)} %get-tuple-element.33.up_ref, bf16[256,256]{1,0:T(8,128)(2,1)S(1)} %copy-done.2, ...), custom_call_target="tpu_custom_call" | custom-call | flops 100663296 | bytes 98304 | tf_op jit(solution)/shard_map/rest/pallas_call | solution.py:399
  4.1 0.1 collective-permute-start
  4.3 0.6 %collective-permute-done.1.came_ref = bf16[640,256]{1,0:T(8,128)(2,1)S(1)} collective-permute-done((bf16[640,256]{1,0:T(8,128)(2,1)S(1)}, bf16[640,256]{1,0:T(8,128)(2,1)S(1)}, u32[]{:S(2)}, u32[]{:S(2)}) %collective-permute-start.1) | collective-permute-done | bytes 327712 | tf_op jit(solution)/shard_map/ppermute | solution.py:415
  4.9 0.1 core_sum.1
  5.0 2.9 %collective-permute-start.2 = (bf16[512,256]{1,0:T(8,128)(2,1)S(1)}, bf16[512,256]{1,0:T(8,128)(2,1)S(1)}, u32[]{:S(2)}, u32[]{:S(2)}) collective-permute-start(bf16[512,256]{1,0:T(8,128)(2,1)S(1)} %get-tuple-element.51), channel_id=1, source_target_pairs={{0,2},{2,0},{1,3},{3,1},{4,6},{6,4},{5,7},{7,5},{8,10},{10,8},{9,1... | collective-permute-start | bytes 786440 | tf_op jit(solution)/shard_map/ppermute | solution.py:415
  7.9 12.9 %all_to_all.10.recv_ref = bf16[32,8,256]{2,1,0:T(8,128)(2,1)S(1)} all-to-all(bf16[32,8,256]{2,1,0:T(8,128)(2,1)S(1)} %get-tuple-element.48), channel_id=1, replica_groups=mesh['hst'=8,'chip'=2,'core'=2] {'chip','hst','core'}, dimensions={0} | all-to-all | bytes 262144 | tf_op jit(solution)/shard_map/all_to_all | solution.py:458
  20.8 0.0 collective-permute-done.2.refs_0_
  20.8 0.2 merge.1
  21.0 0.3 collective-permute-start.3
  21.4 0.0 collective-permute-done.lent_ref
  21.4 0.0 copy-done.3
  21.4 0.0 copy-done.4
  21.4 0.0 copy-done.7
  21.4 0.4 %early_one.1 = (f32[512,256]{1,0:T(8,128)S(1)}, f32[512,256]{1,0:T(8,128)S(1)}, f32[512,256]{1,0:T(8,128)S(1)}, bf16[640,256]{1,0:T(8,128)(2,1)S(1)}) custom-call(bf16[1280,256]{1,0:T(8,128)(2,1)S(1)} %get-tuple-element.39.adj_ref, bf16[1792,256]{1,0:T(8,128)(2,1)S(1)} %collective-permute-done.lent_ref, bf16[256,256]{1,0:T(8,128)(2,1)S(1)} %copy-done.1, ...), custom_call_target="tpu_custom_call" | custom-call | flops 268435456 | bytes 262144 | tf_op jit(solution)/shard_map/early_one/pallas_call | solution.py:399
  21.8 0.0 copy-start.5
  21.8 0.2 mid.1
  22.1 0.7 %collective-permute-done.3.shared_ref = bf16[640,256]{1,0:T(8,128)(2,1)S(1)} collective-permute-done((bf16[640,256]{1,0:T(8,128)(2,1)S(1)}, bf16[640,256]{1,0:T(8,128)(2,1)S(1)}, u32[]{:S(2)}, u32[]{:S(2)}) %collective-permute-start.3) | collective-permute-done | bytes 327712 | tf_op jit(solution)/shard_map/ppermute | solution.py:415
  22.7 1.0 %middle.1 = (bf16[256,256]{1,0:T(8,128)(2,1)S(1)}, bf16[256,256]{1,0:T(8,128)(2,1)S(1)}, f32[256,256]{1,0:T(8,128)S(1)}, bf16[32,8,256]{2,1,0:T(8,128)(2,1)S(1)}, bf16[512,256]{1,0:T(8,128)(2,1)S(1)}) custom-call(bf16[1280,256]{1,0:T(8,128)(2,1)S(1)} %get-tuple-element.39.adj_ref, bf16[1792,256]{1,0:T(8,128)(2,1)S(1)} %collective-permute-done.lent_ref, ...), custom_call_target="tpu_custom_call" | custom-call | flops 402653184 | bytes 393216 | tf_op jit(solution)/shard_map/middle/pallas_call | solution.py:399
  23.7 0.9 %collective-permute-start.4 = (bf16[512,256]{1,0:T(8,128)(2,1)S(1)}, bf16[512,256]{1,0:T(8,128)(2,1)S(1)}, u32[]{:S(2)}, u32[]{:S(2)}) collective-permute-start(bf16[512,256]{1,0:T(8,128)(2,1)S(1)} %get-tuple-element.61), channel_id=1, source_target_pairs={{0,2},{2,0},{1,3},{3,1},{4,6},{6,4},{5,7},{7,5},{8,10},{10,8},{9,1... | collective-permute-start | bytes 786440 | tf_op jit(solution)/shard_map/ppermute | solution.py:415
  24.6 10.6 %all_to_all.11.recv_ref = bf16[32,8,256]{2,1,0:T(8,128)(2,1)S(1)} all-to-all(bf16[32,8,256]{2,1,0:T(8,128)(2,1)S(1)} %get-tuple-element.58), channel_id=1, replica_groups=mesh['hst'=8,'chip'=2,'core'=2] {'chip','hst','core'}, dimensions={0} | all-to-all | bytes 262144 | tf_op jit(solution)/shard_map/all_to_all | solution.py:458
  35.2 0.0 collective-permute-done.4.refs_0_
  35.2 0.4 %there.1 = bf16[256,256]{1,0:T(8,128)(2,1)S(1)} custom-call(bf16[1792,256]{1,0:T(8,128)(2,1)S(1)} %collective-permute-done.lent_ref, bf16[256,256]{1,0:T(8,128)(2,1)S(1)} %get-tuple-element.57.value_ref, bf16[32,8,256]{2,1,0:T(8,128)(2,1)S(1)} %all_to_all.11.recv_ref, bf16[256,256]{1,0:T(8,128)(2,1)S(1)} %copy-done, ...), custom_call_target="tpu_custom_call" | custom-call | tf_op jit(solution)/shard_map/there/pallas_call | solution.py:399
  35.6 0.3 collective-permute-start.5
  35.9 1.0 %here.1 = (f32[256,256]{1,0:T(8,128)S(1)}, f32[256,256]{1,0:T(8,128)}) custom-call(bf16[1280,256]{1,0:T(8,128)(2,1)S(1)} %get-tuple-element.39.adj_ref, bf16[256,256]{1,0:T(8,128)(2,1)S(1)} %get-tuple-element.57.value_ref, bf16[32,8,256]{2,1,0:T(8,128)(2,1)S(1)} %all_to_all.11.recv_ref, bf16[256,256]{1,0:T(8,128)(2,1)S(1)} %copy-done, ...), custom_call_target="tpu_custom_call" | custom-call | flops 234881024 | bytes 229376 | tf_op jit(solution)/shard_map/here/pallas_call | solution.py:399
  36.9 0.1 collective-permute-done.5.there_ref
  37.0 0.7 %last.1 = bf16[256,256]{1,0:T(8,128)(2,1)} custom-call(f32[256,256]{1,0:T(8,128)S(1)} %get-tuple-element.62.here_ref, bf16[256,256]{1,0:T(8,128)(2,1)S(1)} %collective-permute-done.5.there_ref), custom_call_target="tpu_custom_call" | custom-call | tf_op jit(solution)/shard_map/last/pallas_call | solution.py:399
  (8 shorter events, 0.0 us)
Async XLA Ops:
  0.6 3.0 %copy-start.1 = (bf16[256,256]{1,0:T(8,128)(2,1)S(1)}, bf16[256,256]{1,0:T(8,128)(2,1)}, u32[]{:S(2)}) copy-start(bf16[256,256]{1,0:T(8,128)(2,1)} %value_ref.5) | copy-start | bytes 393220
  0.6 3.0 %copy-start.2 = (bf16[256,256]{1,0:T(8,128)(2,1)S(1)}, bf16[256,256]{1,0:T(8,128)(2,1)}, u32[]{:S(2)}) copy-start(bf16[256,256]{1,0:T(8,128)(2,1)} %up_ref.1) | copy-start | bytes 393220
  3.1 1.8 %collective-permute-start.1 = (bf16[640,256]{1,0:T(8,128)(2,1)S(1)}, bf16[640,256]{1,0:T(8,128)(2,1)S(1)}, u32[]{:S(2)}, u32[]{:S(2)}) collective-permute-start(bf16[640,256]{1,0:T(8,128)(2,1)S(1)} %get-tuple-element.46), channel_id=1, source_target_pairs={{0,1},{1,0},{2,3},{3,2},{4,5},{5,4},{6,7},{7,6},{8,9},{9,8},{10,11... | collective-permute-start | bytes 983048 | tf_op jit(solution)/shard_map/ppermute | solution.py:415
  4.1 17.2 %collective-permute-start = (bf16[1792,256]{1,0:T(8,128)(2,1)S(1)}, bf16[1792,256]{1,0:T(8,128)(2,1)S(1)}, u32[]{:S(2)}, u32[]{:S(2)}) collective-permute-start(bf16[1792,256]{1,0:T(8,128)(2,1)S(1)} %get-tuple-element.40), channel_id=1, source_target_pairs={{0,1},{1,0},{2,3},{3,2},{4,5},{5,4},{6,7},{7,6},{8,9},{9,8},{10,11... | collective-permute-start | bytes 2752520 | tf_op jit(solution)/shard_map/ppermute | solution.py:415
  4.9 16.5 %copy-start.3 = (bf16[256,256]{1,0:T(8,128)(2,1)S(1)}, bf16[256,256]{1,0:T(8,128)(2,1)}, u32[]{:S(2)}) copy-start(bf16[256,256]{1,0:T(8,128)(2,1)} %weight_ref.3) | copy-start | bytes 393220
  4.9 16.5 %copy-start.4 = (bf16[256,256]{1,0:T(8,128)(2,1)S(1)}, bf16[256,256]{1,0:T(8,128)(2,1)}, u32[]{:S(2)}) copy-start(bf16[256,256]{1,0:T(8,128)(2,1)} %self_ref.3) | copy-start | bytes 393220
  4.9 16.5 %copy-start.7 = (f32[256]{0:T(256)S(1)}, f32[256]{0:T(256)}, u32[]{:S(2)}) copy-start(f32[256]{0:T(256)} %bias_ref.2) | copy-start | bytes 3076
  5.0 15.9 %collective-permute-start.2 = (bf16[512,256]{1,0:T(8,128)(2,1)S(1)}, bf16[512,256]{1,0:T(8,128)(2,1)S(1)}, u32[]{:S(2)}, u32[]{:S(2)}) collective-permute-start(bf16[512,256]{1,0:T(8,128)(2,1)S(1)} %get-tuple-element.51), channel_id=1, source_target_pairs={{0,2},{2,0},{1,3},{3,1},{4,6},{6,4},{5,7},{7,5},{8,10},{10,8},{9,1... | collective-permute-start | bytes 786440 | tf_op jit(solution)/shard_map/ppermute | solution.py:415
  21.0 1.7 %collective-permute-start.3 = (bf16[640,256]{1,0:T(8,128)(2,1)S(1)}, bf16[640,256]{1,0:T(8,128)(2,1)S(1)}, u32[]{:S(2)}, u32[]{:S(2)}) collective-permute-start(bf16[640,256]{1,0:T(8,128)(2,1)S(1)} %get-tuple-element.56.here_ref), channel_id=1, source_target_pairs={{0,1},{1,0},{2,3},{3,2},{4,5},{5,4},{6,7},{7,6},{8,9},{9,8},{10,11... | collective-permute-start | bytes 983048 | tf_op jit(solution)/shard_map/ppermute | solution.py:415
  21.8 0.9 %copy-start.5 = (bf16[256,256]{1,0:T(8,128)(2,1)S(1)}, bf16[256,256]{1,0:T(8,128)(2,1)}, u32[]{:S(2)}) copy-start(bf16[256,256]{1,0:T(8,128)(2,1)} %neigh_one_ref.1) | copy-start | bytes 393220
  22.7 12.4 %copy-start = (bf16[256,256]{1,0:T(8,128)(2,1)S(1)}, bf16[256,256]{1,0:T(8,128)(2,1)}, u32[]{:S(2)}) copy-start(bf16[256,256]{1,0:T(8,128)(2,1)} %neigh_ref.3) | copy-start | bytes 393220
  22.7 13.2 %copy-start.6 = (f32[256]{0:T(256)S(1)}, f32[256]{0:T(256)}, u32[]{:S(2)}) copy-start(f32[256]{0:T(256)} %bias_ref.3) | copy-start | bytes 3076
  23.7 11.4 %collective-permute-start.4 = (bf16[512,256]{1,0:T(8,128)(2,1)S(1)}, bf16[512,256]{1,0:T(8,128)(2,1)S(1)}, u32[]{:S(2)}, u32[]{:S(2)}) collective-permute-start(bf16[512,256]{1,0:T(8,128)(2,1)S(1)} %get-tuple-element.61), channel_id=1, source_target_pairs={{0,2},{2,0},{1,3},{3,1},{4,6},{6,4},{5,7},{7,5},{8,10},{10,8},{9,1... | collective-permute-start | bytes 786440 | tf_op jit(solution)/shard_map/ppermute | solution.py:415
  35.6 1.4 %collective-permute-start.5 = (bf16[256,256]{1,0:T(8,128)(2,1)S(1)}, bf16[256,256]{1,0:T(8,128)(2,1)S(1)}, u32[]{:S(2)}, u32[]{:S(2)}) collective-permute-start(bf16[256,256]{1,0:T(8,128)(2,1)S(1)} %there.1), channel_id=1, source_target_pairs={{0,1},{1,0},{2,3},{3,2},{4,5},{5,4},{6,7},{7,6},{8,9},{9,8},{10,11... | collective-permute-start | bytes 393224 | tf_op jit(solution)/shard_map/ppermute | solution.py:415

commit v16 on v15

--- a/solution.py
+++ b/solution.py
@@ -51,6 +51,17 @@
         at = k * each
         out_ref[at : at + rows, :] = adj_ref[pl.ds(pl.multiple_of(d * rows, rows), rows), :].T
         out_ref[at + rows : at + each, :] = far_t[pl.ds(pl.multiple_of(d * far, far), far), :]
+
+
+def far_columns(chips, far_t, out_ref):
+    far = far_t.shape[0] // (chips * CORES)
+    core = lax.axis_index("core")
+    parts = [
+        far_t[pl.ds(pl.multiple_of((x * CORES + side) * far, far), far), :]
+        for side in (1 - core, core)
+        for x in range(chips)
+    ]
+    out_ref[...] = jnp.concatenate(parts, 0).T
 
 
 def prep_kernel(
@@ -160,13 +171,15 @@
 
 
 def rest_kernel(chips, up_ref, cot_ref, value_ref, pick_ref, *refs):
-    accs, (adj_ref, col_ref, keep_ref, lend_ref, place_ref, far_t) = refs[:PARTS], refs[PARTS:]
+    accs = refs[:PARTS]
+    adj_ref, col_ref, keep_ref, lend_ref, place_ref, far_ref, far_t = refs[PARTS:]
     rows = up_ref.shape[0]
     bpd = rows // accs[0].shape[2]
     for d in range(adj_ref.shape[0] // rows):
         put_square(accs, bpd, d, adj_ref, d * rows)
     far = col_ref.shape[0] // chips - rows
     column(chips, far, rows, lax.axis_index("core"), adj_ref, far_t, col_ref)
+    far_columns(chips, far_t, far_ref)
     keep_ref[...] = dot(col_ref[...], up_ref[...]).astype(BF16)
     low = adj_ref.shape[0]
     lend_ref[:low, :] = adj_ref[...]
@@ -190,7 +203,7 @@
         x = lax.rem(chip + k, chips)
         for g in range(hosts):
             at = low + g * send
-            to = (x * hosts + g) * CORES
+            to = (g * chips + x) * CORES
             msg_ref[to + core] = total[at : at + send].astype(BF16)
             msg_ref[to + 1 - core] = picked[g * send : (g + 1) * send].astype(BF16)
 
@@ -205,7 +218,7 @@
 
 def received(recv_ref, hosts, chips, side):
     blocks = [
-        recv_ref[(x * hosts + g) * CORES + side].astype(F32)
+        recv_ref[(g * chips + x) * CORES + side].astype(F32)
         for x in range(chips)
         for g in range(hosts)
     ]
@@ -241,14 +254,6 @@
     return adj_ref[pl.ds(pl.multiple_of((x * CORES + side) * rows, rows), rows), :]
 
 
-def far_pairs(chips, rows, adj_ref, halo):
-    base = chips * CORES * rows
-    return [
-        (adj_ref[base + low : base + low + rows, :], halo[low : low + rows, :])
-        for low in range(0, halo.shape[0], rows)
-    ]
-
-
 def own_chip(adj_refs, blocks):
     chip, core = lax.axis_index("chip"), lax.axis_index("core")
     rows = blocks[0].shape[0]
@@ -260,8 +265,8 @@
 
 
 def early_one_kernel(
-    chips, adj_ref, lent_ref, value_ref, self_ref, bias_ref, up_ref, weight_ref,
-    agg_ref, direct_ref, grad_ref, col_ref, far_t,
+    chips, adj_ref, lent_ref, value_ref, self_ref, bias_ref, up_ref, weight_ref, unused_ref,
+    agg_ref, direct_ref, grad_ref, col_ref, far_ref, far_t,
 ):
     value = value_ref[...]
     rows = value.shape[0]
@@ -274,78 +279,74 @@
     grad_ref[...] = dot_nt(both, weight_ref[...])
     far = col_ref.shape[0] // chips - rows
     column(chips, far, rows, lax.axis_index("core"), lent_ref, far_t, col_ref)
-
-
-def mid_kernel(chips, adj_ref, lent_ref, agg_ref, part_ref, sum_ref, *refs):
+    far_columns(chips, far_t, far_ref)
+
+
+def mid_kernel(
+    chips, adj_ref, lent_ref, far_ref, far_two_ref, agg_ref, part_ref, sum_ref, here_ref, *refs
+):
     came, (agg_out, grad_ref) = refs[:-2], refs[-2:]
     rows = sum_ref.shape[0]
-    chip, core = lax.axis_index("chip"), lax.axis_index("core")
-    for i, ref in enumerate((adj_ref, lent_ref)):
-        agg = agg_ref[i * rows : (i + 1) * rows, :]
-        for k, block in enumerate(came):
-            x = lax.rem(chip - k - 1 + chips, chips)
-            low = pl.multiple_of((x * CORES + core) * rows, rows)
-            agg = agg + dot(ref[pl.ds(low, rows), :], block[rows:, :])
-        agg_out[i * rows : (i + 1) * rows, :] = agg
+    halo = here_ref[(chips - 1) * rows : here_ref.shape[0] - rows, :]
+    for i, (ref, columns) in enumerate(((adj_ref, far_ref), (lent_ref, far_two_ref))):
+        pairs = other_chips(chips, ref, came) + [(columns[:, : halo.shape[0]], halo)]
+        part = slice(i * rows, (i + 1) * rows)
+        agg_out[part, :] = agg_ref[part, :] + joint(pairs)
     grad_ref[:rows, :] = part_ref[:rows, :] + sum_ref[...]
     grad_ref[rows:, :] = part_ref[rows:, :]
 
 
-def column_product(chips, hosts, adj_ref, value_ref, came, recv_ref, neigh_ref, halo):
-    rows = value_ref.shape[0]
-    far = halo.shape[0] // (chips * CORES)
+def other_chips(chips, adj_ref, came):
     chip, core = lax.axis_index("chip"), lax.axis_index("core")
-    pairs = [(square_of(adj_ref, chip, core, rows), value_ref[...])]
+    pairs = []
     for k, block in enumerate(came):
+        rows = block.shape[0] // 2
         x = lax.rem(chip - k - 1 + chips, chips)
         pairs.append((square_of(adj_ref, x, core, rows), block[rows:, :]))
-    rows_here = received(recv_ref, hosts, chips, 1 - core)
-    halo[...] = jnp.zeros_like(halo)
-    for x in range(chips):
-        low = pl.multiple_of((x * CORES + 1 - core) * far, far)
-        halo[pl.ds(low, far), :] = rows_here[x * far : (x + 1) * far]
-    agg = joint(pairs + far_pairs(chips, rows, adj_ref, halo))
-    return dot(agg.astype(BF16), neigh_ref[...])
-
-
-def there_kernel(chips, hosts, lent_ref, value_ref, recv_ref, neigh_ref, *refs):
-    came, out_ref, halo = refs[:-2], refs[-2], refs[-1]
+    return pairs
+
+
+def column_product(chips, hosts, adj_ref, far_ref, value_ref, came, recv_ref, neigh_ref):
+    rows = value_ref.shape[0]
+    chip, core = lax.axis_index("chip"), lax.axis_index("core")
+    halo = received(recv_ref, hosts, chips, 1 - core)
+    pairs = [(square_of(adj_ref, chip, core, rows), value_ref[...])]
+    pairs += other_chips(chips, adj_ref, came) + [(far_ref[:, : halo.shape[0]], halo)]
+    return dot(joint(pairs).astype(BF16), neigh_ref[...])
+
+
+def there_kernel(chips, hosts, lent_ref, far_ref, value_ref, recv_ref, neigh_ref, *refs):
+    came, out_ref = refs[:-1], refs[-1]
     out_ref[...] = column_product(
-        chips, hosts, lent_ref, value_ref, came, recv_ref, neigh_ref, halo
+        chips, hosts, lent_ref, far_ref, value_ref, came, recv_ref, neigh_ref
     ).astype(BF16)
 
 
 def here_kernel(
-    chips, hosts, adj_ref, value_ref, recv_ref, neigh_ref, self_ref, bias_ref, up_ref, weight_ref,
-    mine_ref, place_ref, *refs
+    chips, hosts, adj_ref, far_ref, value_ref, recv_ref, neigh_ref, self_ref, bias_ref, up_ref,
+    weight_ref, mine_ref, place_ref, *refs
 ):
-    came, out_ref, grad_ref, halo = refs[:-3], refs[-3], refs[-2], refs[-1]
+    came, (out_ref, grad_ref) = refs[:-2], refs[-2:]
     rows = mine_ref.shape[0]
     grad = dot_nt(up_ref[...], weight_ref[...]) + mine_ref[...]
     for block in came:
         grad = grad + block[:rows, :].astype(F32)
     grad_ref[...] = grad + returned(place_ref, recv_ref, hosts, chips)
-    out = column_product(chips, hosts, adj_ref, value_ref, came, recv_ref, neigh_ref, halo)
+    out = column_product(chips, hosts, adj_ref, far_ref, value_ref, came, recv_ref, neigh_ref)
     out_ref[...] = out + dot(value_ref[...], self_ref[...]) + bias_ref[...].reshape(1, -1)
 
 
-def put_halo(chips, far, rows, here_ref, shared_ref, halo):
-    core = lax.axis_index("core")
-    at = (chips - 1) * rows
-    for x in range(chips):
-        for side, ref in ((1 - core, here_ref), (core, shared_ref)):
-            low = pl.multiple_of((x * CORES + side) * far, far)
-            halo[pl.ds(low, far), :] = ref[at + x * far : at + (x + 1) * far, :]
-
-
-def add_far(chips, rows, adj_ref, agg, shared_ref, halo):
+def add_rest(chips, rows, adj_ref, far_ref, agg, shared_ref):
     chip, core = lax.axis_index("chip"), lax.axis_index("core")
     pairs = []
     for k in range(chips - 1):
         x = lax.rem(chip - k - 1 + chips, chips)
         block = shared_ref[k * rows : (k + 1) * rows, :]
         pairs.append((square_of(adj_ref, x, 1 - core, rows), block))
-    return agg + joint(pairs + far_pairs(chips, rows, adj_ref, halo))
+    half = far_ref.shape[1] // 2
+    low = (chips - 1) * rows
+    pairs.append((far_ref[:, half:], shared_ref[low : low + half, :]))
+    return agg + joint(pairs)
 
 
 def middle_kernel(
@@ -353,13 +354,14 @@
     hosts,
     adj_ref,
     lent_ref,
+    far_ref,
+    far_two_ref,
     col_ref,
     col_two_ref,
     agg_ref,
     direct_ref,
     grad_ref,
     pick_ref,
-    here_ref,
     shared_ref,
     neigh_one_ref,
     hidden_ref,
@@ -368,12 +370,11 @@
     msg_ref,
     *rest,
 ):
-    to_refs, halo = rest[:-1], rest[-1]
+    to_refs = rest
     far, rows = pick_ref.shape
-    put_halo(chips, far, rows, here_ref, shared_ref, halo)
     parts = [
-        add_far(chips, rows, ref, agg_ref[i * rows : (i + 1) * rows, :], shared_ref, halo)
-        for i, ref in enumerate((adj_ref, lent_ref))
+        add_rest(chips, rows, ref, columns, agg_ref[i * rows : (i + 1) * rows, :], shared_ref)
+        for i, (ref, columns) in enumerate(((adj_ref, far_ref), (lent_ref, far_two_ref)))
     ]
     agg = jnp.concatenate(parts, 0).astype(BF16)
     pre = direct_ref[...] + dot(agg, neigh_one_ref[...])
@@ -446,7 +447,7 @@
     sum_shape = shape(rows, width, F32)
     both_shape = shape(CORES * rows, width, F32)
     square = 2 * rows * width * width
-    halo = pltpu.VMEM((chips * CORES * far, width), BF16)
+    far_shape = shape(rows, chips * CORES * far)
     halo_rows = (chips - 1) * rows + chips * far
     dealt = (
         sum_shape,
@@ -455,7 +456,7 @@
 
     def across(msg, to):
         terms = [shift(block, "chip", k + 1) for k, block in enumerate(to)]
-        recv = lax.all_to_all(msg, ("chip", "hst", "core"), split_axis=0, concat_axis=0, tiled=True)
+        recv = lax.all_to_all(msg, ("hst", "chip", "core"), split_axis=0, concat_axis=0, tiled=True)
         return terms, recv
 
     far_t = pltpu.VMEM((chips * CORES * far, rows), BF16)
@@ -494,7 +495,7 @@
         ],
     )
     came = shift(give, "core", 1)
-    adj, col, keep, lend, place = call(
+    adj, col, keep, lend, place, columns = call(
         functools.partial(rest_kernel, chips),
         "rest",
         (
@@ -503,6 +504,7 @@
             shape(count, width),
             shape(all_rows + 2 * rows, width),
             shape(rows, chips * far),
+            far_shape,
         ),
         [VMEM] * (4 + PARTS),
         (up, cotangent, features, pick, *sums),
@@ -527,12 +529,12 @@
         (recv, mine, place, *terms),
     )
     shared = shift(here, "core", 1)
-    agg, direct, grad, col_two = call(
+    agg, direct, grad, col_two, columns_two = call(
         functools.partial(early_one_kernel, chips),
         "early_one",
-        (both_shape,) * 3 + (shape(count, rows),),
-        [VMEM] * 7,
-        (adj, lent, features, self_one, bias_one, cotangent, self_two),
+        (both_shape,) * 3 + (shape(count, rows), far_shape),
+        [VMEM] * 8,
+        (adj, lent, features, self_one, bias_one, cotangent, self_two, neigh_one),
         [far_t],
         flops=8 * square,
     )
@@ -540,17 +542,29 @@
         functools.partial(mid_kernel, chips),
         "mid",
         (both_shape,) * 2,
-        [VMEM] * (4 + chips),
-        (adj, lent, agg, grad, summed, *terms),
+        [VMEM] * (7 + chips),
+        (adj, lent, columns, columns_two, agg, grad, summed, here, *terms),
         flops=3 * square,
     )
     hidden, grad_pre, mine, msg, *to = call(
         functools.partial(middle_kernel, chips, hosts),
         "middle",
         (rows_shape,) * 2 + dealt,
-        [VMEM] * 11,
-        (adj, lent, col, col_two, agg, direct, grad, pick, here, shared, neigh_one),
-        [halo],
+        [VMEM] * 12,
+        (
+            adj,
+            lent,
+            columns,
+            columns_two,
+            col,
+            col_two,
+            agg,
+            direct,
+            grad,
+            pick,
+            shared,
+            neigh_one,
+        ),
         flops=12 * square,
     )
     terms, recv = across(msg, to)
@@ -558,18 +572,18 @@
         functools.partial(there_kernel, chips, hosts),
         "there",
         rows_shape,
-        [VMEM] * (3 + chips),
-        (lent, hidden, recv, neigh_two, *terms),
-        [halo],
+        [VMEM] * (4 + chips),
+        (lent, columns_two, hidden, recv, neigh_two, *terms),
     )
     shared = shift(there, "core", 1)
     here, grad = call(
         functools.partial(here_kernel, chips, hosts),
         "here",
         (sum_shape,) * 2,
-        [VMEM] * (9 + chips),
+        [VMEM] * (10 + chips),
         (
             adj,
+            columns,
             hidden,
             recv,
             neigh_two,
@@ -581,7 +595,6 @@
             place,
             *terms,
         ),
-        [halo],
         flops=7 * square,
     )
     output = call(last_kernel, "last", rows_shape, [VMEM] * 2, (here, shared))

time: 37.9 us -> 37.8 us (level)
  starting transfers between devices: 5.07 us -> 4.65 us
    ppermute x6, starting transfers between devices: 5.07 us -> 4.65 us  [shift(): return lax.ppermute(value, axis, [(i, (i + k) % size) for i in range(size)])]
  transfers between devices with their start and end apart: 6 -> 6, of which waited for: 3 -> 3; matrix products, arithmetic and copies ran while one was open for 0% -> 0% of each run, Pallas kernels for 6% -> 7%
where the time goes in v16:
time: 37.8 us; the launch traced here: 37.6 us
  blocking collectives  23.8 us (63%)
  Pallas kernels  7.02 us (19%)
  starting transfers between devices  4.65 us (12%)
  waiting for transfers between devices  1.38 us (4%)
  between operations  0.75 us (2%)
    all_to_all x2, blocking collectives, across(): lax.all_to_all(msg, ('hst', 'chip', 'core'), split_axis=0, concat_axis=0,...  23.8 us
    pallas_call x10, Pallas kernels, call(): pl.pallas_call(kernel, out_shape=out_shape, in_specs=in_specs, out_specs=...  7.02 us
    ppermute x6, starting transfers between devices, shift(): return lax.ppermute(value, axis, [(i, (i + k) % size) for i in range(size)])  4.65 us
    ppermute x6, waiting for transfers between devices, shift(): return lax.ppermute(value, axis, [(i, (i + k) % size) for i in range(size)])  1.38 us
  transfers between devices with their start and end apart: 6, of which 3 were waited for; matrix products, arithmetic and copies ran while one was open for 0% of the time, Pallas kernels for 7%

profile of v16, /device:TPU:0, one launch (start us, length us, event | category | flops | bytes accessed | tf_op | source)
XLA Modules:
  0.0 37.6 jit_solution(16364110636415701880)
XLA Ops:
  0.6 0.0 copy-start
  0.6 0.0 copy-start.1
  0.7 2.4 %prep.1 = (bf16[640,256]{1,0:T(8,128)(2,1)S(1)}, bf16[256,256]{1,0:T(8,128)(2,1)S(1)}, bf16[64,256]{1,0:T(8,128)(2,1)S(1)}, bf16[64,256]{1,0:T(8,128)(2,1)S(1)},...) custom-call(s32[64]{0:T(128)} %dst_hbm.1, ...), custom_call_target="tpu_custom_call" | custom-call | tf_op jit(solution)/shard_map/prep/pallas_call | solution.py:400
  3.1 0.5 %collective-permute-start.1 = (bf16[640,256]{1,0:T(8,128)(2,1)S(1)}, bf16[640,256]{1,0:T(8,128)(2,1)S(1)}, u32[]{:S(2)}, u32[]{:S(2)}) collective-permute-start(bf16[640,256]{1,0:T(8,128)(2,1)S(1)} %get-tuple-element.50), channel_id=1, source_target_pairs={{0,1},{1,0},{2,3},{3,2},{4,5},{5,4},{6,7},{7,6},{8,9},{9,8},{10,11... | collective-permute-start | bytes 983048 | tf_op jit(solution)/shard_map/ppermute | solution.py:416
  3.6 0.0 copy-done
  3.6 0.0 copy-done.1
  3.6 0.5 %rest.1 = (bf16[1280,256]{1,0:T(8,128)(2,1)S(1)}, bf16[640,256]{1,0:T(8,128)(2,1)S(1)}, bf16[640,256]{1,0:T(8,128)(2,1)S(1)}, bf16[1792,256]{1,0:T(8,128)(2,1)S(...) custom-call(bf16[256,256]{1,0:T(8,128)(2,1)S(1)} %get-tuple-element.35.up_ref, ...), custom_call_target="tpu_custom_call" | custom-call | flops 100663296 | bytes 98304 | tf_op jit(solution)/shard_map/rest/pallas_call | solution.py:400
  4.1 0.1 collective-permute-start
  4.3 0.6 %collective-permute-done.1.came_ref = bf16[640,256]{1,0:T(8,128)(2,1)S(1)} collective-permute-done((bf16[640,256]{1,0:T(8,128)(2,1)S(1)}, bf16[640,256]{1,0:T(8,128)(2,1)S(1)}, u32[]{:S(2)}, u32[]{:S(2)}) %collective-permute-start.1) | collective-permute-done | bytes 327712 | tf_op jit(solution)/shard_map/ppermute | solution.py:416
  4.9 0.1 core_sum.1
  5.0 2.9 %collective-permute-start.2 = (bf16[512,256]{1,0:T(8,128)(2,1)S(1)}, bf16[512,256]{1,0:T(8,128)(2,1)S(1)}, u32[]{:S(2)}, u32[]{:S(2)}) collective-permute-start(bf16[512,256]{1,0:T(8,128)(2,1)S(1)} %get-tuple-element.55), channel_id=1, source_target_pairs={{0,2},{2,0},{1,3},{3,1},{4,6},{6,4},{5,7},{7,5},{8,10},{10,8},{9,1... | collective-permute-start | bytes 786440 | tf_op jit(solution)/shard_map/ppermute | solution.py:416
  7.9 12.9 %all_to_all.10.recv_ref = bf16[32,8,256]{2,1,0:T(8,128)(2,1)S(1)} all-to-all(bf16[32,8,256]{2,1,0:T(8,128)(2,1)S(1)} %get-tuple-element.52), channel_id=1, replica_groups=mesh['hst'=8,'chip'=2,'core'=2] {'hst','chip','core'}, dimensions={0} | all-to-all | bytes 262144 | tf_op jit(solution)/shard_map/all_to_all | solution.py:459
  20.8 0.0 collective-permute-done.2.refs_0_
  20.8 0.2 merge.1
  21.0 0.3 collective-permute-start.3
  21.3 0.0 collective-permute-done.lent_ref
  21.3 0.0 copy-done.5
  21.3 0.0 copy-done.6
  21.4 0.5 %early_one.1 = (f32[512,256]{1,0:T(8,128)S(1)}, f32[512,256]{1,0:T(8,128)S(1)}, f32[512,256]{1,0:T(8,128)S(1)}, bf16[640,256]{1,0:T(8,128)(2,1)S(1)}, bf16[256,256]{1,0:T(8,128)(2,1)S(1)}) custom-call(bf16[1280,256]{1,0:T(8,128)(2,1)S(1)} %get-tuple-element.41.adj_ref, bf16[1792,256]{1,0:T(8,128)(2,1)S(1)} %collective-permute-done.lent_ref, ...), custom_call_target="tpu_custom_call" | custom-call | flops 268435456 | bytes 262144 | tf_op jit(solution)/shard_map/early_one/pallas_call | solution.py:400
  21.8 0.3 mid.1
  22.1 0.6 %collective-permute-done.3.shared_ref = bf16[640,256]{1,0:T(8,128)(2,1)S(1)} collective-permute-done((bf16[640,256]{1,0:T(8,128)(2,1)S(1)}, bf16[640,256]{1,0:T(8,128)(2,1)S(1)}, u32[]{:S(2)}, u32[]{:S(2)}) %collective-permute-start.3) | collective-permute-done | bytes 327712 | tf_op jit(solution)/shard_map/ppermute | solution.py:416
  22.7 1.0 %middle.1 = (bf16[256,256]{1,0:T(8,128)(2,1)S(1)}, bf16[256,256]{1,0:T(8,128)(2,1)S(1)}, f32[256,256]{1,0:T(8,128)S(1)}, bf16[32,8,256]{2,1,0:T(8,128)(2,1)S(1)}, bf16[512,256]{1,0:T(8,128)(2,1)S(1)}) custom-call(bf16[1280,256]{1,0:T(8,128)(2,1)S(1)} %get-tuple-element.41.adj_ref, bf16[1792,256]{1,0:T(8,128)(2,1)S(1)} %collective-permute-done.lent_ref, ...), custom_call_target="tpu_custom_call" | custom-call | flops 402653184 | bytes 393216 | tf_op jit(solution)/shard_map/middle/pallas_call | solution.py:400
  23.7 0.0 copy-start.7
  23.7 0.5 %collective-permute-start.4 = (bf16[512,256]{1,0:T(8,128)(2,1)S(1)}, bf16[512,256]{1,0:T(8,128)(2,1)S(1)}, u32[]{:S(2)}, u32[]{:S(2)}) collective-permute-start(bf16[512,256]{1,0:T(8,128)(2,1)S(1)} %get-tuple-element.65), channel_id=1, source_target_pairs={{0,2},{2,0},{1,3},{3,1},{4,6},{6,4},{5,7},{7,5},{8,10},{10,8},{9,1... | collective-permute-start | bytes 786440 | tf_op jit(solution)/shard_map/ppermute | solution.py:416
  24.2 10.8 %all_to_all.11.recv_ref = bf16[32,8,256]{2,1,0:T(8,128)(2,1)S(1)} all-to-all(bf16[32,8,256]{2,1,0:T(8,128)(2,1)S(1)} %get-tuple-element.62), channel_id=1, replica_groups=mesh['hst'=8,'chip'=2,'core'=2] {'hst','chip','core'}, dimensions={0} | all-to-all | bytes 262144 | tf_op jit(solution)/shard_map/all_to_all | solution.py:459
  35.1 0.0 collective-permute-done.4.refs_0_
  35.1 0.0 copy-done.2
  35.1 0.4 %there.1 = bf16[256,256]{1,0:T(8,128)(2,1)S(1)} custom-call(bf16[1792,256]{1,0:T(8,128)(2,1)S(1)} %collective-permute-done.lent_ref, bf16[256,256]{1,0:T(8,128)(2,1)S(1)} %get-tuple-element.44.far_two_ref.far_ref, bf16[256,256]{1,0:T(8,128)(2,1)S(1)} %get-tuple-element.61.value_ref, bf16[32,8,256]{2,1,0:T(8,128)(2,1)S(1)} %all_to_all.11.recv_ref, ...), custom_call_target="tpu_custom_call" | custom-call | tf_op jit(solution)/shard_map/there/pallas_call | solution.py:400
  35.5 0.3 collective-permute-start.5
  35.8 1.0 %here.1 = (f32[256,256]{1,0:T(8,128)S(1)}, f32[256,256]{1,0:T(8,128)}) custom-call(bf16[1280,256]{1,0:T(8,128)(2,1)S(1)} %get-tuple-element.41.adj_ref, bf16[256,256]{1,0:T(8,128)(2,1)S(1)} %get-tuple-element.42.far_ref, bf16[256,256]{1,0:T(8,128)(2,1)S(1)} %get-tuple-element.61.value_ref, bf16[32,8,256]{2,1,0:T(8,128)(2,1)S(1)} %all_to_all.11.recv_ref, ...), custom_call_target="tpu_custom_call" | custom-call | flops 234881024 | bytes 229376 | tf_op jit(solution)/shard_map/here/pallas_call | solution.py:400
  36.8 0.2 collective-permute-done.5.there_ref
  36.9 0.7 %last.1 = bf16[256,256]{1,0:T(8,128)(2,1)} custom-call(f32[256,256]{1,0:T(8,128)S(1)} %get-tuple-element.66.here_ref, bf16[256,256]{1,0:T(8,128)(2,1)S(1)} %collective-permute-done.5.there_ref), custom_call_target="tpu_custom_call" | custom-call | tf_op jit(solution)/shard_map/last/pallas_call | solution.py:400
  (8 shorter events, 0.0 us)
Async XLA Ops:
  0.6 3.0 %copy-start = (bf16[256,256]{1,0:T(8,128)(2,1)S(1)}, bf16[256,256]{1,0:T(8,128)(2,1)}, u32[]{:S(2)}) copy-start(bf16[256,256]{1,0:T(8,128)(2,1)} %value_ref.5) | copy-start | bytes 393220
  0.6 3.0 %copy-start.1 = (bf16[256,256]{1,0:T(8,128)(2,1)S(1)}, bf16[256,256]{1,0:T(8,128)(2,1)}, u32[]{:S(2)}) copy-start(bf16[256,256]{1,0:T(8,128)(2,1)} %up_ref.1) | copy-start | bytes 393220
  3.1 1.8 %collective-permute-start.1 = (bf16[640,256]{1,0:T(8,128)(2,1)S(1)}, bf16[640,256]{1,0:T(8,128)(2,1)S(1)}, u32[]{:S(2)}, u32[]{:S(2)}) collective-permute-start(bf16[640,256]{1,0:T(8,128)(2,1)S(1)} %get-tuple-element.50), channel_id=1, source_target_pairs={{0,1},{1,0},{2,3},{3,2},{4,5},{5,4},{6,7},{7,6},{8,9},{9,8},{10,11... | collective-permute-start | bytes 983048 | tf_op jit(solution)/shard_map/ppermute | solution.py:416
  4.1 17.2 %collective-permute-start = (bf16[1792,256]{1,0:T(8,128)(2,1)S(1)}, bf16[1792,256]{1,0:T(8,128)(2,1)S(1)}, u32[]{:S(2)}, u32[]{:S(2)}) collective-permute-start(bf16[1792,256]{1,0:T(8,128)(2,1)S(1)} %get-tuple-element.43), channel_id=1, source_target_pairs={{0,1},{1,0},{2,3},{3,2},{4,5},{5,4},{6,7},{7,6},{8,9},{9,8},{10,11... | collective-permute-start | bytes 2752520 | tf_op jit(solution)/shard_map/ppermute | solution.py:416
  4.9 16.5 %copy-start.3 = (bf16[256,256]{1,0:T(8,128)(2,1)S(1)}, bf16[256,256]{1,0:T(8,128)(2,1)}, u32[]{:S(2)}) copy-start(bf16[256,256]{1,0:T(8,128)(2,1)} %neigh_one_ref.1) | copy-start | bytes 393220
  4.9 16.5 %copy-start.4 = (bf16[256,256]{1,0:T(8,128)(2,1)S(1)}, bf16[256,256]{1,0:T(8,128)(2,1)}, u32[]{:S(2)}) copy-start(bf16[256,256]{1,0:T(8,128)(2,1)} %weight_ref.3) | copy-start | bytes 393220
  4.9 16.5 %copy-start.5 = (bf16[256,256]{1,0:T(8,128)(2,1)S(1)}, bf16[256,256]{1,0:T(8,128)(2,1)}, u32[]{:S(2)}) copy-start(bf16[256,256]{1,0:T(8,128)(2,1)} %self_ref.3) | copy-start | bytes 393220
  4.9 16.5 %copy-start.6 = (f32[256]{0:T(256)S(1)}, f32[256]{0:T(256)}, u32[]{:S(2)}) copy-start(f32[256]{0:T(256)} %bias_ref.2) | copy-start | bytes 3076
  5.0 15.9 %collective-permute-start.2 = (bf16[512,256]{1,0:T(8,128)(2,1)S(1)}, bf16[512,256]{1,0:T(8,128)(2,1)S(1)}, u32[]{:S(2)}, u32[]{:S(2)}) collective-permute-start(bf16[512,256]{1,0:T(8,128)(2,1)S(1)} %get-tuple-element.55), channel_id=1, source_target_pairs={{0,2},{2,0},{1,3},{3,1},{4,6},{6,4},{5,7},{7,5},{8,10},{10,8},{9,1... | collective-permute-start | bytes 786440 | tf_op jit(solution)/shard_map/ppermute | solution.py:416
  21.0 1.7 %collective-permute-start.3 = (bf16[640,256]{1,0:T(8,128)(2,1)S(1)}, bf16[640,256]{1,0:T(8,128)(2,1)S(1)}, u32[]{:S(2)}, u32[]{:S(2)}) collective-permute-start(bf16[640,256]{1,0:T(8,128)(2,1)S(1)} %get-tuple-element.57.here_ref), channel_id=1, source_target_pairs={{0,1},{1,0},{2,3},{3,2},{4,5},{5,4},{6,7},{7,6},{8,9},{9,8},{10,11... | collective-permute-start | bytes 983048 | tf_op jit(solution)/shard_map/ppermute | solution.py:416
  22.7 12.3 %copy-start.2 = (bf16[256,256]{1,0:T(8,128)(2,1)S(1)}, bf16[256,256]{1,0:T(8,128)(2,1)}, u32[]{:S(2)}) copy-start(bf16[256,256]{1,0:T(8,128)(2,1)} %neigh_ref.3) | copy-start | bytes 393220
  23.7 12.1 %copy-start.7 = (f32[256]{0:T(256)S(1)}, f32[256]{0:T(256)}, u32[]{:S(2)}) copy-start(f32[256]{0:T(256)} %bias_ref.3) | copy-start | bytes 3076
  23.7 11.3 %collective-permute-start.4 = (bf16[512,256]{1,0:T(8,128)(2,1)S(1)}, bf16[512,256]{1,0:T(8,128)(2,1)S(1)}, u32[]{:S(2)}, u32[]{:S(2)}) collective-permute-start(bf16[512,256]{1,0:T(8,128)(2,1)S(1)} %get-tuple-element.65), channel_id=1, source_target_pairs={{0,2},{2,0},{1,3},{3,1},{4,6},{6,4},{5,7},{7,5},{8,10},{10,8},{9,1... | collective-permute-start | bytes 786440 | tf_op jit(solution)/shard_map/ppermute | solution.py:416
  35.5 1.4 %collective-permute-start.5 = (bf16[256,256]{1,0:T(8,128)(2,1)S(1)}, bf16[256,256]{1,0:T(8,128)(2,1)S(1)}, u32[]{:S(2)}, u32[]{:S(2)}) collective-permute-start(bf16[256,256]{1,0:T(8,128)(2,1)S(1)} %there.1), channel_id=1, source_target_pairs={{0,1},{1,0},{2,3},{3,2},{4,5},{5,4},{6,7},{7,6},{8,9},{9,8},{10,11... | collective-permute-start | bytes 393224 | tf_op jit(solution)/shard_map/ppermute | solution.py:416

commit v17 on v16

--- a/solution.py
+++ b/solution.py
@@ -188,24 +188,33 @@
     place_ref[...] = jnp.concatenate([pick_ref[...]] * chips, 0).T
 
 
-def deal(chips, hosts, total, picked, value, mine_ref, msg_ref, to_refs):
+def node_part(rows, far, value):
+    each = rows + far
+    return [value[low : low + rows, :] for low in range(each, value.shape[0], each)]
+
+
+def far_part(rows, far, value):
+    each = rows + far
+    return [value[low + rows : low + each, :] for low in range(0, value.shape[0], each)]
+
+
+def send_to_chips(blocks, value, to_refs):
     rows = value.shape[0]
-    far = picked.shape[0]
-    send = far // hosts
-    each = rows + far
+    for block, ref in zip(blocks, to_refs):
+        ref[:rows, :] = block.astype(BF16)
+        ref[rows:, :] = value
+
+
+def send_to_hosts(chips, hosts, terms, picked, msg_ref):
+    send = picked.shape[0] // hosts
     chip, core = lax.axis_index("chip"), lax.axis_index("core")
-    mine_ref[...] = total[:rows]
-    for k in range(chips):
-        low = k * each + rows
-        if k > 0:
-            to_refs[k - 1][:rows, :] = total[k * each : low].astype(BF16)
-            to_refs[k - 1][rows:, :] = value
+    for k, block in enumerate(terms):
         x = lax.rem(chip + k, chips)
         for g in range(hosts):
-            at = low + g * send
+            part = slice(g * send, (g + 1) * send)
             to = (g * chips + x) * CORES
-            msg_ref[to + core] = total[at : at + send].astype(BF16)
-            msg_ref[to + 1 - core] = picked[g * send : (g + 1) * send].astype(BF16)
+            msg_ref[to + core] = block[part].astype(BF16)
+            msg_ref[to + 1 - core] = picked[part].astype(BF16)
 
 
 def core_sum_kernel(
@@ -213,7 +222,11 @@
 ):
     total = keep_ref[...].astype(F32) + came_ref[...].astype(F32)
     picked = picked_ref[...].astype(F32)
-    deal(chips, hosts, total, picked, value_ref[...], mine_ref, msg_ref, rest)
+    rows = value_ref.shape[0]
+    far = picked.shape[0]
+    mine_ref[...] = total[:rows]
+    send_to_chips(node_part(rows, far, total), value_ref[...], rest)
+    send_to_hosts(chips, hosts, far_part(rows, far, total), picked, msg_ref)
 
 
 def received(recv_ref, hosts, chips, side):
@@ -351,7 +364,6 @@
 
 def middle_kernel(
     chips,
-    hosts,
     adj_ref,
     lent_ref,
     far_ref,
@@ -366,11 +378,9 @@
     neigh_one_ref,
     hidden_ref,
     grad_pre_ref,
-    mine_ref,
-    msg_ref,
-    *rest,
-):
-    to_refs = rest
+    up_ref,
+    *to_refs,
+):
     far, rows = pick_ref.shape
     parts = [
         add_rest(chips, rows, ref, columns, agg_ref[i * rows : (i + 1) * rows, :], shared_ref)
@@ -387,9 +397,25 @@
     grad_pre = (grad * sigmoid * (1.0 + pre * (1.0 - sigmoid))).astype(BF16)
     grad_pre_ref[...] = grad_pre[:rows]
     u = dot_nt(grad_pre, neigh_one_ref[...]).astype(BF16)
-    total = joint([(col_ref[...], u[:rows]), (col_two_ref[...], u[rows:])])
-    picked = dot(pick_ref[...], hidden)
-    deal(chips, hosts, total, picked, hidden, mine_ref, msg_ref, to_refs)
+    up_ref[...] = u
+    columns = [node_part(rows, far, ref) for ref in (col_ref, col_two_ref)]
+    blocks = [joint([(one, u[:rows]), (two, u[rows:])]) for one, two in zip(*columns)]
+    send_to_chips(blocks, hidden, to_refs)
+
+
+def messages_kernel(
+    chips, hosts, col_ref, col_two_ref, up_ref, hidden_ref, pick_ref, mine_ref, msg_ref
+):
+    far, rows = pick_ref.shape
+    u = up_ref[...]
+    columns = [
+        jnp.concatenate([ref[:rows, :]] + far_part(rows, far, ref), 0)
+        for ref in (col_ref, col_two_ref)
+    ]
+    total = joint([(columns[0], u[:rows]), (columns[1], u[rows:])])
+    mine_ref[...] = total[:rows]
+    terms = [total[low : low + far] for low in range(rows, total.shape[0], far)]
+    send_to_hosts(chips, hosts, terms, dot(pick_ref[...], hidden_ref[...]), msg_ref)
 
 
 def last_kernel(here_ref, there_ref, output_ref):
@@ -449,15 +475,14 @@
     square = 2 * rows * width * width
     far_shape = shape(rows, chips * CORES * far)
     halo_rows = (chips - 1) * rows + chips * far
-    dealt = (
-        sum_shape,
-        jax.ShapeDtypeStruct((chips * hosts * CORES, send, width), BF16),
-    ) + (shape(2 * rows, width),) * (chips - 1)
-
-    def across(msg, to):
-        terms = [shift(block, "chip", k + 1) for k, block in enumerate(to)]
-        recv = lax.all_to_all(msg, ("hst", "chip", "core"), split_axis=0, concat_axis=0, tiled=True)
-        return terms, recv
+    dealt = (sum_shape, jax.ShapeDtypeStruct((chips * hosts * CORES, send, width), BF16))
+    to_shapes = (shape(2 * rows, width),) * (chips - 1)
+
+    def to_chips(blocks):
+        return [shift(block, "chip", k + 1) for k, block in enumerate(blocks)]
+
+    def to_hosts(msg):
+        return lax.all_to_all(msg, ("hst", "chip", "core"), split_axis=0, concat_axis=0, tiled=True)
 
     far_t = pltpu.VMEM((chips * CORES * far, rows), BF16)
     sums = jax.ShapeDtypeStruct(((rows // blk) * (all_rows // blk), blk // PARTS, blk), F32)
@@ -515,12 +540,13 @@
     mine, msg, *to = call(
         functools.partial(core_sum_kernel, chips, hosts),
         "core_sum",
-        dealt,
+        dealt + to_shapes,
         [VMEM] * 4,
         (keep, came, features, picked),
         flops=60 * square,
     )
-    terms, recv = across(msg, to)
+    terms = to_chips(to)
+    recv = to_hosts(msg)
     here, summed = call(
         functools.partial(merge_kernel, chips, hosts),
         "merge",
@@ -546,10 +572,10 @@
         (adj, lent, columns, columns_two, agg, grad, summed, here, *terms),
         flops=3 * square,
     )
-    hidden, grad_pre, mine, msg, *to = call(
-        functools.partial(middle_kernel, chips, hosts),
+    hidden, grad_pre, up, *to = call(
+        functools.partial(middle_kernel, chips),
         "middle",
-        (rows_shape,) * 2 + dealt,
+        (rows_shape,) * 2 + (shape(CORES * rows, width),) + to_shapes,
         [VMEM] * 12,
         (
             adj,
@@ -567,7 +593,16 @@
         ),
         flops=12 * square,
     )
-    terms, recv = across(msg, to)
+    terms = to_chips(to)
+    mine, msg = call(
+        functools.partial(messages_kernel, chips, hosts),
+        "messages",
+        dealt,
+        [VMEM] * 5,
+        (col, col_two, up, hidden, pick),
+        flops=5 * square,
+    )
+    recv = to_hosts(msg)
     there = call(
         functools.partial(there_kernel, chips, hosts),
         "there",

time: 37.8 us -> 38 us (level)
    pallas_call x10 -> x11, Pallas kernels: 7.02 us -> 7.19 us  [call(): pl.pallas_call(kernel, out_shape=out_shape, in_specs=in_specs, out_specs=...]
where the time goes in v17:
time: 38 us; the launch traced here: 37.8 us
  blocking collectives  23.8 us (63%)
  Pallas kernels  7.19 us (19%)
  starting transfers between devices  4.63 us (12%)
  waiting for transfers between devices  1.36 us (4%)
  between operations  0.75 us (2%)
    all_to_all x2, blocking collectives, to_hosts(): lax.all_to_all(msg, ('hst', 'chip', 'core'), split_axis=0, concat_axis=0,...  23.8 us
    pallas_call x11, Pallas kernels, call(): pl.pallas_call(kernel, out_shape=out_shape, in_specs=in_specs, out_specs=...  7.19 us
    ppermute x6, starting transfers between devices, shift(): return lax.ppermute(value, axis, [(i, (i + k) % size) for i in range(size)])  4.63 us
    ppermute x6, waiting for transfers between devices, shift(): return lax.ppermute(value, axis, [(i, (i + k) % size) for i in range(size)])  1.36 us
  transfers between devices with their start and end apart: 6, of which 3 were waited for; matrix products, arithmetic and copies ran while one was open for 0% of the time, Pallas kernels for 7%

profile of v17, /device:TPU:0, one launch (start us, length us, event | category | flops | bytes accessed | tf_op | source)
XLA Modules:
  0.0 37.8 jit_solution(12341655434108335509)
XLA Ops:
  0.6 0.0 copy-start
  0.7 2.4 %prep.1 = (bf16[640,256]{1,0:T(8,128)(2,1)S(1)}, bf16[256,256]{1,0:T(8,128)(2,1)S(1)}, bf16[64,256]{1,0:T(8,128)(2,1)S(1)}, bf16[64,256]{1,0:T(8,128)(2,1)S(1)},...) custom-call(s32[64]{0:T(128)} %dst_hbm.1, ...), custom_call_target="tpu_custom_call" | custom-call | tf_op jit(solution)/shard_map/prep/pallas_call | solution.py:426
  3.1 0.5 %collective-permute-start.1 = (bf16[640,256]{1,0:T(8,128)(2,1)S(1)}, bf16[640,256]{1,0:T(8,128)(2,1)S(1)}, u32[]{:S(2)}, u32[]{:S(2)}) collective-permute-start(bf16[640,256]{1,0:T(8,128)(2,1)S(1)} %get-tuple-element.51), channel_id=1, source_target_pairs={{0,1},{1,0},{2,3},{3,2},{4,5},{5,4},{6,7},{7,6},{8,9},{9,8},{10,11... | collective-permute-start | bytes 983048 | tf_op jit(solution)/shard_map/ppermute | solution.py:442
  3.6 0.0 copy-done.1
  3.6 0.5 %rest.1 = (bf16[1280,256]{1,0:T(8,128)(2,1)S(1)}, bf16[640,256]{1,0:T(8,128)(2,1)S(1)}, bf16[640,256]{1,0:T(8,128)(2,1)S(1)}, bf16[1792,256]{1,0:T(8,128)(2,1)S(...) custom-call(bf16[256,256]{1,0:T(8,128)(2,1)S(1)} %get-tuple-element.36.up_ref, ...), custom_call_target="tpu_custom_call" | custom-call | flops 100663296 | bytes 98304 | tf_op jit(solution)/shard_map/rest/pallas_call | solution.py:426
  4.1 0.1 collective-permute-start
  4.3 0.6 %collective-permute-done.1.came_ref = bf16[640,256]{1,0:T(8,128)(2,1)S(1)} collective-permute-done((bf16[640,256]{1,0:T(8,128)(2,1)S(1)}, bf16[640,256]{1,0:T(8,128)(2,1)S(1)}, u32[]{:S(2)}, u32[]{:S(2)}) %collective-permute-start.1) | collective-permute-done | bytes 327712 | tf_op jit(solution)/shard_map/ppermute | solution.py:442
  4.9 0.1 core_sum.1
  5.0 2.9 %collective-permute-start.2 = (bf16[512,256]{1,0:T(8,128)(2,1)S(1)}, bf16[512,256]{1,0:T(8,128)(2,1)S(1)}, u32[]{:S(2)}, u32[]{:S(2)}) collective-permute-start(bf16[512,256]{1,0:T(8,128)(2,1)S(1)} %get-tuple-element.56), channel_id=1, source_target_pairs={{0,2},{2,0},{1,3},{3,1},{4,6},{6,4},{5,7},{7,5},{8,10},{10,8},{9,1... | collective-permute-start | bytes 786440 | tf_op jit(solution)/shard_map/ppermute | solution.py:442
  7.9 12.9 %all_to_all.10.recv_ref = bf16[32,8,256]{2,1,0:T(8,128)(2,1)S(1)} all-to-all(bf16[32,8,256]{2,1,0:T(8,128)(2,1)S(1)} %get-tuple-element.53), channel_id=1, replica_groups=mesh['hst'=8,'chip'=2,'core'=2] {'hst','chip','core'}, dimensions={0} | all-to-all | bytes 262144 | tf_op jit(solution)/shard_map/all_to_all | solution.py:485
  20.9 0.0 collective-permute-done.2.refs_0_
  20.9 0.2 merge.1
  21.0 0.3 collective-permute-start.3
  21.3 0.0 collective-permute-done.lent_ref
  21.3 0.0 copy-done.4
  21.3 0.0 copy-done.5
  21.4 0.0 copy-done.6
  21.4 0.5 %early_one.1 = (f32[512,256]{1,0:T(8,128)S(1)}, f32[512,256]{1,0:T(8,128)S(1)}, f32[512,256]{1,0:T(8,128)S(1)}, bf16[640,256]{1,0:T(8,128)(2,1)S(1)}, bf16[256,256]{1,0:T(8,128)(2,1)S(1)}) custom-call(bf16[1280,256]{1,0:T(8,128)(2,1)S(1)} %get-tuple-element.42.adj_ref, bf16[1792,256]{1,0:T(8,128)(2,1)S(1)} %collective-permute-done.lent_ref, ...), custom_call_target="tpu_custom_call" | custom-call | flops 268435456 | bytes 262144 | tf_op jit(solution)/shard_map/early_one/pallas_call | solution.py:426
  21.8 0.3 mid.1
  22.2 0.6 %collective-permute-done.3.shared_ref = bf16[640,256]{1,0:T(8,128)(2,1)S(1)} collective-permute-done((bf16[640,256]{1,0:T(8,128)(2,1)S(1)}, bf16[640,256]{1,0:T(8,128)(2,1)S(1)}, u32[]{:S(2)}, u32[]{:S(2)}) %collective-permute-start.3) | collective-permute-done | bytes 327712 | tf_op jit(solution)/shard_map/ppermute | solution.py:442
  22.7 0.8 %middle.1 = (bf16[256,256]{1,0:T(8,128)(2,1)S(1)}, bf16[256,256]{1,0:T(8,128)(2,1)S(1)}, bf16[512,256]{1,0:T(8,128)(2,1)S(1)}, bf16[512,256]{1,0:T(8,128)(2,1)S(1)}) custom-call(bf16[1280,256]{1,0:T(8,128)(2,1)S(1)} %get-tuple-element.42.adj_ref, bf16[1792,256]{1,0:T(8,128)(2,1)S(1)} %collective-permute-done.lent_ref, ...), custom_call_target="tpu_custom_call" | custom-call | flops 402653184 | bytes 393216 | tf_op jit(solution)/shard_map/middle/pallas_call | solution.py:426
  23.6 0.0 copy-start.7
  23.6 0.5 %collective-permute-start.4 = (bf16[512,256]{1,0:T(8,128)(2,1)S(1)}, bf16[512,256]{1,0:T(8,128)(2,1)S(1)}, u32[]{:S(2)}, u32[]{:S(2)}) collective-permute-start(bf16[512,256]{1,0:T(8,128)(2,1)S(1)} %get-tuple-element.67), channel_id=1, source_target_pairs={{0,2},{2,0},{1,3},{3,1},{4,6},{6,4},{5,7},{7,5},{8,10},{10,8},{9,1... | collective-permute-start | bytes 786440 | tf_op jit(solution)/shard_map/ppermute | solution.py:442
  24.1 0.3 messages.1
  24.4 10.9 %all_to_all.11.recv_ref = bf16[32,8,256]{2,1,0:T(8,128)(2,1)S(1)} all-to-all(bf16[32,8,256]{2,1,0:T(8,128)(2,1)S(1)} %get-tuple-element.64), channel_id=1, replica_groups=mesh['hst'=8,'chip'=2,'core'=2] {'hst','chip','core'}, dimensions={0} | all-to-all | bytes 262144 | tf_op jit(solution)/shard_map/all_to_all | solution.py:485
  35.2 0.0 collective-permute-done.4.refs_0_
  35.2 0.0 copy-done.2
  35.2 0.4 %there.1 = bf16[256,256]{1,0:T(8,128)(2,1)S(1)} custom-call(bf16[1792,256]{1,0:T(8,128)(2,1)S(1)} %collective-permute-done.lent_ref, bf16[256,256]{1,0:T(8,128)(2,1)S(1)} %get-tuple-element.45.far_two_ref.far_ref, bf16[256,256]{1,0:T(8,128)(2,1)S(1)} %get-tuple-element.62.hidden_ref.value_ref, bf16[32,8,256]{2,1,0:T(8,128)(2,1)S(1)} %all_to_all.11.recv_ref, ...), custom_call_target="tpu_custom_call" | custom-call | tf_op jit(solution)/shard_map/there/pallas_call | solution.py:426
  35.7 0.3 collective-permute-start.5
  36.0 1.0 %here.1 = (f32[256,256]{1,0:T(8,128)S(1)}, f32[256,256]{1,0:T(8,128)}) custom-call(bf16[1280,256]{1,0:T(8,128)(2,1)S(1)} %get-tuple-element.42.adj_ref, bf16[256,256]{1,0:T(8,128)(2,1)S(1)} %get-tuple-element.43.far_ref, bf16[256,256]{1,0:T(8,128)(2,1)S(1)} %get-tuple-element.62.hidden_ref.value_ref, bf16[32,8,256]{2,1,0:T(8,128)(2,1)S(1)} %all_to_all.11.recv_ref, ...), custom_call_target="tpu_custom_call" | custom-call | flops 234881024 | bytes 229376 | tf_op jit(solution)/shard_map/here/pallas_call | solution.py:426
  36.9 0.2 collective-permute-done.5.there_ref
  37.1 0.7 %last.1 = bf16[256,256]{1,0:T(8,128)(2,1)} custom-call(f32[256,256]{1,0:T(8,128)S(1)} %get-tuple-element.68.here_ref, bf16[256,256]{1,0:T(8,128)(2,1)S(1)} %collective-permute-done.5.there_ref), custom_call_target="tpu_custom_call" | custom-call | tf_op jit(solution)/shard_map/last/pallas_call | solution.py:426
  (9 shorter events, 0.0 us)
Async XLA Ops:
  0.6 3.0 %copy-start = (bf16[256,256]{1,0:T(8,128)(2,1)S(1)}, bf16[256,256]{1,0:T(8,128)(2,1)}, u32[]{:S(2)}) copy-start(bf16[256,256]{1,0:T(8,128)(2,1)} %value_ref.5) | copy-start | bytes 393220
  0.6 3.0 %copy-start.1 = (bf16[256,256]{1,0:T(8,128)(2,1)S(1)}, bf16[256,256]{1,0:T(8,128)(2,1)}, u32[]{:S(2)}) copy-start(bf16[256,256]{1,0:T(8,128)(2,1)} %up_ref.1) | copy-start | bytes 393220
  3.1 1.8 %collective-permute-start.1 = (bf16[640,256]{1,0:T(8,128)(2,1)S(1)}, bf16[640,256]{1,0:T(8,128)(2,1)S(1)}, u32[]{:S(2)}, u32[]{:S(2)}) collective-permute-start(bf16[640,256]{1,0:T(8,128)(2,1)S(1)} %get-tuple-element.51), channel_id=1, source_target_pairs={{0,1},{1,0},{2,3},{3,2},{4,5},{5,4},{6,7},{7,6},{8,9},{9,8},{10,11... | collective-permute-start | bytes 983048 | tf_op jit(solution)/shard_map/ppermute | solution.py:442
  4.1 17.2 %collective-permute-start = (bf16[1792,256]{1,0:T(8,128)(2,1)S(1)}, bf16[1792,256]{1,0:T(8,128)(2,1)S(1)}, u32[]{:S(2)}, u32[]{:S(2)}) collective-permute-start(bf16[1792,256]{1,0:T(8,128)(2,1)S(1)} %get-tuple-element.44), channel_id=1, source_target_pairs={{0,1},{1,0},{2,3},{3,2},{4,5},{5,4},{6,7},{7,6},{8,9},{9,8},{10,11... | collective-permute-start | bytes 2752520 | tf_op jit(solution)/shard_map/ppermute | solution.py:442
  4.9 16.5 %copy-start.3 = (bf16[256,256]{1,0:T(8,128)(2,1)S(1)}, bf16[256,256]{1,0:T(8,128)(2,1)}, u32[]{:S(2)}) copy-start(bf16[256,256]{1,0:T(8,128)(2,1)} %neigh_one_ref.1) | copy-start | bytes 393220
  4.9 16.5 %copy-start.4 = (bf16[256,256]{1,0:T(8,128)(2,1)S(1)}, bf16[256,256]{1,0:T(8,128)(2,1)}, u32[]{:S(2)}) copy-start(bf16[256,256]{1,0:T(8,128)(2,1)} %weight_ref.3) | copy-start | bytes 393220
  4.9 16.5 %copy-start.5 = (bf16[256,256]{1,0:T(8,128)(2,1)S(1)}, bf16[256,256]{1,0:T(8,128)(2,1)}, u32[]{:S(2)}) copy-start(bf16[256,256]{1,0:T(8,128)(2,1)} %self_ref.3) | copy-start | bytes 393220
  4.9 16.5 %copy-start.6 = (f32[256]{0:T(256)S(1)}, f32[256]{0:T(256)}, u32[]{:S(2)}) copy-start(f32[256]{0:T(256)} %bias_ref.2) | copy-start | bytes 3076
  5.0 15.9 %collective-permute-start.2 = (bf16[512,256]{1,0:T(8,128)(2,1)S(1)}, bf16[512,256]{1,0:T(8,128)(2,1)S(1)}, u32[]{:S(2)}, u32[]{:S(2)}) collective-permute-start(bf16[512,256]{1,0:T(8,128)(2,1)S(1)} %get-tuple-element.56), channel_id=1, source_target_pairs={{0,2},{2,0},{1,3},{3,1},{4,6},{6,4},{5,7},{7,5},{8,10},{10,8},{9,1... | collective-permute-start | bytes 786440 | tf_op jit(solution)/shard_map/ppermute | solution.py:442
  21.0 1.7 %collective-permute-start.3 = (bf16[640,256]{1,0:T(8,128)(2,1)S(1)}, bf16[640,256]{1,0:T(8,128)(2,1)S(1)}, u32[]{:S(2)}, u32[]{:S(2)}) collective-permute-start(bf16[640,256]{1,0:T(8,128)(2,1)S(1)} %get-tuple-element.58.here_ref), channel_id=1, source_target_pairs={{0,1},{1,0},{2,3},{3,2},{4,5},{5,4},{6,7},{7,6},{8,9},{9,8},{10,11... | collective-permute-start | bytes 983048 | tf_op jit(solution)/shard_map/ppermute | solution.py:442
  22.7 12.5 %copy-start.2 = (bf16[256,256]{1,0:T(8,128)(2,1)S(1)}, bf16[256,256]{1,0:T(8,128)(2,1)}, u32[]{:S(2)}) copy-start(bf16[256,256]{1,0:T(8,128)(2,1)} %neigh_ref.3) | copy-start | bytes 393220
  23.6 12.4 %copy-start.7 = (f32[256]{0:T(256)S(1)}, f32[256]{0:T(256)}, u32[]{:S(2)}) copy-start(f32[256]{0:T(256)} %bias_ref.3) | copy-start | bytes 3076
  23.6 11.6 %collective-permute-start.4 = (bf16[512,256]{1,0:T(8,128)(2,1)S(1)}, bf16[512,256]{1,0:T(8,128)(2,1)S(1)}, u32[]{:S(2)}, u32[]{:S(2)}) collective-permute-start(bf16[512,256]{1,0:T(8,128)(2,1)S(1)} %get-tuple-element.67), channel_id=1, source_target_pairs={{0,2},{2,0},{1,3},{3,1},{4,6},{6,4},{5,7},{7,5},{8,10},{10,8},{9,1... | collective-permute-start | bytes 786440 | tf_op jit(solution)/shard_map/ppermute | solution.py:442
  35.7 1.4 %collective-permute-start.5 = (bf16[256,256]{1,0:T(8,128)(2,1)S(1)}, bf16[256,256]{1,0:T(8,128)(2,1)S(1)}, u32[]{:S(2)}, u32[]{:S(2)}) collective-permute-start(bf16[256,256]{1,0:T(8,128)(2,1)S(1)} %there.1), channel_id=1, source_target_pairs={{0,1},{1,0},{2,3},{3,2},{4,5},{5,4},{6,7},{7,6},{8,9},{9,8},{10,11... | collective-permute-start | bytes 393224 | tf_op jit(solution)/shard_map/ppermute | solution.py:442

commit v18 on v16

--- a/solution.py
+++ b/solution.py
@@ -74,8 +74,10 @@
     features_hbm,
     cot_hbm,
     neigh_two_hbm,
+    neigh_one_hbm,
     give_ref,
     up_ref,
+    sent_ref,
     picked_ref,
     pick_ref,
     *rest,
@@ -90,6 +92,7 @@
         features_ref,
         cot_ref,
         neigh_two_ref,
+        neigh_one_ref,
         square,
         far_t,
         col,
@@ -107,6 +110,7 @@
     pairs += [
         (cot_hbm, cot_ref),
         (neigh_two_hbm, neigh_two_ref),
+        (neigh_one_hbm, neigh_one_ref),
         (features_hbm, features_ref),
         (send_hbm, send_ref),
     ]
@@ -135,14 +139,15 @@
     for c in range(first):
         copies[3 + c].wait()
         lax.fori_loop(c * each, (c + 1) * each, add, 0, unroll=True)
-    for copy in copies[3 + first : 7 + first]:
+    for copy in copies[3 + first : 8 + first]:
         copy.wait()
     u = dot_nt(cot_ref[...], neigh_two_ref[...]).astype(BF16)
     up_ref[...] = u
     pick_ref[...] = pick_matrix(send_ref, rows)
-    picked_ref[...] = dot(pick_ref[...], features_ref[...]).astype(BF16)
+    sent_ref[...] = dot(features_ref[...], neigh_one_ref[...]).astype(BF16)
+    picked_ref[...] = dot(pick_ref[...], sent_ref[...]).astype(BF16)
     for c in range(first, CHUNKS):
-        copies[7 + c].wait()
+        copies[8 + c].wait()
         lax.fori_loop(c * each, (c + 1) * each, add, 0, unroll=True)
     chip, side = lax.axis_index("chip"), 1 - lax.axis_index("core")
     base = chips * CORES
@@ -265,14 +270,15 @@
 
 
 def early_one_kernel(
-    chips, adj_ref, lent_ref, value_ref, self_ref, bias_ref, up_ref, weight_ref, unused_ref,
+    chips, adj_ref, lent_ref, value_ref, self_ref, bias_ref, up_ref, weight_ref, neigh_ref, sent_ref,
     agg_ref, direct_ref, grad_ref, col_ref, far_ref, far_t,
 ):
     value = value_ref[...]
     rows = value.shape[0]
     low = adj_ref.shape[0]
     there = lent_ref[low + rows :, :]
-    agg_ref[...] = own_chip((adj_ref, lent_ref), (value, there))
+    sent = dot(there, neigh_ref[...]).astype(BF16)
+    agg_ref[...] = own_chip((adj_ref, lent_ref), (sent_ref[...], sent))
     both = jnp.concatenate([value, there], 0)
     direct_ref[...] = dot(both, self_ref[...]) + bias_ref[...].reshape(1, -1)
     both = jnp.concatenate([up_ref[...], lent_ref[low : low + rows, :]], 0)
@@ -306,24 +312,24 @@
     return pairs
 
 
-def column_product(chips, hosts, adj_ref, far_ref, value_ref, came, recv_ref, neigh_ref):
+def column_product(chips, hosts, adj_ref, far_ref, value_ref, came, recv_ref):
     rows = value_ref.shape[0]
     chip, core = lax.axis_index("chip"), lax.axis_index("core")
     halo = received(recv_ref, hosts, chips, 1 - core)
     pairs = [(square_of(adj_ref, chip, core, rows), value_ref[...])]
     pairs += other_chips(chips, adj_ref, came) + [(far_ref[:, : halo.shape[0]], halo)]
-    return dot(joint(pairs).astype(BF16), neigh_ref[...])
-
-
-def there_kernel(chips, hosts, lent_ref, far_ref, value_ref, recv_ref, neigh_ref, *refs):
+    return joint(pairs)
+
+
+def there_kernel(chips, hosts, lent_ref, far_ref, value_ref, recv_ref, *refs):
     came, out_ref = refs[:-1], refs[-1]
     out_ref[...] = column_product(
-        chips, hosts, lent_ref, far_ref, value_ref, came, recv_ref, neigh_ref
+        chips, hosts, lent_ref, far_ref, value_ref, came, recv_ref
     ).astype(BF16)
 
 
 def here_kernel(
-    chips, hosts, adj_ref, far_ref, value_ref, recv_ref, neigh_ref, self_ref, bias_ref, up_ref,
+    chips, hosts, adj_ref, far_ref, sent_ref, recv_ref, value_ref, self_ref, bias_ref, up_ref,
     weight_ref, mine_ref, place_ref, *refs
 ):
     came, (out_ref, grad_ref) = refs[:-2], refs[-2:]
@@ -332,7 +338,7 @@
     for block in came:
         grad = grad + block[:rows, :].astype(F32)
     grad_ref[...] = grad + returned(place_ref, recv_ref, hosts, chips)
-    out = column_product(chips, hosts, adj_ref, far_ref, value_ref, came, recv_ref, neigh_ref)
+    out = column_product(chips, hosts, adj_ref, far_ref, sent_ref, came, recv_ref)
     out_ref[...] = out + dot(value_ref[...], self_ref[...]) + bias_ref[...].reshape(1, -1)
 
 
@@ -364,7 +370,9 @@
     pick_ref,
     shared_ref,
     neigh_one_ref,
+    neigh_two_ref,
     hidden_ref,
+    sent_ref,
     grad_pre_ref,
     mine_ref,
     msg_ref,
@@ -376,11 +384,12 @@
         add_rest(chips, rows, ref, columns, agg_ref[i * rows : (i + 1) * rows, :], shared_ref)
         for i, (ref, columns) in enumerate(((adj_ref, far_ref), (lent_ref, far_two_ref)))
     ]
-    agg = jnp.concatenate(parts, 0).astype(BF16)
-    pre = direct_ref[...] + dot(agg, neigh_one_ref[...])
+    pre = direct_ref[...] + jnp.concatenate(parts, 0)
     sigmoid = jax.nn.sigmoid(pre)
     hidden = (pre[:rows] * sigmoid[:rows]).astype(BF16)
     hidden_ref[...] = hidden
+    sent = dot(hidden, neigh_two_ref[...]).astype(BF16)
+    sent_ref[...] = sent
     low = (chips - 1) * rows + chips * far
     add = shared_ref[low:, :].astype(F32)
     grad = jnp.concatenate([grad_ref[:rows, :], grad_ref[rows:, :] + add], 0)
@@ -388,8 +397,8 @@
     grad_pre_ref[...] = grad_pre[:rows]
     u = dot_nt(grad_pre, neigh_one_ref[...]).astype(BF16)
     total = joint([(col_ref[...], u[:rows]), (col_two_ref[...], u[rows:])])
-    picked = dot(pick_ref[...], hidden)
-    deal(chips, hosts, total, picked, hidden, mine_ref, msg_ref, to_refs)
+    picked = dot(pick_ref[...], sent)
+    deal(chips, hosts, total, picked, sent, mine_ref, msg_ref, to_refs)
 
 
 def last_kernel(here_ref, there_ref, output_ref):
@@ -461,11 +470,12 @@
 
     far_t = pltpu.VMEM((chips * CORES * far, rows), BF16)
     sums = jax.ShapeDtypeStruct(((rows // blk) * (all_rows // blk), blk // PARTS, blk), F32)
-    give, up, picked, pick, *sums = call(
+    give, up, sent, picked, pick, *sums = call(
         functools.partial(prep_kernel, chips),
         "prep",
-        (shape(count, width), rows_shape, shape(far, width), shape(far, rows)) + (sums,) * PARTS,
-        [HBM] * 8,
+        (shape(count, width), rows_shape, rows_shape, shape(far, width), shape(far, rows))
+        + (sums,) * PARTS,
+        [HBM] * 9,
         [
             pltpu.with_memory_space_constraint(value, pltpu.HBM)
             for value in (
@@ -477,6 +487,7 @@
                 features,
                 cotangent,
                 neigh_two,
+                neigh_one,
             )
         ],
         [
@@ -488,10 +499,11 @@
             pltpu.VMEM(features.shape, BF16),
             pltpu.VMEM(cotangent.shape, BF16),
             pltpu.VMEM(neigh_two.shape, BF16),
+            pltpu.VMEM(neigh_one.shape, BF16),
             pltpu.VMEM((rows, rows), BF16),
             far_t,
             pltpu.VMEM((count, rows), BF16),
-            pltpu.SemaphoreType.DMA((7 + CHUNKS,)),
+            pltpu.SemaphoreType.DMA((8 + CHUNKS,)),
         ],
     )
     came = shift(give, "core", 1)
@@ -517,7 +529,7 @@
         "core_sum",
         dealt,
         [VMEM] * 4,
-        (keep, came, features, picked),
+        (keep, came, sent, picked),
         flops=60 * square,
     )
     terms, recv = across(msg, to)
@@ -533,8 +545,8 @@
         functools.partial(early_one_kernel, chips),
         "early_one",
         (both_shape,) * 3 + (shape(count, rows), far_shape),
-        [VMEM] * 8,
-        (adj, lent, features, self_one, bias_one, cotangent, self_two, neigh_one),
+        [VMEM] * 9,
+        (adj, lent, features, self_one, bias_one, cotangent, self_two, neigh_one, sent),
         [far_t],
         flops=8 * square,
     )
@@ -546,11 +558,11 @@
         (adj, lent, columns, columns_two, agg, grad, summed, here, *terms),
         flops=3 * square,
     )
-    hidden, grad_pre, mine, msg, *to = call(
+    hidden, sent, grad_pre, mine, msg, *to = call(
         functools.partial(middle_kernel, chips, hosts),
         "middle",
-        (rows_shape,) * 2 + dealt,
-        [VMEM] * 12,
+        (rows_shape,) * 3 + dealt,
+        [VMEM] * 13,
         (
             adj,
             lent,
@@ -564,6 +576,7 @@
             pick,
             shared,
             neigh_one,
+            neigh_two,
         ),
         flops=12 * square,
     )
@@ -572,8 +585,8 @@
         functools.partial(there_kernel, chips, hosts),
         "there",
         rows_shape,
-        [VMEM] * (4 + chips),
-        (lent, columns_two, hidden, recv, neigh_two, *terms),
+        [VMEM] * (3 + chips),
+        (lent, columns_two, sent, recv, *terms),
     )
     shared = shift(there, "core", 1)
     here, grad = call(
@@ -584,9 +597,9 @@
         (
             adj,
             columns,
+            sent,
+            recv,
             hidden,
-            recv,
-            neigh_two,
             self_two,
             bias_two,
             grad_pre,

time: 37.8 us -> 37.9 us (level)
  no operation moved by 1% of the time
where the time goes in v18:
time: 37.9 us; the launch traced here: 37.7 us
  blocking collectives  23.8 us (63%)
  Pallas kernels  7.29 us (19%)
  starting transfers between devices  4.58 us (12%)
  waiting for transfers between devices  1.2 us (3%)
  between operations  0.75 us (2%)
    all_to_all x2, blocking collectives, across(): lax.all_to_all(msg, ('hst', 'chip', 'core'), split_axis=0, concat_axis=0,...  23.8 us
    pallas_call x10, Pallas kernels, call(): pl.pallas_call(kernel, out_shape=out_shape, in_specs=in_specs, out_specs=...  7.29 us
    ppermute x6, starting transfers between devices, shift(): return lax.ppermute(value, axis, [(i, (i + k) % size) for i in range(size)])  4.58 us
    ppermute x6, waiting for transfers between devices, shift(): return lax.ppermute(value, axis, [(i, (i + k) % size) for i in range(size)])  1.2 us
  transfers between devices with their start and end apart: 6, of which 3 were waited for; matrix products, arithmetic and copies ran while one was open for 0% of the time, Pallas kernels for 7%

profile of v18, /device:TPU:0, one launch (start us, length us, event | category | flops | bytes accessed | tf_op | source)
XLA Modules:
  0.0 37.7 jit_solution(11699223121479823062)
XLA Ops:
  0.6 0.0 copy-start.1
  0.6 0.0 copy-start.2
  0.7 2.8 %prep.1 = (bf16[640,256]{1,0:T(8,128)(2,1)S(1)}, bf16[256,256]{1,0:T(8,128)(2,1)S(1)}, bf16[256,256]{1,0:T(8,128)(2,1)S(1)}, bf16[64,256]{1,0:T(8,128)(2,1)S(1)}...) custom-call(s32[64]{0:T(128)} %dst_hbm.1, ...), custom_call_target="tpu_custom_call" | custom-call | tf_op jit(solution)/shard_map/prep/pallas_call | solution.py:409
  3.4 0.5 %collective-permute-start.1 = (bf16[640,256]{1,0:T(8,128)(2,1)S(1)}, bf16[640,256]{1,0:T(8,128)(2,1)S(1)}, u32[]{:S(2)}, u32[]{:S(2)}) collective-permute-start(bf16[640,256]{1,0:T(8,128)(2,1)S(1)} %get-tuple-element.53), channel_id=1, source_target_pairs={{0,1},{1,0},{2,3},{3,2},{4,5},{5,4},{6,7},{7,6},{8,9},{9,8},{10,11... | collective-permute-start | bytes 983048 | tf_op jit(solution)/shard_map/ppermute | solution.py:425
  3.9 0.0 copy-done.1
  3.9 0.0 copy-done.2
  3.9 0.5 %rest.1 = (bf16[1280,256]{1,0:T(8,128)(2,1)S(1)}, bf16[640,256]{1,0:T(8,128)(2,1)S(1)}, bf16[640,256]{1,0:T(8,128)(2,1)S(1)}, bf16[1792,256]{1,0:T(8,128)(2,1)S(...) custom-call(bf16[256,256]{1,0:T(8,128)(2,1)S(1)} %get-tuple-element.37.up_ref, ...), custom_call_target="tpu_custom_call" | custom-call | flops 100663296 | bytes 98304 | tf_op jit(solution)/shard_map/rest/pallas_call | solution.py:409
  4.5 0.1 collective-permute-start
  4.6 0.6 %collective-permute-done.1.came_ref = bf16[640,256]{1,0:T(8,128)(2,1)S(1)} collective-permute-done((bf16[640,256]{1,0:T(8,128)(2,1)S(1)}, bf16[640,256]{1,0:T(8,128)(2,1)S(1)}, u32[]{:S(2)}, u32[]{:S(2)}) %collective-permute-start.1) | collective-permute-done | bytes 327712 | tf_op jit(solution)/shard_map/ppermute | solution.py:425
  5.2 0.1 core_sum.1
  5.3 2.9 %collective-permute-start.2 = (bf16[512,256]{1,0:T(8,128)(2,1)S(1)}, bf16[512,256]{1,0:T(8,128)(2,1)S(1)}, u32[]{:S(2)}, u32[]{:S(2)}) collective-permute-start(bf16[512,256]{1,0:T(8,128)(2,1)S(1)} %get-tuple-element.58), channel_id=1, source_target_pairs={{0,2},{2,0},{1,3},{3,1},{4,6},{6,4},{5,7},{7,5},{8,10},{10,8},{9,1... | collective-permute-start | bytes 786440 | tf_op jit(solution)/shard_map/ppermute | solution.py:425
  8.2 12.9 %all_to_all.10.recv_ref = bf16[32,8,256]{2,1,0:T(8,128)(2,1)S(1)} all-to-all(bf16[32,8,256]{2,1,0:T(8,128)(2,1)S(1)} %get-tuple-element.55), channel_id=1, replica_groups=mesh['hst'=8,'chip'=2,'core'=2] {'hst','chip','core'}, dimensions={0} | all-to-all | bytes 262144 | tf_op jit(solution)/shard_map/all_to_all | solution.py:468
  21.2 0.0 collective-permute-done.2.refs_0_
  21.2 0.2 merge.1
  21.4 0.3 collective-permute-start.3
  21.6 0.0 collective-permute-done.lent_ref
  21.6 0.0 copy-done.5
  21.7 0.0 copy-done.6
  21.7 0.6 %early_one.1 = (f32[512,256]{1,0:T(8,128)S(1)}, f32[512,256]{1,0:T(8,128)S(1)}, f32[512,256]{1,0:T(8,128)S(1)}, bf16[640,256]{1,0:T(8,128)(2,1)S(1)}, bf16[256,256]{1,0:T(8,128)(2,1)S(1)}) custom-call(bf16[1280,256]{1,0:T(8,128)(2,1)S(1)} %get-tuple-element.43.adj_ref, bf16[1792,256]{1,0:T(8,128)(2,1)S(1)} %collective-permute-done.lent_ref, ...), custom_call_target="tpu_custom_call" | custom-call | flops 268435456 | bytes 262144 | tf_op jit(solution)/shard_map/early_one/pallas_call | solution.py:409
  22.2 0.0 copy-start.3
  22.2 0.3 mid.1
  22.6 0.5 %collective-permute-done.3.shared_ref = bf16[640,256]{1,0:T(8,128)(2,1)S(1)} collective-permute-done((bf16[640,256]{1,0:T(8,128)(2,1)S(1)}, bf16[640,256]{1,0:T(8,128)(2,1)S(1)}, u32[]{:S(2)}, u32[]{:S(2)}) %collective-permute-start.3) | collective-permute-done | bytes 327712 | tf_op jit(solution)/shard_map/ppermute | solution.py:425
  23.0 0.1 copy-done.3
  23.1 0.9 %middle.1 = (bf16[256,256]{1,0:T(8,128)(2,1)S(1)}, bf16[256,256]{1,0:T(8,128)(2,1)S(1)}, bf16[256,256]{1,0:T(8,128)(2,1)S(1)}, f32[256,256]{1,0:T(8,128)S(1)}, b...) custom-call(bf16[1280,256]{1,0:T(8,128)(2,1)S(1)} %get-tuple-element.43.adj_ref, ...), custom_call_target="tpu_custom_call" | custom-call | flops 402653184 | bytes 393216 | tf_op jit(solution)/shard_map/middle/pallas_call | solution.py:409
  24.1 0.4 %collective-permute-start.4 = (bf16[512,256]{1,0:T(8,128)(2,1)S(1)}, bf16[512,256]{1,0:T(8,128)(2,1)S(1)}, u32[]{:S(2)}, u32[]{:S(2)}) collective-permute-start(bf16[512,256]{1,0:T(8,128)(2,1)S(1)} %get-tuple-element.69), channel_id=1, source_target_pairs={{0,2},{2,0},{1,3},{3,1},{4,6},{6,4},{5,7},{7,5},{8,10},{10,8},{9,1... | collective-permute-start | bytes 786440 | tf_op jit(solution)/shard_map/ppermute | solution.py:425
  24.5 10.8 %all_to_all.11.recv_ref = bf16[32,8,256]{2,1,0:T(8,128)(2,1)S(1)} all-to-all(bf16[32,8,256]{2,1,0:T(8,128)(2,1)S(1)} %get-tuple-element.65), channel_id=1, replica_groups=mesh['hst'=8,'chip'=2,'core'=2] {'hst','chip','core'}, dimensions={0} | all-to-all | bytes 262144 | tf_op jit(solution)/shard_map/all_to_all | solution.py:468
  35.3 0.0 collective-permute-done.4.refs_0_
  35.3 0.3 there.1
  35.6 0.3 collective-permute-start.5
  35.9 1.0 %here.1 = (f32[256,256]{1,0:T(8,128)S(1)}, f32[256,256]{1,0:T(8,128)}) custom-call(bf16[1280,256]{1,0:T(8,128)(2,1)S(1)} %get-tuple-element.43.adj_ref, bf16[256,256]{1,0:T(8,128)(2,1)S(1)} %get-tuple-element.44.far_ref, bf16[256,256]{1,0:T(8,128)(2,1)S(1)} %get-tuple-element.64.sent_ref.value_ref, bf16[32,8,256]{2,1,0:T(8,128)(2,1)S(1)} %all_to_all.11.recv_ref, ...), custom_call_target="tpu_custom_call" | custom-call | flops 234881024 | bytes 229376 | tf_op jit(solution)/shard_map/here/pallas_call | solution.py:409
  36.9 0.1 collective-permute-done.5.there_ref
  37.0 0.7 %last.1 = bf16[256,256]{1,0:T(8,128)(2,1)} custom-call(f32[256,256]{1,0:T(8,128)S(1)} %get-tuple-element.70.here_ref, bf16[256,256]{1,0:T(8,128)(2,1)S(1)} %collective-permute-done.5.there_ref), custom_call_target="tpu_custom_call" | custom-call | tf_op jit(solution)/shard_map/last/pallas_call | solution.py:409
  (8 shorter events, 0.0 us)
Async XLA Ops:
  0.6 3.3 %copy-start.1 = (bf16[256,256]{1,0:T(8,128)(2,1)S(1)}, bf16[256,256]{1,0:T(8,128)(2,1)}, u32[]{:S(2)}) copy-start(bf16[256,256]{1,0:T(8,128)(2,1)} %value_ref.3) | copy-start | bytes 393220
  0.6 3.3 %copy-start.2 = (bf16[256,256]{1,0:T(8,128)(2,1)S(1)}, bf16[256,256]{1,0:T(8,128)(2,1)}, u32[]{:S(2)}) copy-start(bf16[256,256]{1,0:T(8,128)(2,1)} %up_ref.1) | copy-start | bytes 393220
  3.4 1.8 %collective-permute-start.1 = (bf16[640,256]{1,0:T(8,128)(2,1)S(1)}, bf16[640,256]{1,0:T(8,128)(2,1)S(1)}, u32[]{:S(2)}, u32[]{:S(2)}) collective-permute-start(bf16[640,256]{1,0:T(8,128)(2,1)S(1)} %get-tuple-element.53), channel_id=1, source_target_pairs={{0,1},{1,0},{2,3},{3,2},{4,5},{5,4},{6,7},{7,6},{8,9},{9,8},{10,11... | collective-permute-start | bytes 983048 | tf_op jit(solution)/shard_map/ppermute | solution.py:425
  4.5 17.2 %collective-permute-start = (bf16[1792,256]{1,0:T(8,128)(2,1)S(1)}, bf16[1792,256]{1,0:T(8,128)(2,1)S(1)}, u32[]{:S(2)}, u32[]{:S(2)}) collective-permute-start(bf16[1792,256]{1,0:T(8,128)(2,1)S(1)} %get-tuple-element.45), channel_id=1, source_target_pairs={{0,1},{1,0},{2,3},{3,2},{4,5},{5,4},{6,7},{7,6},{8,9},{9,8},{10,11... | collective-permute-start | bytes 2752520 | tf_op jit(solution)/shard_map/ppermute | solution.py:425
  5.2 16.5 %copy-start = (bf16[256,256]{1,0:T(8,128)(2,1)S(1)}, bf16[256,256]{1,0:T(8,128)(2,1)}, u32[]{:S(2)}) copy-start(bf16[256,256]{1,0:T(8,128)(2,1)} %neigh_one_ref.1) | copy-start | bytes 393220
  5.2 16.5 %copy-start.4 = (bf16[256,256]{1,0:T(8,128)(2,1)S(1)}, bf16[256,256]{1,0:T(8,128)(2,1)}, u32[]{:S(2)}) copy-start(bf16[256,256]{1,0:T(8,128)(2,1)} %weight_ref.3) | copy-start | bytes 393220
  5.2 16.5 %copy-start.5 = (bf16[256,256]{1,0:T(8,128)(2,1)S(1)}, bf16[256,256]{1,0:T(8,128)(2,1)}, u32[]{:S(2)}) copy-start(bf16[256,256]{1,0:T(8,128)(2,1)} %self_ref.3) | copy-start | bytes 393220
  5.2 16.5 %copy-start.6 = (f32[256]{0:T(256)S(1)}, f32[256]{0:T(256)}, u32[]{:S(2)}) copy-start(f32[256]{0:T(256)} %bias_ref.2) | copy-start | bytes 3076
  5.3 15.9 %collective-permute-start.2 = (bf16[512,256]{1,0:T(8,128)(2,1)S(1)}, bf16[512,256]{1,0:T(8,128)(2,1)S(1)}, u32[]{:S(2)}, u32[]{:S(2)}) collective-permute-start(bf16[512,256]{1,0:T(8,128)(2,1)S(1)} %get-tuple-element.58), channel_id=1, source_target_pairs={{0,2},{2,0},{1,3},{3,1},{4,6},{6,4},{5,7},{7,5},{8,10},{10,8},{9,1... | collective-permute-start | bytes 786440 | tf_op jit(solution)/shard_map/ppermute | solution.py:425
  21.4 1.7 %collective-permute-start.3 = (bf16[640,256]{1,0:T(8,128)(2,1)S(1)}, bf16[640,256]{1,0:T(8,128)(2,1)S(1)}, u32[]{:S(2)}, u32[]{:S(2)}) collective-permute-start(bf16[640,256]{1,0:T(8,128)(2,1)S(1)} %get-tuple-element.60.here_ref), channel_id=1, source_target_pairs={{0,1},{1,0},{2,3},{3,2},{4,5},{5,4},{6,7},{7,6},{8,9},{9,8},{10,11... | collective-permute-start | bytes 983048 | tf_op jit(solution)/shard_map/ppermute | solution.py:425
  22.2 0.9 %copy-start.3 = (bf16[256,256]{1,0:T(8,128)(2,1)S(1)}, bf16[256,256]{1,0:T(8,128)(2,1)}, u32[]{:S(2)}) copy-start(bf16[256,256]{1,0:T(8,128)(2,1)} %neigh_two_ref.1) | copy-start | bytes 393220
  23.1 12.8 %copy-start.7 = (f32[256]{0:T(256)S(1)}, f32[256]{0:T(256)}, u32[]{:S(2)}) copy-start(f32[256]{0:T(256)} %bias_ref.3) | copy-start | bytes 3076
  24.1 11.3 %collective-permute-start.4 = (bf16[512,256]{1,0:T(8,128)(2,1)S(1)}, bf16[512,256]{1,0:T(8,128)(2,1)S(1)}, u32[]{:S(2)}, u32[]{:S(2)}) collective-permute-start(bf16[512,256]{1,0:T(8,128)(2,1)S(1)} %get-tuple-element.69), channel_id=1, source_target_pairs={{0,2},{2,0},{1,3},{3,1},{4,6},{6,4},{5,7},{7,5},{8,10},{10,8},{9,1... | collective-permute-start | bytes 786440 | tf_op jit(solution)/shard_map/ppermute | solution.py:425
  35.6 1.4 %collective-permute-start.5 = (bf16[256,256]{1,0:T(8,128)(2,1)S(1)}, bf16[256,256]{1,0:T(8,128)(2,1)S(1)}, u32[]{:S(2)}, u32[]{:S(2)}) collective-permute-start(bf16[256,256]{1,0:T(8,128)(2,1)S(1)} %there.1), channel_id=1, source_target_pairs={{0,1},{1,0},{2,3},{3,2},{4,5},{5,4},{6,7},{7,6},{8,9},{9,8},{10,11... | collective-permute-start | bytes 393224 | tf_op jit(solution)/shard_map/ppermute | solution.py:425

commit v19 on v18

--- a/solution.py
+++ b/solution.py
@@ -71,14 +71,10 @@
     rows_hbm,
     send_hbm,
     tile_hbm,
-    features_hbm,
     cot_hbm,
     neigh_two_hbm,
-    neigh_one_hbm,
     give_ref,
     up_ref,
-    sent_ref,
-    picked_ref,
     pick_ref,
     *rest,
 ):
@@ -89,10 +85,8 @@
         rows_ref,
         send_ref,
         tile_buf,
-        features_ref,
         cot_ref,
         neigh_two_ref,
-        neigh_one_ref,
         square,
         far_t,
         col,
@@ -110,15 +104,13 @@
     pairs += [
         (cot_hbm, cot_ref),
         (neigh_two_hbm, neigh_two_ref),
-        (neigh_one_hbm, neigh_one_ref),
-        (features_hbm, features_ref),
         (send_hbm, send_ref),
     ]
     pairs += chunks[first:]
     copies = [pltpu.make_async_copy(a, b, sems.at[i]) for i, (a, b) in enumerate(pairs)]
     for copy in copies:
         copy.start()
-    rows = features_ref.shape[0]
+    rows = cot_ref.shape[0]
     bpd = rows // blk
     sources = accs[0].shape[0] // bpd
     part = accs[0].shape[1]
@@ -139,15 +131,13 @@
     for c in range(first):
         copies[3 + c].wait()
         lax.fori_loop(c * each, (c + 1) * each, add, 0, unroll=True)
-    for copy in copies[3 + first : 8 + first]:
+    for copy in copies[3 + first : 6 + first]:
         copy.wait()
     u = dot_nt(cot_ref[...], neigh_two_ref[...]).astype(BF16)
     up_ref[...] = u
     pick_ref[...] = pick_matrix(send_ref, rows)
-    sent_ref[...] = dot(features_ref[...], neigh_one_ref[...]).astype(BF16)
-    picked_ref[...] = dot(pick_ref[...], sent_ref[...]).astype(BF16)
     for c in range(first, CHUNKS):
-        copies[8 + c].wait()
+        copies[6 + c].wait()
         lax.fori_loop(c * each, (c + 1) * each, add, 0, unroll=True)
     chip, side = lax.axis_index("chip"), 1 - lax.axis_index("core")
     base = chips * CORES
@@ -175,9 +165,12 @@
                 out_ref[low : low + part, j * blk : (j + 1) * blk] = value
 
 
-def rest_kernel(chips, up_ref, cot_ref, value_ref, pick_ref, *refs):
+def rest_kernel(chips, up_ref, cot_ref, value_ref, pick_ref, neigh_ref, *refs):
     accs = refs[:PARTS]
-    adj_ref, col_ref, keep_ref, lend_ref, place_ref, far_ref, far_t = refs[PARTS:]
+    sent_ref, picked_ref, adj_ref, col_ref, keep_ref, lend_ref, place_ref, far_ref, far_t = refs[PARTS:]
+    sent = dot(value_ref[...], neigh_ref[...]).astype(BF16)
+    sent_ref[...] = sent
+    picked_ref[...] = dot(pick_ref[...], sent).astype(BF16)
     rows = up_ref.shape[0]
     bpd = rows // accs[0].shape[2]
     for d in range(adj_ref.shape[0] // rows):
@@ -270,7 +263,7 @@
 
 
 def early_one_kernel(
-    chips, adj_ref, lent_ref, value_ref, self_ref, bias_ref, up_ref, weight_ref, neigh_ref, sent_ref,
+    chips, adj_ref, lent_ref, value_ref, self_ref, bias_ref, up_ref, weight_ref, neigh_ref, sent_ref, unused_ref,
     agg_ref, direct_ref, grad_ref, col_ref, far_ref, far_t,
 ):
     value = value_ref[...]
@@ -470,12 +463,11 @@
 
     far_t = pltpu.VMEM((chips * CORES * far, rows), BF16)
     sums = jax.ShapeDtypeStruct(((rows // blk) * (all_rows // blk), blk // PARTS, blk), F32)
-    give, up, sent, picked, pick, *sums = call(
+    give, up, pick, *sums = call(
         functools.partial(prep_kernel, chips),
         "prep",
-        (shape(count, width), rows_shape, rows_shape, shape(far, width), shape(far, rows))
-        + (sums,) * PARTS,
-        [HBM] * 9,
+        (shape(count, width), rows_shape, shape(far, rows)) + (sums,) * PARTS,
+        [HBM] * 7,
         [
             pltpu.with_memory_space_constraint(value, pltpu.HBM)
             for value in (
@@ -484,10 +476,8 @@
                 tile_rows,
                 send_list,
                 tile_val,
-                features,
                 cotangent,
                 neigh_two,
-                neigh_one,
             )
         ],
         [
@@ -496,21 +486,21 @@
             pltpu.SMEM(tile_rows.shape, jnp.int32),
             pltpu.SMEM(send_list.shape, jnp.int32),
             pltpu.VMEM(tile_val.shape, BF16),
-            pltpu.VMEM(features.shape, BF16),
             pltpu.VMEM(cotangent.shape, BF16),
             pltpu.VMEM(neigh_two.shape, BF16),
-            pltpu.VMEM(neigh_one.shape, BF16),
             pltpu.VMEM((rows, rows), BF16),
             far_t,
             pltpu.VMEM((count, rows), BF16),
-            pltpu.SemaphoreType.DMA((8 + CHUNKS,)),
+            pltpu.SemaphoreType.DMA((6 + CHUNKS,)),
         ],
     )
     came = shift(give, "core", 1)
-    adj, col, keep, lend, place, columns = call(
+    sent, picked, adj, col, keep, lend, place, columns = call(
         functools.partial(rest_kernel, chips),
         "rest",
         (
+            rows_shape,
+            shape(far, width),
             shape(all_rows, rows),
             shape(count, rows),
             shape(count, width),
@@ -518,8 +508,8 @@
             shape(rows, chips * far),
             far_shape,
         ),
-        [VMEM] * (4 + PARTS),
-        (up, cotangent, features, pick, *sums),
+        [VMEM] * (5 + PARTS),
+        (up, cotangent, features, pick, neigh_one, *sums),
         [far_t],
         flops=3 * square,
     )
@@ -545,8 +535,19 @@
         functools.partial(early_one_kernel, chips),
         "early_one",
         (both_shape,) * 3 + (shape(count, rows), far_shape),
-        [VMEM] * 9,
-        (adj, lent, features, self_one, bias_one, cotangent, self_two, neigh_one, sent),
+        [VMEM] * 10,
+        (
+            adj,
+            lent,
+            features,
+            self_one,
+            bias_one,
+            cotangent,
+            self_two,
+            neigh_one,
+            sent,
+            neigh_two,
+        ),
         [far_t],
         flops=8 * square,
     )

time: 37.9 us -> 37.6 us (level)
  no operation moved by 1% of the time
where the time goes in v19:
time: 37.6 us; the launch traced here: 37.4 us
  blocking collectives  23.8 us (63%)
  Pallas kernels  7.05 us (19%)
  starting transfers between devices  4.66 us (12%)
  waiting for transfers between devices  1.11 us (3%)
  between operations  0.74 us (2%)
    all_to_all x2, blocking collectives, across(): lax.all_to_all(msg, ('hst', 'chip', 'core'), split_axis=0, concat_axis=0,...  23.8 us
    pallas_call x10, Pallas kernels, call(): pl.pallas_call(kernel, out_shape=out_shape, in_specs=in_specs, out_specs=...  7.05 us
    ppermute x6, starting transfers between devices, shift(): return lax.ppermute(value, axis, [(i, (i + k) % size) for i in range(size)])  4.66 us
    ppermute x6, waiting for transfers between devices, shift(): return lax.ppermute(value, axis, [(i, (i + k) % size) for i in range(size)])  1.11 us
  transfers between devices with their start and end apart: 6, of which 3 were waited for; matrix products, arithmetic and copies ran while one was open for 0% of the time, Pallas kernels for 7%

profile of v19, /device:TPU:0, one launch (start us, length us, event | category | flops | bytes accessed | tf_op | source)
XLA Modules:
  0.0 37.4 jit_solution(18315975376393004722)
XLA Ops:
  0.6 0.0 copy-start
  0.6 0.0 copy-start.3
  0.7 0.0 copy-start.1
  0.7 2.4 %prep.1 = (bf16[640,256]{1,0:T(8,128)(2,1)S(1)}, bf16[256,256]{1,0:T(8,128)(2,1)S(1)}, bf16[64,256]{1,0:T(8,128)(2,1)S(1)}, f32[20,32,128]{2,1,0:T(8,128)S(1)}, ...) custom-call(s32[64]{0:T(128)} %dst_hbm.1, s32[64]{0:T(128)} %src_hbm.1, ...), custom_call_target="tpu_custom_call" | custom-call | tf_op jit(solution)/shard_map/prep/pallas_call | solution.py:402
  3.1 0.5 %collective-permute-start.1 = (bf16[640,256]{1,0:T(8,128)(2,1)S(1)}, bf16[640,256]{1,0:T(8,128)(2,1)S(1)}, u32[]{:S(2)}, u32[]{:S(2)}) collective-permute-start(bf16[640,256]{1,0:T(8,128)(2,1)S(1)} %get-tuple-element.53), channel_id=1, source_target_pairs={{0,1},{1,0},{2,3},{3,2},{4,5},{5,4},{6,7},{7,6},{8,9},{9,8},{10,11... | collective-permute-start | bytes 983048 | tf_op jit(solution)/shard_map/ppermute | solution.py:418
  3.6 0.0 copy-done
  3.6 0.0 copy-done.3
  3.6 0.0 copy-done.1
  3.6 0.6 %rest.1 = (bf16[256,256]{1,0:T(8,128)(2,1)S(1)}, bf16[64,256]{1,0:T(8,128)(2,1)S(1)}, bf16[1280,256]{1,0:T(8,128)(2,1)S(1)}, bf16[640,256]{1,0:T(8,128)(2,1)S(1)...) custom-call(bf16[256,256]{1,0:T(8,128)(2,1)S(1)} %get-tuple-element., ...), custom_call_target="tpu_custom_call" | custom-call | flops 100663296 | bytes 98304 | tf_op jit(solution)/shard_map/rest/pallas_call | solution.py:402
  4.2 0.1 collective-permute-start
  4.4 0.5 %collective-permute-done.1.came_ref = bf16[640,256]{1,0:T(8,128)(2,1)S(1)} collective-permute-done((bf16[640,256]{1,0:T(8,128)(2,1)S(1)}, bf16[640,256]{1,0:T(8,128)(2,1)S(1)}, u32[]{:S(2)}, u32[]{:S(2)}) %collective-permute-start.1) | collective-permute-done | bytes 327712 | tf_op jit(solution)/shard_map/ppermute | solution.py:418
  4.9 0.1 core_sum.1
  5.0 2.9 %collective-permute-start.2 = (bf16[512,256]{1,0:T(8,128)(2,1)S(1)}, bf16[512,256]{1,0:T(8,128)(2,1)S(1)}, u32[]{:S(2)}, u32[]{:S(2)}) collective-permute-start(bf16[512,256]{1,0:T(8,128)(2,1)S(1)} %get-tuple-element.58), channel_id=1, source_target_pairs={{0,2},{2,0},{1,3},{3,1},{4,6},{6,4},{5,7},{7,5},{8,10},{10,8},{9,1... | collective-permute-start | bytes 786440 | tf_op jit(solution)/shard_map/ppermute | solution.py:418
  7.9 12.9 %all_to_all.10.recv_ref = bf16[32,8,256]{2,1,0:T(8,128)(2,1)S(1)} all-to-all(bf16[32,8,256]{2,1,0:T(8,128)(2,1)S(1)} %get-tuple-element.55), channel_id=1, replica_groups=mesh['hst'=8,'chip'=2,'core'=2] {'hst','chip','core'}, dimensions={0} | all-to-all | bytes 262144 | tf_op jit(solution)/shard_map/all_to_all | solution.py:461
  20.9 0.0 collective-permute-done.2.refs_0_
  20.9 0.2 merge.1
  21.1 0.3 collective-permute-start.3
  21.3 0.0 collective-permute-done.lent_ref
  21.3 0.0 copy-done.2
  21.3 0.0 copy-done.4
  21.4 0.6 %early_one.1 = (f32[512,256]{1,0:T(8,128)S(1)}, f32[512,256]{1,0:T(8,128)S(1)}, f32[512,256]{1,0:T(8,128)S(1)}, bf16[640,256]{1,0:T(8,128)(2,1)S(1)}, bf16[256,256]{1,0:T(8,128)(2,1)S(1)}) custom-call(bf16[1280,256]{1,0:T(8,128)(2,1)S(1)} %get-tuple-element.43.adj_ref, bf16[1792,256]{1,0:T(8,128)(2,1)S(1)} %collective-permute-done.lent_ref, ...), custom_call_target="tpu_custom_call" | custom-call | flops 268435456 | bytes 262144 | tf_op jit(solution)/shard_map/early_one/pallas_call | solution.py:402
  21.9 0.3 mid.1
  22.2 0.5 %collective-permute-done.3.shared_ref = bf16[640,256]{1,0:T(8,128)(2,1)S(1)} collective-permute-done((bf16[640,256]{1,0:T(8,128)(2,1)S(1)}, bf16[640,256]{1,0:T(8,128)(2,1)S(1)}, u32[]{:S(2)}, u32[]{:S(2)}) %collective-permute-start.3) | collective-permute-done | bytes 327712 | tf_op jit(solution)/shard_map/ppermute | solution.py:418
  22.7 0.9 %middle.1 = (bf16[256,256]{1,0:T(8,128)(2,1)S(1)}, bf16[256,256]{1,0:T(8,128)(2,1)S(1)}, bf16[256,256]{1,0:T(8,128)(2,1)S(1)}, f32[256,256]{1,0:T(8,128)S(1)}, b...) custom-call(bf16[1280,256]{1,0:T(8,128)(2,1)S(1)} %get-tuple-element.43.adj_ref, ...), custom_call_target="tpu_custom_call" | custom-call | flops 402653184 | bytes 393216 | tf_op jit(solution)/shard_map/middle/pallas_call | solution.py:402
  23.7 0.5 %collective-permute-start.4 = (bf16[512,256]{1,0:T(8,128)(2,1)S(1)}, bf16[512,256]{1,0:T(8,128)(2,1)S(1)}, u32[]{:S(2)}, u32[]{:S(2)}) collective-permute-start(bf16[512,256]{1,0:T(8,128)(2,1)S(1)} %get-tuple-element.69), channel_id=1, source_target_pairs={{0,2},{2,0},{1,3},{3,1},{4,6},{6,4},{5,7},{7,5},{8,10},{10,8},{9,1... | collective-permute-start | bytes 786440 | tf_op jit(solution)/shard_map/ppermute | solution.py:418
  24.2 10.8 %all_to_all.11.recv_ref = bf16[32,8,256]{2,1,0:T(8,128)(2,1)S(1)} all-to-all(bf16[32,8,256]{2,1,0:T(8,128)(2,1)S(1)} %get-tuple-element.65), channel_id=1, replica_groups=mesh['hst'=8,'chip'=2,'core'=2] {'hst','chip','core'}, dimensions={0} | all-to-all | bytes 262144 | tf_op jit(solution)/shard_map/all_to_all | solution.py:461
  35.0 0.0 collective-permute-done.4.refs_0_
  35.0 0.3 there.1
  35.3 0.3 collective-permute-start.5
  35.6 1.0 %here.1 = (f32[256,256]{1,0:T(8,128)S(1)}, f32[256,256]{1,0:T(8,128)}) custom-call(bf16[1280,256]{1,0:T(8,128)(2,1)S(1)} %get-tuple-element.43.adj_ref, bf16[256,256]{1,0:T(8,128)(2,1)S(1)} %get-tuple-element.44.far_ref, bf16[256,256]{1,0:T(8,128)(2,1)S(1)} %get-tuple-element.64.sent_ref.value_ref, bf16[32,8,256]{2,1,0:T(8,128)(2,1)S(1)} %all_to_all.11.recv_ref, ...), custom_call_target="tpu_custom_call" | custom-call | flops 234881024 | bytes 229376 | tf_op jit(solution)/shard_map/here/pallas_call | solution.py:402
  36.6 0.1 collective-permute-done.5.there_ref
  36.7 0.7 %last.1 = bf16[256,256]{1,0:T(8,128)(2,1)} custom-call(f32[256,256]{1,0:T(8,128)S(1)} %get-tuple-element.70.here_ref, bf16[256,256]{1,0:T(8,128)(2,1)S(1)} %collective-permute-done.5.there_ref), custom_call_target="tpu_custom_call" | custom-call | tf_op jit(solution)/shard_map/last/pallas_call | solution.py:402
  (8 shorter events, 0.0 us)
Async XLA Ops:
  0.6 3.0 %copy-start = (bf16[256,256]{1,0:T(8,128)(2,1)S(1)}, bf16[256,256]{1,0:T(8,128)(2,1)}, u32[]{:S(2)}) copy-start(bf16[256,256]{1,0:T(8,128)(2,1)} %up_ref.1) | copy-start | bytes 393220
  0.6 3.0 %copy-start.3 = (bf16[256,256]{1,0:T(8,128)(2,1)S(1)}, bf16[256,256]{1,0:T(8,128)(2,1)}, u32[]{:S(2)}) copy-start(bf16[256,256]{1,0:T(8,128)(2,1)} %value_ref.3) | copy-start | bytes 393220
  0.7 3.0 %copy-start.1 = (bf16[256,256]{1,0:T(8,128)(2,1)S(1)}, bf16[256,256]{1,0:T(8,128)(2,1)}, u32[]{:S(2)}) copy-start(bf16[256,256]{1,0:T(8,128)(2,1)} %neigh_one_ref.1) | copy-start | bytes 393220
  3.1 1.8 %collective-permute-start.1 = (bf16[640,256]{1,0:T(8,128)(2,1)S(1)}, bf16[640,256]{1,0:T(8,128)(2,1)S(1)}, u32[]{:S(2)}, u32[]{:S(2)}) collective-permute-start(bf16[640,256]{1,0:T(8,128)(2,1)S(1)} %get-tuple-element.53), channel_id=1, source_target_pairs={{0,1},{1,0},{2,3},{3,2},{4,5},{5,4},{6,7},{7,6},{8,9},{9,8},{10,11... | collective-permute-start | bytes 983048 | tf_op jit(solution)/shard_map/ppermute | solution.py:418
  4.2 17.1 %collective-permute-start = (bf16[1792,256]{1,0:T(8,128)(2,1)S(1)}, bf16[1792,256]{1,0:T(8,128)(2,1)S(1)}, u32[]{:S(2)}, u32[]{:S(2)}) collective-permute-start(bf16[1792,256]{1,0:T(8,128)(2,1)S(1)} %get-tuple-element.45), channel_id=1, source_target_pairs={{0,1},{1,0},{2,3},{3,2},{4,5},{5,4},{6,7},{7,6},{8,9},{9,8},{10,11... | collective-permute-start | bytes 2752520 | tf_op jit(solution)/shard_map/ppermute | solution.py:418
  4.9 16.5 %copy-start.2 = (bf16[256,256]{1,0:T(8,128)(2,1)S(1)}, bf16[256,256]{1,0:T(8,128)(2,1)}, u32[]{:S(2)}) copy-start(bf16[256,256]{1,0:T(8,128)(2,1)} %neigh_two_ref.1) | copy-start | bytes 393220
  4.9 16.5 %copy-start.4 = (bf16[256,256]{1,0:T(8,128)(2,1)S(1)}, bf16[256,256]{1,0:T(8,128)(2,1)}, u32[]{:S(2)}) copy-start(bf16[256,256]{1,0:T(8,128)(2,1)} %weight_ref.3) | copy-start | bytes 393220
  4.9 16.5 %copy-start.5 = (bf16[256,256]{1,0:T(8,128)(2,1)S(1)}, bf16[256,256]{1,0:T(8,128)(2,1)}, u32[]{:S(2)}) copy-start(bf16[256,256]{1,0:T(8,128)(2,1)} %self_ref.3) | copy-start | bytes 393220
  4.9 16.5 %copy-start.6 = (f32[256]{0:T(256)S(1)}, f32[256]{0:T(256)}, u32[]{:S(2)}) copy-start(f32[256]{0:T(256)} %bias_ref.2) | copy-start | bytes 3076
  5.0 15.9 %collective-permute-start.2 = (bf16[512,256]{1,0:T(8,128)(2,1)S(1)}, bf16[512,256]{1,0:T(8,128)(2,1)S(1)}, u32[]{:S(2)}, u32[]{:S(2)}) collective-permute-start(bf16[512,256]{1,0:T(8,128)(2,1)S(1)} %get-tuple-element.58), channel_id=1, source_target_pairs={{0,2},{2,0},{1,3},{3,1},{4,6},{6,4},{5,7},{7,5},{8,10},{10,8},{9,1... | collective-permute-start | bytes 786440 | tf_op jit(solution)/shard_map/ppermute | solution.py:418
  21.1 1.7 %collective-permute-start.3 = (bf16[640,256]{1,0:T(8,128)(2,1)S(1)}, bf16[640,256]{1,0:T(8,128)(2,1)S(1)}, u32[]{:S(2)}, u32[]{:S(2)}) collective-permute-start(bf16[640,256]{1,0:T(8,128)(2,1)S(1)} %get-tuple-element.60.here_ref), channel_id=1, source_target_pairs={{0,1},{1,0},{2,3},{3,2},{4,5},{5,4},{6,7},{7,6},{8,9},{9,8},{10,11... | collective-permute-start | bytes 983048 | tf_op jit(solution)/shard_map/ppermute | solution.py:418
  22.7 12.8 %copy-start.7 = (f32[256]{0:T(256)S(1)}, f32[256]{0:T(256)}, u32[]{:S(2)}) copy-start(f32[256]{0:T(256)} %bias_ref.3) | copy-start | bytes 3076
  23.7 11.3 %collective-permute-start.4 = (bf16[512,256]{1,0:T(8,128)(2,1)S(1)}, bf16[512,256]{1,0:T(8,128)(2,1)S(1)}, u32[]{:S(2)}, u32[]{:S(2)}) collective-permute-start(bf16[512,256]{1,0:T(8,128)(2,1)S(1)} %get-tuple-element.69), channel_id=1, source_target_pairs={{0,2},{2,0},{1,3},{3,1},{4,6},{6,4},{5,7},{7,5},{8,10},{10,8},{9,1... | collective-permute-start | bytes 786440 | tf_op jit(solution)/shard_map/ppermute | solution.py:418
  35.3 1.4 %collective-permute-start.5 = (bf16[256,256]{1,0:T(8,128)(2,1)S(1)}, bf16[256,256]{1,0:T(8,128)(2,1)S(1)}, u32[]{:S(2)}, u32[]{:S(2)}) collective-permute-start(bf16[256,256]{1,0:T(8,128)(2,1)S(1)} %there.1), channel_id=1, source_target_pairs={{0,1},{1,0},{2,3},{3,2},{4,5},{5,4},{6,7},{7,6},{8,9},{9,8},{10,11... | collective-permute-start | bytes 393224 | tf_op jit(solution)/shard_map/ppermute | solution.py:418

commit v20 on v19

--- a/solution.py
+++ b/solution.py
@@ -323,14 +323,15 @@
 
 def here_kernel(
     chips, hosts, adj_ref, far_ref, sent_ref, recv_ref, value_ref, self_ref, bias_ref, up_ref,
-    weight_ref, mine_ref, place_ref, *refs
+    weight_ref, neigh_ref, mine_ref, place_ref, *refs
 ):
     came, (out_ref, grad_ref) = refs[:-2], refs[-2:]
     rows = mine_ref.shape[0]
-    grad = dot_nt(up_ref[...], weight_ref[...]) + mine_ref[...]
+    total = mine_ref[...] + returned(place_ref, recv_ref, hosts, chips)
     for block in came:
-        grad = grad + block[:rows, :].astype(F32)
-    grad_ref[...] = grad + returned(place_ref, recv_ref, hosts, chips)
+        total = total + block[:rows, :].astype(F32)
+    grad = dot_nt(total.astype(BF16), neigh_ref[...])
+    grad_ref[...] = grad + dot_nt(up_ref[...], weight_ref[...])
     out = column_product(chips, hosts, adj_ref, far_ref, sent_ref, came, recv_ref)
     out_ref[...] = out + dot(value_ref[...], self_ref[...]) + bias_ref[...].reshape(1, -1)
 
@@ -362,7 +363,6 @@
     grad_ref,
     pick_ref,
     shared_ref,
-    neigh_one_ref,
     neigh_two_ref,
     hidden_ref,
     sent_ref,
@@ -388,8 +388,7 @@
     grad = jnp.concatenate([grad_ref[:rows, :], grad_ref[rows:, :] + add], 0)
     grad_pre = (grad * sigmoid * (1.0 + pre * (1.0 - sigmoid))).astype(BF16)
     grad_pre_ref[...] = grad_pre[:rows]
-    u = dot_nt(grad_pre, neigh_one_ref[...]).astype(BF16)
-    total = joint([(col_ref[...], u[:rows]), (col_two_ref[...], u[rows:])])
+    total = joint([(col_ref[...], grad_pre[:rows]), (col_two_ref[...], grad_pre[rows:])])
     picked = dot(pick_ref[...], sent)
     deal(chips, hosts, total, picked, sent, mine_ref, msg_ref, to_refs)
 
@@ -563,7 +562,7 @@
         functools.partial(middle_kernel, chips, hosts),
         "middle",
         (rows_shape,) * 3 + dealt,
-        [VMEM] * 13,
+        [VMEM] * 12,
         (
             adj,
             lent,
@@ -576,7 +575,6 @@
             grad,
             pick,
             shared,
-            neigh_one,
             neigh_two,
         ),
         flops=12 * square,
@@ -594,7 +592,7 @@
         functools.partial(here_kernel, chips, hosts),
         "here",
         (sum_shape,) * 2,
-        [VMEM] * (10 + chips),
+        [VMEM] * (11 + chips),
         (
             adj,
             columns,
@@ -605,6 +603,7 @@
             bias_two,
             grad_pre,
             self_one,
+            neigh_one,
             mine,
             place,
             *terms,

time: 37.6 us -> 37.4 us (level)
  no operation moved by 1% of the time
where the time goes in v20:
time: 37.4 us; the launch traced here: 37.2 us
  blocking collectives  23.8 us (64%)
  Pallas kernels  6.91 us (18%)
  starting transfers between devices  4.66 us (12%)
  waiting for transfers between devices  1.11 us (3%)
  between operations  0.74 us (2%)
    all_to_all x2, blocking collectives, across(): lax.all_to_all(msg, ('hst', 'chip', 'core'), split_axis=0, concat_axis=0,...  23.8 us
    pallas_call x10, Pallas kernels, call(): pl.pallas_call(kernel, out_shape=out_shape, in_specs=in_specs, out_specs=...  6.91 us
    ppermute x6, starting transfers between devices, shift(): return lax.ppermute(value, axis, [(i, (i + k) % size) for i in range(size)])  4.66 us
    ppermute x6, waiting for transfers between devices, shift(): return lax.ppermute(value, axis, [(i, (i + k) % size) for i in range(size)])  1.11 us
  transfers between devices with their start and end apart: 6, of which 3 were waited for; matrix products, arithmetic and copies ran while one was open for 0% of the time, Pallas kernels for 7%

profile of v20, /device:TPU:0, one launch (start us, length us, event | category | flops | bytes accessed | tf_op | source)
XLA Modules:
  0.0 37.2 jit_solution(12176421994499888801)
XLA Ops:
  0.6 0.0 copy-start
  0.6 0.0 copy-start.3
  0.7 0.0 copy-start.1
  0.7 2.4 %prep.1 = (bf16[640,256]{1,0:T(8,128)(2,1)S(1)}, bf16[256,256]{1,0:T(8,128)(2,1)S(1)}, bf16[64,256]{1,0:T(8,128)(2,1)S(1)}, f32[20,32,128]{2,1,0:T(8,128)S(1)}, ...) custom-call(s32[64]{0:T(128)} %dst_hbm.1, s32[64]{0:T(128)} %src_hbm.1, ...), custom_call_target="tpu_custom_call" | custom-call | tf_op jit(solution)/shard_map/prep/pallas_call | solution.py:401
  3.1 0.5 %collective-permute-start.1 = (bf16[640,256]{1,0:T(8,128)(2,1)S(1)}, bf16[640,256]{1,0:T(8,128)(2,1)S(1)}, u32[]{:S(2)}, u32[]{:S(2)}) collective-permute-start(bf16[640,256]{1,0:T(8,128)(2,1)S(1)} %get-tuple-element.53), channel_id=1, source_target_pairs={{0,1},{1,0},{2,3},{3,2},{4,5},{5,4},{6,7},{7,6},{8,9},{9,8},{10,11... | collective-permute-start | bytes 983048 | tf_op jit(solution)/shard_map/ppermute | solution.py:417
  3.6 0.0 copy-done
  3.6 0.0 copy-done.3
  3.6 0.0 copy-done.1
  3.6 0.6 %rest.1 = (bf16[256,256]{1,0:T(8,128)(2,1)S(1)}, bf16[64,256]{1,0:T(8,128)(2,1)S(1)}, bf16[1280,256]{1,0:T(8,128)(2,1)S(1)}, bf16[640,256]{1,0:T(8,128)(2,1)S(1)...) custom-call(bf16[256,256]{1,0:T(8,128)(2,1)S(1)} %get-tuple-element., ...), custom_call_target="tpu_custom_call" | custom-call | flops 100663296 | bytes 98304 | tf_op jit(solution)/shard_map/rest/pallas_call | solution.py:401
  4.2 0.1 collective-permute-start
  4.4 0.5 %collective-permute-done.1.came_ref = bf16[640,256]{1,0:T(8,128)(2,1)S(1)} collective-permute-done((bf16[640,256]{1,0:T(8,128)(2,1)S(1)}, bf16[640,256]{1,0:T(8,128)(2,1)S(1)}, u32[]{:S(2)}, u32[]{:S(2)}) %collective-permute-start.1) | collective-permute-done | bytes 327712 | tf_op jit(solution)/shard_map/ppermute | solution.py:417
  4.9 0.1 core_sum.1
  5.0 2.9 %collective-permute-start.2 = (bf16[512,256]{1,0:T(8,128)(2,1)S(1)}, bf16[512,256]{1,0:T(8,128)(2,1)S(1)}, u32[]{:S(2)}, u32[]{:S(2)}) collective-permute-start(bf16[512,256]{1,0:T(8,128)(2,1)S(1)} %get-tuple-element.58), channel_id=1, source_target_pairs={{0,2},{2,0},{1,3},{3,1},{4,6},{6,4},{5,7},{7,5},{8,10},{10,8},{9,1... | collective-permute-start | bytes 786440 | tf_op jit(solution)/shard_map/ppermute | solution.py:417
  7.9 12.9 %all_to_all.10.recv_ref = bf16[32,8,256]{2,1,0:T(8,128)(2,1)S(1)} all-to-all(bf16[32,8,256]{2,1,0:T(8,128)(2,1)S(1)} %get-tuple-element.55), channel_id=1, replica_groups=mesh['hst'=8,'chip'=2,'core'=2] {'hst','chip','core'}, dimensions={0} | all-to-all | bytes 262144 | tf_op jit(solution)/shard_map/all_to_all | solution.py:460
  20.9 0.0 collective-permute-done.2.refs_0_
  20.9 0.2 merge.1
  21.1 0.3 collective-permute-start.3
  21.3 0.0 collective-permute-done.lent_ref
  21.3 0.0 copy-done.2
  21.3 0.0 copy-done.4
  21.4 0.6 %early_one.1 = (f32[512,256]{1,0:T(8,128)S(1)}, f32[512,256]{1,0:T(8,128)S(1)}, f32[512,256]{1,0:T(8,128)S(1)}, bf16[640,256]{1,0:T(8,128)(2,1)S(1)}, bf16[256,256]{1,0:T(8,128)(2,1)S(1)}) custom-call(bf16[1280,256]{1,0:T(8,128)(2,1)S(1)} %get-tuple-element.43.adj_ref, bf16[1792,256]{1,0:T(8,128)(2,1)S(1)} %collective-permute-done.lent_ref, ...), custom_call_target="tpu_custom_call" | custom-call | flops 268435456 | bytes 262144 | tf_op jit(solution)/shard_map/early_one/pallas_call | solution.py:401
  21.9 0.3 mid.1
  22.3 0.5 %collective-permute-done.3.shared_ref = bf16[640,256]{1,0:T(8,128)(2,1)S(1)} collective-permute-done((bf16[640,256]{1,0:T(8,128)(2,1)S(1)}, bf16[640,256]{1,0:T(8,128)(2,1)S(1)}, u32[]{:S(2)}, u32[]{:S(2)}) %collective-permute-start.3) | collective-permute-done | bytes 327712 | tf_op jit(solution)/shard_map/ppermute | solution.py:417
  22.7 0.8 %middle.1 = (bf16[256,256]{1,0:T(8,128)(2,1)S(1)}, bf16[256,256]{1,0:T(8,128)(2,1)S(1)}, bf16[256,256]{1,0:T(8,128)(2,1)S(1)}, f32[256,256]{1,0:T(8,128)S(1)}, b...) custom-call(bf16[1280,256]{1,0:T(8,128)(2,1)S(1)} %get-tuple-element.43.adj_ref, ...), custom_call_target="tpu_custom_call" | custom-call | flops 402653184 | bytes 393216 | tf_op jit(solution)/shard_map/middle/pallas_call | solution.py:401
  23.5 0.5 %collective-permute-start.4 = (bf16[512,256]{1,0:T(8,128)(2,1)S(1)}, bf16[512,256]{1,0:T(8,128)(2,1)S(1)}, u32[]{:S(2)}, u32[]{:S(2)}) collective-permute-start(bf16[512,256]{1,0:T(8,128)(2,1)S(1)} %get-tuple-element.69), channel_id=1, source_target_pairs={{0,2},{2,0},{1,3},{3,1},{4,6},{6,4},{5,7},{7,5},{8,10},{10,8},{9,1... | collective-permute-start | bytes 786440 | tf_op jit(solution)/shard_map/ppermute | solution.py:417
  24.0 10.8 %all_to_all.11.recv_ref = bf16[32,8,256]{2,1,0:T(8,128)(2,1)S(1)} all-to-all(bf16[32,8,256]{2,1,0:T(8,128)(2,1)S(1)} %get-tuple-element.65), channel_id=1, replica_groups=mesh['hst'=8,'chip'=2,'core'=2] {'hst','chip','core'}, dimensions={0} | all-to-all | bytes 262144 | tf_op jit(solution)/shard_map/all_to_all | solution.py:460
  34.9 0.0 collective-permute-done.4.refs_0_
  34.9 0.3 there.1
  35.1 0.3 collective-permute-start.5
  35.4 1.0 %here.1 = (f32[256,256]{1,0:T(8,128)S(1)}, f32[256,256]{1,0:T(8,128)}) custom-call(bf16[1280,256]{1,0:T(8,128)(2,1)S(1)} %get-tuple-element.43.adj_ref, bf16[256,256]{1,0:T(8,128)(2,1)S(1)} %get-tuple-element.44.far_ref, bf16[256,256]{1,0:T(8,128)(2,1)S(1)} %get-tuple-element.64.sent_ref.value_ref, bf16[32,8,256]{2,1,0:T(8,128)(2,1)S(1)} %all_to_all.11.recv_ref, ...), custom_call_target="tpu_custom_call" | custom-call | flops 234881024 | bytes 229376 | tf_op jit(solution)/shard_map/here/pallas_call | solution.py:401
  36.5 0.1 collective-permute-done.5.there_ref
  36.6 0.7 %last.1 = bf16[256,256]{1,0:T(8,128)(2,1)} custom-call(f32[256,256]{1,0:T(8,128)S(1)} %get-tuple-element.70.here_ref, bf16[256,256]{1,0:T(8,128)(2,1)S(1)} %collective-permute-done.5.there_ref), custom_call_target="tpu_custom_call" | custom-call | tf_op jit(solution)/shard_map/last/pallas_call | solution.py:401
  (8 shorter events, 0.0 us)
Async XLA Ops:
  0.6 3.0 %copy-start = (bf16[256,256]{1,0:T(8,128)(2,1)S(1)}, bf16[256,256]{1,0:T(8,128)(2,1)}, u32[]{:S(2)}) copy-start(bf16[256,256]{1,0:T(8,128)(2,1)} %up_ref.1) | copy-start | bytes 393220
  0.6 3.0 %copy-start.3 = (bf16[256,256]{1,0:T(8,128)(2,1)S(1)}, bf16[256,256]{1,0:T(8,128)(2,1)}, u32[]{:S(2)}) copy-start(bf16[256,256]{1,0:T(8,128)(2,1)} %value_ref.3) | copy-start | bytes 393220
  0.7 3.0 %copy-start.1 = (bf16[256,256]{1,0:T(8,128)(2,1)S(1)}, bf16[256,256]{1,0:T(8,128)(2,1)}, u32[]{:S(2)}) copy-start(bf16[256,256]{1,0:T(8,128)(2,1)} %neigh_ref.5) | copy-start | bytes 393220
  3.1 1.8 %collective-permute-start.1 = (bf16[640,256]{1,0:T(8,128)(2,1)S(1)}, bf16[640,256]{1,0:T(8,128)(2,1)S(1)}, u32[]{:S(2)}, u32[]{:S(2)}) collective-permute-start(bf16[640,256]{1,0:T(8,128)(2,1)S(1)} %get-tuple-element.53), channel_id=1, source_target_pairs={{0,1},{1,0},{2,3},{3,2},{4,5},{5,4},{6,7},{7,6},{8,9},{9,8},{10,11... | collective-permute-start | bytes 983048 | tf_op jit(solution)/shard_map/ppermute | solution.py:417
  4.2 17.1 %collective-permute-start = (bf16[1792,256]{1,0:T(8,128)(2,1)S(1)}, bf16[1792,256]{1,0:T(8,128)(2,1)S(1)}, u32[]{:S(2)}, u32[]{:S(2)}) collective-permute-start(bf16[1792,256]{1,0:T(8,128)(2,1)S(1)} %get-tuple-element.45), channel_id=1, source_target_pairs={{0,1},{1,0},{2,3},{3,2},{4,5},{5,4},{6,7},{7,6},{8,9},{9,8},{10,11... | collective-permute-start | bytes 2752520 | tf_op jit(solution)/shard_map/ppermute | solution.py:417
  4.9 16.5 %copy-start.2 = (bf16[256,256]{1,0:T(8,128)(2,1)S(1)}, bf16[256,256]{1,0:T(8,128)(2,1)}, u32[]{:S(2)}) copy-start(bf16[256,256]{1,0:T(8,128)(2,1)} %neigh_two_ref.1) | copy-start | bytes 393220
  4.9 16.5 %copy-start.4 = (bf16[256,256]{1,0:T(8,128)(2,1)S(1)}, bf16[256,256]{1,0:T(8,128)(2,1)}, u32[]{:S(2)}) copy-start(bf16[256,256]{1,0:T(8,128)(2,1)} %weight_ref.3) | copy-start | bytes 393220
  4.9 16.5 %copy-start.5 = (bf16[256,256]{1,0:T(8,128)(2,1)S(1)}, bf16[256,256]{1,0:T(8,128)(2,1)}, u32[]{:S(2)}) copy-start(bf16[256,256]{1,0:T(8,128)(2,1)} %self_ref.3) | copy-start | bytes 393220
  4.9 16.5 %copy-start.6 = (f32[256]{0:T(256)S(1)}, f32[256]{0:T(256)}, u32[]{:S(2)}) copy-start(f32[256]{0:T(256)} %bias_ref.2) | copy-start | bytes 3076
  5.0 15.9 %collective-permute-start.2 = (bf16[512,256]{1,0:T(8,128)(2,1)S(1)}, bf16[512,256]{1,0:T(8,128)(2,1)S(1)}, u32[]{:S(2)}, u32[]{:S(2)}) collective-permute-start(bf16[512,256]{1,0:T(8,128)(2,1)S(1)} %get-tuple-element.58), channel_id=1, source_target_pairs={{0,2},{2,0},{1,3},{3,1},{4,6},{6,4},{5,7},{7,5},{8,10},{10,8},{9,1... | collective-permute-start | bytes 786440 | tf_op jit(solution)/shard_map/ppermute | solution.py:417
  21.1 1.7 %collective-permute-start.3 = (bf16[640,256]{1,0:T(8,128)(2,1)S(1)}, bf16[640,256]{1,0:T(8,128)(2,1)S(1)}, u32[]{:S(2)}, u32[]{:S(2)}) collective-permute-start(bf16[640,256]{1,0:T(8,128)(2,1)S(1)} %get-tuple-element.60.here_ref), channel_id=1, source_target_pairs={{0,1},{1,0},{2,3},{3,2},{4,5},{5,4},{6,7},{7,6},{8,9},{9,8},{10,11... | collective-permute-start | bytes 983048 | tf_op jit(solution)/shard_map/ppermute | solution.py:417
  22.7 12.7 %copy-start.7 = (f32[256]{0:T(256)S(1)}, f32[256]{0:T(256)}, u32[]{:S(2)}) copy-start(f32[256]{0:T(256)} %bias_ref.3) | copy-start | bytes 3076
  23.5 11.3 %collective-permute-start.4 = (bf16[512,256]{1,0:T(8,128)(2,1)S(1)}, bf16[512,256]{1,0:T(8,128)(2,1)S(1)}, u32[]{:S(2)}, u32[]{:S(2)}) collective-permute-start(bf16[512,256]{1,0:T(8,128)(2,1)S(1)} %get-tuple-element.69), channel_id=1, source_target_pairs={{0,2},{2,0},{1,3},{3,1},{4,6},{6,4},{5,7},{7,5},{8,10},{10,8},{9,1... | collective-permute-start | bytes 786440 | tf_op jit(solution)/shard_map/ppermute | solution.py:417
  35.1 1.4 %collective-permute-start.5 = (bf16[256,256]{1,0:T(8,128)(2,1)S(1)}, bf16[256,256]{1,0:T(8,128)(2,1)S(1)}, u32[]{:S(2)}, u32[]{:S(2)}) collective-permute-start(bf16[256,256]{1,0:T(8,128)(2,1)S(1)} %there.1), channel_id=1, source_target_pairs={{0,1},{1,0},{2,3},{3,2},{4,5},{5,4},{6,7},{7,6},{8,9},{9,8},{10,11... | collective-permute-start | bytes 393224 | tf_op jit(solution)/shard_map/ppermute | solution.py:417

commit v21 on v20

--- a/solution.py
+++ b/solution.py
@@ -72,9 +72,7 @@
     send_hbm,
     tile_hbm,
     cot_hbm,
-    neigh_two_hbm,
     give_ref,
-    up_ref,
     pick_ref,
     *rest,
 ):
@@ -86,7 +84,6 @@
         send_ref,
         tile_buf,
         cot_ref,
-        neigh_two_ref,
         square,
         far_t,
         col,
@@ -103,7 +100,6 @@
     pairs += chunks[:first]
     pairs += [
         (cot_hbm, cot_ref),
-        (neigh_two_hbm, neigh_two_ref),
         (send_hbm, send_ref),
     ]
     pairs += chunks[first:]
@@ -131,13 +127,11 @@
     for c in range(first):
         copies[3 + c].wait()
         lax.fori_loop(c * each, (c + 1) * each, add, 0, unroll=True)
-    for copy in copies[3 + first : 6 + first]:
+    for copy in copies[3 + first : 5 + first]:
         copy.wait()
-    u = dot_nt(cot_ref[...], neigh_two_ref[...]).astype(BF16)
-    up_ref[...] = u
     pick_ref[...] = pick_matrix(send_ref, rows)
     for c in range(first, CHUNKS):
-        copies[6 + c].wait()
+        copies[5 + c].wait()
         lax.fori_loop(c * each, (c + 1) * each, add, 0, unroll=True)
     chip, side = lax.axis_index("chip"), 1 - lax.axis_index("core")
     base = chips * CORES
@@ -151,7 +145,7 @@
         col[at : at + rows, :] = square[...].T
         low = pl.multiple_of(d * far, far)
         col[at + rows : at + rows + far, :] = far_t[pl.ds(low, far), :]
-    give_ref[...] = dot(col[...], u).astype(BF16)
+    give_ref[...] = dot(col[...], cot_ref[...]).astype(BF16)
 
 
 def put_square(accs, bpd, d, out_ref, base):
@@ -165,20 +159,20 @@
                 out_ref[low : low + part, j * blk : (j + 1) * blk] = value
 
 
-def rest_kernel(chips, up_ref, cot_ref, value_ref, pick_ref, neigh_ref, *refs):
+def rest_kernel(chips, cot_ref, value_ref, pick_ref, neigh_ref, *refs):
     accs = refs[:PARTS]
     sent_ref, picked_ref, adj_ref, col_ref, keep_ref, lend_ref, place_ref, far_ref, far_t = refs[PARTS:]
     sent = dot(value_ref[...], neigh_ref[...]).astype(BF16)
     sent_ref[...] = sent
     picked_ref[...] = dot(pick_ref[...], sent).astype(BF16)
-    rows = up_ref.shape[0]
+    rows = cot_ref.shape[0]
     bpd = rows // accs[0].shape[2]
     for d in range(adj_ref.shape[0] // rows):
         put_square(accs, bpd, d, adj_ref, d * rows)
     far = col_ref.shape[0] // chips - rows
     column(chips, far, rows, lax.axis_index("core"), adj_ref, far_t, col_ref)
     far_columns(chips, far_t, far_ref)
-    keep_ref[...] = dot(col_ref[...], up_ref[...]).astype(BF16)
+    keep_ref[...] = dot(col_ref[...], cot_ref[...]).astype(BF16)
     low = adj_ref.shape[0]
     lend_ref[:low, :] = adj_ref[...]
     lend_ref[low : low + rows, :] = cot_ref[...]
@@ -263,7 +257,7 @@
 
 
 def early_one_kernel(
-    chips, adj_ref, lent_ref, value_ref, self_ref, bias_ref, up_ref, weight_ref, neigh_ref, sent_ref, unused_ref,
+    chips, adj_ref, lent_ref, value_ref, self_ref, bias_ref, up_ref, weight_ref, neigh_ref, sent_ref,
     agg_ref, direct_ref, grad_ref, col_ref, far_ref, far_t,
 ):
     value = value_ref[...]
@@ -282,7 +276,7 @@
 
 
 def mid_kernel(
-    chips, adj_ref, lent_ref, far_ref, far_two_ref, agg_ref, part_ref, sum_ref, here_ref, *refs
+    chips, adj_ref, lent_ref, far_ref, far_two_ref, agg_ref, part_ref, sum_ref, neigh_ref, here_ref, *refs
 ):
     came, (agg_out, grad_ref) = refs[:-2], refs[-2:]
     rows = sum_ref.shape[0]
@@ -291,7 +285,8 @@
         pairs = other_chips(chips, ref, came) + [(columns[:, : halo.shape[0]], halo)]
         part = slice(i * rows, (i + 1) * rows)
         agg_out[part, :] = agg_ref[part, :] + joint(pairs)
-    grad_ref[:rows, :] = part_ref[:rows, :] + sum_ref[...]
+    total = sum_ref[...].astype(BF16)
+    grad_ref[:rows, :] = part_ref[:rows, :] + dot_nt(total, neigh_ref[...])
     grad_ref[rows:, :] = part_ref[rows:, :]
 
 
@@ -384,7 +379,7 @@
     sent = dot(hidden, neigh_two_ref[...]).astype(BF16)
     sent_ref[...] = sent
     low = (chips - 1) * rows + chips * far
-    add = shared_ref[low:, :].astype(F32)
+    add = dot_nt(shared_ref[low:, :], neigh_two_ref[...])
     grad = jnp.concatenate([grad_ref[:rows, :], grad_ref[rows:, :] + add], 0)
     grad_pre = (grad * sigmoid * (1.0 + pre * (1.0 - sigmoid))).astype(BF16)
     grad_pre_ref[...] = grad_pre[:rows]
@@ -462,11 +457,11 @@
 
     far_t = pltpu.VMEM((chips * CORES * far, rows), BF16)
     sums = jax.ShapeDtypeStruct(((rows // blk) * (all_rows // blk), blk // PARTS, blk), F32)
-    give, up, pick, *sums = call(
+    give, pick, *sums = call(
         functools.partial(prep_kernel, chips),
         "prep",
-        (shape(count, width), rows_shape, shape(far, rows)) + (sums,) * PARTS,
-        [HBM] * 7,
+        (shape(count, width), shape(far, rows)) + (sums,) * PARTS,
+        [HBM] * 6,
         [
             pltpu.with_memory_space_constraint(value, pltpu.HBM)
             for value in (
@@ -476,7 +471,6 @@
                 send_list,
                 tile_val,
                 cotangent,
-                neigh_two,
             )
         ],
         [
@@ -486,11 +480,10 @@
             pltpu.SMEM(send_list.shape, jnp.int32),
             pltpu.VMEM(tile_val.shape, BF16),
             pltpu.VMEM(cotangent.shape, BF16),
-            pltpu.VMEM(neigh_two.shape, BF16),
             pltpu.VMEM((rows, rows), BF16),
             far_t,
             pltpu.VMEM((count, rows), BF16),
-            pltpu.SemaphoreType.DMA((6 + CHUNKS,)),
+            pltpu.SemaphoreType.DMA((5 + CHUNKS,)),
         ],
     )
     came = shift(give, "core", 1)
@@ -507,8 +500,8 @@
             shape(rows, chips * far),
             far_shape,
         ),
-        [VMEM] * (5 + PARTS),
-        (up, cotangent, features, pick, neigh_one, *sums),
+        [VMEM] * (4 + PARTS),
+        (cotangent, features, pick, neigh_one, *sums),
         [far_t],
         flops=3 * square,
     )
@@ -534,7 +527,7 @@
         functools.partial(early_one_kernel, chips),
         "early_one",
         (both_shape,) * 3 + (shape(count, rows), far_shape),
-        [VMEM] * 10,
+        [VMEM] * 9,
         (
             adj,
             lent,
@@ -545,7 +538,6 @@
             self_two,
             neigh_one,
             sent,
-            neigh_two,
         ),
         [far_t],
         flops=8 * square,
@@ -554,8 +546,8 @@
         functools.partial(mid_kernel, chips),
         "mid",
         (both_shape,) * 2,
-        [VMEM] * (7 + chips),
-        (adj, lent, columns, columns_two, agg, grad, summed, here, *terms),
+        [VMEM] * (8 + chips),
+        (adj, lent, columns, columns_two, agg, grad, summed, neigh_two, here, *terms),
         flops=3 * square,
     )
     hidden, sent, grad_pre, mine, msg, *to = call(

time: 37.4 us -> 37.2 us (level)
  transfers between devices with their start and end apart: 6 -> 6, of which waited for: 3 -> 3; matrix products, arithmetic and copies ran while one was open for 0% -> 0% of each run, Pallas kernels for 7% -> 8%
where the time goes in v21:
time: 37.2 us; the launch traced here: 37 us
  blocking collectives  23.8 us (64%)
  Pallas kernels  6.68 us (18%)
  starting transfers between devices  4.63 us (12%)
  waiting for transfers between devices  1.09 us (3%)
  between operations  0.75 us (2%)
    all_to_all x2, blocking collectives, across(): lax.all_to_all(msg, ('hst', 'chip', 'core'), split_axis=0, concat_axis=0,...  23.8 us
    pallas_call x10, Pallas kernels, call(): pl.pallas_call(kernel, out_shape=out_shape, in_specs=in_specs, out_specs=...  6.68 us
    ppermute x6, starting transfers between devices, shift(): return lax.ppermute(value, axis, [(i, (i + k) % size) for i in range(size)])  4.63 us
    ppermute x6, waiting for transfers between devices, shift(): return lax.ppermute(value, axis, [(i, (i + k) % size) for i in range(size)])  1.09 us
  transfers between devices with their start and end apart: 6, of which 3 were waited for; matrix products, arithmetic and copies ran while one was open for 0% of the time, Pallas kernels for 8%

profile of v21, /device:TPU:0, one launch (start us, length us, event | category | flops | bytes accessed | tf_op | source)
XLA Modules:
  0.0 37.0 jit_solution(8195051381464121798)
XLA Ops:
  0.6 0.0 copy-start
  0.6 0.0 copy-start.4
  0.7 0.0 copy-start.1
  0.7 2.2 %prep.1 = (bf16[640,256]{1,0:T(8,128)(2,1)S(1)}, bf16[64,256]{1,0:T(8,128)(2,1)S(1)}, f32[20,32,128]{2,1,0:T(8,128)S(1)}, f32[20,32,128]{2,1,0:T(8,128)S(1)}, f3...) custom-call(s32[64]{0:T(128)} %dst_hbm.1, s32[64]{0:T(128)} %src_hbm.1, s32[64]{0:T(128)} %rows_hbm.1, ...), custom_call_target="tpu_custom_call" | custom-call | tf_op jit(solution)/shard_map/prep/pallas_call | solution.py:396
  2.8 0.5 %collective-permute-start.1 = (bf16[640,256]{1,0:T(8,128)(2,1)S(1)}, bf16[640,256]{1,0:T(8,128)(2,1)S(1)}, u32[]{:S(2)}, u32[]{:S(2)}) collective-permute-start(bf16[640,256]{1,0:T(8,128)(2,1)S(1)} %get-tuple-element.51), channel_id=1, source_target_pairs={{0,1},{1,0},{2,3},{3,2},{4,5},{5,4},{6,7},{7,6},{8,9},{9,8},{10,11... | collective-permute-start | bytes 983048 | tf_op jit(solution)/shard_map/ppermute | solution.py:412
  3.4 0.0 copy-done
  3.4 0.0 copy-done.4
  3.4 0.6 %rest.1 = (bf16[256,256]{1,0:T(8,128)(2,1)S(1)}, bf16[64,256]{1,0:T(8,128)(2,1)S(1)}, bf16[1280,256]{1,0:T(8,128)(2,1)S(1)}, bf16[640,256]{1,0:T(8,128)(2,1)S(1)...) custom-call(bf16[256,256]{1,0:T(8,128)(2,1)S(1)} %copy-done, ...), custom_call_target="tpu_custom_call" | custom-call | flops 100663296 | bytes 98304 | tf_op jit(solution)/shard_map/rest/pallas_call | solution.py:396
  4.0 0.1 collective-permute-start
  4.1 0.5 %collective-permute-done.1.came_ref = bf16[640,256]{1,0:T(8,128)(2,1)S(1)} collective-permute-done((bf16[640,256]{1,0:T(8,128)(2,1)S(1)}, bf16[640,256]{1,0:T(8,128)(2,1)S(1)}, u32[]{:S(2)}, u32[]{:S(2)}) %collective-permute-start.1) | collective-permute-done | bytes 327712 | tf_op jit(solution)/shard_map/ppermute | solution.py:412
  4.6 0.1 core_sum.1
  4.7 0.0 copy-start.5
  4.7 2.9 %collective-permute-start.2 = (bf16[512,256]{1,0:T(8,128)(2,1)S(1)}, bf16[512,256]{1,0:T(8,128)(2,1)S(1)}, u32[]{:S(2)}, u32[]{:S(2)}) collective-permute-start(bf16[512,256]{1,0:T(8,128)(2,1)S(1)} %get-tuple-element.56), channel_id=1, source_target_pairs={{0,2},{2,0},{1,3},{3,1},{4,6},{6,4},{5,7},{7,5},{8,10},{10,8},{9,1... | collective-permute-start | bytes 786440 | tf_op jit(solution)/shard_map/ppermute | solution.py:412
  7.6 12.9 %all_to_all.10.recv_ref = bf16[32,8,256]{2,1,0:T(8,128)(2,1)S(1)} all-to-all(bf16[32,8,256]{2,1,0:T(8,128)(2,1)S(1)} %get-tuple-element.53), channel_id=1, replica_groups=mesh['hst'=8,'chip'=2,'core'=2] {'hst','chip','core'}, dimensions={0} | all-to-all | bytes 262144 | tf_op jit(solution)/shard_map/all_to_all | solution.py:455
  20.6 0.0 collective-permute-done.2.refs_0_
  20.6 0.2 merge.1
  20.8 0.3 collective-permute-start.3
  21.1 0.0 collective-permute-done.lent_ref
  21.1 0.0 copy-done.3
  21.1 0.6 %early_one.1 = (f32[512,256]{1,0:T(8,128)S(1)}, f32[512,256]{1,0:T(8,128)S(1)}, f32[512,256]{1,0:T(8,128)S(1)}, bf16[640,256]{1,0:T(8,128)(2,1)S(1)}, bf16[256,256]{1,0:T(8,128)(2,1)S(1)}) custom-call(bf16[1280,256]{1,0:T(8,128)(2,1)S(1)} %get-tuple-element.41.adj_ref, bf16[1792,256]{1,0:T(8,128)(2,1)S(1)} %collective-permute-done.lent_ref, ...), custom_call_target="tpu_custom_call" | custom-call | flops 268435456 | bytes 262144 | tf_op jit(solution)/shard_map/early_one/pallas_call | solution.py:396
  21.7 0.0 copy-done.5
  21.7 0.3 mid.1
  22.0 0.5 %collective-permute-done.3.shared_ref = bf16[640,256]{1,0:T(8,128)(2,1)S(1)} collective-permute-done((bf16[640,256]{1,0:T(8,128)(2,1)S(1)}, bf16[640,256]{1,0:T(8,128)(2,1)S(1)}, u32[]{:S(2)}, u32[]{:S(2)}) %collective-permute-start.3) | collective-permute-done | bytes 327712 | tf_op jit(solution)/shard_map/ppermute | solution.py:412
  22.5 0.8 %middle.1 = (bf16[256,256]{1,0:T(8,128)(2,1)S(1)}, bf16[256,256]{1,0:T(8,128)(2,1)S(1)}, bf16[256,256]{1,0:T(8,128)(2,1)S(1)}, f32[256,256]{1,0:T(8,128)S(1)}, b...) custom-call(bf16[1280,256]{1,0:T(8,128)(2,1)S(1)} %get-tuple-element.41.adj_ref, ...), custom_call_target="tpu_custom_call" | custom-call | flops 402653184 | bytes 393216 | tf_op jit(solution)/shard_map/middle/pallas_call | solution.py:396
  23.3 0.5 %collective-permute-start.4 = (bf16[512,256]{1,0:T(8,128)(2,1)S(1)}, bf16[512,256]{1,0:T(8,128)(2,1)S(1)}, u32[]{:S(2)}, u32[]{:S(2)}) collective-permute-start(bf16[512,256]{1,0:T(8,128)(2,1)S(1)} %get-tuple-element.67), channel_id=1, source_target_pairs={{0,2},{2,0},{1,3},{3,1},{4,6},{6,4},{5,7},{7,5},{8,10},{10,8},{9,1... | collective-permute-start | bytes 786440 | tf_op jit(solution)/shard_map/ppermute | solution.py:412
  23.8 10.8 %all_to_all.11.recv_ref = bf16[32,8,256]{2,1,0:T(8,128)(2,1)S(1)} all-to-all(bf16[32,8,256]{2,1,0:T(8,128)(2,1)S(1)} %get-tuple-element.63), channel_id=1, replica_groups=mesh['hst'=8,'chip'=2,'core'=2] {'hst','chip','core'}, dimensions={0} | all-to-all | bytes 262144 | tf_op jit(solution)/shard_map/all_to_all | solution.py:455
  34.6 0.0 collective-permute-done.4.refs_0_
  34.6 0.3 there.1
  34.9 0.3 collective-permute-start.5
  35.2 1.0 %here.1 = (f32[256,256]{1,0:T(8,128)S(1)}, f32[256,256]{1,0:T(8,128)}) custom-call(bf16[1280,256]{1,0:T(8,128)(2,1)S(1)} %get-tuple-element.41.adj_ref, bf16[256,256]{1,0:T(8,128)(2,1)S(1)} %get-tuple-element.42.far_ref, bf16[256,256]{1,0:T(8,128)(2,1)S(1)} %get-tuple-element.62.sent_ref.value_ref, bf16[32,8,256]{2,1,0:T(8,128)(2,1)S(1)} %all_to_all.11.recv_ref, ...), custom_call_target="tpu_custom_call" | custom-call | flops 234881024 | bytes 229376 | tf_op jit(solution)/shard_map/here/pallas_call | solution.py:396
  36.2 0.1 collective-permute-done.5.there_ref
  36.3 0.7 %last.1 = bf16[256,256]{1,0:T(8,128)(2,1)} custom-call(f32[256,256]{1,0:T(8,128)S(1)} %get-tuple-element.68.here_ref, bf16[256,256]{1,0:T(8,128)(2,1)S(1)} %collective-permute-done.5.there_ref), custom_call_target="tpu_custom_call" | custom-call | tf_op jit(solution)/shard_map/last/pallas_call | solution.py:396
  (8 shorter events, 0.0 us)
Async XLA Ops:
  0.6 2.7 %copy-start = (bf16[256,256]{1,0:T(8,128)(2,1)S(1)}, bf16[256,256]{1,0:T(8,128)(2,1)}, u32[]{:S(2)}) copy-start(bf16[256,256]{1,0:T(8,128)(2,1)} %up_ref.1) | copy-start | bytes 393220
  0.6 2.7 %copy-start.4 = (bf16[256,256]{1,0:T(8,128)(2,1)S(1)}, bf16[256,256]{1,0:T(8,128)(2,1)}, u32[]{:S(2)}) copy-start(bf16[256,256]{1,0:T(8,128)(2,1)} %value_ref.3) | copy-start | bytes 393220
  0.7 2.7 %copy-start.1 = (bf16[256,256]{1,0:T(8,128)(2,1)S(1)}, bf16[256,256]{1,0:T(8,128)(2,1)}, u32[]{:S(2)}) copy-start(bf16[256,256]{1,0:T(8,128)(2,1)} %neigh_ref.7) | copy-start | bytes 393220
  2.8 1.8 %collective-permute-start.1 = (bf16[640,256]{1,0:T(8,128)(2,1)S(1)}, bf16[640,256]{1,0:T(8,128)(2,1)S(1)}, u32[]{:S(2)}, u32[]{:S(2)}) collective-permute-start(bf16[640,256]{1,0:T(8,128)(2,1)S(1)} %get-tuple-element.51), channel_id=1, source_target_pairs={{0,1},{1,0},{2,3},{3,2},{4,5},{5,4},{6,7},{7,6},{8,9},{9,8},{10,11... | collective-permute-start | bytes 983048 | tf_op jit(solution)/shard_map/ppermute | solution.py:412
  4.0 17.1 %collective-permute-start = (bf16[1792,256]{1,0:T(8,128)(2,1)S(1)}, bf16[1792,256]{1,0:T(8,128)(2,1)S(1)}, u32[]{:S(2)}, u32[]{:S(2)}) collective-permute-start(bf16[1792,256]{1,0:T(8,128)(2,1)S(1)} %get-tuple-element.43), channel_id=1, source_target_pairs={{0,1},{1,0},{2,3},{3,2},{4,5},{5,4},{6,7},{7,6},{8,9},{9,8},{10,11... | collective-permute-start | bytes 2752520 | tf_op jit(solution)/shard_map/ppermute | solution.py:412
  4.6 16.5 %copy-start.2 = (bf16[256,256]{1,0:T(8,128)(2,1)S(1)}, bf16[256,256]{1,0:T(8,128)(2,1)}, u32[]{:S(2)}) copy-start(bf16[256,256]{1,0:T(8,128)(2,1)} %weight_ref.3) | copy-start | bytes 393220
  4.6 16.5 %copy-start.3 = (bf16[256,256]{1,0:T(8,128)(2,1)S(1)}, bf16[256,256]{1,0:T(8,128)(2,1)}, u32[]{:S(2)}) copy-start(bf16[256,256]{1,0:T(8,128)(2,1)} %self_ref.3) | copy-start | bytes 393220
  4.6 16.5 %copy-start.6 = (f32[256]{0:T(256)S(1)}, f32[256]{0:T(256)}, u32[]{:S(2)}) copy-start(f32[256]{0:T(256)} %bias_ref.2) | copy-start | bytes 3076
  4.7 17.0 %copy-start.5 = (bf16[256,256]{1,0:T(8,128)(2,1)S(1)}, bf16[256,256]{1,0:T(8,128)(2,1)}, u32[]{:S(2)}) copy-start(bf16[256,256]{1,0:T(8,128)(2,1)} %neigh_two_ref.1) | copy-start | bytes 393220
  4.7 15.9 %collective-permute-start.2 = (bf16[512,256]{1,0:T(8,128)(2,1)S(1)}, bf16[512,256]{1,0:T(8,128)(2,1)S(1)}, u32[]{:S(2)}, u32[]{:S(2)}) collective-permute-start(bf16[512,256]{1,0:T(8,128)(2,1)S(1)} %get-tuple-element.56), channel_id=1, source_target_pairs={{0,2},{2,0},{1,3},{3,1},{4,6},{6,4},{5,7},{7,5},{8,10},{10,8},{9,1... | collective-permute-start | bytes 786440 | tf_op jit(solution)/shard_map/ppermute | solution.py:412
  20.8 1.7 %collective-permute-start.3 = (bf16[640,256]{1,0:T(8,128)(2,1)S(1)}, bf16[640,256]{1,0:T(8,128)(2,1)S(1)}, u32[]{:S(2)}, u32[]{:S(2)}) collective-permute-start(bf16[640,256]{1,0:T(8,128)(2,1)S(1)} %get-tuple-element.58.here_ref), channel_id=1, source_target_pairs={{0,1},{1,0},{2,3},{3,2},{4,5},{5,4},{6,7},{7,6},{8,9},{9,8},{10,11... | collective-permute-start | bytes 983048 | tf_op jit(solution)/shard_map/ppermute | solution.py:412
  22.5 12.7 %copy-start.7 = (f32[256]{0:T(256)S(1)}, f32[256]{0:T(256)}, u32[]{:S(2)}) copy-start(f32[256]{0:T(256)} %bias_ref.3) | copy-start | bytes 3076
  23.3 11.3 %collective-permute-start.4 = (bf16[512,256]{1,0:T(8,128)(2,1)S(1)}, bf16[512,256]{1,0:T(8,128)(2,1)S(1)}, u32[]{:S(2)}, u32[]{:S(2)}) collective-permute-start(bf16[512,256]{1,0:T(8,128)(2,1)S(1)} %get-tuple-element.67), channel_id=1, source_target_pairs={{0,2},{2,0},{1,3},{3,1},{4,6},{6,4},{5,7},{7,5},{8,10},{10,8},{9,1... | collective-permute-start | bytes 786440 | tf_op jit(solution)/shard_map/ppermute | solution.py:412
  34.9 1.4 %collective-permute-start.5 = (bf16[256,256]{1,0:T(8,128)(2,1)S(1)}, bf16[256,256]{1,0:T(8,128)(2,1)S(1)}, u32[]{:S(2)}, u32[]{:S(2)}) collective-permute-start(bf16[256,256]{1,0:T(8,128)(2,1)S(1)} %there.1), channel_id=1, source_target_pairs={{0,1},{1,0},{2,3},{3,2},{4,5},{5,4},{6,7},{7,6},{8,9},{9,8},{10,11... | collective-permute-start | bytes 393224 | tf_op jit(solution)/shard_map/ppermute | solution.py:412

commit v22 on v21

--- a/solution.py
+++ b/solution.py
@@ -24,6 +24,12 @@
 
 def dot_nt(a, b):
     return lax.dot_general(a, b, (((1,), (1,)), ((), ())), preferred_element_type=F32)
+
+
+def precise_nt(a, b):
+    high = a.astype(BF16)
+    low = (a - high.astype(F32)).astype(BF16)
+    return dot_nt(high, b) + dot_nt(low, b)
 
 
 def pick_matrix(send_ref, rows):
@@ -91,18 +97,12 @@
     ) = rest
     tiles, blk = tile_buf.shape[0], tile_buf.shape[1]
     each = tiles // CHUNKS
-    first = CHUNKS * 3 // 4
     chunks = [
         (tile_hbm.at[pl.ds(c * each, each)], tile_buf.at[pl.ds(c * each, each)])
         for c in range(CHUNKS)
     ]
-    pairs = [(dst_hbm, dst_ref), (src_hbm, src_ref), (rows_hbm, rows_ref)]
-    pairs += chunks[:first]
-    pairs += [
-        (cot_hbm, cot_ref),
-        (send_hbm, send_ref),
-    ]
-    pairs += chunks[first:]
+    pairs = [(send_hbm, send_ref), (dst_hbm, dst_ref), (src_hbm, src_ref), (rows_hbm, rows_ref)]
+    pairs += chunks + [(cot_hbm, cot_ref)]
     copies = [pltpu.make_async_copy(a, b, sems.at[i]) for i, (a, b) in enumerate(pairs)]
     for copy in copies:
         copy.start()
@@ -122,17 +122,14 @@
             acc[slot] += jnp.where(place < rows_ref[t] - i * part, value, 0.0)
         return carry
 
-    for copy in copies[:3]:
+    copies[0].wait()
+    pick_ref[...] = pick_matrix(send_ref, rows)
+    for copy in copies[1:4]:
         copy.wait()
-    for c in range(first):
-        copies[3 + c].wait()
+    for c in range(CHUNKS):
+        copies[4 + c].wait()
         lax.fori_loop(c * each, (c + 1) * each, add, 0, unroll=True)
-    for copy in copies[3 + first : 5 + first]:
-        copy.wait()
-    pick_ref[...] = pick_matrix(send_ref, rows)
-    for c in range(first, CHUNKS):
-        copies[5 + c].wait()
-        lax.fori_loop(c * each, (c + 1) * each, add, 0, unroll=True)
+    copies[4 + CHUNKS].wait()
     chip, side = lax.axis_index("chip"), 1 - lax.axis_index("core")
     base = chips * CORES
     for j in range(far_t.shape[0] // rows):
@@ -285,8 +282,7 @@
         pairs = other_chips(chips, ref, came) + [(columns[:, : halo.shape[0]], halo)]
         part = slice(i * rows, (i + 1) * rows)
         agg_out[part, :] = agg_ref[part, :] + joint(pairs)
-    total = sum_ref[...].astype(BF16)
-    grad_ref[:rows, :] = part_ref[:rows, :] + dot_nt(total, neigh_ref[...])
+    grad_ref[:rows, :] = part_ref[:rows, :] + precise_nt(sum_ref[...], neigh_ref[...])
     grad_ref[rows:, :] = part_ref[rows:, :]
 
 
@@ -325,7 +321,7 @@
     total = mine_ref[...] + returned(place_ref, recv_ref, hosts, chips)
     for block in came:
         total = total + block[:rows, :].astype(F32)
-    grad = dot_nt(total.astype(BF16), neigh_ref[...])
+    grad = precise_nt(total, neigh_ref[...])
     grad_ref[...] = grad + dot_nt(up_ref[...], weight_ref[...])
     out = column_product(chips, hosts, adj_ref, far_ref, sent_ref, came, recv_ref)
     out_ref[...] = out + dot(value_ref[...], self_ref[...]) + bias_ref[...].reshape(1, -1)

time: 37.2 us -> 37.2 us (level)
  transfers between devices with their start and end apart: 6 -> 6, of which waited for: 3 -> 2; matrix products, arithmetic and copies ran while one was open for 0% -> 0% of each run, Pallas kernels for 8% -> 8%
where the time goes in v22:
time: 37.2 us; the launch traced here: 37 us
  blocking collectives  23.8 us (64%)
  Pallas kernels  6.81 us (18%)
  starting transfers between devices  4.64 us (12%)
  waiting for transfers between devices  0.98 us (3%)
  between operations  0.75 us (2%)
    all_to_all x2, blocking collectives, across(): lax.all_to_all(msg, ('hst', 'chip', 'core'), split_axis=0, concat_axis=0,...  23.8 us
    pallas_call x10, Pallas kernels, call(): pl.pallas_call(kernel, out_shape=out_shape, in_specs=in_specs, out_specs=...  6.81 us
    ppermute x6, starting transfers between devices, shift(): return lax.ppermute(value, axis, [(i, (i + k) % size) for i in range(size)])  4.64 us
    ppermute x6, waiting for transfers between devices, shift(): return lax.ppermute(value, axis, [(i, (i + k) % size) for i in range(size)])  0.98 us
  transfers between devices with their start and end apart: 6, of which 2 were waited for; matrix products, arithmetic and copies ran while one was open for 0% of the time, Pallas kernels for 8%

profile of v22, /device:TPU:0, one launch (start us, length us, event | category | flops | bytes accessed | tf_op | source)
XLA Modules:
  0.0 37.0 jit_solution(14726787066983443175)
XLA Ops:
  0.6 0.0 copy-start
  0.6 0.0 copy-start.4
  0.7 0.0 copy-start.1
  0.7 2.1 %prep.1 = (bf16[640,256]{1,0:T(8,128)(2,1)S(1)}, bf16[64,256]{1,0:T(8,128)(2,1)S(1)}, f32[20,32,128]{2,1,0:T(8,128)S(1)}, f32[20,32,128]{2,1,0:T(8,128)S(1)}, f3...) custom-call(s32[64]{0:T(128)} %dst_hbm.1, s32[64]{0:T(128)} %src_hbm.1, s32[64]{0:T(128)} %rows_hbm.1, ...), custom_call_target="tpu_custom_call" | custom-call | tf_op jit(solution)/shard_map/prep/pallas_call | solution.py:392
  2.8 0.5 %collective-permute-start.1 = (bf16[640,256]{1,0:T(8,128)(2,1)S(1)}, bf16[640,256]{1,0:T(8,128)(2,1)S(1)}, u32[]{:S(2)}, u32[]{:S(2)}) collective-permute-start(bf16[640,256]{1,0:T(8,128)(2,1)S(1)} %get-tuple-element.51), channel_id=1, source_target_pairs={{0,1},{1,0},{2,3},{3,2},{4,5},{5,4},{6,7},{7,6},{8,9},{9,8},{10,11... | collective-permute-start | bytes 983048 | tf_op jit(solution)/shard_map/ppermute | solution.py:408
  3.3 0.0 copy-done
  3.3 0.0 copy-done.4
  3.3 0.0 copy-done.1
  3.3 0.6 %rest.1 = (bf16[256,256]{1,0:T(8,128)(2,1)S(1)}, bf16[64,256]{1,0:T(8,128)(2,1)S(1)}, bf16[1280,256]{1,0:T(8,128)(2,1)S(1)}, bf16[640,256]{1,0:T(8,128)(2,1)S(1)...) custom-call(bf16[256,256]{1,0:T(8,128)(2,1)S(1)} %copy-done, ...), custom_call_target="tpu_custom_call" | custom-call | flops 100663296 | bytes 98304 | tf_op jit(solution)/shard_map/rest/pallas_call | solution.py:392
  3.9 0.1 collective-permute-start
  4.0 0.5 %collective-permute-done.1.came_ref = bf16[640,256]{1,0:T(8,128)(2,1)S(1)} collective-permute-done((bf16[640,256]{1,0:T(8,128)(2,1)S(1)}, bf16[640,256]{1,0:T(8,128)(2,1)S(1)}, u32[]{:S(2)}, u32[]{:S(2)}) %collective-permute-start.1) | collective-permute-done | bytes 327712 | tf_op jit(solution)/shard_map/ppermute | solution.py:408
  4.6 0.1 core_sum.1
  4.7 0.0 copy-start.5
  4.7 2.9 %collective-permute-start.2 = (bf16[512,256]{1,0:T(8,128)(2,1)S(1)}, bf16[512,256]{1,0:T(8,128)(2,1)S(1)}, u32[]{:S(2)}, u32[]{:S(2)}) collective-permute-start(bf16[512,256]{1,0:T(8,128)(2,1)S(1)} %get-tuple-element.56), channel_id=1, source_target_pairs={{0,2},{2,0},{1,3},{3,1},{4,6},{6,4},{5,7},{7,5},{8,10},{10,8},{9,1... | collective-permute-start | bytes 786440 | tf_op jit(solution)/shard_map/ppermute | solution.py:408
  7.6 13.0 %all_to_all.10.recv_ref = bf16[32,8,256]{2,1,0:T(8,128)(2,1)S(1)} all-to-all(bf16[32,8,256]{2,1,0:T(8,128)(2,1)S(1)} %get-tuple-element.53), channel_id=1, replica_groups=mesh['hst'=8,'chip'=2,'core'=2] {'hst','chip','core'}, dimensions={0} | all-to-all | bytes 262144 | tf_op jit(solution)/shard_map/all_to_all | solution.py:451
  20.5 0.0 collective-permute-done.2.refs_0_
  20.5 0.2 merge.1
  20.7 0.3 collective-permute-start.3
  21.0 0.0 collective-permute-done.lent_ref
  21.0 0.0 copy-done.2
  21.0 0.6 %early_one.1 = (f32[512,256]{1,0:T(8,128)S(1)}, f32[512,256]{1,0:T(8,128)S(1)}, f32[512,256]{1,0:T(8,128)S(1)}, bf16[640,256]{1,0:T(8,128)(2,1)S(1)}, bf16[256,256]{1,0:T(8,128)(2,1)S(1)}) custom-call(bf16[1280,256]{1,0:T(8,128)(2,1)S(1)} %get-tuple-element.41.adj_ref, bf16[1792,256]{1,0:T(8,128)(2,1)S(1)} %collective-permute-done.lent_ref, ...), custom_call_target="tpu_custom_call" | custom-call | flops 268435456 | bytes 262144 | tf_op jit(solution)/shard_map/early_one/pallas_call | solution.py:392
  21.6 0.4 %mid.1 = (f32[512,256]{1,0:T(8,128)S(1)}, f32[512,256]{1,0:T(8,128)S(1)}) custom-call(bf16[1280,256]{1,0:T(8,128)(2,1)S(1)} %get-tuple-element.41.adj_ref, bf16[1792,256]{1,0:T(8,128)(2,1)S(1)} %collective-permute-done.lent_ref, bf16[256,256]{1,0:T(8,128)(2,1)S(1)} %get-tuple-element.42.far_ref, bf16[256,256]{1,0:T(8,128)(2,1)S(1)} %get-tuple-element.45.far_two_ref.far_ref, ...), custom_call_target="tpu_custom_call" | custom-call | flops 100663296 | bytes 98304 | tf_op jit(solution)/shard_map/mid/pallas_call | solution.py:392
  22.0 0.4 %collective-permute-done.3.shared_ref = bf16[640,256]{1,0:T(8,128)(2,1)S(1)} collective-permute-done((bf16[640,256]{1,0:T(8,128)(2,1)S(1)}, bf16[640,256]{1,0:T(8,128)(2,1)S(1)}, u32[]{:S(2)}, u32[]{:S(2)}) %collective-permute-start.3) | collective-permute-done | bytes 327712 | tf_op jit(solution)/shard_map/ppermute | solution.py:408
  22.4 0.8 %middle.1 = (bf16[256,256]{1,0:T(8,128)(2,1)S(1)}, bf16[256,256]{1,0:T(8,128)(2,1)S(1)}, bf16[256,256]{1,0:T(8,128)(2,1)S(1)}, f32[256,256]{1,0:T(8,128)S(1)}, b...) custom-call(bf16[1280,256]{1,0:T(8,128)(2,1)S(1)} %get-tuple-element.41.adj_ref, ...), custom_call_target="tpu_custom_call" | custom-call | flops 402653184 | bytes 393216 | tf_op jit(solution)/shard_map/middle/pallas_call | solution.py:392
  23.2 0.5 %collective-permute-start.4 = (bf16[512,256]{1,0:T(8,128)(2,1)S(1)}, bf16[512,256]{1,0:T(8,128)(2,1)S(1)}, u32[]{:S(2)}, u32[]{:S(2)}) collective-permute-start(bf16[512,256]{1,0:T(8,128)(2,1)S(1)} %get-tuple-element.67), channel_id=1, source_target_pairs={{0,2},{2,0},{1,3},{3,1},{4,6},{6,4},{5,7},{7,5},{8,10},{10,8},{9,1... | collective-permute-start | bytes 786440 | tf_op jit(solution)/shard_map/ppermute | solution.py:408
  23.7 10.8 %all_to_all.11.recv_ref = bf16[32,8,256]{2,1,0:T(8,128)(2,1)S(1)} all-to-all(bf16[32,8,256]{2,1,0:T(8,128)(2,1)S(1)} %get-tuple-element.63), channel_id=1, replica_groups=mesh['hst'=8,'chip'=2,'core'=2] {'hst','chip','core'}, dimensions={0} | all-to-all | bytes 262144 | tf_op jit(solution)/shard_map/all_to_all | solution.py:451
  34.6 0.0 collective-permute-done.4.refs_0_
  34.6 0.3 there.1
  34.8 0.3 collective-permute-start.5
  35.1 1.2 %here.1 = (f32[256,256]{1,0:T(8,128)S(1)}, f32[256,256]{1,0:T(8,128)}) custom-call(bf16[1280,256]{1,0:T(8,128)(2,1)S(1)} %get-tuple-element.41.adj_ref, bf16[256,256]{1,0:T(8,128)(2,1)S(1)} %get-tuple-element.42.far_ref, bf16[256,256]{1,0:T(8,128)(2,1)S(1)} %get-tuple-element.62.sent_ref.value_ref, bf16[32,8,256]{2,1,0:T(8,128)(2,1)S(1)} %all_to_all.11.recv_ref, ...), custom_call_target="tpu_custom_call" | custom-call | flops 234881024 | bytes 229376 | tf_op jit(solution)/shard_map/here/pallas_call | solution.py:392
  36.3 0.0 collective-permute-done.5.there_ref
  36.3 0.7 %last.1 = bf16[256,256]{1,0:T(8,128)(2,1)} custom-call(f32[256,256]{1,0:T(8,128)S(1)} %get-tuple-element.68.here_ref, bf16[256,256]{1,0:T(8,128)(2,1)S(1)} %collective-permute-done.5.there_ref), custom_call_target="tpu_custom_call" | custom-call | tf_op jit(solution)/shard_map/last/pallas_call | solution.py:392
  (8 shorter events, 0.0 us)
Async XLA Ops:
  0.6 2.7 %copy-start = (bf16[256,256]{1,0:T(8,128)(2,1)S(1)}, bf16[256,256]{1,0:T(8,128)(2,1)}, u32[]{:S(2)}) copy-start(bf16[256,256]{1,0:T(8,128)(2,1)} %up_ref.1) | copy-start | bytes 393220
  0.6 2.7 %copy-start.4 = (bf16[256,256]{1,0:T(8,128)(2,1)S(1)}, bf16[256,256]{1,0:T(8,128)(2,1)}, u32[]{:S(2)}) copy-start(bf16[256,256]{1,0:T(8,128)(2,1)} %value_ref.3) | copy-start | bytes 393220
  0.7 2.7 %copy-start.1 = (bf16[256,256]{1,0:T(8,128)(2,1)S(1)}, bf16[256,256]{1,0:T(8,128)(2,1)}, u32[]{:S(2)}) copy-start(bf16[256,256]{1,0:T(8,128)(2,1)} %neigh_ref.7) | copy-start | bytes 393220
  2.8 1.8 %collective-permute-start.1 = (bf16[640,256]{1,0:T(8,128)(2,1)S(1)}, bf16[640,256]{1,0:T(8,128)(2,1)S(1)}, u32[]{:S(2)}, u32[]{:S(2)}) collective-permute-start(bf16[640,256]{1,0:T(8,128)(2,1)S(1)} %get-tuple-element.51), channel_id=1, source_target_pairs={{0,1},{1,0},{2,3},{3,2},{4,5},{5,4},{6,7},{7,6},{8,9},{9,8},{10,11... | collective-permute-start | bytes 983048 | tf_op jit(solution)/shard_map/ppermute | solution.py:408
  3.9 17.1 %collective-permute-start = (bf16[1792,256]{1,0:T(8,128)(2,1)S(1)}, bf16[1792,256]{1,0:T(8,128)(2,1)S(1)}, u32[]{:S(2)}, u32[]{:S(2)}) collective-permute-start(bf16[1792,256]{1,0:T(8,128)(2,1)S(1)} %get-tuple-element.43), channel_id=1, source_target_pairs={{0,1},{1,0},{2,3},{3,2},{4,5},{5,4},{6,7},{7,6},{8,9},{9,8},{10,11... | collective-permute-start | bytes 2752520 | tf_op jit(solution)/shard_map/ppermute | solution.py:408
  4.6 16.5 %copy-start.2 = (bf16[256,256]{1,0:T(8,128)(2,1)S(1)}, bf16[256,256]{1,0:T(8,128)(2,1)}, u32[]{:S(2)}) copy-start(bf16[256,256]{1,0:T(8,128)(2,1)} %weight_ref.3) | copy-start | bytes 393220
  4.6 16.5 %copy-start.3 = (bf16[256,256]{1,0:T(8,128)(2,1)S(1)}, bf16[256,256]{1,0:T(8,128)(2,1)}, u32[]{:S(2)}) copy-start(bf16[256,256]{1,0:T(8,128)(2,1)} %self_ref.3) | copy-start | bytes 393220
  4.6 16.5 %copy-start.6 = (f32[256]{0:T(256)S(1)}, f32[256]{0:T(256)}, u32[]{:S(2)}) copy-start(f32[256]{0:T(256)} %bias_ref.2) | copy-start | bytes 3076
  4.7 16.9 %copy-start.5 = (bf16[256,256]{1,0:T(8,128)(2,1)S(1)}, bf16[256,256]{1,0:T(8,128)(2,1)}, u32[]{:S(2)}) copy-start(bf16[256,256]{1,0:T(8,128)(2,1)} %neigh_two_ref.1) | copy-start | bytes 393220
  4.7 15.9 %collective-permute-start.2 = (bf16[512,256]{1,0:T(8,128)(2,1)S(1)}, bf16[512,256]{1,0:T(8,128)(2,1)S(1)}, u32[]{:S(2)}, u32[]{:S(2)}) collective-permute-start(bf16[512,256]{1,0:T(8,128)(2,1)S(1)} %get-tuple-element.56), channel_id=1, source_target_pairs={{0,2},{2,0},{1,3},{3,1},{4,6},{6,4},{5,7},{7,5},{8,10},{10,8},{9,1... | collective-permute-start | bytes 786440 | tf_op jit(solution)/shard_map/ppermute | solution.py:408
  20.7 1.7 %collective-permute-start.3 = (bf16[640,256]{1,0:T(8,128)(2,1)S(1)}, bf16[640,256]{1,0:T(8,128)(2,1)S(1)}, u32[]{:S(2)}, u32[]{:S(2)}) collective-permute-start(bf16[640,256]{1,0:T(8,128)(2,1)S(1)} %get-tuple-element.58.here_ref), channel_id=1, source_target_pairs={{0,1},{1,0},{2,3},{3,2},{4,5},{5,4},{6,7},{7,6},{8,9},{9,8},{10,11... | collective-permute-start | bytes 983048 | tf_op jit(solution)/shard_map/ppermute | solution.py:408
  22.4 12.7 %copy-start.7 = (f32[256]{0:T(256)S(1)}, f32[256]{0:T(256)}, u32[]{:S(2)}) copy-start(f32[256]{0:T(256)} %bias_ref.3) | copy-start | bytes 3076
  23.2 11.3 %collective-permute-start.4 = (bf16[512,256]{1,0:T(8,128)(2,1)S(1)}, bf16[512,256]{1,0:T(8,128)(2,1)S(1)}, u32[]{:S(2)}, u32[]{:S(2)}) collective-permute-start(bf16[512,256]{1,0:T(8,128)(2,1)S(1)} %get-tuple-element.67), channel_id=1, source_target_pairs={{0,2},{2,0},{1,3},{3,1},{4,6},{6,4},{5,7},{7,5},{8,10},{10,8},{9,1... | collective-permute-start | bytes 786440 | tf_op jit(solution)/shard_map/ppermute | solution.py:408
  34.8 1.5 %collective-permute-start.5 = (bf16[256,256]{1,0:T(8,128)(2,1)S(1)}, bf16[256,256]{1,0:T(8,128)(2,1)S(1)}, u32[]{:S(2)}, u32[]{:S(2)}) collective-permute-start(bf16[256,256]{1,0:T(8,128)(2,1)S(1)} %there.1), channel_id=1, source_target_pairs={{0,1},{1,0},{2,3},{3,2},{4,5},{5,4},{6,7},{7,6},{8,9},{9,8},{10,11... | collective-permute-start | bytes 393224 | tf_op jit(solution)/shard_map/ppermute | solution.py:408

commit v23 on v22

--- a/solution.py
+++ b/solution.py
@@ -10,7 +10,7 @@
 F32 = jnp.float32
 BF16 = jnp.bfloat16
 MIB = 1024 * 1024
-CHUNKS = 8
+CHUNKS = 16
 PARTS = 4
 CORES = 2
 
@@ -321,7 +321,7 @@
     total = mine_ref[...] + returned(place_ref, recv_ref, hosts, chips)
     for block in came:
         total = total + block[:rows, :].astype(F32)
-    grad = precise_nt(total, neigh_ref[...])
+    grad = dot_nt(total.astype(BF16), neigh_ref[...])
     grad_ref[...] = grad + dot_nt(up_ref[...], weight_ref[...])
     out = column_product(chips, hosts, adj_ref, far_ref, sent_ref, came, recv_ref)
     out_ref[...] = out + dot(value_ref[...], self_ref[...]) + bias_ref[...].reshape(1, -1)

time: 37.2 us -> 37.3 us (level)
  transfers between devices with their start and end apart: 6 -> 6, of which waited for: 2 -> 3; matrix products, arithmetic and copies ran while one was open for 0% -> 0% of each run, Pallas kernels for 8% -> 8%
where the time goes in v23:
time: 37.3 us; the launch traced here: 37.1 us
  blocking collectives  23.8 us (64%)
  Pallas kernels  6.81 us (18%)
  starting transfers between devices  4.63 us (12%)
  waiting for transfers between devices  1.06 us (3%)
  between operations  0.75 us (2%)
    all_to_all x2, blocking collectives, across(): lax.all_to_all(msg, ('hst', 'chip', 'core'), split_axis=0, concat_axis=0,...  23.8 us
    pallas_call x10, Pallas kernels, call(): pl.pallas_call(kernel, out_shape=out_shape, in_specs=in_specs, out_specs=...  6.81 us
    ppermute x6, starting transfers between devices, shift(): return lax.ppermute(value, axis, [(i, (i + k) % size) for i in range(size)])  4.63 us
    ppermute x6, waiting for transfers between devices, shift(): return lax.ppermute(value, axis, [(i, (i + k) % size) for i in range(size)])  1.06 us
  transfers between devices with their start and end apart: 6, of which 3 were waited for; matrix products, arithmetic and copies ran while one was open for 0% of the time, Pallas kernels for 8%

profile of v23, /device:TPU:0, one launch (start us, length us, event | category | flops | bytes accessed | tf_op | source)
XLA Modules:
  0.0 37.1 jit_solution(5120223757984758403)
XLA Ops:
  0.6 0.0 copy-start
  0.6 0.0 copy-start.4
  0.7 0.0 copy-start.1
  0.7 2.3 %prep.1 = (bf16[640,256]{1,0:T(8,128)(2,1)S(1)}, bf16[64,256]{1,0:T(8,128)(2,1)S(1)}, f32[20,32,128]{2,1,0:T(8,128)S(1)}, f32[20,32,128]{2,1,0:T(8,128)S(1)}, f3...) custom-call(s32[64]{0:T(128)} %dst_hbm.1, s32[64]{0:T(128)} %src_hbm.1, s32[64]{0:T(128)} %rows_hbm.1, ...), custom_call_target="tpu_custom_call" | custom-call | tf_op jit(solution)/shard_map/prep/pallas_call | solution.py:392
  2.9 0.5 %collective-permute-start.1 = (bf16[640,256]{1,0:T(8,128)(2,1)S(1)}, bf16[640,256]{1,0:T(8,128)(2,1)S(1)}, u32[]{:S(2)}, u32[]{:S(2)}) collective-permute-start(bf16[640,256]{1,0:T(8,128)(2,1)S(1)} %get-tuple-element.51), channel_id=1, source_target_pairs={{0,1},{1,0},{2,3},{3,2},{4,5},{5,4},{6,7},{7,6},{8,9},{9,8},{10,11... | collective-permute-start | bytes 983048 | tf_op jit(solution)/shard_map/ppermute | solution.py:408
  3.5 0.0 copy-done
  3.5 0.0 copy-done.1
  3.5 0.6 %rest.1 = (bf16[256,256]{1,0:T(8,128)(2,1)S(1)}, bf16[64,256]{1,0:T(8,128)(2,1)S(1)}, bf16[1280,256]{1,0:T(8,128)(2,1)S(1)}, bf16[640,256]{1,0:T(8,128)(2,1)S(1)...) custom-call(bf16[256,256]{1,0:T(8,128)(2,1)S(1)} %copy-done, ...), custom_call_target="tpu_custom_call" | custom-call | flops 100663296 | bytes 98304 | tf_op jit(solution)/shard_map/rest/pallas_call | solution.py:392
  4.1 0.1 collective-permute-start
  4.2 0.5 %collective-permute-done.1.came_ref = bf16[640,256]{1,0:T(8,128)(2,1)S(1)} collective-permute-done((bf16[640,256]{1,0:T(8,128)(2,1)S(1)}, bf16[640,256]{1,0:T(8,128)(2,1)S(1)}, u32[]{:S(2)}, u32[]{:S(2)}) %collective-permute-start.1) | collective-permute-done | bytes 327712 | tf_op jit(solution)/shard_map/ppermute | solution.py:408
  4.7 0.1 core_sum.1
  4.8 0.0 copy-start.5
  4.8 2.9 %collective-permute-start.2 = (bf16[512,256]{1,0:T(8,128)(2,1)S(1)}, bf16[512,256]{1,0:T(8,128)(2,1)S(1)}, u32[]{:S(2)}, u32[]{:S(2)}) collective-permute-start(bf16[512,256]{1,0:T(8,128)(2,1)S(1)} %get-tuple-element.56), channel_id=1, source_target_pairs={{0,2},{2,0},{1,3},{3,1},{4,6},{6,4},{5,7},{7,5},{8,10},{10,8},{9,1... | collective-permute-start | bytes 786440 | tf_op jit(solution)/shard_map/ppermute | solution.py:408
  7.7 12.9 %all_to_all.10.recv_ref = bf16[32,8,256]{2,1,0:T(8,128)(2,1)S(1)} all-to-all(bf16[32,8,256]{2,1,0:T(8,128)(2,1)S(1)} %get-tuple-element.53), channel_id=1, replica_groups=mesh['hst'=8,'chip'=2,'core'=2] {'hst','chip','core'}, dimensions={0} | all-to-all | bytes 262144 | tf_op jit(solution)/shard_map/all_to_all | solution.py:451
  20.7 0.0 collective-permute-done.2.refs_0_
  20.7 0.2 merge.1
  20.9 0.3 collective-permute-start.3
  21.2 0.0 collective-permute-done.lent_ref
  21.2 0.0 copy-done.2
  21.2 0.6 %early_one.1 = (f32[512,256]{1,0:T(8,128)S(1)}, f32[512,256]{1,0:T(8,128)S(1)}, f32[512,256]{1,0:T(8,128)S(1)}, bf16[640,256]{1,0:T(8,128)(2,1)S(1)}, bf16[256,256]{1,0:T(8,128)(2,1)S(1)}) custom-call(bf16[1280,256]{1,0:T(8,128)(2,1)S(1)} %get-tuple-element.41.adj_ref, bf16[1792,256]{1,0:T(8,128)(2,1)S(1)} %collective-permute-done.lent_ref, ...), custom_call_target="tpu_custom_call" | custom-call | flops 268435456 | bytes 262144 | tf_op jit(solution)/shard_map/early_one/pallas_call | solution.py:392
  21.8 0.4 mid.1
  22.1 0.4 %collective-permute-done.3.shared_ref = bf16[640,256]{1,0:T(8,128)(2,1)S(1)} collective-permute-done((bf16[640,256]{1,0:T(8,128)(2,1)S(1)}, bf16[640,256]{1,0:T(8,128)(2,1)S(1)}, u32[]{:S(2)}, u32[]{:S(2)}) %collective-permute-start.3) | collective-permute-done | bytes 327712 | tf_op jit(solution)/shard_map/ppermute | solution.py:408
  22.6 0.8 %middle.1 = (bf16[256,256]{1,0:T(8,128)(2,1)S(1)}, bf16[256,256]{1,0:T(8,128)(2,1)S(1)}, bf16[256,256]{1,0:T(8,128)(2,1)S(1)}, f32[256,256]{1,0:T(8,128)S(1)}, b...) custom-call(bf16[1280,256]{1,0:T(8,128)(2,1)S(1)} %get-tuple-element.41.adj_ref, ...), custom_call_target="tpu_custom_call" | custom-call | flops 402653184 | bytes 393216 | tf_op jit(solution)/shard_map/middle/pallas_call | solution.py:392
  23.4 0.5 %collective-permute-start.4 = (bf16[512,256]{1,0:T(8,128)(2,1)S(1)}, bf16[512,256]{1,0:T(8,128)(2,1)S(1)}, u32[]{:S(2)}, u32[]{:S(2)}) collective-permute-start(bf16[512,256]{1,0:T(8,128)(2,1)S(1)} %get-tuple-element.67), channel_id=1, source_target_pairs={{0,2},{2,0},{1,3},{3,1},{4,6},{6,4},{5,7},{7,5},{8,10},{10,8},{9,1... | collective-permute-start | bytes 786440 | tf_op jit(solution)/shard_map/ppermute | solution.py:408
  23.9 10.8 %all_to_all.11.recv_ref = bf16[32,8,256]{2,1,0:T(8,128)(2,1)S(1)} all-to-all(bf16[32,8,256]{2,1,0:T(8,128)(2,1)S(1)} %get-tuple-element.63), channel_id=1, replica_groups=mesh['hst'=8,'chip'=2,'core'=2] {'hst','chip','core'}, dimensions={0} | all-to-all | bytes 262144 | tf_op jit(solution)/shard_map/all_to_all | solution.py:451
  34.7 0.0 collective-permute-done.4.refs_0_
  34.7 0.3 there.1
  35.0 0.3 collective-permute-start.5
  35.3 0.0 copy-done.7
  35.3 1.0 %here.1 = (f32[256,256]{1,0:T(8,128)S(1)}, f32[256,256]{1,0:T(8,128)}) custom-call(bf16[1280,256]{1,0:T(8,128)(2,1)S(1)} %get-tuple-element.41.adj_ref, bf16[256,256]{1,0:T(8,128)(2,1)S(1)} %get-tuple-element.42.far_ref, bf16[256,256]{1,0:T(8,128)(2,1)S(1)} %get-tuple-element.62.sent_ref.value_ref, bf16[32,8,256]{2,1,0:T(8,128)(2,1)S(1)} %all_to_all.11.recv_ref, ...), custom_call_target="tpu_custom_call" | custom-call | flops 234881024 | bytes 229376 | tf_op jit(solution)/shard_map/here/pallas_call | solution.py:392
  36.3 0.1 collective-permute-done.5.there_ref
  36.4 0.7 %last.1 = bf16[256,256]{1,0:T(8,128)(2,1)} custom-call(f32[256,256]{1,0:T(8,128)S(1)} %get-tuple-element.68.here_ref, bf16[256,256]{1,0:T(8,128)(2,1)S(1)} %collective-permute-done.5.there_ref), custom_call_target="tpu_custom_call" | custom-call | tf_op jit(solution)/shard_map/last/pallas_call | solution.py:392
  (8 shorter events, 0.0 us)
Async XLA Ops:
  0.6 2.8 %copy-start = (bf16[256,256]{1,0:T(8,128)(2,1)S(1)}, bf16[256,256]{1,0:T(8,128)(2,1)}, u32[]{:S(2)}) copy-start(bf16[256,256]{1,0:T(8,128)(2,1)} %up_ref.1) | copy-start | bytes 393220
  0.6 2.8 %copy-start.4 = (bf16[256,256]{1,0:T(8,128)(2,1)S(1)}, bf16[256,256]{1,0:T(8,128)(2,1)}, u32[]{:S(2)}) copy-start(bf16[256,256]{1,0:T(8,128)(2,1)} %value_ref.3) | copy-start | bytes 393220
  0.7 2.8 %copy-start.1 = (bf16[256,256]{1,0:T(8,128)(2,1)S(1)}, bf16[256,256]{1,0:T(8,128)(2,1)}, u32[]{:S(2)}) copy-start(bf16[256,256]{1,0:T(8,128)(2,1)} %neigh_ref.7) | copy-start | bytes 393220
  2.9 1.8 %collective-permute-start.1 = (bf16[640,256]{1,0:T(8,128)(2,1)S(1)}, bf16[640,256]{1,0:T(8,128)(2,1)S(1)}, u32[]{:S(2)}, u32[]{:S(2)}) collective-permute-start(bf16[640,256]{1,0:T(8,128)(2,1)S(1)} %get-tuple-element.51), channel_id=1, source_target_pairs={{0,1},{1,0},{2,3},{3,2},{4,5},{5,4},{6,7},{7,6},{8,9},{9,8},{10,11... | collective-permute-start | bytes 983048 | tf_op jit(solution)/shard_map/ppermute | solution.py:408
  4.1 17.1 %collective-permute-start = (bf16[1792,256]{1,0:T(8,128)(2,1)S(1)}, bf16[1792,256]{1,0:T(8,128)(2,1)S(1)}, u32[]{:S(2)}, u32[]{:S(2)}) collective-permute-start(bf16[1792,256]{1,0:T(8,128)(2,1)S(1)} %get-tuple-element.43), channel_id=1, source_target_pairs={{0,1},{1,0},{2,3},{3,2},{4,5},{5,4},{6,7},{7,6},{8,9},{9,8},{10,11... | collective-permute-start | bytes 2752520 | tf_op jit(solution)/shard_map/ppermute | solution.py:408
  4.7 16.5 %copy-start.2 = (bf16[256,256]{1,0:T(8,128)(2,1)S(1)}, bf16[256,256]{1,0:T(8,128)(2,1)}, u32[]{:S(2)}) copy-start(bf16[256,256]{1,0:T(8,128)(2,1)} %weight_ref.3) | copy-start | bytes 393220
  4.7 16.5 %copy-start.3 = (bf16[256,256]{1,0:T(8,128)(2,1)S(1)}, bf16[256,256]{1,0:T(8,128)(2,1)}, u32[]{:S(2)}) copy-start(bf16[256,256]{1,0:T(8,128)(2,1)} %self_ref.3) | copy-start | bytes 393220
  4.7 16.5 %copy-start.6 = (f32[256]{0:T(256)S(1)}, f32[256]{0:T(256)}, u32[]{:S(2)}) copy-start(f32[256]{0:T(256)} %bias_ref.2) | copy-start | bytes 3076
  4.8 17.0 %copy-start.5 = (bf16[256,256]{1,0:T(8,128)(2,1)S(1)}, bf16[256,256]{1,0:T(8,128)(2,1)}, u32[]{:S(2)}) copy-start(bf16[256,256]{1,0:T(8,128)(2,1)} %neigh_two_ref.1) | copy-start | bytes 393220
  4.8 15.9 %collective-permute-start.2 = (bf16[512,256]{1,0:T(8,128)(2,1)S(1)}, bf16[512,256]{1,0:T(8,128)(2,1)S(1)}, u32[]{:S(2)}, u32[]{:S(2)}) collective-permute-start(bf16[512,256]{1,0:T(8,128)(2,1)S(1)} %get-tuple-element.56), channel_id=1, source_target_pairs={{0,2},{2,0},{1,3},{3,1},{4,6},{6,4},{5,7},{7,5},{8,10},{10,8},{9,1... | collective-permute-start | bytes 786440 | tf_op jit(solution)/shard_map/ppermute | solution.py:408
  20.9 1.7 %collective-permute-start.3 = (bf16[640,256]{1,0:T(8,128)(2,1)S(1)}, bf16[640,256]{1,0:T(8,128)(2,1)S(1)}, u32[]{:S(2)}, u32[]{:S(2)}) collective-permute-start(bf16[640,256]{1,0:T(8,128)(2,1)S(1)} %get-tuple-element.58.here_ref), channel_id=1, source_target_pairs={{0,1},{1,0},{2,3},{3,2},{4,5},{5,4},{6,7},{7,6},{8,9},{9,8},{10,11... | collective-permute-start | bytes 983048 | tf_op jit(solution)/shard_map/ppermute | solution.py:408
  22.6 12.7 %copy-start.7 = (f32[256]{0:T(256)S(1)}, f32[256]{0:T(256)}, u32[]{:S(2)}) copy-start(f32[256]{0:T(256)} %bias_ref.3) | copy-start | bytes 3076
  23.4 11.3 %collective-permute-start.4 = (bf16[512,256]{1,0:T(8,128)(2,1)S(1)}, bf16[512,256]{1,0:T(8,128)(2,1)S(1)}, u32[]{:S(2)}, u32[]{:S(2)}) collective-permute-start(bf16[512,256]{1,0:T(8,128)(2,1)S(1)} %get-tuple-element.67), channel_id=1, source_target_pairs={{0,2},{2,0},{1,3},{3,1},{4,6},{6,4},{5,7},{7,5},{8,10},{10,8},{9,1... | collective-permute-start | bytes 786440 | tf_op jit(solution)/shard_map/ppermute | solution.py:408
  35.0 1.4 %collective-permute-start.5 = (bf16[256,256]{1,0:T(8,128)(2,1)S(1)}, bf16[256,256]{1,0:T(8,128)(2,1)S(1)}, u32[]{:S(2)}, u32[]{:S(2)}) collective-permute-start(bf16[256,256]{1,0:T(8,128)(2,1)S(1)} %there.1), channel_id=1, source_target_pairs={{0,1},{1,0},{2,3},{3,2},{4,5},{5,4},{6,7},{7,6},{8,9},{9,8},{10,11... | collective-permute-start | bytes 393224 | tf_op jit(solution)/shard_map/ppermute | solution.py:408

commit v24 on v23

--- a/solution.py
+++ b/solution.py
@@ -10,7 +10,7 @@
 F32 = jnp.float32
 BF16 = jnp.bfloat16
 MIB = 1024 * 1024
-CHUNKS = 16
+CHUNKS = 8
 PARTS = 4
 CORES = 2
 
@@ -97,9 +97,10 @@
     ) = rest
     tiles, blk = tile_buf.shape[0], tile_buf.shape[1]
     each = tiles // CHUNKS
+    cuts = [c * each for c in range(CHUNKS)] + [tiles - each // 2, tiles]
     chunks = [
-        (tile_hbm.at[pl.ds(c * each, each)], tile_buf.at[pl.ds(c * each, each)])
-        for c in range(CHUNKS)
+        (tile_hbm.at[pl.ds(low, high - low)], tile_buf.at[pl.ds(low, high - low)])
+        for low, high in zip(cuts, cuts[1:])
     ]
     pairs = [(send_hbm, send_ref), (dst_hbm, dst_ref), (src_hbm, src_ref), (rows_hbm, rows_ref)]
     pairs += chunks + [(cot_hbm, cot_ref)]
@@ -126,10 +127,10 @@
     pick_ref[...] = pick_matrix(send_ref, rows)
     for copy in copies[1:4]:
         copy.wait()
-    for c in range(CHUNKS):
-        copies[4 + c].wait()
-        lax.fori_loop(c * each, (c + 1) * each, add, 0, unroll=True)
-    copies[4 + CHUNKS].wait()
+    for copy, low, high in zip(copies[4:], cuts, cuts[1:]):
+        copy.wait()
+        lax.fori_loop(low, high, add, 0, unroll=True)
+    copies[-1].wait()
     chip, side = lax.axis_index("chip"), 1 - lax.axis_index("core")
     base = chips * CORES
     for j in range(far_t.shape[0] // rows):
@@ -479,7 +480,7 @@
             pltpu.VMEM((rows, rows), BF16),
             far_t,
             pltpu.VMEM((count, rows), BF16),
-            pltpu.SemaphoreType.DMA((5 + CHUNKS,)),
+            pltpu.SemaphoreType.DMA((6 + CHUNKS,)),
         ],
     )
     came = shift(give, "core", 1)

time: 37.3 us -> 37.1 us (level)
  no operation moved by 1% of the time
where the time goes in v24:
time: 37.1 us; the launch traced here: 36.9 us
  blocking collectives  23.8 us (64%)
  Pallas kernels  6.67 us (18%)
  starting transfers between devices  4.64 us (13%)
  waiting for transfers between devices  1.07 us (3%)
  between operations  0.75 us (2%)
    all_to_all x2, blocking collectives, across(): lax.all_to_all(msg, ('hst', 'chip', 'core'), split_axis=0, concat_axis=0,...  23.8 us
    pallas_call x10, Pallas kernels, call(): pl.pallas_call(kernel, out_shape=out_shape, in_specs=in_specs, out_specs=...  6.67 us
    ppermute x6, starting transfers between devices, shift(): return lax.ppermute(value, axis, [(i, (i + k) % size) for i in range(size)])  4.64 us
    ppermute x6, waiting for transfers between devices, shift(): return lax.ppermute(value, axis, [(i, (i + k) % size) for i in range(size)])  1.07 us
  transfers between devices with their start and end apart: 6, of which 3 were waited for; matrix products, arithmetic and copies ran while one was open for 0% of the time, Pallas kernels for 8%

profile of v24, /device:TPU:0, one launch (start us, length us, event | category | flops | bytes accessed | tf_op | source)
XLA Modules:
  0.0 36.9 jit_solution(14861949097689943306)
XLA Ops:
  0.6 0.0 copy-start
  0.6 0.0 copy-start.4
  0.7 0.0 copy-start.1
  0.7 2.1 %prep.1 = (bf16[640,256]{1,0:T(8,128)(2,1)S(1)}, bf16[64,256]{1,0:T(8,128)(2,1)S(1)}, f32[20,32,128]{2,1,0:T(8,128)S(1)}, f32[20,32,128]{2,1,0:T(8,128)S(1)}, f3...) custom-call(s32[64]{0:T(128)} %dst_hbm.1, s32[64]{0:T(128)} %src_hbm.1, s32[64]{0:T(128)} %rows_hbm.1, ...), custom_call_target="tpu_custom_call" | custom-call | tf_op jit(solution)/shard_map/prep/pallas_call | solution.py:393
  2.8 0.5 %collective-permute-start.1 = (bf16[640,256]{1,0:T(8,128)(2,1)S(1)}, bf16[640,256]{1,0:T(8,128)(2,1)S(1)}, u32[]{:S(2)}, u32[]{:S(2)}) collective-permute-start(bf16[640,256]{1,0:T(8,128)(2,1)S(1)} %get-tuple-element.51), channel_id=1, source_target_pairs={{0,1},{1,0},{2,3},{3,2},{4,5},{5,4},{6,7},{7,6},{8,9},{9,8},{10,11... | collective-permute-start | bytes 983048 | tf_op jit(solution)/shard_map/ppermute | solution.py:409
  3.3 0.0 copy-done
  3.3 0.0 copy-done.4
  3.3 0.0 copy-done.1
  3.3 0.6 %rest.1 = (bf16[256,256]{1,0:T(8,128)(2,1)S(1)}, bf16[64,256]{1,0:T(8,128)(2,1)S(1)}, bf16[1280,256]{1,0:T(8,128)(2,1)S(1)}, bf16[640,256]{1,0:T(8,128)(2,1)S(1)...) custom-call(bf16[256,256]{1,0:T(8,128)(2,1)S(1)} %copy-done, ...), custom_call_target="tpu_custom_call" | custom-call | flops 100663296 | bytes 98304 | tf_op jit(solution)/shard_map/rest/pallas_call | solution.py:393
  3.9 0.1 collective-permute-start
  4.1 0.5 %collective-permute-done.1.came_ref = bf16[640,256]{1,0:T(8,128)(2,1)S(1)} collective-permute-done((bf16[640,256]{1,0:T(8,128)(2,1)S(1)}, bf16[640,256]{1,0:T(8,128)(2,1)S(1)}, u32[]{:S(2)}, u32[]{:S(2)}) %collective-permute-start.1) | collective-permute-done | bytes 327712 | tf_op jit(solution)/shard_map/ppermute | solution.py:409
  4.6 0.1 core_sum.1
  4.7 0.0 copy-start.5
  4.7 2.9 %collective-permute-start.2 = (bf16[512,256]{1,0:T(8,128)(2,1)S(1)}, bf16[512,256]{1,0:T(8,128)(2,1)S(1)}, u32[]{:S(2)}, u32[]{:S(2)}) collective-permute-start(bf16[512,256]{1,0:T(8,128)(2,1)S(1)} %get-tuple-element.56), channel_id=1, source_target_pairs={{0,2},{2,0},{1,3},{3,1},{4,6},{6,4},{5,7},{7,5},{8,10},{10,8},{9,1... | collective-permute-start | bytes 786440 | tf_op jit(solution)/shard_map/ppermute | solution.py:409
  7.6 12.9 %all_to_all.10.recv_ref = bf16[32,8,256]{2,1,0:T(8,128)(2,1)S(1)} all-to-all(bf16[32,8,256]{2,1,0:T(8,128)(2,1)S(1)} %get-tuple-element.53), channel_id=1, replica_groups=mesh['hst'=8,'chip'=2,'core'=2] {'hst','chip','core'}, dimensions={0} | all-to-all | bytes 262144 | tf_op jit(solution)/shard_map/all_to_all | solution.py:452
  20.6 0.0 collective-permute-done.2.refs_0_
  20.6 0.2 merge.1
  20.8 0.3 collective-permute-start.3
  21.0 0.0 collective-permute-done.lent_ref
  21.0 0.0 copy-done.3
  21.1 0.6 %early_one.1 = (f32[512,256]{1,0:T(8,128)S(1)}, f32[512,256]{1,0:T(8,128)S(1)}, f32[512,256]{1,0:T(8,128)S(1)}, bf16[640,256]{1,0:T(8,128)(2,1)S(1)}, bf16[256,256]{1,0:T(8,128)(2,1)S(1)}) custom-call(bf16[1280,256]{1,0:T(8,128)(2,1)S(1)} %get-tuple-element.41.adj_ref, bf16[1792,256]{1,0:T(8,128)(2,1)S(1)} %collective-permute-done.lent_ref, ...), custom_call_target="tpu_custom_call" | custom-call | flops 268435456 | bytes 262144 | tf_op jit(solution)/shard_map/early_one/pallas_call | solution.py:393
  21.6 0.4 %mid.1 = (f32[512,256]{1,0:T(8,128)S(1)}, f32[512,256]{1,0:T(8,128)S(1)}) custom-call(bf16[1280,256]{1,0:T(8,128)(2,1)S(1)} %get-tuple-element.41.adj_ref, bf16[1792,256]{1,0:T(8,128)(2,1)S(1)} %collective-permute-done.lent_ref, bf16[256,256]{1,0:T(8,128)(2,1)S(1)} %get-tuple-element.42.far_ref, bf16[256,256]{1,0:T(8,128)(2,1)S(1)} %get-tuple-element.45.far_two_ref.far_ref, ...), custom_call_target="tpu_custom_call" | custom-call | flops 100663296 | bytes 98304 | tf_op jit(solution)/shard_map/mid/pallas_call | solution.py:393
  22.0 0.4 %collective-permute-done.3.shared_ref = bf16[640,256]{1,0:T(8,128)(2,1)S(1)} collective-permute-done((bf16[640,256]{1,0:T(8,128)(2,1)S(1)}, bf16[640,256]{1,0:T(8,128)(2,1)S(1)}, u32[]{:S(2)}, u32[]{:S(2)}) %collective-permute-start.3) | collective-permute-done | bytes 327712 | tf_op jit(solution)/shard_map/ppermute | solution.py:409
  22.5 0.8 %middle.1 = (bf16[256,256]{1,0:T(8,128)(2,1)S(1)}, bf16[256,256]{1,0:T(8,128)(2,1)S(1)}, bf16[256,256]{1,0:T(8,128)(2,1)S(1)}, f32[256,256]{1,0:T(8,128)S(1)}, b...) custom-call(bf16[1280,256]{1,0:T(8,128)(2,1)S(1)} %get-tuple-element.41.adj_ref, ...), custom_call_target="tpu_custom_call" | custom-call | flops 402653184 | bytes 393216 | tf_op jit(solution)/shard_map/middle/pallas_call | solution.py:393
  23.2 0.5 %collective-permute-start.4 = (bf16[512,256]{1,0:T(8,128)(2,1)S(1)}, bf16[512,256]{1,0:T(8,128)(2,1)S(1)}, u32[]{:S(2)}, u32[]{:S(2)}) collective-permute-start(bf16[512,256]{1,0:T(8,128)(2,1)S(1)} %get-tuple-element.67), channel_id=1, source_target_pairs={{0,2},{2,0},{1,3},{3,1},{4,6},{6,4},{5,7},{7,5},{8,10},{10,8},{9,1... | collective-permute-start | bytes 786440 | tf_op jit(solution)/shard_map/ppermute | solution.py:409
  23.7 10.8 %all_to_all.11.recv_ref = bf16[32,8,256]{2,1,0:T(8,128)(2,1)S(1)} all-to-all(bf16[32,8,256]{2,1,0:T(8,128)(2,1)S(1)} %get-tuple-element.63), channel_id=1, replica_groups=mesh['hst'=8,'chip'=2,'core'=2] {'hst','chip','core'}, dimensions={0} | all-to-all | bytes 262144 | tf_op jit(solution)/shard_map/all_to_all | solution.py:452
  34.6 0.0 collective-permute-done.4.refs_0_
  34.6 0.3 there.1
  34.9 0.3 collective-permute-start.5
  35.1 1.0 %here.1 = (f32[256,256]{1,0:T(8,128)S(1)}, f32[256,256]{1,0:T(8,128)}) custom-call(bf16[1280,256]{1,0:T(8,128)(2,1)S(1)} %get-tuple-element.41.adj_ref, bf16[256,256]{1,0:T(8,128)(2,1)S(1)} %get-tuple-element.42.far_ref, bf16[256,256]{1,0:T(8,128)(2,1)S(1)} %get-tuple-element.62.sent_ref.value_ref, bf16[32,8,256]{2,1,0:T(8,128)(2,1)S(1)} %all_to_all.11.recv_ref, ...), custom_call_target="tpu_custom_call" | custom-call | flops 234881024 | bytes 229376 | tf_op jit(solution)/shard_map/here/pallas_call | solution.py:393
  36.2 0.1 collective-permute-done.5.there_ref
  36.3 0.7 %last.1 = bf16[256,256]{1,0:T(8,128)(2,1)} custom-call(f32[256,256]{1,0:T(8,128)S(1)} %get-tuple-element.68.here_ref, bf16[256,256]{1,0:T(8,128)(2,1)S(1)} %collective-permute-done.5.there_ref), custom_call_target="tpu_custom_call" | custom-call | tf_op jit(solution)/shard_map/last/pallas_call | solution.py:393
  (8 shorter events, 0.0 us)
Async XLA Ops:
  0.6 2.7 %copy-start = (bf16[256,256]{1,0:T(8,128)(2,1)S(1)}, bf16[256,256]{1,0:T(8,128)(2,1)}, u32[]{:S(2)}) copy-start(bf16[256,256]{1,0:T(8,128)(2,1)} %up_ref.1) | copy-start | bytes 393220
  0.6 2.7 %copy-start.4 = (bf16[256,256]{1,0:T(8,128)(2,1)S(1)}, bf16[256,256]{1,0:T(8,128)(2,1)}, u32[]{:S(2)}) copy-start(bf16[256,256]{1,0:T(8,128)(2,1)} %value_ref.3) | copy-start | bytes 393220
  0.7 2.7 %copy-start.1 = (bf16[256,256]{1,0:T(8,128)(2,1)S(1)}, bf16[256,256]{1,0:T(8,128)(2,1)}, u32[]{:S(2)}) copy-start(bf16[256,256]{1,0:T(8,128)(2,1)} %neigh_ref.7) | copy-start | bytes 393220
  2.8 1.8 %collective-permute-start.1 = (bf16[640,256]{1,0:T(8,128)(2,1)S(1)}, bf16[640,256]{1,0:T(8,128)(2,1)S(1)}, u32[]{:S(2)}, u32[]{:S(2)}) collective-permute-start(bf16[640,256]{1,0:T(8,128)(2,1)S(1)} %get-tuple-element.51), channel_id=1, source_target_pairs={{0,1},{1,0},{2,3},{3,2},{4,5},{5,4},{6,7},{7,6},{8,9},{9,8},{10,11... | collective-permute-start | bytes 983048 | tf_op jit(solution)/shard_map/ppermute | solution.py:409
  3.9 17.1 %collective-permute-start = (bf16[1792,256]{1,0:T(8,128)(2,1)S(1)}, bf16[1792,256]{1,0:T(8,128)(2,1)S(1)}, u32[]{:S(2)}, u32[]{:S(2)}) collective-permute-start(bf16[1792,256]{1,0:T(8,128)(2,1)S(1)} %get-tuple-element.43), channel_id=1, source_target_pairs={{0,1},{1,0},{2,3},{3,2},{4,5},{5,4},{6,7},{7,6},{8,9},{9,8},{10,11... | collective-permute-start | bytes 2752520 | tf_op jit(solution)/shard_map/ppermute | solution.py:409
  4.6 16.4 %copy-start.2 = (bf16[256,256]{1,0:T(8,128)(2,1)S(1)}, bf16[256,256]{1,0:T(8,128)(2,1)}, u32[]{:S(2)}) copy-start(bf16[256,256]{1,0:T(8,128)(2,1)} %weight_ref.3) | copy-start | bytes 393220
  4.6 16.4 %copy-start.3 = (bf16[256,256]{1,0:T(8,128)(2,1)S(1)}, bf16[256,256]{1,0:T(8,128)(2,1)}, u32[]{:S(2)}) copy-start(bf16[256,256]{1,0:T(8,128)(2,1)} %self_ref.3) | copy-start | bytes 393220
  4.6 16.5 %copy-start.6 = (f32[256]{0:T(256)S(1)}, f32[256]{0:T(256)}, u32[]{:S(2)}) copy-start(f32[256]{0:T(256)} %bias_ref.2) | copy-start | bytes 3076
  4.7 16.9 %copy-start.5 = (bf16[256,256]{1,0:T(8,128)(2,1)S(1)}, bf16[256,256]{1,0:T(8,128)(2,1)}, u32[]{:S(2)}) copy-start(bf16[256,256]{1,0:T(8,128)(2,1)} %neigh_two_ref.1) | copy-start | bytes 393220
  4.7 15.9 %collective-permute-start.2 = (bf16[512,256]{1,0:T(8,128)(2,1)S(1)}, bf16[512,256]{1,0:T(8,128)(2,1)S(1)}, u32[]{:S(2)}, u32[]{:S(2)}) collective-permute-start(bf16[512,256]{1,0:T(8,128)(2,1)S(1)} %get-tuple-element.56), channel_id=1, source_target_pairs={{0,2},{2,0},{1,3},{3,1},{4,6},{6,4},{5,7},{7,5},{8,10},{10,8},{9,1... | collective-permute-start | bytes 786440 | tf_op jit(solution)/shard_map/ppermute | solution.py:409
  20.8 1.7 %collective-permute-start.3 = (bf16[640,256]{1,0:T(8,128)(2,1)S(1)}, bf16[640,256]{1,0:T(8,128)(2,1)S(1)}, u32[]{:S(2)}, u32[]{:S(2)}) collective-permute-start(bf16[640,256]{1,0:T(8,128)(2,1)S(1)} %get-tuple-element.58.here_ref), channel_id=1, source_target_pairs={{0,1},{1,0},{2,3},{3,2},{4,5},{5,4},{6,7},{7,6},{8,9},{9,8},{10,11... | collective-permute-start | bytes 983048 | tf_op jit(solution)/shard_map/ppermute | solution.py:409
  22.5 12.7 %copy-start.7 = (f32[256]{0:T(256)S(1)}, f32[256]{0:T(256)}, u32[]{:S(2)}) copy-start(f32[256]{0:T(256)} %bias_ref.3) | copy-start | bytes 3076
  23.2 11.3 %collective-permute-start.4 = (bf16[512,256]{1,0:T(8,128)(2,1)S(1)}, bf16[512,256]{1,0:T(8,128)(2,1)S(1)}, u32[]{:S(2)}, u32[]{:S(2)}) collective-permute-start(bf16[512,256]{1,0:T(8,128)(2,1)S(1)} %get-tuple-element.67), channel_id=1, source_target_pairs={{0,2},{2,0},{1,3},{3,1},{4,6},{6,4},{5,7},{7,5},{8,10},{10,8},{9,1... | collective-permute-start | bytes 786440 | tf_op jit(solution)/shard_map/ppermute | solution.py:409
  34.9 1.4 %collective-permute-start.5 = (bf16[256,256]{1,0:T(8,128)(2,1)S(1)}, bf16[256,256]{1,0:T(8,128)(2,1)S(1)}, u32[]{:S(2)}, u32[]{:S(2)}) collective-permute-start(bf16[256,256]{1,0:T(8,128)(2,1)S(1)} %there.1), channel_id=1, source_target_pairs={{0,1},{1,0},{2,3},{3,2},{4,5},{5,4},{6,7},{7,6},{8,9},{9,8},{10,11... | collective-permute-start | bytes 393224 | tf_op jit(solution)/shard_map/ppermute | solution.py:409

commit v25 on v24

--- a/solution.py
+++ b/solution.py
@@ -216,19 +216,17 @@
 
 
 def merge_kernel(chips, hosts, recv_ref, mine_ref, place_ref, *refs):
-    came, (out_ref, sum_ref) = refs[: chips - 1], refs[chips - 1 :]
+    came, (nodes_ref, out_ref, sum_ref) = refs[: chips - 1], refs[chips - 1 :]
     rows = mine_ref.shape[0]
     total = mine_ref[...]
     for k, ref in enumerate(came):
         total = total + ref[:rows, :].astype(F32)
-        out_ref[k * rows : (k + 1) * rows, :] = ref[rows:, :]
+        nodes_ref[k * rows : (k + 1) * rows, :] = ref[rows:, :]
     total = total + returned(place_ref, recv_ref, hosts, chips)
     sum_ref[...] = total
-    low = len(came) * rows
     halo = received(recv_ref, hosts, chips, 1 - lax.axis_index("core"))
-    high = low + halo.shape[0]
-    out_ref[low:high, :] = halo
-    out_ref[high:, :] = total.astype(BF16)
+    out_ref[: halo.shape[0], :] = halo
+    out_ref[halo.shape[0] :, :] = total.astype(BF16)
 
 
 def returned(place_ref, recv_ref, hosts, chips):
@@ -278,7 +276,7 @@
 ):
     came, (agg_out, grad_ref) = refs[:-2], refs[-2:]
     rows = sum_ref.shape[0]
-    halo = here_ref[(chips - 1) * rows : here_ref.shape[0] - rows, :]
+    halo = here_ref[: here_ref.shape[0] - rows, :]
     for i, (ref, columns) in enumerate(((adj_ref, far_ref), (lent_ref, far_two_ref))):
         pairs = other_chips(chips, ref, came) + [(columns[:, : halo.shape[0]], halo)]
         part = slice(i * rows, (i + 1) * rows)
@@ -328,16 +326,15 @@
     out_ref[...] = out + dot(value_ref[...], self_ref[...]) + bias_ref[...].reshape(1, -1)
 
 
-def add_rest(chips, rows, adj_ref, far_ref, agg, shared_ref):
+def add_rest(chips, rows, adj_ref, far_ref, agg, nodes_ref, shared_ref):
     chip, core = lax.axis_index("chip"), lax.axis_index("core")
     pairs = []
     for k in range(chips - 1):
         x = lax.rem(chip - k - 1 + chips, chips)
-        block = shared_ref[k * rows : (k + 1) * rows, :]
+        block = nodes_ref[k * rows : (k + 1) * rows, :]
         pairs.append((square_of(adj_ref, x, 1 - core, rows), block))
     half = far_ref.shape[1] // 2
-    low = (chips - 1) * rows
-    pairs.append((far_ref[:, half:], shared_ref[low : low + half, :]))
+    pairs.append((far_ref[:, half:], shared_ref[:half, :]))
     return agg + joint(pairs)
 
 
@@ -354,6 +351,7 @@
     direct_ref,
     grad_ref,
     pick_ref,
+    nodes_ref,
     shared_ref,
     neigh_two_ref,
     hidden_ref,
@@ -366,7 +364,9 @@
     to_refs = rest
     far, rows = pick_ref.shape
     parts = [
-        add_rest(chips, rows, ref, columns, agg_ref[i * rows : (i + 1) * rows, :], shared_ref)
+        add_rest(
+            chips, rows, ref, columns, agg_ref[i * rows : (i + 1) * rows, :], nodes_ref, shared_ref
+        )
         for i, (ref, columns) in enumerate(((adj_ref, far_ref), (lent_ref, far_two_ref)))
     ]
     pre = direct_ref[...] + jnp.concatenate(parts, 0)
@@ -375,8 +375,7 @@
     hidden_ref[...] = hidden
     sent = dot(hidden, neigh_two_ref[...]).astype(BF16)
     sent_ref[...] = sent
-    low = (chips - 1) * rows + chips * far
-    add = dot_nt(shared_ref[low:, :], neigh_two_ref[...])
+    add = dot_nt(shared_ref[chips * far :, :], neigh_two_ref[...])
     grad = jnp.concatenate([grad_ref[:rows, :], grad_ref[rows:, :] + add], 0)
     grad_pre = (grad * sigmoid * (1.0 + pre * (1.0 - sigmoid))).astype(BF16)
     grad_pre_ref[...] = grad_pre[:rows]
@@ -441,7 +440,6 @@
     both_shape = shape(CORES * rows, width, F32)
     square = 2 * rows * width * width
     far_shape = shape(rows, chips * CORES * far)
-    halo_rows = (chips - 1) * rows + chips * far
     dealt = (
         sum_shape,
         jax.ShapeDtypeStruct((chips * hosts * CORES, send, width), BF16),
@@ -512,13 +510,14 @@
         flops=60 * square,
     )
     terms, recv = across(msg, to)
-    here, summed = call(
+    nodes, here, summed = call(
         functools.partial(merge_kernel, chips, hosts),
         "merge",
-        (shape(halo_rows + rows, width), sum_shape),
+        (shape((chips - 1) * rows, width), shape(chips * far + rows, width), sum_shape),
         [VMEM] * (2 + chips),
         (recv, mine, place, *terms),
     )
+    nodes = shift(nodes, "core", 1)
     shared = shift(here, "core", 1)
     agg, direct, grad, col_two, columns_two = call(
         functools.partial(early_one_kernel, chips),
@@ -551,7 +550,7 @@
         functools.partial(middle_kernel, chips, hosts),
         "middle",
         (rows_shape,) * 3 + dealt,
-        [VMEM] * 12,
+        [VMEM] * 13,
         (
             adj,
             lent,
@@ -563,6 +562,7 @@
             direct,
             grad,
             pick,
+            nodes,
             shared,
             neigh_two,
         ),

time: 37.1 us -> 37.1 us (level)
    ppermute x6 -> x7, waiting for transfers between devices: 1.07 us -> 0.77 us  [shift(): return lax.ppermute(value, axis, [(i, (i + k) % size) for i in range(size)])]
    ppermute x6 -> x7, starting transfers between devices: 4.64 us -> 4.92 us  [shift(): return lax.ppermute(value, axis, [(i, (i + k) % size) for i in range(size)])]
  transfers between devices with their start and end apart: 6 -> 7, of which waited for: 3 -> 3; matrix products, arithmetic and copies ran while one was open for 0% -> 0% of each run, Pallas kernels for 8% -> 8%
where the time goes in v25:
time: 37.1 us; the launch traced here: 37 us
  blocking collectives  23.8 us (64%)
  Pallas kernels  6.69 us (18%)
  starting transfers between devices  4.92 us (13%)
  waiting for transfers between devices  0.77 us (2%)
  between operations  0.75 us (2%)
    all_to_all x2, blocking collectives, across(): lax.all_to_all(msg, ('hst', 'chip', 'core'), split_axis=0, concat_axis=0,...  23.8 us
    pallas_call x10, Pallas kernels, call(): pl.pallas_call(kernel, out_shape=out_shape, in_specs=in_specs, out_specs=...  6.69 us
    ppermute x7, starting transfers between devices, shift(): return lax.ppermute(value, axis, [(i, (i + k) % size) for i in range(size)])  4.92 us
    ppermute x7, waiting for transfers between devices, shift(): return lax.ppermute(value, axis, [(i, (i + k) % size) for i in range(size)])  0.77 us
  transfers between devices with their start and end apart: 7, of which 3 were waited for; matrix products, arithmetic and copies ran while one was open for 0% of the time, Pallas kernels for 8%

profile of v25, /device:TPU:0, one launch (start us, length us, event | category | flops | bytes accessed | tf_op | source)
XLA Modules:
  0.0 37.0 jit_solution(6722446485895092627)
XLA Ops:
  0.6 0.0 copy-start
  0.6 0.0 copy-start.5
  0.7 0.0 copy-start.1
  0.7 2.1 %prep.1 = (bf16[640,256]{1,0:T(8,128)(2,1)S(1)}, bf16[64,256]{1,0:T(8,128)(2,1)S(1)}, f32[20,32,128]{2,1,0:T(8,128)S(1)}, f32[20,32,128]{2,1,0:T(8,128)S(1)}, f3...) custom-call(s32[64]{0:T(128)} %dst_hbm.1, s32[64]{0:T(128)} %src_hbm.1, s32[64]{0:T(128)} %rows_hbm.1, ...), custom_call_target="tpu_custom_call" | custom-call | tf_op jit(solution)/shard_map/prep/pallas_call | solution.py:392
  2.8 0.5 %collective-permute-start.1 = (bf16[640,256]{1,0:T(8,128)(2,1)S(1)}, bf16[640,256]{1,0:T(8,128)(2,1)S(1)}, u32[]{:S(2)}, u32[]{:S(2)}) collective-permute-start(bf16[640,256]{1,0:T(8,128)(2,1)S(1)} %get-tuple-element.52), channel_id=1, source_target_pairs={{0,1},{1,0},{2,3},{3,2},{4,5},{5,4},{6,7},{7,6},{8,9},{9,8},{10,11... | collective-permute-start | bytes 983048 | tf_op jit(solution)/shard_map/ppermute | solution.py:408
  3.3 0.0 copy-done
  3.3 0.0 copy-done.1
  3.3 0.6 %rest.1 = (bf16[256,256]{1,0:T(8,128)(2,1)S(1)}, bf16[64,256]{1,0:T(8,128)(2,1)S(1)}, bf16[1280,256]{1,0:T(8,128)(2,1)S(1)}, bf16[640,256]{1,0:T(8,128)(2,1)S(1)...) custom-call(bf16[256,256]{1,0:T(8,128)(2,1)S(1)} %copy-done, ...), custom_call_target="tpu_custom_call" | custom-call | flops 100663296 | bytes 98304 | tf_op jit(solution)/shard_map/rest/pallas_call | solution.py:392
  3.9 0.1 collective-permute-start
  4.1 0.5 %collective-permute-done.1.came_ref = bf16[640,256]{1,0:T(8,128)(2,1)S(1)} collective-permute-done((bf16[640,256]{1,0:T(8,128)(2,1)S(1)}, bf16[640,256]{1,0:T(8,128)(2,1)S(1)}, u32[]{:S(2)}, u32[]{:S(2)}) %collective-permute-start.1) | collective-permute-done | bytes 327712 | tf_op jit(solution)/shard_map/ppermute | solution.py:408
  4.6 0.1 core_sum.1
  4.7 0.0 copy-start.2
  4.7 2.9 %collective-permute-start.2 = (bf16[512,256]{1,0:T(8,128)(2,1)S(1)}, bf16[512,256]{1,0:T(8,128)(2,1)S(1)}, u32[]{:S(2)}, u32[]{:S(2)}) collective-permute-start(bf16[512,256]{1,0:T(8,128)(2,1)S(1)} %get-tuple-element.57), channel_id=1, source_target_pairs={{0,2},{2,0},{1,3},{3,1},{4,6},{6,4},{5,7},{7,5},{8,10},{10,8},{9,1... | collective-permute-start | bytes 786440 | tf_op jit(solution)/shard_map/ppermute | solution.py:408
  7.6 12.9 %all_to_all.10.recv_ref = bf16[32,8,256]{2,1,0:T(8,128)(2,1)S(1)} all-to-all(bf16[32,8,256]{2,1,0:T(8,128)(2,1)S(1)} %get-tuple-element.54), channel_id=1, replica_groups=mesh['hst'=8,'chip'=2,'core'=2] {'hst','chip','core'}, dimensions={0} | all-to-all | bytes 262144 | tf_op jit(solution)/shard_map/all_to_all | solution.py:450
  20.6 0.0 collective-permute-done.2.refs_0_
  20.6 0.2 merge.1
  20.8 0.3 collective-permute-start.4
  21.0 0.3 collective-permute-start.3
  21.3 0.0 collective-permute-done.lent_ref
  21.4 0.6 %early_one.1 = (f32[512,256]{1,0:T(8,128)S(1)}, f32[512,256]{1,0:T(8,128)S(1)}, f32[512,256]{1,0:T(8,128)S(1)}, bf16[640,256]{1,0:T(8,128)(2,1)S(1)}, bf16[256,256]{1,0:T(8,128)(2,1)S(1)}) custom-call(bf16[1280,256]{1,0:T(8,128)(2,1)S(1)} %get-tuple-element.42.adj_ref, bf16[1792,256]{1,0:T(8,128)(2,1)S(1)} %collective-permute-done.lent_ref, ...), custom_call_target="tpu_custom_call" | custom-call | flops 268435456 | bytes 262144 | tf_op jit(solution)/shard_map/early_one/pallas_call | solution.py:392
  21.9 0.4 %mid.1 = (f32[512,256]{1,0:T(8,128)S(1)}, f32[512,256]{1,0:T(8,128)S(1)}) custom-call(bf16[1280,256]{1,0:T(8,128)(2,1)S(1)} %get-tuple-element.42.adj_ref, bf16[1792,256]{1,0:T(8,128)(2,1)S(1)} %collective-permute-done.lent_ref, bf16[256,256]{1,0:T(8,128)(2,1)S(1)} %get-tuple-element.43.far_ref, bf16[256,256]{1,0:T(8,128)(2,1)S(1)} %get-tuple-element.46.far_two_ref.far_ref, ...), custom_call_target="tpu_custom_call" | custom-call | flops 100663296 | bytes 98304 | tf_op jit(solution)/shard_map/mid/pallas_call | solution.py:392
  22.3 0.1 collective-permute-done.3.nodes_ref
  22.5 0.0 collective-permute-done.4.shared_ref
  22.5 0.8 %middle.1 = (bf16[256,256]{1,0:T(8,128)(2,1)S(1)}, bf16[256,256]{1,0:T(8,128)(2,1)S(1)}, bf16[256,256]{1,0:T(8,128)(2,1)S(1)}, f32[256,256]{1,0:T(8,128)S(1)}, b...) custom-call(bf16[1280,256]{1,0:T(8,128)(2,1)S(1)} %get-tuple-element.42.adj_ref, ...), custom_call_target="tpu_custom_call" | custom-call | flops 402653184 | bytes 393216 | tf_op jit(solution)/shard_map/middle/pallas_call | solution.py:392
  23.2 0.5 %collective-permute-start.5 = (bf16[512,256]{1,0:T(8,128)(2,1)S(1)}, bf16[512,256]{1,0:T(8,128)(2,1)S(1)}, u32[]{:S(2)}, u32[]{:S(2)}) collective-permute-start(bf16[512,256]{1,0:T(8,128)(2,1)S(1)} %get-tuple-element.69), channel_id=1, source_target_pairs={{0,2},{2,0},{1,3},{3,1},{4,6},{6,4},{5,7},{7,5},{8,10},{10,8},{9,1... | collective-permute-start | bytes 786440 | tf_op jit(solution)/shard_map/ppermute | solution.py:408
  23.7 10.8 %all_to_all.11.recv_ref = bf16[32,8,256]{2,1,0:T(8,128)(2,1)S(1)} all-to-all(bf16[32,8,256]{2,1,0:T(8,128)(2,1)S(1)} %get-tuple-element.65), channel_id=1, replica_groups=mesh['hst'=8,'chip'=2,'core'=2] {'hst','chip','core'}, dimensions={0} | all-to-all | bytes 262144 | tf_op jit(solution)/shard_map/all_to_all | solution.py:450
  34.6 0.0 collective-permute-done.5.refs_0_
  34.6 0.3 there.1
  34.9 0.3 collective-permute-start.6
  35.1 1.0 %here.1 = (f32[256,256]{1,0:T(8,128)S(1)}, f32[256,256]{1,0:T(8,128)}) custom-call(bf16[1280,256]{1,0:T(8,128)(2,1)S(1)} %get-tuple-element.42.adj_ref, bf16[256,256]{1,0:T(8,128)(2,1)S(1)} %get-tuple-element.43.far_ref, bf16[256,256]{1,0:T(8,128)(2,1)S(1)} %get-tuple-element.64.sent_ref.value_ref, bf16[32,8,256]{2,1,0:T(8,128)(2,1)S(1)} %all_to_all.11.recv_ref, ...), custom_call_target="tpu_custom_call" | custom-call | flops 234881024 | bytes 229376 | tf_op jit(solution)/shard_map/here/pallas_call | solution.py:392
  36.2 0.1 collective-permute-done.6.there_ref
  36.3 0.7 %last.1 = bf16[256,256]{1,0:T(8,128)(2,1)} custom-call(f32[256,256]{1,0:T(8,128)S(1)} %get-tuple-element.70.here_ref, bf16[256,256]{1,0:T(8,128)(2,1)S(1)} %collective-permute-done.6.there_ref), custom_call_target="tpu_custom_call" | custom-call | tf_op jit(solution)/shard_map/last/pallas_call | solution.py:392
  (10 shorter events, 0.0 us)
Async XLA Ops:
  0.6 2.7 %copy-start = (bf16[256,256]{1,0:T(8,128)(2,1)S(1)}, bf16[256,256]{1,0:T(8,128)(2,1)}, u32[]{:S(2)}) copy-start(bf16[256,256]{1,0:T(8,128)(2,1)} %up_ref.1) | copy-start | bytes 393220
  0.6 2.7 %copy-start.5 = (bf16[256,256]{1,0:T(8,128)(2,1)S(1)}, bf16[256,256]{1,0:T(8,128)(2,1)}, u32[]{:S(2)}) copy-start(bf16[256,256]{1,0:T(8,128)(2,1)} %value_ref.3) | copy-start | bytes 393220
  0.7 2.7 %copy-start.1 = (bf16[256,256]{1,0:T(8,128)(2,1)S(1)}, bf16[256,256]{1,0:T(8,128)(2,1)}, u32[]{:S(2)}) copy-start(bf16[256,256]{1,0:T(8,128)(2,1)} %neigh_ref.7) | copy-start | bytes 393220
  2.8 1.8 %collective-permute-start.1 = (bf16[640,256]{1,0:T(8,128)(2,1)S(1)}, bf16[640,256]{1,0:T(8,128)(2,1)S(1)}, u32[]{:S(2)}, u32[]{:S(2)}) collective-permute-start(bf16[640,256]{1,0:T(8,128)(2,1)S(1)} %get-tuple-element.52), channel_id=1, source_target_pairs={{0,1},{1,0},{2,3},{3,2},{4,5},{5,4},{6,7},{7,6},{8,9},{9,8},{10,11... | collective-permute-start | bytes 983048 | tf_op jit(solution)/shard_map/ppermute | solution.py:408
  3.9 17.4 %collective-permute-start = (bf16[1792,256]{1,0:T(8,128)(2,1)S(1)}, bf16[1792,256]{1,0:T(8,128)(2,1)S(1)}, u32[]{:S(2)}, u32[]{:S(2)}) collective-permute-start(bf16[1792,256]{1,0:T(8,128)(2,1)S(1)} %get-tuple-element.44), channel_id=1, source_target_pairs={{0,1},{1,0},{2,3},{3,2},{4,5},{5,4},{6,7},{7,6},{8,9},{9,8},{10,11... | collective-permute-start | bytes 2752520 | tf_op jit(solution)/shard_map/ppermute | solution.py:408
  4.6 16.8 %copy-start.3 = (bf16[256,256]{1,0:T(8,128)(2,1)S(1)}, bf16[256,256]{1,0:T(8,128)(2,1)}, u32[]{:S(2)}) copy-start(bf16[256,256]{1,0:T(8,128)(2,1)} %weight_ref.3) | copy-start | bytes 393220
  4.6 16.8 %copy-start.4 = (bf16[256,256]{1,0:T(8,128)(2,1)S(1)}, bf16[256,256]{1,0:T(8,128)(2,1)}, u32[]{:S(2)}) copy-start(bf16[256,256]{1,0:T(8,128)(2,1)} %self_ref.3) | copy-start | bytes 393220
  4.6 16.8 %copy-start.6 = (f32[256]{0:T(256)S(1)}, f32[256]{0:T(256)}, u32[]{:S(2)}) copy-start(f32[256]{0:T(256)} %bias_ref.2) | copy-start | bytes 3076
  4.7 17.3 %copy-start.2 = (bf16[256,256]{1,0:T(8,128)(2,1)S(1)}, bf16[256,256]{1,0:T(8,128)(2,1)}, u32[]{:S(2)}) copy-start(bf16[256,256]{1,0:T(8,128)(2,1)} %neigh_two_ref.1) | copy-start | bytes 393220
  4.7 15.9 %collective-permute-start.2 = (bf16[512,256]{1,0:T(8,128)(2,1)S(1)}, bf16[512,256]{1,0:T(8,128)(2,1)S(1)}, u32[]{:S(2)}, u32[]{:S(2)}) collective-permute-start(bf16[512,256]{1,0:T(8,128)(2,1)S(1)} %get-tuple-element.57), channel_id=1, source_target_pairs={{0,2},{2,0},{1,3},{3,1},{4,6},{6,4},{5,7},{7,5},{8,10},{10,8},{9,1... | collective-permute-start | bytes 786440 | tf_op jit(solution)/shard_map/ppermute | solution.py:408
  20.8 1.7 %collective-permute-start.4 = (bf16[384,256]{1,0:T(8,128)(2,1)S(1)}, bf16[384,256]{1,0:T(8,128)(2,1)S(1)}, u32[]{:S(2)}, u32[]{:S(2)}) collective-permute-start(bf16[384,256]{1,0:T(8,128)(2,1)S(1)} %get-tuple-element.59.here_ref), channel_id=1, source_target_pairs={{0,1},{1,0},{2,3},{3,2},{4,5},{5,4},{6,7},{7,6},{8,9},{9,8},{10,11... | collective-permute-start | bytes 589832 | tf_op jit(solution)/shard_map/ppermute | solution.py:408
  21.0 1.4 %collective-permute-start.3 = (bf16[256,256]{1,0:T(8,128)(2,1)S(1)}, bf16[256,256]{1,0:T(8,128)(2,1)S(1)}, u32[]{:S(2)}, u32[]{:S(2)}) collective-permute-start(bf16[256,256]{1,0:T(8,128)(2,1)S(1)} %get-tuple-element.63), channel_id=1, source_target_pairs={{0,1},{1,0},{2,3},{3,2},{4,5},{5,4},{6,7},{7,6},{8,9},{9,8},{10,11... | collective-permute-start | bytes 393224 | tf_op jit(solution)/shard_map/ppermute | solution.py:408
  22.5 12.7 %copy-start.7 = (f32[256]{0:T(256)S(1)}, f32[256]{0:T(256)}, u32[]{:S(2)}) copy-start(f32[256]{0:T(256)} %bias_ref.3) | copy-start | bytes 3076
  23.2 11.3 %collective-permute-start.5 = (bf16[512,256]{1,0:T(8,128)(2,1)S(1)}, bf16[512,256]{1,0:T(8,128)(2,1)S(1)}, u32[]{:S(2)}, u32[]{:S(2)}) collective-permute-start(bf16[512,256]{1,0:T(8,128)(2,1)S(1)} %get-tuple-element.69), channel_id=1, source_target_pairs={{0,2},{2,0},{1,3},{3,1},{4,6},{6,4},{5,7},{7,5},{8,10},{10,8},{9,1... | collective-permute-start | bytes 786440 | tf_op jit(solution)/shard_map/ppermute | solution.py:408
  34.9 1.4 %collective-permute-start.6 = (bf16[256,256]{1,0:T(8,128)(2,1)S(1)}, bf16[256,256]{1,0:T(8,128)(2,1)S(1)}, u32[]{:S(2)}, u32[]{:S(2)}) collective-permute-start(bf16[256,256]{1,0:T(8,128)(2,1)S(1)} %there.1), channel_id=1, source_target_pairs={{0,1},{1,0},{2,3},{3,2},{4,5},{5,4},{6,7},{7,6},{8,9},{9,8},{10,11... | collective-permute-start | bytes 393224 | tf_op jit(solution)/shard_map/ppermute | solution.py:408

commit v26 on v24

--- a/solution.py
+++ b/solution.py
@@ -11,7 +11,7 @@
 BF16 = jnp.bfloat16
 MIB = 1024 * 1024
 CHUNKS = 8
-PARTS = 4
+PARTS = 8
 CORES = 2
 
 VMEM = pl.BlockSpec(memory_space=pltpu.VMEM)
@@ -80,6 +80,7 @@
     cot_hbm,
     give_ref,
     pick_ref,
+    cot_ref,
     *rest,
 ):
     accs, rest = rest[:PARTS], rest[PARTS:]
@@ -89,7 +90,6 @@
         rows_ref,
         send_ref,
         tile_buf,
-        cot_ref,
         square,
         far_t,
         col,
@@ -454,10 +454,10 @@
 
     far_t = pltpu.VMEM((chips * CORES * far, rows), BF16)
     sums = jax.ShapeDtypeStruct(((rows // blk) * (all_rows // blk), blk // PARTS, blk), F32)
-    give, pick, *sums = call(
+    give, pick, cot, *sums = call(
         functools.partial(prep_kernel, chips),
         "prep",
-        (shape(count, width), shape(far, rows)) + (sums,) * PARTS,
+        (shape(count, width), shape(far, rows), rows_shape) + (sums,) * PARTS,
         [HBM] * 6,
         [
             pltpu.with_memory_space_constraint(value, pltpu.HBM)
@@ -476,7 +476,6 @@
             pltpu.SMEM(tile_rows.shape, jnp.int32),
             pltpu.SMEM(send_list.shape, jnp.int32),
             pltpu.VMEM(tile_val.shape, BF16),
-            pltpu.VMEM(cotangent.shape, BF16),
             pltpu.VMEM((rows, rows), BF16),
             far_t,
             pltpu.VMEM((count, rows), BF16),
@@ -498,7 +497,7 @@
             far_shape,
         ),
         [VMEM] * (4 + PARTS),
-        (cotangent, features, pick, neigh_one, *sums),
+        (cot, features, pick, neigh_one, *sums),
         [far_t],
         flops=3 * square,
     )
@@ -531,7 +530,7 @@
             features,
             self_one,
             bias_one,
-            cotangent,
+            cot,
             self_two,
             neigh_one,
             sent,

time: 37.1 us -> 37.2 us (level)
  no operation moved by 1% of the time
where the time goes in v26:
time: 37.2 us; the launch traced here: 37 us
  blocking collectives  23.8 us (64%)
  Pallas kernels  6.73 us (18%)
  starting transfers between devices  4.64 us (12%)
  waiting for transfers between devices  1.07 us (3%)
  between operations  0.74 us (2%)
    all_to_all x2, blocking collectives, across(): lax.all_to_all(msg, ('hst', 'chip', 'core'), split_axis=0, concat_axis=0,...  23.8 us
    pallas_call x10, Pallas kernels, call(): pl.pallas_call(kernel, out_shape=out_shape, in_specs=in_specs, out_specs=...  6.73 us
    ppermute x6, starting transfers between devices, shift(): return lax.ppermute(value, axis, [(i, (i + k) % size) for i in range(size)])  4.64 us
    ppermute x6, waiting for transfers between devices, shift(): return lax.ppermute(value, axis, [(i, (i + k) % size) for i in range(size)])  1.07 us
  transfers between devices with their start and end apart: 6, of which 3 were waited for; matrix products, arithmetic and copies ran while one was open for 0% of the time, Pallas kernels for 8%

profile of v26, /device:TPU:0, one launch (start us, length us, event | category | flops | bytes accessed | tf_op | source)
XLA Modules:
  0.0 37.0 jit_solution(4754634354687631036)
XLA Ops:
  0.6 0.0 copy-start.3
  0.6 0.0 copy-start
  0.7 2.2 %prep.1 = (bf16[640,256]{1,0:T(8,128)(2,1)S(1)}, bf16[64,256]{1,0:T(8,128)(2,1)S(1)}, bf16[256,256]{1,0:T(8,128)(2,1)S(1)}, f32[20,16,128]{2,1,0:T(8,128)S(1)}, ...) custom-call(s32[64]{0:T(128)} %dst_hbm.1, ...), custom_call_target="tpu_custom_call" | custom-call | tf_op jit(solution)/shard_map/prep/pallas_call | solution.py:393
  2.9 0.5 %collective-permute-start.1 = (bf16[640,256]{1,0:T(8,128)(2,1)S(1)}, bf16[640,256]{1,0:T(8,128)(2,1)S(1)}, u32[]{:S(2)}, u32[]{:S(2)}) collective-permute-start(bf16[640,256]{1,0:T(8,128)(2,1)S(1)} %get-tuple-element.61), channel_id=1, source_target_pairs={{0,1},{1,0},{2,3},{3,2},{4,5},{5,4},{6,7},{7,6},{8,9},{9,8},{10,11... | collective-permute-start | bytes 983048 | tf_op jit(solution)/shard_map/ppermute | solution.py:409
  3.4 0.0 copy-done.3
  3.4 0.0 copy-done
  3.4 0.6 %rest.1 = (bf16[256,256]{1,0:T(8,128)(2,1)S(1)}, bf16[64,256]{1,0:T(8,128)(2,1)S(1)}, bf16[1280,256]{1,0:T(8,128)(2,1)S(1)}, bf16[640,256]{1,0:T(8,128)(2,1)S(1)...) custom-call(bf16[256,256]{1,0:T(8,128)(2,1)S(1)} %get-tuple-element., ...), custom_call_target="tpu_custom_call" | custom-call | flops 100663296 | bytes 98304 | tf_op jit(solution)/shard_map/rest/pallas_call | solution.py:393
  4.0 0.1 collective-permute-start
  4.1 0.5 %collective-permute-done.1.came_ref = bf16[640,256]{1,0:T(8,128)(2,1)S(1)} collective-permute-done((bf16[640,256]{1,0:T(8,128)(2,1)S(1)}, bf16[640,256]{1,0:T(8,128)(2,1)S(1)}, u32[]{:S(2)}, u32[]{:S(2)}) %collective-permute-start.1) | collective-permute-done | bytes 327712 | tf_op jit(solution)/shard_map/ppermute | solution.py:409
  4.6 0.1 core_sum.1
  4.7 0.0 copy-start.4
  4.7 2.9 %collective-permute-start.2 = (bf16[512,256]{1,0:T(8,128)(2,1)S(1)}, bf16[512,256]{1,0:T(8,128)(2,1)S(1)}, u32[]{:S(2)}, u32[]{:S(2)}) collective-permute-start(bf16[512,256]{1,0:T(8,128)(2,1)S(1)} %get-tuple-element.66), channel_id=1, source_target_pairs={{0,2},{2,0},{1,3},{3,1},{4,6},{6,4},{5,7},{7,5},{8,10},{10,8},{9,1... | collective-permute-start | bytes 786440 | tf_op jit(solution)/shard_map/ppermute | solution.py:409
  7.7 13.0 %all_to_all.10.recv_ref = bf16[32,8,256]{2,1,0:T(8,128)(2,1)S(1)} all-to-all(bf16[32,8,256]{2,1,0:T(8,128)(2,1)S(1)} %get-tuple-element.63), channel_id=1, replica_groups=mesh['hst'=8,'chip'=2,'core'=2] {'hst','chip','core'}, dimensions={0} | all-to-all | bytes 262144 | tf_op jit(solution)/shard_map/all_to_all | solution.py:452
  20.6 0.0 collective-permute-done.2.refs_0_
  20.6 0.2 merge.1
  20.8 0.3 collective-permute-start.3
  21.1 0.0 collective-permute-done.lent_ref
  21.1 0.0 copy-done.1
  21.1 0.0 copy-done.2
  21.1 0.0 copy-done.5
  21.1 0.6 %early_one.1 = (f32[512,256]{1,0:T(8,128)S(1)}, f32[512,256]{1,0:T(8,128)S(1)}, f32[512,256]{1,0:T(8,128)S(1)}, bf16[640,256]{1,0:T(8,128)(2,1)S(1)}, bf16[256,256]{1,0:T(8,128)(2,1)S(1)}) custom-call(bf16[1280,256]{1,0:T(8,128)(2,1)S(1)} %get-tuple-element.51.adj_ref, bf16[1792,256]{1,0:T(8,128)(2,1)S(1)} %collective-permute-done.lent_ref, ...), custom_call_target="tpu_custom_call" | custom-call | flops 268435456 | bytes 262144 | tf_op jit(solution)/shard_map/early_one/pallas_call | solution.py:393
  21.7 0.4 mid.1
  22.1 0.4 %collective-permute-done.3.shared_ref = bf16[640,256]{1,0:T(8,128)(2,1)S(1)} collective-permute-done((bf16[640,256]{1,0:T(8,128)(2,1)S(1)}, bf16[640,256]{1,0:T(8,128)(2,1)S(1)}, u32[]{:S(2)}, u32[]{:S(2)}) %collective-permute-start.3) | collective-permute-done | bytes 327712 | tf_op jit(solution)/shard_map/ppermute | solution.py:409
  22.5 0.8 %middle.1 = (bf16[256,256]{1,0:T(8,128)(2,1)S(1)}, bf16[256,256]{1,0:T(8,128)(2,1)S(1)}, bf16[256,256]{1,0:T(8,128)(2,1)S(1)}, f32[256,256]{1,0:T(8,128)S(1)}, b...) custom-call(bf16[1280,256]{1,0:T(8,128)(2,1)S(1)} %get-tuple-element.51.adj_ref, ...), custom_call_target="tpu_custom_call" | custom-call | flops 402653184 | bytes 393216 | tf_op jit(solution)/shard_map/middle/pallas_call | solution.py:393
  23.3 0.5 %collective-permute-start.4 = (bf16[512,256]{1,0:T(8,128)(2,1)S(1)}, bf16[512,256]{1,0:T(8,128)(2,1)S(1)}, u32[]{:S(2)}, u32[]{:S(2)}) collective-permute-start(bf16[512,256]{1,0:T(8,128)(2,1)S(1)} %get-tuple-element.77), channel_id=1, source_target_pairs={{0,2},{2,0},{1,3},{3,1},{4,6},{6,4},{5,7},{7,5},{8,10},{10,8},{9,1... | collective-permute-start | bytes 786440 | tf_op jit(solution)/shard_map/ppermute | solution.py:409
  23.8 10.8 %all_to_all.11.recv_ref = bf16[32,8,256]{2,1,0:T(8,128)(2,1)S(1)} all-to-all(bf16[32,8,256]{2,1,0:T(8,128)(2,1)S(1)} %get-tuple-element.73), channel_id=1, replica_groups=mesh['hst'=8,'chip'=2,'core'=2] {'hst','chip','core'}, dimensions={0} | all-to-all | bytes 262144 | tf_op jit(solution)/shard_map/all_to_all | solution.py:452
  34.6 0.0 collective-permute-done.4.refs_0_
  34.6 0.3 there.1
  34.9 0.3 collective-permute-start.5
  35.2 1.0 %here.1 = (f32[256,256]{1,0:T(8,128)S(1)}, f32[256,256]{1,0:T(8,128)}) custom-call(bf16[1280,256]{1,0:T(8,128)(2,1)S(1)} %get-tuple-element.51.adj_ref, bf16[256,256]{1,0:T(8,128)(2,1)S(1)} %get-tuple-element.52.far_ref, bf16[256,256]{1,0:T(8,128)(2,1)S(1)} %get-tuple-element.72.sent_ref.value_ref, bf16[32,8,256]{2,1,0:T(8,128)(2,1)S(1)} %all_to_all.11.recv_ref, ...), custom_call_target="tpu_custom_call" | custom-call | flops 234881024 | bytes 229376 | tf_op jit(solution)/shard_map/here/pallas_call | solution.py:393
  36.2 0.1 collective-permute-done.5.there_ref
  36.3 0.7 %last.1 = bf16[256,256]{1,0:T(8,128)(2,1)} custom-call(f32[256,256]{1,0:T(8,128)S(1)} %get-tuple-element.78.here_ref, bf16[256,256]{1,0:T(8,128)(2,1)S(1)} %collective-permute-done.5.there_ref), custom_call_target="tpu_custom_call" | custom-call | tf_op jit(solution)/shard_map/last/pallas_call | solution.py:393
  (6 shorter events, 0.0 us)
Async XLA Ops:
  0.6 2.7 %copy-start.3 = (bf16[256,256]{1,0:T(8,128)(2,1)S(1)}, bf16[256,256]{1,0:T(8,128)(2,1)}, u32[]{:S(2)}) copy-start(bf16[256,256]{1,0:T(8,128)(2,1)} %value_ref.3) | copy-start | bytes 393220
  0.6 2.7 %copy-start = (bf16[256,256]{1,0:T(8,128)(2,1)S(1)}, bf16[256,256]{1,0:T(8,128)(2,1)}, u32[]{:S(2)}) copy-start(bf16[256,256]{1,0:T(8,128)(2,1)} %neigh_ref.7) | copy-start | bytes 393220
  2.9 1.8 %collective-permute-start.1 = (bf16[640,256]{1,0:T(8,128)(2,1)S(1)}, bf16[640,256]{1,0:T(8,128)(2,1)S(1)}, u32[]{:S(2)}, u32[]{:S(2)}) collective-permute-start(bf16[640,256]{1,0:T(8,128)(2,1)S(1)} %get-tuple-element.61), channel_id=1, source_target_pairs={{0,1},{1,0},{2,3},{3,2},{4,5},{5,4},{6,7},{7,6},{8,9},{9,8},{10,11... | collective-permute-start | bytes 983048 | tf_op jit(solution)/shard_map/ppermute | solution.py:409
  4.0 17.1 %collective-permute-start = (bf16[1792,256]{1,0:T(8,128)(2,1)S(1)}, bf16[1792,256]{1,0:T(8,128)(2,1)S(1)}, u32[]{:S(2)}, u32[]{:S(2)}) collective-permute-start(bf16[1792,256]{1,0:T(8,128)(2,1)S(1)} %get-tuple-element.53), channel_id=1, source_target_pairs={{0,1},{1,0},{2,3},{3,2},{4,5},{5,4},{6,7},{7,6},{8,9},{9,8},{10,11... | collective-permute-start | bytes 2752520 | tf_op jit(solution)/shard_map/ppermute | solution.py:409
  4.6 16.5 %copy-start.1 = (bf16[256,256]{1,0:T(8,128)(2,1)S(1)}, bf16[256,256]{1,0:T(8,128)(2,1)}, u32[]{:S(2)}) copy-start(bf16[256,256]{1,0:T(8,128)(2,1)} %weight_ref.3) | copy-start | bytes 393220
  4.6 16.5 %copy-start.2 = (bf16[256,256]{1,0:T(8,128)(2,1)S(1)}, bf16[256,256]{1,0:T(8,128)(2,1)}, u32[]{:S(2)}) copy-start(bf16[256,256]{1,0:T(8,128)(2,1)} %self_ref.3) | copy-start | bytes 393220
  4.6 16.5 %copy-start.5 = (f32[256]{0:T(256)S(1)}, f32[256]{0:T(256)}, u32[]{:S(2)}) copy-start(f32[256]{0:T(256)} %bias_ref.2) | copy-start | bytes 3076
  4.7 17.0 %copy-start.4 = (bf16[256,256]{1,0:T(8,128)(2,1)S(1)}, bf16[256,256]{1,0:T(8,128)(2,1)}, u32[]{:S(2)}) copy-start(bf16[256,256]{1,0:T(8,128)(2,1)} %neigh_two_ref.1) | copy-start | bytes 393220
  4.7 15.9 %collective-permute-start.2 = (bf16[512,256]{1,0:T(8,128)(2,1)S(1)}, bf16[512,256]{1,0:T(8,128)(2,1)S(1)}, u32[]{:S(2)}, u32[]{:S(2)}) collective-permute-start(bf16[512,256]{1,0:T(8,128)(2,1)S(1)} %get-tuple-element.66), channel_id=1, source_target_pairs={{0,2},{2,0},{1,3},{3,1},{4,6},{6,4},{5,7},{7,5},{8,10},{10,8},{9,1... | collective-permute-start | bytes 786440 | tf_op jit(solution)/shard_map/ppermute | solution.py:409
  20.8 1.7 %collective-permute-start.3 = (bf16[640,256]{1,0:T(8,128)(2,1)S(1)}, bf16[640,256]{1,0:T(8,128)(2,1)S(1)}, u32[]{:S(2)}, u32[]{:S(2)}) collective-permute-start(bf16[640,256]{1,0:T(8,128)(2,1)S(1)} %get-tuple-element.68.here_ref), channel_id=1, source_target_pairs={{0,1},{1,0},{2,3},{3,2},{4,5},{5,4},{6,7},{7,6},{8,9},{9,8},{10,11... | collective-permute-start | bytes 983048 | tf_op jit(solution)/shard_map/ppermute | solution.py:409
  22.5 12.7 %copy-start.6 = (f32[256]{0:T(256)S(1)}, f32[256]{0:T(256)}, u32[]{:S(2)}) copy-start(f32[256]{0:T(256)} %bias_ref.3) | copy-start | bytes 3076
  23.3 11.3 %collective-permute-start.4 = (bf16[512,256]{1,0:T(8,128)(2,1)S(1)}, bf16[512,256]{1,0:T(8,128)(2,1)S(1)}, u32[]{:S(2)}, u32[]{:S(2)}) collective-permute-start(bf16[512,256]{1,0:T(8,128)(2,1)S(1)} %get-tuple-element.77), channel_id=1, source_target_pairs={{0,2},{2,0},{1,3},{3,1},{4,6},{6,4},{5,7},{7,5},{8,10},{10,8},{9,1... | collective-permute-start | bytes 786440 | tf_op jit(solution)/shard_map/ppermute | solution.py:409
  34.9 1.4 %collective-permute-start.5 = (bf16[256,256]{1,0:T(8,128)(2,1)S(1)}, bf16[256,256]{1,0:T(8,128)(2,1)S(1)}, u32[]{:S(2)}, u32[]{:S(2)}) collective-permute-start(bf16[256,256]{1,0:T(8,128)(2,1)S(1)} %there.1), channel_id=1, source_target_pairs={{0,1},{1,0},{2,3},{3,2},{4,5},{5,4},{6,7},{7,6},{8,9},{9,8},{10,11... | collective-permute-start | bytes 393224 | tf_op jit(solution)/shard_map/ppermute | solution.py:409

commit v27 on v26

--- a/solution.py
+++ b/solution.py
@@ -11,7 +11,7 @@
 BF16 = jnp.bfloat16
 MIB = 1024 * 1024
 CHUNKS = 8
-PARTS = 8
+PARTS = 4
 CORES = 2
 
 VMEM = pl.BlockSpec(memory_space=pltpu.VMEM)

time: 37.2 us -> 37.1 us (level)
  no operation moved by 1% of the time
where the time goes in v27:
time: 37.1 us; the launch traced here: 36.9 us
  blocking collectives  23.8 us (64%)
  Pallas kernels  6.67 us (18%)
  starting transfers between devices  4.64 us (13%)
  waiting for transfers between devices  1.06 us (3%)
  between operations  0.74 us (2%)
    all_to_all x2, blocking collectives, across(): lax.all_to_all(msg, ('hst', 'chip', 'core'), split_axis=0, concat_axis=0,...  23.8 us
    pallas_call x10, Pallas kernels, call(): pl.pallas_call(kernel, out_shape=out_shape, in_specs=in_specs, out_specs=...  6.67 us
    ppermute x6, starting transfers between devices, shift(): return lax.ppermute(value, axis, [(i, (i + k) % size) for i in range(size)])  4.64 us
    ppermute x6, waiting for transfers between devices, shift(): return lax.ppermute(value, axis, [(i, (i + k) % size) for i in range(size)])  1.06 us
  transfers between devices with their start and end apart: 6, of which 3 were waited for; matrix products, arithmetic and copies ran while one was open for 0% of the time, Pallas kernels for 8%

profile of v27, /device:TPU:0, one launch (start us, length us, event | category | flops | bytes accessed | tf_op | source)
XLA Modules:
  0.0 36.9 jit_solution(516466359152453976)
XLA Ops:
  0.6 0.0 copy-start.3
  0.6 0.0 copy-start
  0.7 2.1 %prep.1 = (bf16[640,256]{1,0:T(8,128)(2,1)S(1)}, bf16[64,256]{1,0:T(8,128)(2,1)S(1)}, bf16[256,256]{1,0:T(8,128)(2,1)S(1)}, f32[20,32,128]{2,1,0:T(8,128)S(1)}, ...) custom-call(s32[64]{0:T(128)} %dst_hbm.1, s32[64]{0:T(128)} %src_hbm.1, ...), custom_call_target="tpu_custom_call" | custom-call | tf_op jit(solution)/shard_map/prep/pallas_call | solution.py:393
  2.8 0.5 %collective-permute-start.1 = (bf16[640,256]{1,0:T(8,128)(2,1)S(1)}, bf16[640,256]{1,0:T(8,128)(2,1)S(1)}, u32[]{:S(2)}, u32[]{:S(2)}) collective-permute-start(bf16[640,256]{1,0:T(8,128)(2,1)S(1)} %get-tuple-element.53), channel_id=1, source_target_pairs={{0,1},{1,0},{2,3},{3,2},{4,5},{5,4},{6,7},{7,6},{8,9},{9,8},{10,11... | collective-permute-start | bytes 983048 | tf_op jit(solution)/shard_map/ppermute | solution.py:409
  3.3 0.0 copy-done.3
  3.3 0.0 copy-done
  3.3 0.6 %rest.1 = (bf16[256,256]{1,0:T(8,128)(2,1)S(1)}, bf16[64,256]{1,0:T(8,128)(2,1)S(1)}, bf16[1280,256]{1,0:T(8,128)(2,1)S(1)}, bf16[640,256]{1,0:T(8,128)(2,1)S(1)...) custom-call(bf16[256,256]{1,0:T(8,128)(2,1)S(1)} %get-tuple-element., ...), custom_call_target="tpu_custom_call" | custom-call | flops 100663296 | bytes 98304 | tf_op jit(solution)/shard_map/rest/pallas_call | solution.py:393
  3.9 0.1 collective-permute-start
  4.0 0.5 %collective-permute-done.1.came_ref = bf16[640,256]{1,0:T(8,128)(2,1)S(1)} collective-permute-done((bf16[640,256]{1,0:T(8,128)(2,1)S(1)}, bf16[640,256]{1,0:T(8,128)(2,1)S(1)}, u32[]{:S(2)}, u32[]{:S(2)}) %collective-permute-start.1) | collective-permute-done | bytes 327712 | tf_op jit(solution)/shard_map/ppermute | solution.py:409
  4.6 0.1 core_sum.1
  4.7 0.0 copy-start.4
  4.7 2.9 %collective-permute-start.2 = (bf16[512,256]{1,0:T(8,128)(2,1)S(1)}, bf16[512,256]{1,0:T(8,128)(2,1)S(1)}, u32[]{:S(2)}, u32[]{:S(2)}) collective-permute-start(bf16[512,256]{1,0:T(8,128)(2,1)S(1)} %get-tuple-element.58), channel_id=1, source_target_pairs={{0,2},{2,0},{1,3},{3,1},{4,6},{6,4},{5,7},{7,5},{8,10},{10,8},{9,1... | collective-permute-start | bytes 786440 | tf_op jit(solution)/shard_map/ppermute | solution.py:409
  7.6 12.9 %all_to_all.10.recv_ref = bf16[32,8,256]{2,1,0:T(8,128)(2,1)S(1)} all-to-all(bf16[32,8,256]{2,1,0:T(8,128)(2,1)S(1)} %get-tuple-element.55), channel_id=1, replica_groups=mesh['hst'=8,'chip'=2,'core'=2] {'hst','chip','core'}, dimensions={0} | all-to-all | bytes 262144 | tf_op jit(solution)/shard_map/all_to_all | solution.py:452
  20.5 0.0 collective-permute-done.2.refs_0_
  20.5 0.2 merge.1
  20.7 0.3 collective-permute-start.3
  21.0 0.0 collective-permute-done.lent_ref
  21.0 0.0 copy-done.1
  21.0 0.0 copy-done.2
  21.0 0.6 %early_one.1 = (f32[512,256]{1,0:T(8,128)S(1)}, f32[512,256]{1,0:T(8,128)S(1)}, f32[512,256]{1,0:T(8,128)S(1)}, bf16[640,256]{1,0:T(8,128)(2,1)S(1)}, bf16[256,256]{1,0:T(8,128)(2,1)S(1)}) custom-call(bf16[1280,256]{1,0:T(8,128)(2,1)S(1)} %get-tuple-element.43.adj_ref, bf16[1792,256]{1,0:T(8,128)(2,1)S(1)} %collective-permute-done.lent_ref, ...), custom_call_target="tpu_custom_call" | custom-call | flops 268435456 | bytes 262144 | tf_op jit(solution)/shard_map/early_one/pallas_call | solution.py:393
  21.6 0.4 %mid.1 = (f32[512,256]{1,0:T(8,128)S(1)}, f32[512,256]{1,0:T(8,128)S(1)}) custom-call(bf16[1280,256]{1,0:T(8,128)(2,1)S(1)} %get-tuple-element.43.adj_ref, bf16[1792,256]{1,0:T(8,128)(2,1)S(1)} %collective-permute-done.lent_ref, bf16[256,256]{1,0:T(8,128)(2,1)S(1)} %get-tuple-element.44.far_ref, bf16[256,256]{1,0:T(8,128)(2,1)S(1)} %get-tuple-element.47.far_two_ref.far_ref, ...), custom_call_target="tpu_custom_call" | custom-call | flops 100663296 | bytes 98304 | tf_op jit(solution)/shard_map/mid/pallas_call | solution.py:393
  22.0 0.4 %collective-permute-done.3.shared_ref = bf16[640,256]{1,0:T(8,128)(2,1)S(1)} collective-permute-done((bf16[640,256]{1,0:T(8,128)(2,1)S(1)}, bf16[640,256]{1,0:T(8,128)(2,1)S(1)}, u32[]{:S(2)}, u32[]{:S(2)}) %collective-permute-start.3) | collective-permute-done | bytes 327712 | tf_op jit(solution)/shard_map/ppermute | solution.py:409
  22.4 0.8 %middle.1 = (bf16[256,256]{1,0:T(8,128)(2,1)S(1)}, bf16[256,256]{1,0:T(8,128)(2,1)S(1)}, bf16[256,256]{1,0:T(8,128)(2,1)S(1)}, f32[256,256]{1,0:T(8,128)S(1)}, b...) custom-call(bf16[1280,256]{1,0:T(8,128)(2,1)S(1)} %get-tuple-element.43.adj_ref, ...), custom_call_target="tpu_custom_call" | custom-call | flops 402653184 | bytes 393216 | tf_op jit(solution)/shard_map/middle/pallas_call | solution.py:393
  23.2 0.5 %collective-permute-start.4 = (bf16[512,256]{1,0:T(8,128)(2,1)S(1)}, bf16[512,256]{1,0:T(8,128)(2,1)S(1)}, u32[]{:S(2)}, u32[]{:S(2)}) collective-permute-start(bf16[512,256]{1,0:T(8,128)(2,1)S(1)} %get-tuple-element.69), channel_id=1, source_target_pairs={{0,2},{2,0},{1,3},{3,1},{4,6},{6,4},{5,7},{7,5},{8,10},{10,8},{9,1... | collective-permute-start | bytes 786440 | tf_op jit(solution)/shard_map/ppermute | solution.py:409
  23.7 10.8 %all_to_all.11.recv_ref = bf16[32,8,256]{2,1,0:T(8,128)(2,1)S(1)} all-to-all(bf16[32,8,256]{2,1,0:T(8,128)(2,1)S(1)} %get-tuple-element.65), channel_id=1, replica_groups=mesh['hst'=8,'chip'=2,'core'=2] {'hst','chip','core'}, dimensions={0} | all-to-all | bytes 262144 | tf_op jit(solution)/shard_map/all_to_all | solution.py:452
  34.6 0.0 collective-permute-done.4.refs_0_
  34.6 0.3 there.1
  34.8 0.3 collective-permute-start.5
  35.1 0.0 copy-done.6
  35.1 1.0 %here.1 = (f32[256,256]{1,0:T(8,128)S(1)}, f32[256,256]{1,0:T(8,128)}) custom-call(bf16[1280,256]{1,0:T(8,128)(2,1)S(1)} %get-tuple-element.43.adj_ref, bf16[256,256]{1,0:T(8,128)(2,1)S(1)} %get-tuple-element.44.far_ref, bf16[256,256]{1,0:T(8,128)(2,1)S(1)} %get-tuple-element.64.sent_ref.value_ref, bf16[32,8,256]{2,1,0:T(8,128)(2,1)S(1)} %all_to_all.11.recv_ref, ...), custom_call_target="tpu_custom_call" | custom-call | flops 234881024 | bytes 229376 | tf_op jit(solution)/shard_map/here/pallas_call | solution.py:393
  36.2 0.1 collective-permute-done.5.there_ref
  36.2 0.7 %last.1 = bf16[256,256]{1,0:T(8,128)(2,1)} custom-call(f32[256,256]{1,0:T(8,128)S(1)} %get-tuple-element.70.here_ref, bf16[256,256]{1,0:T(8,128)(2,1)S(1)} %collective-permute-done.5.there_ref), custom_call_target="tpu_custom_call" | custom-call | tf_op jit(solution)/shard_map/last/pallas_call | solution.py:393
  (6 shorter events, 0.0 us)
Async XLA Ops:
  0.6 2.7 %copy-start.3 = (bf16[256,256]{1,0:T(8,128)(2,1)S(1)}, bf16[256,256]{1,0:T(8,128)(2,1)}, u32[]{:S(2)}) copy-start(bf16[256,256]{1,0:T(8,128)(2,1)} %value_ref.3) | copy-start | bytes 393220
  0.6 2.7 %copy-start = (bf16[256,256]{1,0:T(8,128)(2,1)S(1)}, bf16[256,256]{1,0:T(8,128)(2,1)}, u32[]{:S(2)}) copy-start(bf16[256,256]{1,0:T(8,128)(2,1)} %neigh_ref.7) | copy-start | bytes 393220
  2.8 1.8 %collective-permute-start.1 = (bf16[640,256]{1,0:T(8,128)(2,1)S(1)}, bf16[640,256]{1,0:T(8,128)(2,1)S(1)}, u32[]{:S(2)}, u32[]{:S(2)}) collective-permute-start(bf16[640,256]{1,0:T(8,128)(2,1)S(1)} %get-tuple-element.53), channel_id=1, source_target_pairs={{0,1},{1,0},{2,3},{3,2},{4,5},{5,4},{6,7},{7,6},{8,9},{9,8},{10,11... | collective-permute-start | bytes 983048 | tf_op jit(solution)/shard_map/ppermute | solution.py:409
  3.9 17.1 %collective-permute-start = (bf16[1792,256]{1,0:T(8,128)(2,1)S(1)}, bf16[1792,256]{1,0:T(8,128)(2,1)S(1)}, u32[]{:S(2)}, u32[]{:S(2)}) collective-permute-start(bf16[1792,256]{1,0:T(8,128)(2,1)S(1)} %get-tuple-element.45), channel_id=1, source_target_pairs={{0,1},{1,0},{2,3},{3,2},{4,5},{5,4},{6,7},{7,6},{8,9},{9,8},{10,11... | collective-permute-start | bytes 2752520 | tf_op jit(solution)/shard_map/ppermute | solution.py:409
  4.6 16.5 %copy-start.1 = (bf16[256,256]{1,0:T(8,128)(2,1)S(1)}, bf16[256,256]{1,0:T(8,128)(2,1)}, u32[]{:S(2)}) copy-start(bf16[256,256]{1,0:T(8,128)(2,1)} %weight_ref.3) | copy-start | bytes 393220
  4.6 16.5 %copy-start.2 = (bf16[256,256]{1,0:T(8,128)(2,1)S(1)}, bf16[256,256]{1,0:T(8,128)(2,1)}, u32[]{:S(2)}) copy-start(bf16[256,256]{1,0:T(8,128)(2,1)} %self_ref.3) | copy-start | bytes 393220
  4.6 16.5 %copy-start.5 = (f32[256]{0:T(256)S(1)}, f32[256]{0:T(256)}, u32[]{:S(2)}) copy-start(f32[256]{0:T(256)} %bias_ref.2) | copy-start | bytes 3076
  4.7 16.9 %copy-start.4 = (bf16[256,256]{1,0:T(8,128)(2,1)S(1)}, bf16[256,256]{1,0:T(8,128)(2,1)}, u32[]{:S(2)}) copy-start(bf16[256,256]{1,0:T(8,128)(2,1)} %neigh_two_ref.1) | copy-start | bytes 393220
  4.7 15.9 %collective-permute-start.2 = (bf16[512,256]{1,0:T(8,128)(2,1)S(1)}, bf16[512,256]{1,0:T(8,128)(2,1)S(1)}, u32[]{:S(2)}, u32[]{:S(2)}) collective-permute-start(bf16[512,256]{1,0:T(8,128)(2,1)S(1)} %get-tuple-element.58), channel_id=1, source_target_pairs={{0,2},{2,0},{1,3},{3,1},{4,6},{6,4},{5,7},{7,5},{8,10},{10,8},{9,1... | collective-permute-start | bytes 786440 | tf_op jit(solution)/shard_map/ppermute | solution.py:409
  20.7 1.7 %collective-permute-start.3 = (bf16[640,256]{1,0:T(8,128)(2,1)S(1)}, bf16[640,256]{1,0:T(8,128)(2,1)S(1)}, u32[]{:S(2)}, u32[]{:S(2)}) collective-permute-start(bf16[640,256]{1,0:T(8,128)(2,1)S(1)} %get-tuple-element.60.here_ref), channel_id=1, source_target_pairs={{0,1},{1,0},{2,3},{3,2},{4,5},{5,4},{6,7},{7,6},{8,9},{9,8},{10,11... | collective-permute-start | bytes 983048 | tf_op jit(solution)/shard_map/ppermute | solution.py:409
  22.4 12.7 %copy-start.6 = (f32[256]{0:T(256)S(1)}, f32[256]{0:T(256)}, u32[]{:S(2)}) copy-start(f32[256]{0:T(256)} %bias_ref.3) | copy-start | bytes 3076
  23.2 11.4 %collective-permute-start.4 = (bf16[512,256]{1,0:T(8,128)(2,1)S(1)}, bf16[512,256]{1,0:T(8,128)(2,1)S(1)}, u32[]{:S(2)}, u32[]{:S(2)}) collective-permute-start(bf16[512,256]{1,0:T(8,128)(2,1)S(1)} %get-tuple-element.69), channel_id=1, source_target_pairs={{0,2},{2,0},{1,3},{3,1},{4,6},{6,4},{5,7},{7,5},{8,10},{10,8},{9,1... | collective-permute-start | bytes 786440 | tf_op jit(solution)/shard_map/ppermute | solution.py:409
  34.8 1.4 %collective-permute-start.5 = (bf16[256,256]{1,0:T(8,128)(2,1)S(1)}, bf16[256,256]{1,0:T(8,128)(2,1)S(1)}, u32[]{:S(2)}, u32[]{:S(2)}) collective-permute-start(bf16[256,256]{1,0:T(8,128)(2,1)S(1)} %there.1), channel_id=1, source_target_pairs={{0,1},{1,0},{2,3},{3,2},{4,5},{5,4},{6,7},{7,6},{8,9},{9,8},{10,11... | collective-permute-start | bytes 393224 | tf_op jit(solution)/shard_map/ppermute | solution.py:409

commit v28 on v27

--- a/solution.py
+++ b/solution.py
@@ -97,7 +97,7 @@
     ) = rest
     tiles, blk = tile_buf.shape[0], tile_buf.shape[1]
     each = tiles // CHUNKS
-    cuts = [c * each for c in range(CHUNKS)] + [tiles - each // 2, tiles]
+    cuts = [c * each for c in range(CHUNKS)] + [tiles]
     chunks = [
         (tile_hbm.at[pl.ds(low, high - low)], tile_buf.at[pl.ds(low, high - low)])
         for low, high in zip(cuts, cuts[1:])
@@ -479,7 +479,7 @@
             pltpu.VMEM((rows, rows), BF16),
             far_t,
             pltpu.VMEM((count, rows), BF16),
-            pltpu.SemaphoreType.DMA((6 + CHUNKS,)),
+            pltpu.SemaphoreType.DMA((5 + CHUNKS,)),
         ],
     )
     came = shift(give, "core", 1)

time: 37.1 us -> 37.1 us (level)
  no operation moved by 1% of the time
where the time goes in v28:
time: 37.1 us; the launch traced here: 36.9 us
  blocking collectives  23.8 us (64%)
  Pallas kernels  6.65 us (18%)
  starting transfers between devices  4.64 us (13%)
  waiting for transfers between devices  1.07 us (3%)
  between operations  0.74 us (2%)
    all_to_all x2, blocking collectives, across(): lax.all_to_all(msg, ('hst', 'chip', 'core'), split_axis=0, concat_axis=0,...  23.8 us
    pallas_call x10, Pallas kernels, call(): pl.pallas_call(kernel, out_shape=out_shape, in_specs=in_specs, out_specs=...  6.65 us
    ppermute x6, starting transfers between devices, shift(): return lax.ppermute(value, axis, [(i, (i + k) % size) for i in range(size)])  4.64 us
    ppermute x6, waiting for transfers between devices, shift(): return lax.ppermute(value, axis, [(i, (i + k) % size) for i in range(size)])  1.07 us
  transfers between devices with their start and end apart: 6, of which 3 were waited for; matrix products, arithmetic and copies ran while one was open for 0% of the time, Pallas kernels for 8%

profile of v28, /device:TPU:0, one launch (start us, length us, event | category | flops | bytes accessed | tf_op | source)
XLA Modules:
  0.0 36.9 jit_solution(10985361277855699467)
XLA Ops:
  0.6 0.0 copy-start.3
  0.6 0.0 copy-start
  0.7 2.1 %prep.1 = (bf16[640,256]{1,0:T(8,128)(2,1)S(1)}, bf16[64,256]{1,0:T(8,128)(2,1)S(1)}, bf16[256,256]{1,0:T(8,128)(2,1)S(1)}, f32[20,32,128]{2,1,0:T(8,128)S(1)}, ...) custom-call(s32[64]{0:T(128)} %dst_hbm.1, s32[64]{0:T(128)} %src_hbm.1, ...), custom_call_target="tpu_custom_call" | custom-call | tf_op jit(solution)/shard_map/prep/pallas_call | solution.py:393
  2.8 0.5 %collective-permute-start.1 = (bf16[640,256]{1,0:T(8,128)(2,1)S(1)}, bf16[640,256]{1,0:T(8,128)(2,1)S(1)}, u32[]{:S(2)}, u32[]{:S(2)}) collective-permute-start(bf16[640,256]{1,0:T(8,128)(2,1)S(1)} %get-tuple-element.53), channel_id=1, source_target_pairs={{0,1},{1,0},{2,3},{3,2},{4,5},{5,4},{6,7},{7,6},{8,9},{9,8},{10,11... | collective-permute-start | bytes 983048 | tf_op jit(solution)/shard_map/ppermute | solution.py:409
  3.3 0.0 copy-done.3
  3.3 0.0 copy-done
  3.3 0.6 %rest.1 = (bf16[256,256]{1,0:T(8,128)(2,1)S(1)}, bf16[64,256]{1,0:T(8,128)(2,1)S(1)}, bf16[1280,256]{1,0:T(8,128)(2,1)S(1)}, bf16[640,256]{1,0:T(8,128)(2,1)S(1)...) custom-call(bf16[256,256]{1,0:T(8,128)(2,1)S(1)} %get-tuple-element., ...), custom_call_target="tpu_custom_call" | custom-call | flops 100663296 | bytes 98304 | tf_op jit(solution)/shard_map/rest/pallas_call | solution.py:393
  3.9 0.1 collective-permute-start
  4.0 0.5 %collective-permute-done.1.came_ref = bf16[640,256]{1,0:T(8,128)(2,1)S(1)} collective-permute-done((bf16[640,256]{1,0:T(8,128)(2,1)S(1)}, bf16[640,256]{1,0:T(8,128)(2,1)S(1)}, u32[]{:S(2)}, u32[]{:S(2)}) %collective-permute-start.1) | collective-permute-done | bytes 327712 | tf_op jit(solution)/shard_map/ppermute | solution.py:409
  4.6 0.1 core_sum.1
  4.6 0.0 copy-start.4
  4.7 2.9 %collective-permute-start.2 = (bf16[512,256]{1,0:T(8,128)(2,1)S(1)}, bf16[512,256]{1,0:T(8,128)(2,1)S(1)}, u32[]{:S(2)}, u32[]{:S(2)}) collective-permute-start(bf16[512,256]{1,0:T(8,128)(2,1)S(1)} %get-tuple-element.58), channel_id=1, source_target_pairs={{0,2},{2,0},{1,3},{3,1},{4,6},{6,4},{5,7},{7,5},{8,10},{10,8},{9,1... | collective-permute-start | bytes 786440 | tf_op jit(solution)/shard_map/ppermute | solution.py:409
  7.6 12.9 %all_to_all.10.recv_ref = bf16[32,8,256]{2,1,0:T(8,128)(2,1)S(1)} all-to-all(bf16[32,8,256]{2,1,0:T(8,128)(2,1)S(1)} %get-tuple-element.55), channel_id=1, replica_groups=mesh['hst'=8,'chip'=2,'core'=2] {'hst','chip','core'}, dimensions={0} | all-to-all | bytes 262144 | tf_op jit(solution)/shard_map/all_to_all | solution.py:452
  20.5 0.0 collective-permute-done.2.refs_0_
  20.5 0.2 merge.1
  20.7 0.3 collective-permute-start.3
  21.0 0.0 collective-permute-done.lent_ref
  21.0 0.0 copy-done.1
  21.0 0.0 copy-done.2
  21.0 0.0 copy-done.5
  21.0 0.6 %early_one.1 = (f32[512,256]{1,0:T(8,128)S(1)}, f32[512,256]{1,0:T(8,128)S(1)}, f32[512,256]{1,0:T(8,128)S(1)}, bf16[640,256]{1,0:T(8,128)(2,1)S(1)}, bf16[256,256]{1,0:T(8,128)(2,1)S(1)}) custom-call(bf16[1280,256]{1,0:T(8,128)(2,1)S(1)} %get-tuple-element.43.adj_ref, bf16[1792,256]{1,0:T(8,128)(2,1)S(1)} %collective-permute-done.lent_ref, ...), custom_call_target="tpu_custom_call" | custom-call | flops 268435456 | bytes 262144 | tf_op jit(solution)/shard_map/early_one/pallas_call | solution.py:393
  21.6 0.4 %mid.1 = (f32[512,256]{1,0:T(8,128)S(1)}, f32[512,256]{1,0:T(8,128)S(1)}) custom-call(bf16[1280,256]{1,0:T(8,128)(2,1)S(1)} %get-tuple-element.43.adj_ref, bf16[1792,256]{1,0:T(8,128)(2,1)S(1)} %collective-permute-done.lent_ref, bf16[256,256]{1,0:T(8,128)(2,1)S(1)} %get-tuple-element.44.far_ref, bf16[256,256]{1,0:T(8,128)(2,1)S(1)} %get-tuple-element.47.far_two_ref.far_ref, ...), custom_call_target="tpu_custom_call" | custom-call | flops 100663296 | bytes 98304 | tf_op jit(solution)/shard_map/mid/pallas_call | solution.py:393
  22.0 0.4 %collective-permute-done.3.shared_ref = bf16[640,256]{1,0:T(8,128)(2,1)S(1)} collective-permute-done((bf16[640,256]{1,0:T(8,128)(2,1)S(1)}, bf16[640,256]{1,0:T(8,128)(2,1)S(1)}, u32[]{:S(2)}, u32[]{:S(2)}) %collective-permute-start.3) | collective-permute-done | bytes 327712 | tf_op jit(solution)/shard_map/ppermute | solution.py:409
  22.4 0.8 %middle.1 = (bf16[256,256]{1,0:T(8,128)(2,1)S(1)}, bf16[256,256]{1,0:T(8,128)(2,1)S(1)}, bf16[256,256]{1,0:T(8,128)(2,1)S(1)}, f32[256,256]{1,0:T(8,128)S(1)}, b...) custom-call(bf16[1280,256]{1,0:T(8,128)(2,1)S(1)} %get-tuple-element.43.adj_ref, ...), custom_call_target="tpu_custom_call" | custom-call | flops 402653184 | bytes 393216 | tf_op jit(solution)/shard_map/middle/pallas_call | solution.py:393
  23.2 0.5 %collective-permute-start.4 = (bf16[512,256]{1,0:T(8,128)(2,1)S(1)}, bf16[512,256]{1,0:T(8,128)(2,1)S(1)}, u32[]{:S(2)}, u32[]{:S(2)}) collective-permute-start(bf16[512,256]{1,0:T(8,128)(2,1)S(1)} %get-tuple-element.69), channel_id=1, source_target_pairs={{0,2},{2,0},{1,3},{3,1},{4,6},{6,4},{5,7},{7,5},{8,10},{10,8},{9,1... | collective-permute-start | bytes 786440 | tf_op jit(solution)/shard_map/ppermute | solution.py:409
  23.7 10.8 %all_to_all.11.recv_ref = bf16[32,8,256]{2,1,0:T(8,128)(2,1)S(1)} all-to-all(bf16[32,8,256]{2,1,0:T(8,128)(2,1)S(1)} %get-tuple-element.65), channel_id=1, replica_groups=mesh['hst'=8,'chip'=2,'core'=2] {'hst','chip','core'}, dimensions={0} | all-to-all | bytes 262144 | tf_op jit(solution)/shard_map/all_to_all | solution.py:452
  34.5 0.0 collective-permute-done.4.refs_0_
  34.5 0.3 there.1
  34.8 0.3 collective-permute-start.5
  35.1 1.0 %here.1 = (f32[256,256]{1,0:T(8,128)S(1)}, f32[256,256]{1,0:T(8,128)}) custom-call(bf16[1280,256]{1,0:T(8,128)(2,1)S(1)} %get-tuple-element.43.adj_ref, bf16[256,256]{1,0:T(8,128)(2,1)S(1)} %get-tuple-element.44.far_ref, bf16[256,256]{1,0:T(8,128)(2,1)S(1)} %get-tuple-element.64.sent_ref.value_ref, bf16[32,8,256]{2,1,0:T(8,128)(2,1)S(1)} %all_to_all.11.recv_ref, ...), custom_call_target="tpu_custom_call" | custom-call | flops 234881024 | bytes 229376 | tf_op jit(solution)/shard_map/here/pallas_call | solution.py:393
  36.1 0.1 collective-permute-done.5.there_ref
  36.2 0.7 %last.1 = bf16[256,256]{1,0:T(8,128)(2,1)} custom-call(f32[256,256]{1,0:T(8,128)S(1)} %get-tuple-element.70.here_ref, bf16[256,256]{1,0:T(8,128)(2,1)S(1)} %collective-permute-done.5.there_ref), custom_call_target="tpu_custom_call" | custom-call | tf_op jit(solution)/shard_map/last/pallas_call | solution.py:393
  (6 shorter events, 0.0 us)
Async XLA Ops:
  0.6 2.7 %copy-start.3 = (bf16[256,256]{1,0:T(8,128)(2,1)S(1)}, bf16[256,256]{1,0:T(8,128)(2,1)}, u32[]{:S(2)}) copy-start(bf16[256,256]{1,0:T(8,128)(2,1)} %value_ref.3) | copy-start | bytes 393220
  0.6 2.7 %copy-start = (bf16[256,256]{1,0:T(8,128)(2,1)S(1)}, bf16[256,256]{1,0:T(8,128)(2,1)}, u32[]{:S(2)}) copy-start(bf16[256,256]{1,0:T(8,128)(2,1)} %neigh_ref.7) | copy-start | bytes 393220
  2.8 1.8 %collective-permute-start.1 = (bf16[640,256]{1,0:T(8,128)(2,1)S(1)}, bf16[640,256]{1,0:T(8,128)(2,1)S(1)}, u32[]{:S(2)}, u32[]{:S(2)}) collective-permute-start(bf16[640,256]{1,0:T(8,128)(2,1)S(1)} %get-tuple-element.53), channel_id=1, source_target_pairs={{0,1},{1,0},{2,3},{3,2},{4,5},{5,4},{6,7},{7,6},{8,9},{9,8},{10,11... | collective-permute-start | bytes 983048 | tf_op jit(solution)/shard_map/ppermute | solution.py:409
  3.9 17.1 %collective-permute-start = (bf16[1792,256]{1,0:T(8,128)(2,1)S(1)}, bf16[1792,256]{1,0:T(8,128)(2,1)S(1)}, u32[]{:S(2)}, u32[]{:S(2)}) collective-permute-start(bf16[1792,256]{1,0:T(8,128)(2,1)S(1)} %get-tuple-element.45), channel_id=1, source_target_pairs={{0,1},{1,0},{2,3},{3,2},{4,5},{5,4},{6,7},{7,6},{8,9},{9,8},{10,11... | collective-permute-start | bytes 2752520 | tf_op jit(solution)/shard_map/ppermute | solution.py:409
  4.6 16.5 %copy-start.1 = (bf16[256,256]{1,0:T(8,128)(2,1)S(1)}, bf16[256,256]{1,0:T(8,128)(2,1)}, u32[]{:S(2)}) copy-start(bf16[256,256]{1,0:T(8,128)(2,1)} %weight_ref.3) | copy-start | bytes 393220
  4.6 16.5 %copy-start.2 = (bf16[256,256]{1,0:T(8,128)(2,1)S(1)}, bf16[256,256]{1,0:T(8,128)(2,1)}, u32[]{:S(2)}) copy-start(bf16[256,256]{1,0:T(8,128)(2,1)} %self_ref.3) | copy-start | bytes 393220
  4.6 16.5 %copy-start.5 = (f32[256]{0:T(256)S(1)}, f32[256]{0:T(256)}, u32[]{:S(2)}) copy-start(f32[256]{0:T(256)} %bias_ref.2) | copy-start | bytes 3076
  4.6 17.0 %copy-start.4 = (bf16[256,256]{1,0:T(8,128)(2,1)S(1)}, bf16[256,256]{1,0:T(8,128)(2,1)}, u32[]{:S(2)}) copy-start(bf16[256,256]{1,0:T(8,128)(2,1)} %neigh_two_ref.1) | copy-start | bytes 393220
  4.7 15.9 %collective-permute-start.2 = (bf16[512,256]{1,0:T(8,128)(2,1)S(1)}, bf16[512,256]{1,0:T(8,128)(2,1)S(1)}, u32[]{:S(2)}, u32[]{:S(2)}) collective-permute-start(bf16[512,256]{1,0:T(8,128)(2,1)S(1)} %get-tuple-element.58), channel_id=1, source_target_pairs={{0,2},{2,0},{1,3},{3,1},{4,6},{6,4},{5,7},{7,5},{8,10},{10,8},{9,1... | collective-permute-start | bytes 786440 | tf_op jit(solution)/shard_map/ppermute | solution.py:409
  20.7 1.7 %collective-permute-start.3 = (bf16[640,256]{1,0:T(8,128)(2,1)S(1)}, bf16[640,256]{1,0:T(8,128)(2,1)S(1)}, u32[]{:S(2)}, u32[]{:S(2)}) collective-permute-start(bf16[640,256]{1,0:T(8,128)(2,1)S(1)} %get-tuple-element.60.here_ref), channel_id=1, source_target_pairs={{0,1},{1,0},{2,3},{3,2},{4,5},{5,4},{6,7},{7,6},{8,9},{9,8},{10,11... | collective-permute-start | bytes 983048 | tf_op jit(solution)/shard_map/ppermute | solution.py:409
  22.4 12.7 %copy-start.6 = (f32[256]{0:T(256)S(1)}, f32[256]{0:T(256)}, u32[]{:S(2)}) copy-start(f32[256]{0:T(256)} %bias_ref.3) | copy-start | bytes 3076
  23.2 11.4 %collective-permute-start.4 = (bf16[512,256]{1,0:T(8,128)(2,1)S(1)}, bf16[512,256]{1,0:T(8,128)(2,1)S(1)}, u32[]{:S(2)}, u32[]{:S(2)}) collective-permute-start(bf16[512,256]{1,0:T(8,128)(2,1)S(1)} %get-tuple-element.69), channel_id=1, source_target_pairs={{0,2},{2,0},{1,3},{3,1},{4,6},{6,4},{5,7},{7,5},{8,10},{10,8},{9,1... | collective-permute-start | bytes 786440 | tf_op jit(solution)/shard_map/ppermute | solution.py:409
  34.8 1.4 %collective-permute-start.5 = (bf16[256,256]{1,0:T(8,128)(2,1)S(1)}, bf16[256,256]{1,0:T(8,128)(2,1)S(1)}, u32[]{:S(2)}, u32[]{:S(2)}) collective-permute-start(bf16[256,256]{1,0:T(8,128)(2,1)S(1)} %there.1), channel_id=1, source_target_pairs={{0,1},{1,0},{2,3},{3,2},{4,5},{5,4},{6,7},{7,6},{8,9},{9,8},{10,11... | collective-permute-start | bytes 393224 | tf_op jit(solution)/shard_map/ppermute | solution.py:409
